TPU v7x, 512 devices: a whole 4x8x8 slice. The times are simulated.
512 devices in a mesh: gz: 4 (over x), row: 16 (over y, core), col: 8 (over z).
Axes of the slice: x: 4, y: 8, z: 8, core: 2. Of those that a mesh axis runs over, the one named last changes fastest.
Arguments:
- root_factor: bfloat16 [12288, 12288], P('row', 'col'), may hold values from -1.5 to 1.5
- partials: bfloat16 [4, 128, 12288], P('gz', 'row', 'col'), may hold values from -3 to 3
- pattern: int32 [48, 48], P('row', 'col'), may hold values 0 or 1
- coupling: bfloat16 [4, 6144, 8192], P('gz', 'row', 'col'), may hold values from -0.0390625 to 0.0390625
- child_factor: bfloat16 [4, 8192, 8192], P('gz', 'row', 'col'), may hold values from -1.5 to 1.5
- child_bits: int32 [4, 128, 8192], P('gz', None, 'col'), may hold values from 0 to 1
Outputs:
- root_adjoint: bfloat16 [128, 12288], P(None, 'row')
- child_adjoint: bfloat16 [4, 128, 8192], P('gz', None, 'row')
All inputs are finite; a program needn't handle non-finite values. No bound on the sum of `pattern` on one device may be relied on, other than what follows from the above.
Results may differ from a plain program's by a relative error of at most 0.023.
Values may be sent and summed in bfloat16 or wider, within the bound.
No kernel may reach another device: no remote copies, remote signals or barrier semaphores. Data moves between devices by JAX's collectives and lax.ppermute only.
A program may use at most 64 MiB of HBM per device.

v0:
```python
import jax
import jax.numpy as jnp
from jax import lax
from jax.sharding import PartitionSpec as P

BLK = 256
PANELS = 4
RP = 3072
CP = 2048


def panel_solve(factor_blk, right_cols, panel, row_total, diag_total):
    rows_here = factor_blk.shape[0]
    cols_here = factor_blk.shape[1]
    probes = right_cols.shape[0]
    group = lax.axis_size("row") // PANELS
    row_index = lax.axis_index("row")
    col_index = lax.axis_index("col")
    width = min(cols_here, panel)
    current = jnp.zeros((probes, rows_here), jnp.bfloat16)
    for target in range(PANELS - 1, -1, -1):
        inside = col_index * cols_here // panel == target
        if target == PANELS - 1:
            totals = jnp.zeros((probes, width), jnp.float32)
        else:
            totals = row_total(jnp.dot(current, factor_blk, preferred_element_type=jnp.float32))
        residual = (right_cols - totals).astype(jnp.bfloat16)
        partial_term = lax.dot_general(
            residual, factor_blk, (((1,), (1,)), ((), ())), preferred_element_type=jnp.float32
        )
        partial_term = jnp.where(inside, partial_term, 0.0)
        solved = diag_total(partial_term).astype(jnp.bfloat16)
        current = jnp.where(row_index // group == target, solved, current)
    return current


def root_total(values):
    return lax.psum(values.astype(jnp.bfloat16), "row").astype(jnp.float32)


def child_total(values):
    return lax.psum(values.astype(jnp.bfloat16), "row").astype(jnp.float32)


def root_diag(values):
    return lax.psum(values.astype(jnp.bfloat16), "col").astype(jnp.float32)


def child_diag(values):
    return lax.psum(values.astype(jnp.bfloat16), "col").astype(jnp.float32)


def per_device(root_factor, partials, pattern, coupling, child_factor, child_bits):
    rows_here = root_factor.shape[0]
    cols_here = root_factor.shape[1]
    row_index = lax.axis_index("row")
    col_index = lax.axis_index("col")
    expanded = jnp.repeat(jnp.repeat(pattern, BLK, 0), BLK, 1)
    row_panel = (row_index * rows_here + lax.broadcasted_iota(jnp.int32, (rows_here, 1), 0)) // RP
    col_panel = (col_index * cols_here + lax.broadcasted_iota(jnp.int32, (1, cols_here), 1)) // RP
    keep_mask = jnp.where(row_panel == col_panel, 1, expanded).astype(jnp.bfloat16)
    masked_root = root_factor * keep_mask
    summed = lax.psum(partials[0].astype(jnp.float32).astype(jnp.bfloat16), "gz").astype(
        jnp.float32
    )
    root_rhs = lax.all_gather(summed.astype(jnp.bfloat16), "row", axis=0, tiled=True).astype(
        summed.dtype
    )
    root_rows = panel_solve(masked_root, root_rhs, RP, root_total, root_diag)
    half_rows = root_rows[:, : rows_here // 2]
    coupled = lax.psum(
        jnp.dot(half_rows, coupling[0], preferred_element_type=jnp.float32).astype(jnp.bfloat16),
        "row",
    ).astype(jnp.float32)
    sign_values = (2 * child_bits[0] - 1).astype(jnp.float32)
    child_rhs = sign_values - coupled
    child_rows = panel_solve(child_factor[0], child_rhs, CP, child_total, child_diag)
    return (root_rows, child_rows[None])


def solution(mesh):
    placed = (
        P("row", "col"),
        P("gz", "row", "col"),
        P("row", "col"),
        P("gz", "row", "col"),
        P("gz", "row", "col"),
        P("gz", None, "col"),
    )
    return jax.shard_map(
        per_device,
        mesh=mesh,
        in_specs=placed,
        out_specs=(P(None, "row"), P("gz", None, "row")),
        check_vma=False,
    )
```

profile of v0, /device:TPU:1, one launch (start us, length us, event | category | flops | bytes accessed | tf_op | source)
XLA Modules:
  0.0 1514.5 jit_solution(5851421226377237335)
XLA Ops:
  7.3 4.3 copy.13
  11.7 0.1 copy.12
  11.8 0.1 broadcast_bitcast_fusion
  11.9 14.4 psum.112
  26.3 24.0 %all_gather.3 = bf16[128,1536]{1,0:T(8,128)(2,1)} all-gather(bf16[8,1536]{1,0:T(8,128)(2,1)S(1)} %psum.112), channel_id=1, replica_groups=mesh['gz'=4,'row'=16,'col'=8] {'row'}, dimensions={0}, use_global_device_ids=true | all-gather | bytes 417792 | tf_op jit(solution)/shard_map/all_gather | solution.py:66
  50.3 2.6 fusion.1
  52.9 1.5 fusion.6
  54.4 0.0 all-reduce.18.cloned.1.call-start
  54.5 73.7 %all-reduce.16.cloned.1.call-done = bf16[128,768]{0,1:T(8,128)(2,1)} async-done(((bf16[128,768]{0,1:T(8,128)(2,1)}), bf16[128,768]{0,1:T(8,128)(2,1)}) %all-reduce.16.cloned.1.call-update) | async-done | bytes 196624 | tf_op jit(solution)/shard_map/psum | solution.py:46
  128.2 1.7 convolution_convert_fusion.2
  129.9 0.0 all-reduce.20.cloned.1.call-start
  129.9 117.9 %all-reduce.18.cloned.1.call-done = bf16[128,1536]{1,0:T(8,128)(2,1)} async-done(((bf16[128,1536]{1,0:T(8,128)(2,1)}), bf16[128,1536]{1,0:T(8,128)(2,1)}) %all-reduce.18.cloned.1.call-update) | async-done | bytes 393232 | tf_op jit(solution)/shard_map/psum | solution.py:38
  247.8 2.8 fusion.3
  250.6 0.0 all-reduce.22.cloned.1.call-start
  250.7 74.7 %all-reduce.20.cloned.1.call-done = bf16[128,768]{0,1:T(8,128)(2,1)} async-done(((bf16[128,768]{0,1:T(8,128)(2,1)}), bf16[128,768]{0,1:T(8,128)(2,1)}) %all-reduce.20.cloned.1.call-update) | async-done | bytes 196624 | tf_op jit(solution)/shard_map/psum | solution.py:46
  325.5 0.7 copy-done.4
  326.1 1.7 convolution_convert_fusion.1
  327.8 0.0 all-reduce.24.cloned.1.call-start
  327.9 118.2 %all-reduce.22.cloned.1.call-done = bf16[128,1536]{1,0:T(8,128)(2,1)} async-done(((bf16[128,1536]{1,0:T(8,128)(2,1)}), bf16[128,1536]{1,0:T(8,128)(2,1)}) %all-reduce.22.cloned.1.call-update) | async-done | bytes 393232 | tf_op jit(solution)/shard_map/psum | solution.py:38
  446.1 2.8 fusion.4
  448.9 0.0 all-reduce.26.cloned.1.call-start
  449.0 74.7 %all-reduce.24.cloned.1.call-done = bf16[128,768]{0,1:T(8,128)(2,1)} async-done(((bf16[128,768]{0,1:T(8,128)(2,1)}), bf16[128,768]{0,1:T(8,128)(2,1)}) %all-reduce.24.cloned.1.call-update) | async-done | bytes 196624 | tf_op jit(solution)/shard_map/psum | solution.py:46
  523.7 2.6 convolution_convert_fusion
  526.4 0.0 all-reduce.28.cloned.1.call-start
  526.4 117.3 %all-reduce.26.cloned.1.call-done = bf16[128,1536]{1,0:T(8,128)(2,1)} async-done(((bf16[128,1536]{1,0:T(8,128)(2,1)}), bf16[128,1536]{1,0:T(8,128)(2,1)}) %all-reduce.26.cloned.1.call-update) | async-done | bytes 393232 | tf_op jit(solution)/shard_map/psum | solution.py:38
  643.7 2.8 fusion.5
  646.6 74.7 %all-reduce.28.cloned.1.call-done = bf16[128,768]{0,1:T(8,128)(2,1)} async-done(((bf16[128,768]{0,1:T(8,128)(2,1)}), bf16[128,768]{0,1:T(8,128)(2,1)}) %all-reduce.28.cloned.1.call-update) | async-done | bytes 196624 | tf_op jit(solution)/shard_map/psum | solution.py:46
  721.3 1.1 broadcast_select_fusion.3
  722.4 2.2 convolution_convert_fusion.6
  724.6 116.5 %all-reduce.30.cloned.1.call-done = bf16[128,1024]{1,0:T(8,128)(2,1)} async-done(((bf16[128,1024]{1,0:T(8,128)(2,1)}), bf16[128,1024]{1,0:T(8,128)(2,1)}) %all-reduce.30.cloned.1.call-update) | async-done | bytes 262160 | tf_op jit(solution)/shard_map/psum | solution.py:71
  841.1 2.2 fusion.7
  843.4 75.0 %all-reduce.32.cloned.1.call-done = bf16[128,512]{1,0:T(8,128)(2,1)} async-done(((bf16[128,512]{1,0:T(8,128)(2,1)}), bf16[128,512]{1,0:T(8,128)(2,1)}) %all-reduce.32.cloned.1.call-update) | async-done | bytes 131088 | tf_op jit(solution)/shard_map/psum | solution.py:50
  918.4 1.0 convolution_convert_fusion.5
  919.5 117.7 %all-reduce.34.cloned.1.call-done = bf16[128,1024]{1,0:T(8,128)(2,1)} async-done(((bf16[128,1024]{1,0:T(8,128)(2,1)}), bf16[128,1024]{1,0:T(8,128)(2,1)}) %all-reduce.34.cloned.1.call-update) | async-done | bytes 262160 | tf_op jit(solution)/shard_map/psum | solution.py:42
  1037.2 2.1 fusion.8
  1039.3 75.1 %all-reduce.36.cloned.1.call-done = bf16[128,512]{1,0:T(8,128)(2,1)} async-done(((bf16[128,512]{1,0:T(8,128)(2,1)}), bf16[128,512]{1,0:T(8,128)(2,1)}) %all-reduce.36.cloned.1.call-update) | async-done | bytes 131088 | tf_op jit(solution)/shard_map/psum | solution.py:50
  1114.5 1.0 convolution_convert_fusion.4
  1115.6 117.7 %all-reduce.38.cloned.1.call-done = bf16[128,1024]{1,0:T(8,128)(2,1)} async-done(((bf16[128,1024]{1,0:T(8,128)(2,1)}), bf16[128,1024]{1,0:T(8,128)(2,1)}) %all-reduce.38.cloned.1.call-update) | async-done | bytes 262160 | tf_op jit(solution)/shard_map/psum | solution.py:42
  1233.2 2.1 fusion.9
  1235.3 0.0 all-reduce.42.cloned.1.call-start
  1235.4 75.1 %all-reduce.40.cloned.1.call-done = bf16[128,512]{1,0:T(8,128)(2,1)} async-done(((bf16[128,512]{1,0:T(8,128)(2,1)}), bf16[128,512]{1,0:T(8,128)(2,1)}) %all-reduce.40.cloned.1.call-update) | async-done | bytes 131088 | tf_op jit(solution)/shard_map/psum | solution.py:50
  1310.5 1.0 convolution_convert_fusion.3
  1311.5 0.0 all-reduce.44.cloned.1.call-start
  1311.6 117.7 %all-reduce.42.cloned.1.call-done = bf16[128,1024]{1,0:T(8,128)(2,1)} async-done(((bf16[128,1024]{1,0:T(8,128)(2,1)}), bf16[128,1024]{1,0:T(8,128)(2,1)}) %all-reduce.42.cloned.1.call-update) | async-done | bytes 262160 | tf_op jit(solution)/shard_map/psum | solution.py:42
  1429.3 2.1 fusion.10
  1431.4 0.8 copy.17
  1432.2 74.2 %all-reduce.44.cloned.1.call-done = bf16[128,512]{1,0:T(8,128)(2,1)} async-done(((bf16[128,512]{1,0:T(8,128)(2,1)}), bf16[128,512]{1,0:T(8,128)(2,1)}) %all-reduce.44.cloned.1.call-update) | async-done | bytes 131088 | tf_op jit(solution)/shard_map/psum | solution.py:50
  1506.4 1.6 select_bitcast_fusion
  (44 shorter events, 0.7 us)
Async XLA Ops:
  7.2 834.0 %copy-start = (bf16[1,512,1024]{2,1,0:T(8,128)(2,1)S(1)}, bf16[1,512,1024]{2,1,0:T(8,128)(2,1)}, u32[]{:S(2)}) copy-start(bf16[1,512,1024]{2,1,0:T(8,128)(2,1)} %param.10) | copy-start | bytes 3145732
  7.2 121.0 %all-reduce.16.cloned.1.call-start = ((), (), s32[]{:S(2)}) async-start(), calls=%async_computation | async-start | bytes 393216 | tf_op jit(solution)/shard_map/psum | solution.py:46
  7.3 4.4 copy-start.8
  7.3 4.5 copy-start.7
  50.3 2.6 copy-start.2
  54.4 193.3 %all-reduce.18.cloned.1.call-start = ((), (), s32[]{:S(2)}) async-start(), calls=%async_computation.1 | async-start | bytes 786432 | tf_op jit(solution)/shard_map/psum | solution.py:38
  129.9 195.6 %all-reduce.20.cloned.1.call-start = ((), (), s32[]{:S(2)}) async-start(), calls=%async_computation.2 | async-start | bytes 393216 | tf_op jit(solution)/shard_map/psum | solution.py:46
  250.6 195.5 %all-reduce.22.cloned.1.call-start = ((), (), s32[]{:S(2)}) async-start(), calls=%async_computation.3 | async-start | bytes 786432 | tf_op jit(solution)/shard_map/psum | solution.py:38
  325.5 0.7 copy-start.4
  327.8 195.9 %all-reduce.24.cloned.1.call-start = ((), (), s32[]{:S(2)}) async-start(), calls=%async_computation.4 | async-start | bytes 393216 | tf_op jit(solution)/shard_map/psum | solution.py:46
  448.9 194.7 %all-reduce.26.cloned.1.call-start = ((), (), s32[]{:S(2)}) async-start(), calls=%async_computation.5 | async-start | bytes 786432 | tf_op jit(solution)/shard_map/psum | solution.py:38
  526.4 195.0 %all-reduce.28.cloned.1.call-start = ((), (), s32[]{:S(2)}) async-start(), calls=%async_computation.6 | async-start | bytes 393216 | tf_op jit(solution)/shard_map/psum | solution.py:46
  646.5 194.6 %copy-start.1 = (s32[1,128,1024]{2,1,0:T(8,128)S(1)}, s32[1,128,1024]{2,1,0:T(8,128)}, u32[]{:S(2)}) copy-start(s32[1,128,1024]{2,1,0:T(8,128)} %param.11) | copy-start | bytes 1572868
  646.5 194.6 %all-reduce.30.cloned.1.call-start = ((), (), s32[]{:S(2)}) async-start(), calls=%async_computation.7 | async-start | bytes 524288 | tf_op jit(solution)/shard_map/psum | solution.py:71
  724.6 193.8 %all-reduce.32.cloned.1.call-start = ((), (), s32[]{:S(2)}) async-start(), calls=%async_computation.8 | async-start | bytes 262144 | tf_op jit(solution)/shard_map/psum | solution.py:50
  841.1 196.1 %copy-start.3 = (bf16[128,1024]{1,0:T(8,128)(2,1)S(1)}, bf16[128,1024]{1,0:T(8,128)(2,1)}, u32[]{:S(2)}) copy-start(bf16[128,1024]{1,0:T(8,128)(2,1)} %all-reduce.30.cloned.1.call-done) | copy-start | bytes 786436
  843.3 193.9 %all-reduce.34.cloned.1.call-start = ((), (), s32[]{:S(2)}) async-start(), calls=%async_computation.9 | async-start | bytes 524288 | tf_op jit(solution)/shard_map/psum | solution.py:42
  918.4 196.1 %copy-start.6 = (bf16[128,512]{1,0:T(8,128)(2,1)S(1)}, bf16[128,512]{1,0:T(8,128)(2,1)}, u32[]{:S(2)}) copy-start(bf16[128,512]{1,0:T(8,128)(2,1)} %all-reduce.32.cloned.1.call-done) | copy-start | bytes 393220
  919.4 195.0 %all-reduce.36.cloned.1.call-start = ((), (), s32[]{:S(2)}) async-start(), calls=%async_computation.10 | async-start | bytes 262144 | tf_op jit(solution)/shard_map/psum | solution.py:50
  1039.3 193.9 %all-reduce.38.cloned.1.call-start = ((), (), s32[]{:S(2)}) async-start(), calls=%async_computation.11 | async-start | bytes 524288 | tf_op jit(solution)/shard_map/psum | solution.py:42
  1115.5 195.0 %all-reduce.40.cloned.1.call-start = ((), (), s32[]{:S(2)}) async-start(), calls=%async_computation.12 | async-start | bytes 262144 | tf_op jit(solution)/shard_map/psum | solution.py:50
  1235.3 193.9 %all-reduce.42.cloned.1.call-start = ((), (), s32[]{:S(2)}) async-start(), calls=%async_computation.13 | async-start | bytes 524288 | tf_op jit(solution)/shard_map/psum | solution.py:42
  1310.5 195.9 %copy-start.5 = (bf16[128,512]{1,0:T(8,128)(2,1)S(1)}, bf16[128,512]{1,0:T(8,128)(2,1)}, u32[]{:S(2)}) copy-start(bf16[128,512]{1,0:T(8,128)(2,1)} %all-reduce.40.cloned.1.call-done) | copy-start | bytes 393220
  1311.5 194.9 %all-reduce.44.cloned.1.call-start = ((), (), s32[]{:S(2)}) async-start(), calls=%async_computation.14 | async-start | bytes 262144 | tf_op jit(solution)/shard_map/psum | solution.py:50
Sparse Core Ops, SparseCore 0:
  54.6 73.5 all-reduce.15
  130.6 117.1 all-reduce.17
  250.7 74.6 all-reduce.19
  328.0 118.0 all-reduce.21
  449.1 74.6 all-reduce.23
  526.5 117.1 all-reduce.25
  646.6 74.6 all-reduce.27
  724.7 116.3 all-reduce.29
  844.0 74.3 all-reduce.31
  920.7 116.4 all-reduce.33
  1040.1 74.3 all-reduce.35
  1116.7 116.4 all-reduce.37
  1236.1 74.3 all-reduce.39
  1312.7 116.4 all-reduce.41
  1432.0 74.3 all-reduce.43
where the time goes:
time: 1520 us; the launch traced here: 1510 us
  waiting for transfers between devices  1420 us (93%)
  blocking collectives  38.4 us (3%)
  matrix products  29.6 us (2%)
    psum x3, waiting for transfers between devices, root_total(): return lax.psum(values.astype(jnp.bfloat16), 'row').astype(jnp.float32)  353 us
    psum x3, waiting for transfers between devices, child_total(): return lax.psum(values.astype(jnp.bfloat16), 'row').astype(jnp.float32)  353 us
    psum x4, waiting for transfers between devices, child_diag(): return lax.psum(values.astype(jnp.bfloat16), 'col').astype(jnp.float32)  299 us
    psum x4, waiting for transfers between devices, root_diag(): return lax.psum(values.astype(jnp.bfloat16), 'col').astype(jnp.float32)  298 us
    psum x1, waiting for transfers between devices, per_device(): lax.psum(jnp.dot(half_rows, coupling[0], preferred_element_type=jnp.float...  116 us
  transfers between devices with their start and end apart: 15, of which 15 were waited for; matrix products, arithmetic and copies ran while one was open for 0% of the time, Pallas kernels for 0%

commit v1 on v0

v1 whole, which is shorter than its diff:
```python
import jax
import jax.numpy as jnp
from jax import lax
from jax.sharding import PartitionSpec as P

PANELS = 4
GROUP = 4
PAIR = 2
ROWS = PANELS * GROUP
COLS = PANELS * PAIR
GRID = ("row", "col")
F32 = jnp.float32
BF16 = jnp.bfloat16


def dot(a, b):
    return jnp.dot(a, b, preferred_element_type=F32)


def dot_t(a, b):
    return lax.dot_general(a, b, (((1,), (1,)), ((), ())), preferred_element_type=F32)


def send(value, moves):
    pairs = []
    for rows, to_rows, row_flip, cols, to_cols, col_flip in moves:
        for j in range(GROUP):
            for q in range(PAIR):
                source = (rows * GROUP + j) * COLS + cols * PAIR + q
                target = (to_rows * GROUP + (j ^ row_flip)) * COLS + to_cols * PAIR + (q ^ col_flip)
                pairs.append((source, target))
    return lax.ppermute(value, GRID, pairs).astype(F32)


def sweep(rhs, forward, diagonal, width, split_rows):
    row_panel = lax.axis_index("row") // GROUP
    col_panel = lax.axis_index("col") // PAIR
    current = jnp.zeros((rhs.shape[0], width), BF16)
    carried = jnp.zeros(rhs.shape, F32)
    totals = jnp.zeros(rhs.shape, F32)
    for r in range(PANELS - 1, -1, -1):
        ahead = None
        if r < PANELS - 1:
            terms = (forward(current) + carried).astype(BF16)
            down = [(r + 1, r, 0, r, r, 0)]
            if r == 1:
                down.append((3, 2, 0, 0, 0, 0))
            first = send(terms, down)
            totals = first
            if split_rows:
                totals = totals + send(terms, [(r + 1, r, 2, r, r, 0)])
            if r >= 1:
                ahead = send(current, [(r + 1, r + 1, 0, r, r - 1, 0)])
            carried = carried + first
        residual = (rhs - totals).astype(BF16)
        piece = diagonal(residual).astype(BF16)
        current = jnp.where((row_panel == r) & (col_panel == r), piece, current)
        if ahead is not None:
            current = (current.astype(F32) + ahead).astype(BF16)
        if r >= 1:
            straight = [(r, r, 0, r, r - 1, 0)]
            crossed = [(r, r, 0, r, r - 1, 1)]
            if r == 2:
                straight.append((3, 3, 0, 1, 0, 0))
                crossed.append((3, 3, 0, 3, 3, 1))
            if r == 1:
                straight.append((2, 2, 0, 0, 3, 0))
                crossed.append((2, 2, 0, 2, 2, 1))
            received = send(current, straight) + send(current, crossed)
            if r < PANELS - 1:
                terms = (forward(current) + carried).astype(BF16)
                carried = carried + send(terms, [(r + 1, r, 0, r - 1, r - 1, 0)])
            current = (current.astype(F32) + received).astype(BF16)
        else:
            received = send(current, [(0, 0, 0, 0, 3, 0), (1, 1, 0, 0, 3, 0)])
            received = received + send(current, [(0, 0, 0, 0, 3, 1), (1, 1, 0, 1, 1, 1)])
            received = received + send(current, [(0, 0, 0, 0, 0, 1)])
            current = (current.astype(F32) + received).astype(BF16)
            received = send(current, [(0, 0, 0, 0, 1, 0), (0, 0, 0, 3, 2, 0), (1, 1, 0, 3, 2, 0)])
            current = (current.astype(F32) + received).astype(BF16)
    return current


def per_device(root_factor, partials, pattern, coupling, child_factor, child_bits):
    layers = lax.axis_size("gz")
    rows_here, cols_here = root_factor.shape
    row_index = lax.axis_index("row")
    col_index = lax.axis_index("col")
    core = row_index % 2
    quarters = [[s * GROUP + j for j in range(GROUP)] for s in range(PANELS)]
    across = [[s * GROUP + j for s in range(PANELS)] for j in range(GROUP)]
    chips = [
        [g * ROWS + 2 * y + k for g in range(layers) for k in range(2)] for y in range(ROWS // 2)
    ]

    with jax.named_scope("mask"):
        block = rows_here // pattern.shape[0]
        expanded = jnp.repeat(jnp.repeat(pattern, block, 0), block, 1)
        on_diagonal = row_index // GROUP == col_index // PAIR
        masked_root = root_factor * jnp.where(on_diagonal, 1, expanded).astype(BF16)
        partner_root = lax.ppermute(masked_root, "row", [(i, i ^ 1) for i in range(ROWS)])

    with jax.named_scope("child_gather"):
        child_panel = lax.all_gather(
            child_factor[0], "row", axis=0, tiled=True, axis_index_groups=quarters
        )

    with jax.named_scope("rhs"):
        probes_here = partials.shape[1]
        lanes = cols_here // 12
        pieces = partials[0].reshape(layers, 1, 2, 12, lanes)
        pieces = jnp.broadcast_to(pieces, (layers, ROWS // 2, 2, 12, lanes))
        pieces = lax.all_to_all(
            pieces.reshape(layers * ROWS, 12, lanes), ("gz", "row"), 0, 0, tiled=True
        )
        root_rhs = jnp.sum(pieces.astype(F32).reshape(layers, ROWS, 12 * lanes), 0)
        root_rhs = root_rhs.astype(BF16).astype(F32)

    with jax.named_scope("root"):
        root_rows = sweep(
            root_rhs,
            lambda x: dot(x[:, :rows_here], masked_root) + dot(x[:, rows_here:], partner_root),
            lambda x: jnp.concatenate([dot_t(x, masked_root), dot_t(x, partner_root)], 1),
            2 * rows_here,
            True,
        )

    with jax.named_scope("coupling"):
        own, other = root_rows[:, :rows_here], root_rows[:, rows_here:]
        by_core = jnp.stack([jnp.where(core == k, own, other) for k in range(2)])
        shared = jnp.broadcast_to(by_core[None], (layers,) + by_core.shape)
        shared = shared.reshape(layers * 2 * ROWS, rows_here)
        shared = lax.all_to_all(shared, ("gz", "row"), 0, 0, tiled=True, axis_index_groups=chips)
        root_all = shared.reshape(layers * 2, ROWS, rows_here).transpose(1, 0, 2)
        root_all = root_all.reshape(layers * 2 * ROWS, rows_here)
        coupled = dot(root_all[:, : rows_here // 2], coupling[0]).astype(BF16)
        coupled = lax.all_to_all(coupled, "row", 0, 0, tiled=True, axis_index_groups=quarters)
        share = coupled.shape[0] // GROUP
        coupled = jnp.sum(coupled.reshape(GROUP, share, -1).astype(F32), 0).astype(BF16)
        coupled = lax.all_gather(coupled, "row", axis=0, axis_index_groups=across)
        coupled = jnp.sum(coupled.astype(F32), 0)
        bits = lax.dynamic_slice_in_dim(child_bits[0], row_index % GROUP * share, share, 0)
        child_rhs = (2 * bits - 1).astype(F32) - coupled

    with jax.named_scope("child"):
        child_rows = sweep(
            child_rhs,
            lambda x: dot(x, child_panel),
            lambda x: dot_t(x, child_panel),
            child_panel.shape[0],
            False,
        )
        child_rows = child_rows.reshape(share, GROUP, -1).transpose(1, 0, 2)
        child_rows = child_rows.reshape(GROUP * share, -1)
        child_rows = lax.all_to_all(child_rows, "row", 0, 0, tiled=True, axis_index_groups=quarters)
    return (root_all, child_rows[None])


def solution(mesh):
    placed = (
        P("row", "col"),
        P("gz", "row", "col"),
        P("row", "col"),
        P("gz", "row", "col"),
        P("gz", "row", "col"),
        P("gz", None, "col"),
    )
    return jax.shard_map(
        per_device,
        mesh=mesh,
        in_specs=placed,
        out_specs=(P(None, "row"), P("gz", None, "row")),
        check_vma=False,
    )
```

time: 1520 us -> 251 us (0.17)
  waiting for transfers between devices: 1420 us -> 90 us
  starting transfers between devices: 0.63 us -> 52.6 us
    psum x15 -> x0, waiting for transfers between devices: 1420 us -> none  [the longest x3 353 us: root_total(): return lax.psum(values.astype(jnp.bfloat16), 'row').astype(jnp.float32)]
    ppermute x0 -> x38, waiting for transfers between devices: none -> 72.9 us  [the longest x37 72.9 us: send(): return lax.ppermute(value, GRID, pairs).astype(F32)]
    ppermute x0 -> x38, starting transfers between devices: none -> 42.6 us  [the longest x37 33.8 us: send(): return lax.ppermute(value, GRID, pairs).astype(F32)]
    all_to_all x0 -> x2, blocking collectives: none -> 30.8 us  [the longest x1 15.8 us: per_device(): lax.all_to_all(child_rows, 'row', 0, 0, tiled=True, axis_index_groups=qua...]
    all_to_all x0 -> x2, waiting for transfers between devices: none -> 17.1 us  [the longest x1 11.9 us: per_device(): lax.all_to_all(pieces.reshape(layers * ROWS, 12, lanes), ('gz', 'row'), 0...]
    dot_general x15 -> x28, matrix products: 29.6 us -> 38.4 us  [the longest x16 20.7 us: dot(): return jnp.dot(a, b, preferred_element_type=F32)]
  transfers between devices with their start and end apart: 15 -> 41, of which waited for: 15 -> 11; matrix products, arithmetic and copies ran while one was open for 0% -> 10% of each run, Pallas kernels for 0% -> 0%
where the time goes in v1:
time: 251 us; the launch traced here: 249 us
  waiting for transfers between devices  90 us (36%)
  starting transfers between devices  52.6 us (21%)
  blocking collectives  42.3 us (17%)
  matrix products  38.4 us (15%)
  between operations  14.9 us (6%)
  local copies, waits for them, and re-layouts  6.83 us (3%)
  other arithmetic  4.24 us (2%)
    ppermute x37, waiting for transfers between devices, send(): return lax.ppermute(value, GRID, pairs).astype(F32)  72.9 us
    ppermute x37, starting transfers between devices, send(): return lax.ppermute(value, GRID, pairs).astype(F32)  33.8 us
    dot_general x16, matrix products, dot(): return jnp.dot(a, b, preferred_element_type=F32)  20.7 us
    dot_general x12, matrix products, dot_t(): lax.dot_general(a, b, (((1,), (1,)), ((), ())), preferred_element_type=F32)  17.7 us
    all_to_all x1, blocking collectives, per_device(): lax.all_to_all(child_rows, 'row', 0, 0, tiled=True, axis_index_groups=qua...  15.8 us
    all_to_all x1, blocking collectives, per_device(): lax.all_to_all(shared, ('gz', 'row'), 0, 0, tiled=True, axis_index_groups...  15 us
    all_to_all x1, waiting for transfers between devices, per_device(): lax.all_to_all(pieces.reshape(layers * ROWS, 12, lanes), ('gz', 'row'), 0...  11.9 us
    all_gather x1, blocking collectives, per_device(): coupled = lax.all_gather(coupled, 'row', axis=0, axis_index_groups=across)  11.5 us
  transfers between devices with their start and end apart: 41, of which 11 were waited for; matrix products, arithmetic and copies ran while one was open for 10% of the time, Pallas kernels for 0%

profile of v1, /device:TPU:1, one launch (start us, length us, event | category | flops | bytes accessed | tf_op | source)
XLA Modules:
  0.0 249.3 jit_solution(15593079429163930574)
XLA Ops:
  7.4 4.3 %copy.22 = bf16[768,1536]{0,1:T(8,128)(2,1)} copy(bf16[768,1536]{1,0:T(8,128)(2,1)} %param.6) | data formatting | bytes 4718592 | tf_op args[0]
  11.7 1.8 bitcast_multiply_fusion
  13.5 8.8 %collective-permute-start = (bf16[768,1536]{0,1:T(8,128)(2,1)S(1)}, bf16[768,1536]{0,1:T(8,128)(2,1)}, u32[]{:S(2)}, u32[]{:S(2)}) collective-permute-start(bf16[768,1536]{0,1:T(8,128)(2,1)S(1)} %bitcast_multiply_fusion), channel_id=1, source_target_pairs={{0,8},{8,0},{16,24},{24,16},{32,40},{40,32},{48,56},{56,48},{64,72... | collective-permute-start | bytes 7077896 | tf_op jit(solution)/shard_map/mask/ppermute | solution.py:101
  23.1 5.6 %all-to-all-start = ((bf16[64,12,128]{2,1,0:T(8,128)(2,1)}), bf16[64,12,128]{2,1,0:T(8,128)(2,1)S(1)}, u32[]{:S(2)}, u32[]{:S(2)}) async-start(bf16[64,12,128]{2,1,0:T(8,128)(2,1)} %bitcast.124), calls=%async_computation | async-start | bytes 524288 | tf_op jit(solution)/shard_map/rhs/all_to_all | solution.py:113
  28.8 11.9 %all-to-all-done = bf16[64,12,128]{2,1,0:T(8,128)(2,1)S(1)} async-done(((bf16[64,12,128]{2,1,0:T(8,128)(2,1)}), bf16[64,12,128]{2,1,0:T(8,128)(2,1)S(1)}, u32[]{:S(2)}, u32[]{:S(2)}) %all-to-all-start) | async-done | bytes 196640 | tf_op jit(solution)/shard_map/rhs/all_to_all | solution.py:113
  41.5 1.0 reduce.2
  42.9 2.1 convolution_convert_fusion.7
  47.1 2.4 fusion.64
  52.0 2.1 convolution_convert_fusion.5
  55.5 2.4 fusion.112
  60.0 2.4 fusion.65
  64.9 2.1 convolution_convert_fusion.3
  68.4 2.4 fusion.106
  72.9 2.4 fusion.67
  75.3 1.3 collective-permute-start.15
  76.6 1.3 collective-permute-start.16
  77.9 25.7 %collective-permute-done.15 = bf16[16,1536]{1,0:T(8,128)(2,1)S(1)} collective-permute-done((bf16[16,1536]{1,0:T(8,128)(2,1)S(1)}, bf16[16,1536]{1,0:T(8,128)(2,1)S(1)}, u32[]{:S(2)}, u32[]{:S(2)}) %collective-permute-start.15) | collective-permute-done | bytes 49184 | tf_op jit(solution)/shard_map/root/ppermute | solution.py:32
  103.7 4.1 %collective-permute-done.16 = bf16[16,1536]{1,0:T(8,128)(2,1)S(1)} collective-permute-done((bf16[16,1536]{1,0:T(8,128)(2,1)S(1)}, bf16[16,1536]{1,0:T(8,128)(2,1)S(1)}, u32[]{:S(2)}, u32[]{:S(2)}) %collective-permute-start.16) | collective-permute-done | bytes 49184 | tf_op jit(solution)/shard_map/root/ppermute | solution.py:32
  108.2 2.1 convolution_convert_fusion.1
  110.3 1.3 collective-permute-start.17
  111.6 1.3 collective-permute-start.18
  112.9 1.9 collective-permute-start.19
  114.9 3.6 %collective-permute-done.19 = bf16[16,1536]{1,0:T(8,128)(2,1)S(1)} collective-permute-done((bf16[16,1536]{1,0:T(8,128)(2,1)S(1)}, bf16[16,1536]{1,0:T(8,128)(2,1)S(1)}, u32[]{:S(2)}, u32[]{:S(2)}) %collective-permute-start.19) | collective-permute-done | bytes 49184 | tf_op jit(solution)/shard_map/root/ppermute | solution.py:32
  118.6 1.3 collective-permute-start.20
  119.9 1.3 collective-permute-done.20
  121.3 15.0 %all_to_all.29 = bf16[8,16,768]{2,1,0:T(8,128)(2,1)S(1)} all-to-all(bf16[8,16,768]{2,1,0:T(8,128)(2,1)S(1)} %bitcast.125), channel_id=1, replica_groups={{0,8,128,136,256,264,384,392},{16,24,144,152,272,280,400,408},{32,40,16..., dimensions={0} | all-to-all | bytes 393216 | tf_op jit(solution)/shard_map/coupling/all_to_all | solution.py:133
  136.3 1.0 convolution_convert_fusion
  137.4 4.3 %all-to-all-start.2 = ((bf16[4,32,1024]{2,1,0:T(8,128)(2,1)}), bf16[4,32,1024]{2,1,0:T(8,128)(2,1)S(1)}, u32[]{:S(2)}, u32[]{:S(2)}) async-start(bf16[4,32,1024]{2,1,0:T(8,128)(2,1)} %bitcast.10), calls=%async_computation.2 | async-start | bytes 524288 | tf_op jit(solution)/shard_map/coupling/all_to_all | solution.py:137
  141.7 5.2 %all-to-all-done.2 = bf16[4,32,1024]{2,1,0:T(8,128)(2,1)S(1)} async-done(((bf16[4,32,1024]{2,1,0:T(8,128)(2,1)}), bf16[4,32,1024]{2,1,0:T(8,128)(2,1)S(1)}, u32[]{:S(2)}, u32[]{:S(2)}) %all-to-all-start.2) | async-done | bytes 262176 | tf_op jit(solution)/shard_map/coupling/all_to_all | solution.py:137
  146.9 11.5 %all-gather = bf16[128,1024]{1,0:T(8,128)(2,1)S(1)} all-gather(bf16[32,1024]{1,0:T(8,128)(2,1)S(1)} %reduce_sum.31), channel_id=2, replica_groups={{0,32,64,96},{8,40,72,104},{16,48,80,112},{24,56,88,120},{1,33,65,97},{..., dimensions={0}, use_global_device_ids=true | all-gather | bytes 327680 | tf_op jit(solution)/shard_map/coupling/all_gather | solution.py:140
  158.5 0.9 bitcast_subtract_fusion
  159.4 3.7 %fusion.61 = bf16[32,2048]{1,0:T(8,128)(2,1)S(1)} fusion(bf16[1,2048,1024]{2,1,0:T(8,128)(2,1)} %all-gather.4.cloned.1.call-done, pred[]{:T(512)S(6)} %and.46, f32[32,1024]{1,0:T(8,128)S(1)} %bitcast_subtract_fusion), kind=kOutput, calls=%fused_computation.41 | convolution fusion | flops 134381568 | bytes 4456449 | tf_op jit(solution)/shard_map/child/dot_general | solution.py:21
  166.1 0.8 collective-permute-start.23
  167.0 1.3 fusion.58
  173.4 1.3 fusion.46
  176.1 0.8 fusion.81
  177.7 0.8 fusion.84
  178.5 1.3 collective-permute-start.33
  179.8 33.2 %collective-permute-done.33 = bf16[32,1024]{1,0:T(8,128)(2,1)S(1)} collective-permute-done((bf16[32,1024]{1,0:T(8,128)(2,1)S(1)}, bf16[32,1024]{1,0:T(8,128)(2,1)S(1)}, u32[]{:S(2)}, u32[]{:S(2)}) %collective-permute-start.33) | collective-permute-done | bytes 65568 | tf_op jit(solution)/shard_map/child/ppermute | solution.py:32
  212.9 1.3 fusion.34
  214.3 1.3 collective-permute-start.34
  215.6 1.3 collective-permute-start.35
  216.9 2.8 %collective-permute-start.36 = (bf16[32,2048]{1,0:T(8,128)(2,1)S(1)}, bf16[32,2048]{1,0:T(8,128)(2,1)S(1)}, u32[]{:S(2)}, u32[]{:S(2)}) collective-permute-start(bf16[32,2048]{1,0:T(8,128)(2,1)S(1)} %fusion.34), channel_id=1, source_target_pairs={{0,1},{1,0},{8,9},{9,8},{16,17},{17,16},{24,25},{25,24},{128,129},... | collective-permute-start | bytes 393224 | tf_op jit(solution)/shard_map/child/ppermute | solution.py:32
  220.3 1.4 collective-permute-done.35
  221.7 0.9 collective-permute-done.36
  222.7 1.3 collective-permute-start.37
  224.0 1.9 collective-permute-done.37
  226.0 15.8 %all_to_all.30 = bf16[4,32,512]{2,1,0:T(8,128)(2,1)S(1)} all-to-all(bf16[4,32,512]{2,1,0:T(8,128)(2,1)S(1)} %bitcast.127), channel_id=1, replica_groups={{0,8,16,24},{32,40,48,56},{64,72,80,88},{96,104,112,120},{1,9,17,25},{3..., dimensions={0} | all-to-all | bytes 262144 | tf_op jit(solution)/shard_map/child/all_to_all | solution.py:155
  (106 shorter events, 28.2 us)
Async XLA Ops:
  7.2 129.2 %copy-start = (bf16[1,384,1024]{2,1,0:T(8,128)(2,1)S(1)}, bf16[1,384,1024]{2,1,0:T(8,128)(2,1)}, u32[]{:S(2)}) copy-start(bf16[1,384,1024]{2,1,0:T(8,128)(2,1)} %param.9) | copy-start | bytes 2359300
  11.7 10.6 %copy-start.3 = (bf16[1,8,1536]{2,1,0:T(8,128)(2,1)S(1)}, bf16[1,8,1536]{2,1,0:T(8,128)(2,1)}, u32[]{:S(2)}) copy-start(bf16[1,8,1536]{2,1,0:T(8,128)(2,1)} %param.7) | copy-start | bytes 73732
  13.5 29.4 %collective-permute-start = (bf16[768,1536]{0,1:T(8,128)(2,1)S(1)}, bf16[768,1536]{0,1:T(8,128)(2,1)}, u32[]{:S(2)}, u32[]{:S(2)}) collective-permute-start(bf16[768,1536]{0,1:T(8,128)(2,1)S(1)} %bitcast_multiply_fusion), channel_id=1, source_target_pairs={{0,8},{8,0},{16,24},{24,16},{32,40},{40,32},{48,56},{56,48},{64,72... | collective-permute-start | bytes 7077896 | tf_op jit(solution)/shard_map/mask/ppermute | solution.py:101
  23.1 17.6 %all-to-all-start = ((bf16[64,12,128]{2,1,0:T(8,128)(2,1)}), bf16[64,12,128]{2,1,0:T(8,128)(2,1)S(1)}, u32[]{:S(2)}, u32[]{:S(2)}) async-start(bf16[64,12,128]{2,1,0:T(8,128)(2,1)} %bitcast.124), calls=%async_computation | async-start | bytes 524288 | tf_op jit(solution)/shard_map/rhs/all_to_all | solution.py:113
  28.7 130.7 %all-gather.4.cloned.1.call-start = ((), (), s32[]{:S(2)}) async-start(), calls=%async_computation.4 | async-start | bytes 5242880 | tf_op jit(solution)/shard_map/child_gather/all_gather | solution.py:104
  45.0 1.3 collective-permute-start.1
  45.7 0.7 collective-permute-start.2
  49.5 2.0 collective-permute-start.3
  50.2 1.4 collective-permute-start.4
  50.9 3.2 %collective-permute-start.5 = (bf16[16,1536]{1,0:T(8,128)(2,1)S(1)}, bf16[16,1536]{1,0:T(8,128)(2,1)S(1)}, u32[]{:S(2)}, u32[]{:S(2)}) collective-permute-start(bf16[16,1536]{1,0:T(8,128)(2,1)S(1)} %add_convert_fusion.11), channel_id=1, source_target_pairs={{100,98},{101,99},{108,106},{109,107},{116,114},{117,115},{124,122... | collective-permute-start | bytes 147464 | tf_op jit(solution)/shard_map/root/ppermute | solution.py:32
  54.1 5.1 %collective-permute-start.6 = (bf16[16,1536]{1,0:T(8,128)(2,1)S(1)}, bf16[16,1536]{1,0:T(8,128)(2,1)S(1)}, u32[]{:S(2)}, u32[]{:S(2)}) collective-permute-start(bf16[16,1536]{1,0:T(8,128)(2,1)S(1)} %add_convert_fusion.10), channel_id=1, source_target_pairs={{68,66},{69,67},{76,74},{77,75},{84,82},{85,83},{92,90},{93,91},{9... | collective-permute-start | bytes 147464 | tf_op jit(solution)/shard_map/root/ppermute | solution.py:32
  54.8 4.5 %collective-permute-start.7 = (bf16[16,1536]{1,0:T(8,128)(2,1)S(1)}, bf16[16,1536]{1,0:T(8,128)(2,1)S(1)}, u32[]{:S(2)}, u32[]{:S(2)}) collective-permute-start(bf16[16,1536]{1,0:T(8,128)(2,1)S(1)} %add_convert_fusion.10), channel_id=1, source_target_pairs={{68,67},{69,66},{76,75},{77,74},{84,83},{85,82},{92,91},{93,90},{1... | collective-permute-start | bytes 147464 | tf_op jit(solution)/shard_map/root/ppermute | solution.py:32
  58.6 1.4 collective-permute-start.8
  62.4 2.1 collective-permute-start.10
  63.1 1.4 collective-permute-start.9
  63.8 3.2 %collective-permute-start.11 = (bf16[16,1536]{1,0:T(8,128)(2,1)S(1)}, bf16[16,1536]{1,0:T(8,128)(2,1)S(1)}, u32[]{:S(2)}, u32[]{:S(2)}) collective-permute-start(bf16[16,1536]{1,0:T(8,128)(2,1)S(1)} %add_convert_fusion.9), channel_id=1, source_target_pairs={{66,64},{67,65},{74,72},{75,73},{82,80},{83,81},{90,88},{91,89},{1... | collective-permute-start | bytes 147464 | tf_op jit(solution)/shard_map/root/ppermute | solution.py:32
  67.0 5.1 %collective-permute-start.12 = (bf16[16,1536]{1,0:T(8,128)(2,1)S(1)}, bf16[16,1536]{1,0:T(8,128)(2,1)S(1)}, u32[]{:S(2)}, u32[]{:S(2)}) collective-permute-start(bf16[16,1536]{1,0:T(8,128)(2,1)S(1)} %add_convert_fusion.8), channel_id=1, source_target_pairs={{34,32},{35,33},{42,40},{43,41},{50,48},{51,49},{58,56},{59,57},{6... | collective-permute-start | bytes 147464 | tf_op jit(solution)/shard_map/root/ppermute | solution.py:32
  67.7 4.5 %collective-permute-start.13 = (bf16[16,1536]{1,0:T(8,128)(2,1)S(1)}, bf16[16,1536]{1,0:T(8,128)(2,1)S(1)}, u32[]{:S(2)}, u32[]{:S(2)}) collective-permute-start(bf16[16,1536]{1,0:T(8,128)(2,1)S(1)} %add_convert_fusion.8), channel_id=1, source_target_pairs={{34,33},{35,32},{42,41},{43,40},{50,49},{51,48},{58,57},{59,56},{6... | collective-permute-start | bytes 147464 | tf_op jit(solution)/shard_map/root/ppermute | solution.py:32
  71.5 1.4 collective-permute-start.14
  75.3 28.3 %collective-permute-start.15 = (bf16[16,1536]{1,0:T(8,128)(2,1)S(1)}, bf16[16,1536]{1,0:T(8,128)(2,1)S(1)}, u32[]{:S(2)}, u32[]{:S(2)}) collective-permute-start(bf16[16,1536]{1,0:T(8,128)(2,1)S(1)} %fusion.67), channel_id=1, source_target_pairs={{32,0},{33,1},{40,8},{41,9},{48,16},{49,17},{56,24},{57,25},{160,1... | collective-permute-start | bytes 147464 | tf_op jit(solution)/shard_map/root/ppermute | solution.py:32
  76.6 31.2 %collective-permute-start.16 = (bf16[16,1536]{1,0:T(8,128)(2,1)S(1)}, bf16[16,1536]{1,0:T(8,128)(2,1)S(1)}, u32[]{:S(2)}, u32[]{:S(2)}) collective-permute-start(bf16[16,1536]{1,0:T(8,128)(2,1)S(1)} %fusion.67), channel_id=1, source_target_pairs={{32,16},{33,17},{40,24},{41,25},{48,0},{49,1},{56,8},{57,9},{160,1... | collective-permute-start | bytes 147464 | tf_op jit(solution)/shard_map/root/ppermute | solution.py:32
  110.3 4.5 %collective-permute-start.17 = (bf16[16,1536]{1,0:T(8,128)(2,1)S(1)}, bf16[16,1536]{1,0:T(8,128)(2,1)S(1)}, u32[]{:S(2)}, u32[]{:S(2)}) collective-permute-start(bf16[16,1536]{1,0:T(8,128)(2,1)S(1)} %maximum_select_fusion.3), channel_id=1, source_target_pairs={{0,6},{1,7},{8,14},{9,15},{16,22},{17,23},{24,30},{25,31},{32,38},... | collective-permute-start | bytes 147464 | tf_op jit(solution)/shard_map/root/ppermute | solution.py:32
  111.6 3.2 %collective-permute-start.18 = (bf16[16,1536]{1,0:T(8,128)(2,1)S(1)}, bf16[16,1536]{1,0:T(8,128)(2,1)S(1)}, u32[]{:S(2)}, u32[]{:S(2)}) collective-permute-start(bf16[16,1536]{1,0:T(8,128)(2,1)S(1)} %maximum_select_fusion.3), channel_id=1, source_target_pairs={{0,7},{1,6},{8,15},{9,14},{16,23},{17,22},{24,31},{25,30},{34,35},... | collective-permute-start | bytes 147464 | tf_op jit(solution)/shard_map/root/ppermute | solution.py:32
  112.9 5.6 %collective-permute-start.19 = (bf16[16,1536]{1,0:T(8,128)(2,1)S(1)}, bf16[16,1536]{1,0:T(8,128)(2,1)S(1)}, u32[]{:S(2)}, u32[]{:S(2)}) collective-permute-start(bf16[16,1536]{1,0:T(8,128)(2,1)S(1)} %maximum_select_fusion.3), channel_id=1, source_target_pairs={{0,1},{1,0},{8,9},{9,8},{16,17},{17,16},{24,25},{25,24},{128,129},... | collective-permute-start | bytes 147464 | tf_op jit(solution)/shard_map/root/ppermute | solution.py:32
  118.6 2.6 %collective-permute-start.20 = (bf16[16,1536]{1,0:T(8,128)(2,1)S(1)}, bf16[16,1536]{1,0:T(8,128)(2,1)S(1)}, u32[]{:S(2)}, u32[]{:S(2)}) collective-permute-start(bf16[16,1536]{1,0:T(8,128)(2,1)S(1)} %add_convert_fusion.6), channel_id=1, source_target_pairs={{0,2},{1,3},{8,10},{9,11},{16,18},{17,19},{24,26},{25,27},{6,4},{7... | collective-permute-start | bytes 147464 | tf_op jit(solution)/shard_map/root/ppermute | solution.py:32
  136.3 26.8 %copy-start.2 = (bf16[8,16,768]{2,0,1:T(8,128)(2,1)}, bf16[8,16,768]{2,0,1:T(8,128)(2,1)S(1)}, u32[]{:S(2)}) copy-start(bf16[8,16,768]{2,0,1:T(8,128)(2,1)S(1)} %copy.29) | copy-start | bytes 589828
  137.4 9.5 %all-to-all-start.2 = ((bf16[4,32,1024]{2,1,0:T(8,128)(2,1)}), bf16[4,32,1024]{2,1,0:T(8,128)(2,1)S(1)}, u32[]{:S(2)}, u32[]{:S(2)}) async-start(bf16[4,32,1024]{2,1,0:T(8,128)(2,1)} %bitcast.10), calls=%async_computation.2 | async-start | bytes 524288 | tf_op jit(solution)/shard_map/coupling/all_to_all | solution.py:137
  159.4 5.8 %copy-start.1 = (bf16[1,2048,1024]{2,1,0:T(8,128)(2,1)S(1)}, bf16[1,2048,1024]{2,1,0:T(8,128)(2,1)}, u32[]{:S(2)}) copy-start(bf16[1,2048,1024]{2,1,0:T(8,128)(2,1)} %all-gather.4.cloned.1.call-done) | copy-start | bytes 12582916
  163.1 1.4 collective-permute-start.21
  163.8 0.7 collective-permute-start.22
  164.6 2.4 collective-permute-start.24
  166.1 0.9 collective-permute-start.23
  168.3 2.9 %collective-permute-start.25 = (bf16[32,2048]{1,0:T(8,128)(2,1)S(1)}, bf16[32,2048]{1,0:T(8,128)(2,1)S(1)}, u32[]{:S(2)}, u32[]{:S(2)}) collective-permute-start(bf16[32,2048]{1,0:T(8,128)(2,1)S(1)} %fusion.58), channel_id=1, source_target_pairs={{68,66},{69,67},{76,74},{77,75},{84,82},{85,83},{92,90},{93,91},{9... | collective-permute-start | bytes 393224 | tf_op jit(solution)/shard_map/child/ppermute | solution.py:32
  169.0 2.2 collective-permute-start.26
  170.5 1.4 collective-permute-start.27
  171.2 2.2 collective-permute-start.29
  172.8 0.7 collective-permute-start.28
  174.8 2.9 %collective-permute-start.30 = (bf16[32,2048]{1,0:T(8,128)(2,1)S(1)}, bf16[32,2048]{1,0:T(8,128)(2,1)S(1)}, u32[]{:S(2)}, u32[]{:S(2)}) collective-permute-start(bf16[32,2048]{1,0:T(8,128)(2,1)S(1)} %fusion.46), channel_id=1, source_target_pairs={{34,32},{35,33},{42,40},{43,41},{50,48},{51,49},{58,56},{59,57},{6... | collective-permute-start | bytes 393224 | tf_op jit(solution)/shard_map/child/ppermute | solution.py:32
  175.5 2.2 collective-permute-start.31
  177.0 0.7 collective-permute-start.32
  178.5 34.4 %collective-permute-start.33 = (bf16[32,1024]{1,0:T(8,128)(2,1)S(1)}, bf16[32,1024]{1,0:T(8,128)(2,1)S(1)}, u32[]{:S(2)}, u32[]{:S(2)}) collective-permute-start(bf16[32,1024]{1,0:T(8,128)(2,1)S(1)} %fusion.84), channel_id=1, source_target_pairs={{32,0},{33,1},{40,8},{41,9},{48,16},{49,17},{56,24},{57,25},{160,1... | collective-permute-start | bytes 196616 | tf_op jit(solution)/shard_map/child/ppermute | solution.py:32
  214.3 6.0 %collective-permute-start.34 = (bf16[32,2048]{1,0:T(8,128)(2,1)S(1)}, bf16[32,2048]{1,0:T(8,128)(2,1)S(1)}, u32[]{:S(2)}, u32[]{:S(2)}) collective-permute-start(bf16[32,2048]{1,0:T(8,128)(2,1)S(1)} %fusion.34), channel_id=1, source_target_pairs={{0,6},{1,7},{8,14},{9,15},{16,22},{17,23},{24,30},{25,31},{32,38},... | collective-permute-start | bytes 393224 | tf_op jit(solution)/shard_map/child/ppermute | solution.py:32
  215.6 6.1 %collective-permute-start.35 = (bf16[32,2048]{1,0:T(8,128)(2,1)S(1)}, bf16[32,2048]{1,0:T(8,128)(2,1)S(1)}, u32[]{:S(2)}, u32[]{:S(2)}) collective-permute-start(bf16[32,2048]{1,0:T(8,128)(2,1)S(1)} %fusion.34), channel_id=1, source_target_pairs={{0,7},{1,6},{8,15},{9,14},{16,23},{17,22},{24,31},{25,30},{34,35},... | collective-permute-start | bytes 393224 | tf_op jit(solution)/shard_map/child/ppermute | solution.py:32
  216.9 5.7 %collective-permute-start.36 = (bf16[32,2048]{1,0:T(8,128)(2,1)S(1)}, bf16[32,2048]{1,0:T(8,128)(2,1)S(1)}, u32[]{:S(2)}, u32[]{:S(2)}) collective-permute-start(bf16[32,2048]{1,0:T(8,128)(2,1)S(1)} %fusion.34), channel_id=1, source_target_pairs={{0,1},{1,0},{8,9},{9,8},{16,17},{17,16},{24,25},{25,24},{128,129},... | collective-permute-start | bytes 393224 | tf_op jit(solution)/shard_map/child/ppermute | solution.py:32
  222.7 3.2 %collective-permute-start.37 = (bf16[32,2048]{1,0:T(8,128)(2,1)S(1)}, bf16[32,2048]{1,0:T(8,128)(2,1)S(1)}, u32[]{:S(2)}, u32[]{:S(2)}) collective-permute-start(bf16[32,2048]{1,0:T(8,128)(2,1)S(1)} %add_convert_fusion.1), channel_id=1, source_target_pairs={{0,2},{1,3},{8,10},{9,11},{16,18},{17,19},{24,26},{25,27},{6,4},{7... | collective-permute-start | bytes 393224 | tf_op jit(solution)/shard_map/child/ppermute | solution.py:32
Sparse Core Ops, SparseCore 0:
  63.9 70.9 all-gather.3

commit v2 on v1

--- a/solution.py
+++ b/solution.py
@@ -1,3 +1,5 @@
+import functools
+
 import jax
 import jax.numpy as jnp
 from jax import lax
@@ -81,6 +83,51 @@
     return current
 
 
+def home_sweep(rhs, forward, diagonal, width, then):
+    row_panel = lax.axis_index("row") // GROUP
+    col_panel = lax.axis_index("col") // PAIR
+    current = jnp.zeros((rhs.shape[0], width), BF16)
+    carried = jnp.zeros(rhs.shape, F32)
+    for r in range(PANELS - 1, -1, -1):
+        home = (r + 1) % PANELS
+        ahead = None
+        if r == 2:
+            ahead = send(current, [(3, 3, 0, 2, 1, 0)])
+        if r == 1:
+            ahead = send(current, [(2, 2, 0, 1, 0, 0), (3, 3, 0, 1, 0, 0)])
+        if r < PANELS - 1:
+            residual = (rhs - (forward(current) + carried)).astype(BF16)
+        else:
+            residual = rhs.astype(BF16)
+        piece = diagonal(residual).astype(BF16)
+        if r == 1:
+            piece, then = lax.optimization_barrier((piece, then))
+        shown = jnp.where((row_panel == home) & (col_panel == r), piece, current)
+        if r >= 1:
+            straight = [(home, r, 0, r, r - 1, 0)]
+            if r == 1:
+                straight.append((3, 3, 0, 2, 3, 0))
+            received = send(shown, straight) + send(shown, [(home, r, 0, r, r - 1, 1)])
+            if ahead is not None:
+                current = (current.astype(F32) + ahead).astype(BF16)
+                terms = forward(current).astype(BF16)
+                carried = send(terms, [(r + 1, r, 0, r - 1, r - 1, 0)])
+                if r == 1:
+                    carried = carried + send(terms, [(3, 1, 0, 0, 0, 0)])
+            current = (current.astype(F32) + received).astype(BF16)
+        else:
+            received = send(shown, [(1, 0, 0, 0, 3, 0), (2, 2, 0, 1, 2, 0)])
+            received = received + send(shown, [(1, 0, 0, 0, 3, 1), (2, 2, 0, 0, 3, 0)])
+            received = received + send(shown, [(1, 0, 0, 0, 0, 0)])
+            received = received + send(shown, [(1, 0, 0, 0, 0, 1)])
+            received = received + send(current, [(1, 1, 0, 0, 1, 0)])
+            received = received + send(current, [(1, 1, 0, 0, 3, 0)])
+            current = (current.astype(F32) + received).astype(BF16)
+            received = send(current, [(0, 0, 0, 0, 1, 0), (0, 0, 0, 3, 2, 0), (1, 1, 0, 1, 2, 0)])
+            current = (current.astype(F32) + received).astype(BF16)
+    return current, then
+
+
 def per_device(root_factor, partials, pattern, coupling, child_factor, child_bits):
     layers = lax.axis_size("gz")
     rows_here, cols_here = root_factor.shape
@@ -88,22 +135,40 @@
     col_index = lax.axis_index("col")
     core = row_index % 2
     quarters = [[s * GROUP + j for j in range(GROUP)] for s in range(PANELS)]
-    across = [[s * GROUP + j for s in range(PANELS)] for j in range(GROUP)]
+    panels = [
+        [g * ROWS + s * GROUP + j for g in range(layers) for j in range(GROUP)] for s in range(PANELS)
+    ]
     chips = [
         [g * ROWS + 2 * y + k for g in range(layers) for k in range(2)] for y in range(ROWS // 2)
     ]
 
     with jax.named_scope("mask"):
+        swap = [(i, i ^ 1) for i in range(ROWS)]
+        partner_factor = lax.ppermute(root_factor, "row", swap)
+        partner_pattern = lax.ppermute(pattern, "row", swap)
         block = rows_here // pattern.shape[0]
-        expanded = jnp.repeat(jnp.repeat(pattern, block, 0), block, 1)
         on_diagonal = row_index // GROUP == col_index // PAIR
-        masked_root = root_factor * jnp.where(on_diagonal, 1, expanded).astype(BF16)
-        partner_root = lax.ppermute(masked_root, "row", [(i, i ^ 1) for i in range(ROWS)])
-
-    with jax.named_scope("child_gather"):
-        child_panel = lax.all_gather(
-            child_factor[0], "row", axis=0, tiled=True, axis_index_groups=quarters
-        )
+
+        def masked(factor, blocks):
+            expanded = jnp.repeat(jnp.repeat(blocks, block, 0), block, 1)
+            return factor * jnp.where(on_diagonal, 1, expanded).astype(BF16)
+
+        masked_root = masked(root_factor, pattern)
+        partner_root = masked(partner_factor, partner_pattern)
+
+    with jax.named_scope("gathers"):
+        pairs = [
+            ((r * GROUP + j) * COLS + r * PAIR + q, ((r + 1) % PANELS * GROUP + j) * COLS + r * PAIR + q)
+            for r in range(PANELS)
+            for j in range(GROUP)
+            for q in range(PAIR)
+        ]
+        gather = functools.partial(
+            lax.all_gather, axis_name="row", axis=0, tiled=True, axis_index_groups=quarters
+        )
+        coupling_panel = gather(coupling[0])
+        child_diagonal = gather(lax.ppermute(child_factor[0], GRID, pairs))
+        child_panel = gather(child_factor[0])
 
     with jax.named_scope("rhs"):
         probes_here = partials.shape[1]
@@ -127,32 +192,55 @@
 
     with jax.named_scope("coupling"):
         own, other = root_rows[:, :rows_here], root_rows[:, rows_here:]
+        half = rows_here // 2
+        own_half, other_half = own[:, :half], other[:, :half]
+        halves = jnp.where(
+            core == 0,
+            jnp.concatenate([own_half, other_half], 1),
+            jnp.concatenate([other_half, own_half], 1),
+        )
+        some = ROWS // GROUP
+        shared = jnp.broadcast_to(
+            halves.reshape(1, GROUP, some, rows_here), (layers, GROUP, some, rows_here)
+        )
+        shared = lax.all_to_all(
+            shared.reshape(layers * GROUP, some, rows_here),
+            ("gz", "row"),
+            0,
+            0,
+            tiled=True,
+            axis_index_groups=panels,
+        )
+        shared = shared.reshape(layers, 2, 2, some, rows_here).transpose(3, 0, 2, 1, 4)
+        share = some * layers * 2
+        terms = dot(shared.reshape(share, 2 * rows_here), coupling_panel).astype(BF16)
+        coupled = terms.astype(F32)
+        for d in range(1, PANELS):
+            coupled = coupled + send(
+                terms, [((p + 1 + d) % PANELS, (p + 1) % PANELS, 0, p, p, 0) for p in range(PANELS)]
+            )
+        bits = lax.dynamic_slice_in_dim(child_bits[0], row_index % GROUP * share, share, 0)
+        child_rhs = (2 * bits - 1).astype(F32) - coupled
+
+    with jax.named_scope("child"):
         by_core = jnp.stack([jnp.where(core == k, own, other) for k in range(2)])
+        child_rows, by_core = home_sweep(
+            child_rhs,
+            lambda x: dot(x, child_panel),
+            lambda x: dot_t(x, child_diagonal),
+            child_panel.shape[0],
+            by_core,
+        )
+        child_rows = child_rows.reshape(share, GROUP, -1).transpose(1, 0, 2)
+        child_rows = child_rows.reshape(GROUP * share, -1)
+        child_rows = lax.all_to_all(child_rows, "row", 0, 0, tiled=True, axis_index_groups=quarters)
+
+    with jax.named_scope("root_out"):
         shared = jnp.broadcast_to(by_core[None], (layers,) + by_core.shape)
         shared = shared.reshape(layers * 2 * ROWS, rows_here)
         shared = lax.all_to_all(shared, ("gz", "row"), 0, 0, tiled=True, axis_index_groups=chips)
         root_all = shared.reshape(layers * 2, ROWS, rows_here).transpose(1, 0, 2)
         root_all = root_all.reshape(layers * 2 * ROWS, rows_here)
-        coupled = dot(root_all[:, : rows_here // 2], coupling[0]).astype(BF16)
-        coupled = lax.all_to_all(coupled, "row", 0, 0, tiled=True, axis_index_groups=quarters)
-        share = coupled.shape[0] // GROUP
-        coupled = jnp.sum(coupled.reshape(GROUP, share, -1).astype(F32), 0).astype(BF16)
-        coupled = lax.all_gather(coupled, "row", axis=0, axis_index_groups=across)
-        coupled = jnp.sum(coupled.astype(F32), 0)
-        bits = lax.dynamic_slice_in_dim(child_bits[0], row_index % GROUP * share, share, 0)
-        child_rhs = (2 * bits - 1).astype(F32) - coupled
-
-    with jax.named_scope("child"):
-        child_rows = sweep(
-            child_rhs,
-            lambda x: dot(x, child_panel),
-            lambda x: dot_t(x, child_panel),
-            child_panel.shape[0],
-            False,
-        )
-        child_rows = child_rows.reshape(share, GROUP, -1).transpose(1, 0, 2)
-        child_rows = child_rows.reshape(GROUP * share, -1)
-        child_rows = lax.all_to_all(child_rows, "row", 0, 0, tiled=True, axis_index_groups=quarters)
     return (root_all, child_rows[None])
 
 

time: 251 us -> 374 us (1.49)
  starting transfers between devices: 52.6 us -> 195 us
  blocking collectives: 42.3 us -> 13.8 us
    ppermute x37 -> x41, starting transfers between devices: 33.8 us -> 110 us  [send(): return lax.ppermute(value, GRID, pairs).astype(F32)]
    ppermute x1 -> x3, starting transfers between devices: 8.79 us -> 63.4 us  [the longest x1 41 us: per_device(): partner_pattern = lax.ppermute(pattern, 'row', swap)]
    all_to_all x2 -> x1, blocking collectives: 30.8 us -> 13.8 us  [per_device(): lax.all_to_all(shared.reshape(layers * GROUP, some, rows_here), ('gz', 'r...]
    all_gather x1 -> x0, blocking collectives: 11.5 us -> none  [per_device(): coupled = lax.all_gather(coupled, 'row', axis=0, axis_index_groups=across)]
    all_to_all x1 -> x2, starting transfers between devices: 4.32 us -> 11.7 us  [the longest x1 7.47 us: per_device(): lax.all_to_all(shared, ('gz', 'row'), 0, 0, tiled=True, axis_index_groups...]
    dot_general x12, matrix products: 17.7 us -> 23.5 us  [dot_t(): lax.dot_general(a, b, (((1,), (1,)), ((), ())), preferred_element_type=F32)]
    dot_general x16 -> x13, matrix products: 20.7 us -> 15.7 us  [dot(): return jnp.dot(a, b, preferred_element_type=F32)]
    all_to_all x1, starting transfers between devices: 5.6 us -> 10.3 us  [per_device(): lax.all_to_all(pieces.reshape(layers * ROWS, 12, lanes), ('gz', 'row'), 0...]
  transfers between devices with their start and end apart: 41 -> 50, of which waited for: 11 -> 10; matrix products, arithmetic and copies ran while one was open for 10% -> 13% of each run, Pallas kernels for 0% -> 0%
where the time goes in v2:
time: 374 us; the launch traced here: 373 us
  starting transfers between devices  195 us (52%)
  waiting for transfers between devices  93.7 us (25%)
  matrix products  39.2 us (10%)
  between operations  14.8 us (4%)
  blocking collectives  13.8 us (4%)
  local copies, waits for them, and re-layouts  10.3 us (3%)
  other arithmetic  5.27 us (1%)
    ppermute x41, starting transfers between devices, send(): return lax.ppermute(value, GRID, pairs).astype(F32)  110 us
    ppermute x41, waiting for transfers between devices, send(): return lax.ppermute(value, GRID, pairs).astype(F32)  75.2 us
    ppermute x1, starting transfers between devices, per_device(): partner_pattern = lax.ppermute(pattern, 'row', swap)  41 us
    dot_general x12, matrix products, dot_t(): lax.dot_general(a, b, (((1,), (1,)), ((), ())), preferred_element_type=F32)  23.5 us
    ppermute x1, starting transfers between devices, per_device(): partner_factor = lax.ppermute(root_factor, 'row', swap)  17.2 us
    dot_general x13, matrix products, dot(): return jnp.dot(a, b, preferred_element_type=F32)  15.7 us
    all_to_all x1, blocking collectives, per_device(): lax.all_to_all(shared.reshape(layers * GROUP, some, rows_here), ('gz', 'r...  13.8 us
    all_to_all x1, starting transfers between devices, per_device(): lax.all_to_all(pieces.reshape(layers * ROWS, 12, lanes), ('gz', 'row'), 0...  10.3 us
  transfers between devices with their start and end apart: 50, of which 10 were waited for; matrix products, arithmetic and copies ran while one was open for 13% of the time, Pallas kernels for 0%

profile of v2, /device:TPU:1, one launch (start us, length us, event | category | flops | bytes accessed | tf_op | source)
XLA Modules:
  0.0 372.5 jit_solution(15046519362981816854)
XLA Ops:
  8.0 5.2 %collective-permute-start.25 = (bf16[512,1024]{1,0:T(8,128)(2,1)}, bf16[512,1024]{1,0:T(8,128)(2,1)S(1)}, u32[]{:S(2)}, u32[]{:S(2)}) collective-permute-start(bf16[512,1024]{1,0:T(8,128)(2,1)} %bitcast.113), channel_id=1, source_target_pairs={{0,32},{1,33},{8,40},{9,41},{16,48},{17,49},{24,56},{25,57},{34,66... | collective-permute-start | bytes 3145736 | tf_op jit(solution)/shard_map/gathers/ppermute | solution.py:170
  13.2 4.3 %copy.30 = bf16[768,1536]{0,1:T(8,128)(2,1)} copy(bf16[768,1536]{1,0:T(8,128)(2,1)} %param.6) | data formatting | bytes 4718592 | tf_op args[0]
  17.5 17.2 %collective-permute-start = (bf16[768,1536]{0,1:T(8,128)(2,1)}, bf16[768,1536]{0,1:T(8,128)(2,1)}, u32[]{:S(2)}, u32[]{:S(2)}) collective-permute-start(bf16[768,1536]{0,1:T(8,128)(2,1)} %copy.30), channel_id=1, source_target_pairs={{0,8},{8,0},{16,24},{24,16},{32,40},{40,32},{48,56},{56,48},{64,72... | collective-permute-start | bytes 7077896 | tf_op jit(solution)/shard_map/mask/ppermute | solution.py:147
  34.7 1.0 copy-done.4
  35.7 41.0 %collective-permute-start.1 = (s32[3,6]{1,0:T(4,128)S(1)}, s32[3,6]{1,0:T(4,128)S(1)}, u32[]{:S(2)}, u32[]{:S(2)}) collective-permute-start(s32[3,6]{1,0:T(4,128)S(1)} %copy-done.6), channel_id=1, source_target_pairs={{0,8},{8,0},{16,24},{24,16},{32,40},{40,32},{48,56},{56,48},{64,72... | collective-permute-start | bytes 224 | tf_op jit(solution)/shard_map/mask/ppermute | solution.py:148
  76.8 0.7 broadcast_in_dim.45
  77.5 10.3 %all-to-all-start = ((bf16[64,12,128]{2,1,0:T(8,128)(2,1)}), bf16[64,12,128]{2,1,0:T(8,128)(2,1)S(1)}, u32[]{:S(2)}, u32[]{:S(2)}) async-start(bf16[64,12,128]{2,1,0:T(8,128)(2,1)} %bitcast.1), calls=%async_computation | async-start | bytes 524288 | tf_op jit(solution)/shard_map/rhs/all_to_all | solution.py:178
  88.1 1.8 bitcast_multiply_fusion.1
  90.2 9.7 %all-to-all-done = bf16[64,12,128]{2,1,0:T(8,128)(2,1)S(1)} async-done(((bf16[64,12,128]{2,1,0:T(8,128)(2,1)}), bf16[64,12,128]{2,1,0:T(8,128)(2,1)S(1)}, u32[]{:S(2)}, u32[]{:S(2)}) %all-to-all-start) | async-done | bytes 196640 | tf_op jit(solution)/shard_map/rhs/all_to_all | solution.py:178
  100.5 1.9 bitcast_multiply_fusion
  107.0 0.8 collective-permute-start.6
  109.8 26.3 %collective-permute-start.8 = (bf16[16,1536]{1,0:T(8,128)(2,1)S(1)}, bf16[16,1536]{1,0:T(8,128)(2,1)S(1)}, u32[]{:S(2)}, u32[]{:S(2)}) collective-permute-start(bf16[16,1536]{1,0:T(8,128)(2,1)S(1)} %add_convert_fusion.12), channel_id=1, source_target_pairs={{68,67},{69,66},{76,75},{77,74},{84,83},{85,82},{92,91},{93,90},{1... | collective-permute-start | bytes 147464 | tf_op jit(solution)/shard_map/root/ppermute | solution.py:34
  141.1 0.8 collective-permute-start.12
  147.5 0.7 fusion.22
  148.2 1.3 collective-permute-start.16
  149.5 1.3 collective-permute-start.17
  150.8 19.3 %collective-permute-done.16 = bf16[16,1536]{1,0:T(8,128)(2,1)S(1)} collective-permute-done((bf16[16,1536]{1,0:T(8,128)(2,1)S(1)}, bf16[16,1536]{1,0:T(8,128)(2,1)S(1)}, u32[]{:S(2)}, u32[]{:S(2)}) %collective-permute-start.16) | collective-permute-done | bytes 49184 | tf_op jit(solution)/shard_map/root/ppermute | solution.py:34
  170.1 3.7 collective-permute-done.17
  174.7 1.3 collective-permute-start.18
  176.0 1.3 collective-permute-start.19
  177.3 1.9 collective-permute-start.20
  179.3 3.5 collective-permute-done.20
  182.8 7.4 %collective-permute-start.21 = (bf16[16,1536]{1,0:T(8,128)(2,1)S(1)}, bf16[16,1536]{1,0:T(8,128)(2,1)S(1)}, u32[]{:S(2)}, u32[]{:S(2)}) collective-permute-start(bf16[16,1536]{1,0:T(8,128)(2,1)S(1)} %add_convert_fusion.8), channel_id=1, source_target_pairs={{0,2},{1,3},{8,10},{9,11},{16,18},{17,19},{24,26},{25,27},{6,4},{7... | collective-permute-start | bytes 147464 | tf_op jit(solution)/shard_map/root/ppermute | solution.py:34
  190.2 1.1 collective-permute-done.21
  191.5 13.8 %all_to_all.25 = bf16[16,4,768]{2,1,0:T(4,128)(2,1)S(1)} all-to-all(bf16[16,4,768]{2,1,0:T(4,128)(2,1)S(1)} %bitcast.119), channel_id=1, replica_groups={{0,8,16,24,128,136,144,152,256,264,272,280,384,392,400,408},{32,40,48,5..., dimensions={0} | all-to-all | bytes 196608 | tf_op jit(solution)/shard_map/coupling/all_to_all | solution.py:206
  205.4 2.5 fusion.39
  207.9 12.4 %collective-permute-start.22 = (bf16[32,1024]{1,0:T(8,128)(2,1)S(1)}, bf16[32,1024]{1,0:T(8,128)(2,1)S(1)}, u32[]{:S(2)}, u32[]{:S(2)}) collective-permute-start(bf16[32,1024]{1,0:T(8,128)(2,1)S(1)} %fusion.39), channel_id=1, source_target_pairs={{64,32},{65,33},{72,40},{73,41},{80,48},{81,49},{88,56},{89,57},{9... | collective-permute-start | bytes 196616 | tf_op jit(solution)/shard_map/coupling/ppermute | solution.py:34
  220.3 16.1 %collective-permute-start.23 = (bf16[32,1024]{1,0:T(8,128)(2,1)S(1)}, bf16[32,1024]{1,0:T(8,128)(2,1)S(1)}, u32[]{:S(2)}, u32[]{:S(2)}) collective-permute-start(bf16[32,1024]{1,0:T(8,128)(2,1)S(1)} %fusion.39), channel_id=1, source_target_pairs={{96,32},{97,33},{104,40},{105,41},{112,48},{113,49},{120,56},{121,... | collective-permute-start | bytes 196616 | tf_op jit(solution)/shard_map/coupling/ppermute | solution.py:34
  236.4 4.2 %collective-permute-start.24 = (bf16[32,1024]{1,0:T(8,128)(2,1)S(1)}, bf16[32,1024]{1,0:T(8,128)(2,1)S(1)}, u32[]{:S(2)}, u32[]{:S(2)}) collective-permute-start(bf16[32,1024]{1,0:T(8,128)(2,1)S(1)} %fusion.39), channel_id=1, source_target_pairs={{0,32},{1,33},{8,40},{9,41},{16,48},{17,49},{24,56},{25,57},{34,66... | collective-permute-start | bytes 196616 | tf_op jit(solution)/shard_map/coupling/ppermute | solution.py:34
  240.7 3.0 collective-permute-done.24
  243.7 1.0 bitcast_subtract_fusion
  244.7 3.5 fusion.16
  249.7 0.8 collective-permute-start.28
  250.6 5.5 %fusion.17 = bf16[32,2048]{1,0:T(8,128)(2,1)S(1)} fusion(bf16[32,2048]{1,0:T(8,128)(2,1)S(1)} %add_convert_fusion.6, bf16[2048,1024]{1,0:T(8,128)(2,1)} %all-gather.6.cloned.1.call-done, f32[32,1024]{1,0:T(8,128)S(1)} %bitcast_subtract_fusion, bf16[1,2048,1024]{2,1,0:T(8,128)(2,1)} %all-gather.10.cloned.1.call-done, pred[]{:T(512)S(6)} %and.57), kind=kOutput, calls=%fused_computation.28 | convolution fusion | flops 268632064 | bytes 8781825 | tf_op jit(solution)/shard_map/child/dot_general | solution.py:23
  257.5 3.0 fusion.51
  262.0 5.5 %convolution_convert_fusion.1 = bf16[32,2048]{1,0:T(8,128)(2,1)S(1)} fusion(bf16[2048,1024]{1,0:T(8,128)(2,1)} %all-gather.6.cloned.1.call-done, f32[32,1024]{1,0:T(8,128)S(1)} %bitcast_subtract_fusion, bf16[32,2048]{1,0:T(8,128)(2,1)S(1)} %add_convert_fusion.4, bf16[1,2048,1024]{2,1,0:T(8,128)(2,1)} %all-gather.10.cloned.1.call-done, ...), kind=kOutput, calls=%fused_computation.15 | convolution fusion | flops 268632064 | bytes 8847360 | tf_op jit(solution)/shard_map/child/dot_general | solution.py:23
  268.9 3.0 fusion.54
  273.4 5.5 %fusion.18 = bf16[32,2048]{1,0:T(8,128)(2,1)S(1)} fusion(bf16[32,2048]{1,0:T(8,128)(2,1)S(1)} %add_convert_fusion.2, bf16[2048,1024]{1,0:T(8,128)(2,1)} %all-gather.6.cloned.1.call-done, f32[32,1024]{1,0:T(8,128)S(1)} %bitcast_subtract_fusion, bf16[1,2048,1024]{2,1,0:T(8,128)(2,1)} %all-gather.10.cloned.1.call-done, ...), kind=kOutput, calls=%fused_computation.29 | convolution fusion | flops 268763136 | bytes 8912897 | tf_op jit(solution)/shard_map/child/dot_general | solution.py:23
  280.3 1.3 collective-permute-start.39
  281.6 1.3 collective-permute-start.40
  284.2 35.1 %collective-permute-done.39 = bf16[32,2048]{1,0:T(8,128)(2,1)S(1)} collective-permute-done((bf16[32,2048]{1,0:T(8,128)(2,1)S(1)}, bf16[32,2048]{1,0:T(8,128)(2,1)S(1)}, u32[]{:S(2)}, u32[]{:S(2)}) %collective-permute-start.39) | collective-permute-done | bytes 131104 | tf_op jit(solution)/shard_map/child/ppermute | solution.py:34
  319.3 9.4 %collective-permute-done.40 = bf16[32,2048]{1,0:T(8,128)(2,1)S(1)} collective-permute-done((bf16[32,2048]{1,0:T(8,128)(2,1)S(1)}, bf16[32,2048]{1,0:T(8,128)(2,1)S(1)}, u32[]{:S(2)}, u32[]{:S(2)}) %collective-permute-start.40) | collective-permute-done | bytes 131104 | tf_op jit(solution)/shard_map/child/ppermute | solution.py:34
  328.9 14.5 %collective-permute-start.43 = (bf16[32,2048]{1,0:T(8,128)(2,1)S(1)}, bf16[32,2048]{1,0:T(8,128)(2,1)S(1)}, u32[]{:S(2)}, u32[]{:S(2)}) collective-permute-start(bf16[32,2048]{1,0:T(8,128)(2,1)S(1)} %add_convert_fusion.1), channel_id=1, source_target_pairs={{0,2},{1,3},{8,10},{9,11},{16,18},{17,19},{24,26},{25,27},{6,4},{7... | collective-permute-start | bytes 393224 | tf_op jit(solution)/shard_map/child/ppermute | solution.py:34
  344.1 7.5 %all-to-all-start.2 = ((bf16[8,16,768]{2,1,0:T(8,128)(2,1)}), bf16[8,16,768]{2,1,0:T(8,128)(2,1)S(1)}, u32[]{:S(2)}, u32[]{:S(2)}) async-start(bf16[8,16,768]{2,1,0:T(8,128)(2,1)} %bitcast.12), calls=%async_computation.2 | async-start | bytes 393216 | tf_op jit(solution)/shard_map/root_out/all_to_all | solution.py:241
  352.3 5.2 %all-to-all-done.2 = bf16[8,16,768]{2,1,0:T(8,128)(2,1)S(1)} async-done(((bf16[8,16,768]{2,1,0:T(8,128)(2,1)}), bf16[8,16,768]{2,1,0:T(8,128)(2,1)S(1)}, u32[]{:S(2)}, u32[]{:S(2)}) %all-to-all-start.2) | async-done | bytes 196640 | tf_op jit(solution)/shard_map/root_out/all_to_all | solution.py:241
  357.5 4.2 %all-to-all-start.3 = ((bf16[4,32,512]{2,1,0:T(8,128)(2,1)}), bf16[4,32,512]{2,1,0:T(8,128)(2,1)S(1)}, u32[]{:S(2)}, u32[]{:S(2)}) async-start(bf16[4,32,512]{2,1,0:T(8,128)(2,1)} %bitcast.112), calls=%async_computation.3 | async-start | bytes 262144 | tf_op jit(solution)/shard_map/child/all_to_all | solution.py:236
  361.7 0.7 copy.42
  362.5 2.9 all-to-all-done.3
  (139 shorter events, 31.7 us)
Async XLA Ops:
  7.2 198.2 %all-gather.8.cloned.1.call-start = ((), (), s32[]{:S(2)}) async-start(), calls=%async_computation.5 | async-start | bytes 3932160 | tf_op jit(solution)/shard_map/gathers/all_gather | solution.py:169
  7.9 236.8 %all-gather.6.cloned.1.call-start = ((), (), s32[]{:S(2)}) async-start(), calls=%async_computation.4 | async-start | bytes 5242880 | tf_op jit(solution)/shard_map/gathers/all_gather | solution.py:170
  8.0 26.7 %collective-permute-start.25 = (bf16[512,1024]{1,0:T(8,128)(2,1)}, bf16[512,1024]{1,0:T(8,128)(2,1)S(1)}, u32[]{:S(2)}, u32[]{:S(2)}) collective-permute-start(bf16[512,1024]{1,0:T(8,128)(2,1)} %bitcast.113), channel_id=1, source_target_pairs={{0,32},{1,33},{8,40},{9,41},{16,48},{17,49},{24,56},{25,57},{34,66... | collective-permute-start | bytes 3145736 | tf_op jit(solution)/shard_map/gathers/ppermute | solution.py:170
  17.5 83.0 %collective-permute-start = (bf16[768,1536]{0,1:T(8,128)(2,1)}, bf16[768,1536]{0,1:T(8,128)(2,1)}, u32[]{:S(2)}, u32[]{:S(2)}) collective-permute-start(bf16[768,1536]{0,1:T(8,128)(2,1)} %copy.30), channel_id=1, source_target_pairs={{0,8},{8,0},{16,24},{24,16},{32,40},{40,32},{48,56},{56,48},{64,72... | collective-permute-start | bytes 7077896 | tf_op jit(solution)/shard_map/mask/ppermute | solution.py:147
  35.7 54.3 %collective-permute-start.1 = (s32[3,6]{1,0:T(4,128)S(1)}, s32[3,6]{1,0:T(4,128)S(1)}, u32[]{:S(2)}, u32[]{:S(2)}) collective-permute-start(s32[3,6]{1,0:T(4,128)S(1)} %copy-done.6), channel_id=1, source_target_pairs={{0,8},{8,0},{16,24},{24,16},{32,40},{40,32},{48,56},{56,48},{64,72... | collective-permute-start | bytes 224 | tf_op jit(solution)/shard_map/mask/ppermute | solution.py:148
  77.5 22.3 %all-to-all-start = ((bf16[64,12,128]{2,1,0:T(8,128)(2,1)}), bf16[64,12,128]{2,1,0:T(8,128)(2,1)S(1)}, u32[]{:S(2)}, u32[]{:S(2)}) async-start(bf16[64,12,128]{2,1,0:T(8,128)(2,1)} %bitcast.1), calls=%async_computation | async-start | bytes 524288 | tf_op jit(solution)/shard_map/rhs/all_to_all | solution.py:178
  87.8 162.7 %all-gather.10.cloned.1.call-start = ((), (), s32[]{:S(2)}) async-start(), calls=%async_computation.6 | async-start | bytes 5242880 | tf_op jit(solution)/shard_map/gathers/all_gather | solution.py:171
  102.8 1.3 collective-permute-start.2
  105.6 2.2 collective-permute-start.4
  106.3 1.5 collective-permute-start.5
  107.0 2.1 collective-permute-start.6
  109.1 29.1 %collective-permute-start.7 = (bf16[16,1536]{1,0:T(8,128)(2,1)S(1)}, bf16[16,1536]{1,0:T(8,128)(2,1)S(1)}, u32[]{:S(2)}, u32[]{:S(2)}) collective-permute-start(bf16[16,1536]{1,0:T(8,128)(2,1)S(1)} %add_convert_fusion.12), channel_id=1, source_target_pairs={{68,66},{69,67},{76,74},{77,75},{84,82},{85,83},{92,90},{93,91},{9... | collective-permute-start | bytes 147464 | tf_op jit(solution)/shard_map/root/ppermute | solution.py:34
  109.8 28.5 %collective-permute-start.8 = (bf16[16,1536]{1,0:T(8,128)(2,1)S(1)}, bf16[16,1536]{1,0:T(8,128)(2,1)S(1)}, u32[]{:S(2)}, u32[]{:S(2)}) collective-permute-start(bf16[16,1536]{1,0:T(8,128)(2,1)S(1)} %add_convert_fusion.12), channel_id=1, source_target_pairs={{68,67},{69,66},{76,75},{77,74},{84,83},{85,82},{92,91},{93,90},{1... | collective-permute-start | bytes 147464 | tf_op jit(solution)/shard_map/root/ppermute | solution.py:34
  137.6 1.4 collective-permute-start.9
  139.7 2.2 collective-permute-start.10
  140.4 1.5 collective-permute-start.11
  141.1 2.1 collective-permute-start.12
  143.2 3.5 collective-permute-start.13
  143.9 2.8 collective-permute-start.14
  146.0 1.4 collective-permute-start.15
  148.2 21.9 %collective-permute-start.16 = (bf16[16,1536]{1,0:T(8,128)(2,1)S(1)}, bf16[16,1536]{1,0:T(8,128)(2,1)S(1)}, u32[]{:S(2)}, u32[]{:S(2)}) collective-permute-start(bf16[16,1536]{1,0:T(8,128)(2,1)S(1)} %fusion.22), channel_id=1, source_target_pairs={{32,0},{33,1},{40,8},{41,9},{48,16},{49,17},{56,24},{57,25},{160,1... | collective-permute-start | bytes 147464 | tf_op jit(solution)/shard_map/root/ppermute | solution.py:34
  149.5 24.3 %collective-permute-start.17 = (bf16[16,1536]{1,0:T(8,128)(2,1)S(1)}, bf16[16,1536]{1,0:T(8,128)(2,1)S(1)}, u32[]{:S(2)}, u32[]{:S(2)}) collective-permute-start(bf16[16,1536]{1,0:T(8,128)(2,1)S(1)} %fusion.22), channel_id=1, source_target_pairs={{32,16},{33,17},{40,24},{41,25},{48,0},{49,1},{56,8},{57,9},{160,1... | collective-permute-start | bytes 147464 | tf_op jit(solution)/shard_map/root/ppermute | solution.py:34
  174.7 4.5 %collective-permute-start.18 = (bf16[16,1536]{1,0:T(8,128)(2,1)S(1)}, bf16[16,1536]{1,0:T(8,128)(2,1)S(1)}, u32[]{:S(2)}, u32[]{:S(2)}) collective-permute-start(bf16[16,1536]{1,0:T(8,128)(2,1)S(1)} %maximum_select_fusion.3), channel_id=1, source_target_pairs={{0,6},{1,7},{8,14},{9,15},{16,22},{17,23},{24,30},{25,31},{32,38},... | collective-permute-start | bytes 147464 | tf_op jit(solution)/shard_map/root/ppermute | solution.py:34
  176.0 3.2 collective-permute-start.19
  177.3 5.4 %collective-permute-start.20 = (bf16[16,1536]{1,0:T(8,128)(2,1)S(1)}, bf16[16,1536]{1,0:T(8,128)(2,1)S(1)}, u32[]{:S(2)}, u32[]{:S(2)}) collective-permute-start(bf16[16,1536]{1,0:T(8,128)(2,1)S(1)} %maximum_select_fusion.3), channel_id=1, source_target_pairs={{0,1},{1,0},{8,9},{9,8},{16,17},{17,16},{24,25},{25,24},{128,129},... | collective-permute-start | bytes 147464 | tf_op jit(solution)/shard_map/root/ppermute | solution.py:34
  182.8 8.6 %collective-permute-start.21 = (bf16[16,1536]{1,0:T(8,128)(2,1)S(1)}, bf16[16,1536]{1,0:T(8,128)(2,1)S(1)}, u32[]{:S(2)}, u32[]{:S(2)}) collective-permute-start(bf16[16,1536]{1,0:T(8,128)(2,1)S(1)} %add_convert_fusion.8), channel_id=1, source_target_pairs={{0,2},{1,3},{8,10},{9,11},{16,18},{17,19},{24,26},{25,27},{6,4},{7... | collective-permute-start | bytes 147464 | tf_op jit(solution)/shard_map/root/ppermute | solution.py:34
  207.9 32.7 %collective-permute-start.22 = (bf16[32,1024]{1,0:T(8,128)(2,1)S(1)}, bf16[32,1024]{1,0:T(8,128)(2,1)S(1)}, u32[]{:S(2)}, u32[]{:S(2)}) collective-permute-start(bf16[32,1024]{1,0:T(8,128)(2,1)S(1)} %fusion.39), channel_id=1, source_target_pairs={{64,32},{65,33},{72,40},{73,41},{80,48},{81,49},{88,56},{89,57},{9... | collective-permute-start | bytes 196616 | tf_op jit(solution)/shard_map/coupling/ppermute | solution.py:34
  220.3 20.3 %collective-permute-start.23 = (bf16[32,1024]{1,0:T(8,128)(2,1)S(1)}, bf16[32,1024]{1,0:T(8,128)(2,1)S(1)}, u32[]{:S(2)}, u32[]{:S(2)}) collective-permute-start(bf16[32,1024]{1,0:T(8,128)(2,1)S(1)} %fusion.39), channel_id=1, source_target_pairs={{96,32},{97,33},{104,40},{105,41},{112,48},{113,49},{120,56},{121,... | collective-permute-start | bytes 196616 | tf_op jit(solution)/shard_map/coupling/ppermute | solution.py:34
  236.4 7.3 %collective-permute-start.24 = (bf16[32,1024]{1,0:T(8,128)(2,1)S(1)}, bf16[32,1024]{1,0:T(8,128)(2,1)S(1)}, u32[]{:S(2)}, u32[]{:S(2)}) collective-permute-start(bf16[32,1024]{1,0:T(8,128)(2,1)S(1)} %fusion.39), channel_id=1, source_target_pairs={{0,32},{1,33},{8,40},{9,41},{16,48},{17,49},{24,56},{25,57},{34,66... | collective-permute-start | bytes 196616 | tf_op jit(solution)/shard_map/coupling/ppermute | solution.py:34
  248.2 1.4 collective-permute-start.26
  249.7 7.8 %collective-permute-start.28 = (bf16[32,2048]{1,0:T(8,128)(2,1)S(1)}, bf16[32,2048]{1,0:T(8,128)(2,1)S(1)}, u32[]{:S(2)}, u32[]{:S(2)}) collective-permute-start(bf16[32,2048]{1,0:T(8,128)(2,1)S(1)} %add_convert_fusion.6), channel_id=1, source_target_pairs={{100,98},{101,99},{108,106},{109,107},{116,114},{117,115},{124,122... | collective-permute-start | bytes 393224 | tf_op jit(solution)/shard_map/child/ppermute | solution.py:34
  256.1 5.0 %collective-permute-start.29 = (bf16[32,2048]{1,0:T(8,128)(2,1)S(1)}, bf16[32,2048]{1,0:T(8,128)(2,1)S(1)}, u32[]{:S(2)}, u32[]{:S(2)}) collective-permute-start(bf16[32,2048]{1,0:T(8,128)(2,1)S(1)} %fusion.17), channel_id=1, source_target_pairs={{100,66},{101,67},{108,74},{109,75},{116,82},{117,83},{124,90},{12... | collective-permute-start | bytes 393224 | tf_op jit(solution)/shard_map/child/ppermute | solution.py:34
  256.8 4.4 %collective-permute-start.30 = (bf16[32,2048]{1,0:T(8,128)(2,1)S(1)}, bf16[32,2048]{1,0:T(8,128)(2,1)S(1)}, u32[]{:S(2)}, u32[]{:S(2)}) collective-permute-start(bf16[32,2048]{1,0:T(8,128)(2,1)S(1)} %fusion.17), channel_id=1, source_target_pairs={{100,67},{101,66},{108,75},{109,74},{116,83},{117,82},{124,91},{12... | collective-permute-start | bytes 393224 | tf_op jit(solution)/shard_map/child/ppermute | solution.py:34
  260.5 1.5 collective-permute-start.31
  261.3 7.6 %collective-permute-start.32 = (bf16[32,2048]{1,0:T(8,128)(2,1)S(1)}, bf16[32,2048]{1,0:T(8,128)(2,1)S(1)}, u32[]{:S(2)}, u32[]{:S(2)}) collective-permute-start(bf16[32,2048]{1,0:T(8,128)(2,1)S(1)} %add_convert_fusion.4), channel_id=1, source_target_pairs={{66,64},{67,65},{74,72},{75,73},{82,80},{83,81},{90,88},{91,89},{9... | collective-permute-start | bytes 393224 | tf_op jit(solution)/shard_map/child/ppermute | solution.py:34
  267.5 5.7 %collective-permute-start.33 = (bf16[32,2048]{1,0:T(8,128)(2,1)S(1)}, bf16[32,2048]{1,0:T(8,128)(2,1)S(1)}, u32[]{:S(2)}, u32[]{:S(2)}) collective-permute-start(bf16[32,2048]{1,0:T(8,128)(2,1)S(1)} %broadcast_select_fusion), channel_id=1, source_target_pairs={{66,32},{67,33},{74,40},{75,41},{82,48},{83,49},{90,56},{91,57},{1... | collective-permute-start | bytes 393224 | tf_op jit(solution)/shard_map/child/ppermute | solution.py:34
  268.2 5.1 %collective-permute-start.34 = (bf16[32,2048]{1,0:T(8,128)(2,1)S(1)}, bf16[32,2048]{1,0:T(8,128)(2,1)S(1)}, u32[]{:S(2)}, u32[]{:S(2)}) collective-permute-start(bf16[32,2048]{1,0:T(8,128)(2,1)S(1)} %broadcast_select_fusion), channel_id=1, source_target_pairs={{66,33},{67,32},{74,41},{75,40},{82,49},{83,48},{90,57},{91,56},{1... | collective-permute-start | bytes 393224 | tf_op jit(solution)/shard_map/child/ppermute | solution.py:34
  271.9 1.4 collective-permute-start.35
  272.6 0.8 collective-permute-start.36
  278.9 4.6 %collective-permute-start.37 = (bf16[32,2048]{1,0:T(8,128)(2,1)S(1)}, bf16[32,2048]{1,0:T(8,128)(2,1)S(1)}, u32[]{:S(2)}, u32[]{:S(2)}) collective-permute-start(bf16[32,2048]{1,0:T(8,128)(2,1)S(1)} %fusion.18), channel_id=1, source_target_pairs={{32,6},{33,7},{40,14},{41,15},{48,22},{49,23},{56,30},{57,31},{66,... | collective-permute-start | bytes 393224 | tf_op jit(solution)/shard_map/child/ppermute | solution.py:34
  279.6 4.6 %collective-permute-start.38 = (bf16[32,2048]{1,0:T(8,128)(2,1)S(1)}, bf16[32,2048]{1,0:T(8,128)(2,1)S(1)}, u32[]{:S(2)}, u32[]{:S(2)}) collective-permute-start(bf16[32,2048]{1,0:T(8,128)(2,1)S(1)} %fusion.18), channel_id=1, source_target_pairs={{32,7},{33,6},{40,15},{41,14},{48,23},{49,22},{56,31},{57,30},{64,... | collective-permute-start | bytes 393224 | tf_op jit(solution)/shard_map/child/ppermute | solution.py:34
  280.3 39.0 %collective-permute-start.39 = (bf16[32,2048]{1,0:T(8,128)(2,1)S(1)}, bf16[32,2048]{1,0:T(8,128)(2,1)S(1)}, u32[]{:S(2)}, u32[]{:S(2)}) collective-permute-start(bf16[32,2048]{1,0:T(8,128)(2,1)S(1)} %fusion.18), channel_id=1, source_target_pairs={{32,0},{33,1},{40,8},{41,9},{48,16},{49,17},{56,24},{57,25},{160,1... | collective-permute-start | bytes 393224 | tf_op jit(solution)/shard_map/child/ppermute | solution.py:34
  281.6 47.2 %collective-permute-start.40 = (bf16[32,2048]{1,0:T(8,128)(2,1)S(1)}, bf16[32,2048]{1,0:T(8,128)(2,1)S(1)}, u32[]{:S(2)}, u32[]{:S(2)}) collective-permute-start(bf16[32,2048]{1,0:T(8,128)(2,1)S(1)} %fusion.18), channel_id=1, source_target_pairs={{32,1},{33,0},{40,9},{41,8},{48,17},{49,16},{56,25},{57,24},{160,1... | collective-permute-start | bytes 393224 | tf_op jit(solution)/shard_map/child/ppermute | solution.py:34
  282.9 45.9 %collective-permute-start.41 = (bf16[32,2048]{1,0:T(8,128)(2,1)S(1)}, bf16[32,2048]{1,0:T(8,128)(2,1)S(1)}, u32[]{:S(2)}, u32[]{:S(2)}) collective-permute-start(bf16[32,2048]{1,0:T(8,128)(2,1)S(1)} %add_convert_fusion.2), channel_id=1, source_target_pairs={{32,34},{33,35},{40,42},{41,43},{48,50},{49,51},{56,58},{57,59},{1... | collective-permute-start | bytes 393224 | tf_op jit(solution)/shard_map/child/ppermute | solution.py:34
  283.5 45.2 %collective-permute-start.42 = (bf16[32,2048]{1,0:T(8,128)(2,1)S(1)}, bf16[32,2048]{1,0:T(8,128)(2,1)S(1)}, u32[]{:S(2)}, u32[]{:S(2)}) collective-permute-start(bf16[32,2048]{1,0:T(8,128)(2,1)S(1)} %add_convert_fusion.2), channel_id=1, source_target_pairs={{32,38},{33,39},{40,46},{41,47},{48,54},{49,55},{56,62},{57,63},{1... | collective-permute-start | bytes 393224 | tf_op jit(solution)/shard_map/child/ppermute | solution.py:34
  328.9 22.7 %collective-permute-start.43 = (bf16[32,2048]{1,0:T(8,128)(2,1)S(1)}, bf16[32,2048]{1,0:T(8,128)(2,1)S(1)}, u32[]{:S(2)}, u32[]{:S(2)}) collective-permute-start(bf16[32,2048]{1,0:T(8,128)(2,1)S(1)} %add_convert_fusion.1), channel_id=1, source_target_pairs={{0,2},{1,3},{8,10},{9,11},{16,18},{17,19},{24,26},{25,27},{6,4},{7... | collective-permute-start | bytes 393224 | tf_op jit(solution)/shard_map/child/ppermute | solution.py:34
  344.1 13.4 %all-to-all-start.2 = ((bf16[8,16,768]{2,1,0:T(8,128)(2,1)}), bf16[8,16,768]{2,1,0:T(8,128)(2,1)S(1)}, u32[]{:S(2)}, u32[]{:S(2)}) async-start(bf16[8,16,768]{2,1,0:T(8,128)(2,1)} %bitcast.12), calls=%async_computation.2 | async-start | bytes 393216 | tf_op jit(solution)/shard_map/root_out/all_to_all | solution.py:241
  357.5 7.8 %all-to-all-start.3 = ((bf16[4,32,512]{2,1,0:T(8,128)(2,1)}), bf16[4,32,512]{2,1,0:T(8,128)(2,1)S(1)}, u32[]{:S(2)}, u32[]{:S(2)}) async-start(bf16[4,32,512]{2,1,0:T(8,128)(2,1)} %bitcast.112), calls=%async_computation.3 | async-start | bytes 262144 | tf_op jit(solution)/shard_map/child/all_to_all | solution.py:236
  (9 other events, 128.3 us)
Sparse Core Ops, SparseCore 0:
  10.1 50.9 all-gather.7
  63.2 70.1 all-gather.5
  141.2 63.1 all-gather.9

commit v3 on v1

--- a/solution.py
+++ b/solution.py
@@ -32,10 +32,18 @@
     return lax.ppermute(value, GRID, pairs).astype(F32)
 
 
-def sweep(rhs, forward, diagonal, width, split_rows):
+def sweep(rhs, own, other, then=None):
+    rows = own.shape[0]
+
+    def forward(x):
+        return dot(x[:, :rows], own) + dot(x[:, rows:], other)
+
+    def diagonal(x):
+        return jnp.concatenate([dot_t(x, own), dot_t(x, other)], 1)
+
     row_panel = lax.axis_index("row") // GROUP
     col_panel = lax.axis_index("col") // PAIR
-    current = jnp.zeros((rhs.shape[0], width), BF16)
+    current = jnp.zeros((rhs.shape[0], 2 * rows), BF16)
     carried = jnp.zeros(rhs.shape, F32)
     totals = jnp.zeros(rhs.shape, F32)
     for r in range(PANELS - 1, -1, -1):
@@ -46,14 +54,14 @@
             if r == 1:
                 down.append((3, 2, 0, 0, 0, 0))
             first = send(terms, down)
-            totals = first
-            if split_rows:
-                totals = totals + send(terms, [(r + 1, r, 2, r, r, 0)])
+            totals = first + send(terms, [(r + 1, r, 2, r, r, 0)])
             if r >= 1:
                 ahead = send(current, [(r + 1, r + 1, 0, r, r - 1, 0)])
             carried = carried + first
         residual = (rhs - totals).astype(BF16)
         piece = diagonal(residual).astype(BF16)
+        if r == 1 and then is not None:
+            piece, then = lax.optimization_barrier((piece, then))
         current = jnp.where((row_panel == r) & (col_panel == r), piece, current)
         if ahead is not None:
             current = (current.astype(F32) + ahead).astype(BF16)
@@ -78,7 +86,7 @@
             current = (current.astype(F32) + received).astype(BF16)
             received = send(current, [(0, 0, 0, 0, 1, 0), (0, 0, 0, 3, 2, 0), (1, 1, 0, 3, 2, 0)])
             current = (current.astype(F32) + received).astype(BF16)
-    return current
+    return current[:, :rows], current[:, rows:], then
 
 
 def per_device(root_factor, partials, pattern, coupling, child_factor, child_bits):
@@ -88,22 +96,28 @@
     col_index = lax.axis_index("col")
     core = row_index % 2
     quarters = [[s * GROUP + j for j in range(GROUP)] for s in range(PANELS)]
-    across = [[s * GROUP + j for s in range(PANELS)] for j in range(GROUP)]
+    panels = [
+        [g * ROWS + s * GROUP + j for g in range(layers) for j in range(GROUP)] for s in range(PANELS)
+    ]
     chips = [
         [g * ROWS + 2 * y + k for g in range(layers) for k in range(2)] for y in range(ROWS // 2)
     ]
 
     with jax.named_scope("mask"):
+        swap = [(i, i ^ 1) for i in range(ROWS)]
+        partner_factor = lax.ppermute(root_factor, "row", swap)
+        partner_pattern = lax.ppermute(pattern, "row", swap)
         block = rows_here // pattern.shape[0]
-        expanded = jnp.repeat(jnp.repeat(pattern, block, 0), block, 1)
         on_diagonal = row_index // GROUP == col_index // PAIR
-        masked_root = root_factor * jnp.where(on_diagonal, 1, expanded).astype(BF16)
-        partner_root = lax.ppermute(masked_root, "row", [(i, i ^ 1) for i in range(ROWS)])
-
-    with jax.named_scope("child_gather"):
-        child_panel = lax.all_gather(
-            child_factor[0], "row", axis=0, tiled=True, axis_index_groups=quarters
-        )
+
+        def masked(factor, blocks):
+            expanded = jnp.repeat(jnp.repeat(blocks, block, 0), block, 1)
+            return factor * jnp.where(on_diagonal, 1, expanded).astype(BF16)
+
+        masked_root = masked(root_factor, pattern)
+        partner_root = masked(partner_factor, partner_pattern)
+
+        partner_child = lax.ppermute(child_factor[0], "row", swap)
 
     with jax.named_scope("rhs"):
         probes_here = partials.shape[1]
@@ -116,43 +130,60 @@
         root_rhs = jnp.sum(pieces.astype(F32).reshape(layers, ROWS, 12 * lanes), 0)
         root_rhs = root_rhs.astype(BF16).astype(F32)
 
+    with jax.named_scope("gather"):
+        coupling_here, root_rhs, partner_child = lax.optimization_barrier(
+            (coupling[0], root_rhs, partner_child)
+        )
+        coupling_panel = lax.all_gather(
+            coupling_here, "row", axis=0, tiled=True, axis_index_groups=quarters
+        )
+
     with jax.named_scope("root"):
-        root_rows = sweep(
-            root_rhs,
-            lambda x: dot(x[:, :rows_here], masked_root) + dot(x[:, rows_here:], partner_root),
-            lambda x: jnp.concatenate([dot_t(x, masked_root), dot_t(x, partner_root)], 1),
-            2 * rows_here,
-            True,
-        )
+        own, other, _ = sweep(root_rhs, masked_root, partner_root)
 
     with jax.named_scope("coupling"):
-        own, other = root_rows[:, :rows_here], root_rows[:, rows_here:]
+        half = rows_here // 2
+        own_half, other_half = own[:, :half], other[:, :half]
+        halves = jnp.where(
+            core == 0,
+            jnp.concatenate([own_half, other_half], 1),
+            jnp.concatenate([other_half, own_half], 1),
+        )
+        some = ROWS // 2
+        shared = jnp.broadcast_to(
+            halves.reshape(1, 1, 2, some, rows_here), (layers, 2, 2, some, rows_here)
+        )
+        shared = lax.all_to_all(
+            shared.reshape(layers * GROUP, some, rows_here),
+            ("gz", "row"),
+            0,
+            0,
+            tiled=True,
+            axis_index_groups=panels,
+        )
+        shared = shared.reshape(layers, 2, 2, some, rows_here).transpose(3, 0, 2, 1, 4)
+        share = some * layers * 2
+        terms = dot(shared.reshape(share, 2 * rows_here), coupling_panel).astype(BF16)
+        coupled = terms.astype(F32)
+        for d in range(1, PANELS):
+            coupled = coupled + send(terms, [((p + d) % PANELS, p, 0, p, p, 0) for p in range(PANELS)])
+        bits = lax.dynamic_slice_in_dim(child_bits[0], core * share, share, 0)
+        child_rhs = (2 * bits - 1).astype(F32) - coupled
+
+    with jax.named_scope("child"):
         by_core = jnp.stack([jnp.where(core == k, own, other) for k in range(2)])
+        own, other, by_core = sweep(child_rhs, child_factor[0], partner_child, by_core)
+        other = lax.ppermute(other, "row", swap)
+        child_rows = jnp.where(
+            core == 0, jnp.concatenate([own, other], 0), jnp.concatenate([other, own], 0)
+        )
+
+    with jax.named_scope("root_out"):
         shared = jnp.broadcast_to(by_core[None], (layers,) + by_core.shape)
         shared = shared.reshape(layers * 2 * ROWS, rows_here)
         shared = lax.all_to_all(shared, ("gz", "row"), 0, 0, tiled=True, axis_index_groups=chips)
         root_all = shared.reshape(layers * 2, ROWS, rows_here).transpose(1, 0, 2)
         root_all = root_all.reshape(layers * 2 * ROWS, rows_here)
-        coupled = dot(root_all[:, : rows_here // 2], coupling[0]).astype(BF16)
-        coupled = lax.all_to_all(coupled, "row", 0, 0, tiled=True, axis_index_groups=quarters)
-        share = coupled.shape[0] // GROUP
-        coupled = jnp.sum(coupled.reshape(GROUP, share, -1).astype(F32), 0).astype(BF16)
-        coupled = lax.all_gather(coupled, "row", axis=0, axis_index_groups=across)
-        coupled = jnp.sum(coupled.astype(F32), 0)
-        bits = lax.dynamic_slice_in_dim(child_bits[0], row_index % GROUP * share, share, 0)
-        child_rhs = (2 * bits - 1).astype(F32) - coupled
-
-    with jax.named_scope("child"):
-        child_rows = sweep(
-            child_rhs,
-            lambda x: dot(x, child_panel),
-            lambda x: dot_t(x, child_panel),
-            child_panel.shape[0],
-            False,
-        )
-        child_rows = child_rows.reshape(share, GROUP, -1).transpose(1, 0, 2)
-        child_rows = child_rows.reshape(GROUP * share, -1)
-        child_rows = lax.all_to_all(child_rows, "row", 0, 0, tiled=True, axis_index_groups=quarters)
     return (root_all, child_rows[None])
 
 

time: 251 us -> 270 us (1.076)
  blocking collectives: 42.3 us -> 15.6 us
  waiting for transfers between devices: 90 us -> 113 us
  starting transfers between devices: 52.6 us -> 71.5 us
  other arithmetic: 4.24 us -> 8.72 us
  matrix products: 38.4 us -> 34.2 us
  local copies, waits for them, and re-layouts: 6.83 us -> 9.88 us
    ppermute x37 -> x43, waiting for transfers between devices: 72.9 us -> 100 us  [send(): return lax.ppermute(value, GRID, pairs).astype(F32)]
    all_to_all x2 -> x1, blocking collectives: 30.8 us -> 15.6 us  [per_device(): lax.all_to_all(shared.reshape(layers * GROUP, some, rows_here), ('gz', 'r...]
    all_gather x1 -> x0, blocking collectives: 11.5 us -> none  [per_device(): coupled = lax.all_gather(coupled, 'row', axis=0, axis_index_groups=across)]
    ppermute x37 -> x43, starting transfers between devices: 33.8 us -> 41.5 us  [send(): return lax.ppermute(value, GRID, pairs).astype(F32)]
    ppermute x1 -> x4, starting transfers between devices: 8.79 us -> 15 us  [the longest x1 8.78 us: per_device(): partner_factor = lax.ppermute(root_factor, 'row', swap)]
    dot_general x12 -> x16, matrix products: 17.7 us -> 11.8 us  [dot_t(): lax.dot_general(a, b, (((1,), (1,)), ((), ())), preferred_element_type=F32)]
    all_to_all x1, starting transfers between devices: 4.32 us -> 9.82 us  [per_device(): lax.all_to_all(shared, ('gz', 'row'), 0, 0, tiled=True, axis_index_groups...]
    all_to_all x1, waiting for transfers between devices: 11.9 us -> 8.96 us  [per_device(): lax.all_to_all(pieces.reshape(layers * ROWS, 12, lanes), ('gz', 'row'), 0...]
  transfers between devices with their start and end apart: 41 -> 50, of which waited for: 11 -> 12; matrix products, arithmetic and copies ran while one was open for 10% -> 10% of each run, Pallas kernels for 0% -> 0%
where the time goes in v3:
time: 270 us; the launch traced here: 268 us
  waiting for transfers between devices  113 us (42%)
  starting transfers between devices  71.5 us (26%)
  matrix products  34.2 us (13%)
  blocking collectives  15.6 us (6%)
  between operations  15.2 us (6%)
  local copies, waits for them, and re-layouts  9.88 us (4%)
  other arithmetic  8.72 us (3%)
    ppermute x43, waiting for transfers between devices, send(): return lax.ppermute(value, GRID, pairs).astype(F32)  100 us
    ppermute x43, starting transfers between devices, send(): return lax.ppermute(value, GRID, pairs).astype(F32)  41.5 us
    dot_general x21, matrix products, dot(): return jnp.dot(a, b, preferred_element_type=F32)  22.4 us
    all_to_all x1, blocking collectives, per_device(): lax.all_to_all(shared.reshape(layers * GROUP, some, rows_here), ('gz', 'r...  15.6 us
    dot_general x16, matrix products, dot_t(): lax.dot_general(a, b, (((1,), (1,)), ((), ())), preferred_element_type=F32)  11.8 us
    all_to_all x1, starting transfers between devices, per_device(): lax.all_to_all(shared, ('gz', 'row'), 0, 0, tiled=True, axis_index_groups...  9.82 us
    all_to_all x1, waiting for transfers between devices, per_device(): lax.all_to_all(pieces.reshape(layers * ROWS, 12, lanes), ('gz', 'row'), 0...  8.96 us
    ppermute x1, starting transfers between devices, per_device(): partner_factor = lax.ppermute(root_factor, 'row', swap)  8.78 us
  transfers between devices with their start and end apart: 50, of which 12 were waited for; matrix products, arithmetic and copies ran while one was open for 10% of the time, Pallas kernels for 0%

profile of v3, /device:TPU:1, one launch (start us, length us, event | category | flops | bytes accessed | tf_op | source)
XLA Modules:
  0.0 268.3 jit_solution(9971497863243997783)
XLA Ops:
  7.2 4.4 %copy.26 = bf16[768,1536]{0,1:T(8,128)(2,1)} copy(bf16[768,1536]{1,0:T(8,128)(2,1)} %param.6) | data formatting | bytes 4718592 | tf_op args[0]
  11.6 8.8 %collective-permute-start.1 = (bf16[768,1536]{0,1:T(8,128)(2,1)}, bf16[768,1536]{0,1:T(8,128)(2,1)}, u32[]{:S(2)}, u32[]{:S(2)}) collective-permute-start(bf16[768,1536]{0,1:T(8,128)(2,1)} %copy.26), channel_id=1, source_target_pairs={{0,8},{8,0},{16,24},{24,16},{32,40},{40,32},{48,56},{56,48},{64,72... | collective-permute-start | bytes 7077896 | tf_op jit(solution)/shard_map/mask/ppermute | solution.py:108
  20.4 1.9 collective-permute-start
  22.3 2.4 collective-permute-start.2
  25.5 5.1 %all-to-all-start = ((bf16[64,12,128]{2,1,0:T(8,128)(2,1)}), bf16[64,12,128]{2,1,0:T(8,128)(2,1)}, u32[]{:S(2)}, u32[]{:S(2)}) async-start(bf16[64,12,128]{2,1,0:T(8,128)(2,1)} %bitcast.2), calls=%async_computation | async-start | bytes 524288 | tf_op jit(solution)/shard_map/rhs/all_to_all | solution.py:127
  30.8 1.8 bitcast_multiply_fusion.1
  33.5 9.0 %all-to-all-done = bf16[64,12,128]{2,1,0:T(8,128)(2,1)} async-done(((bf16[64,12,128]{2,1,0:T(8,128)(2,1)}), bf16[64,12,128]{2,1,0:T(8,128)(2,1)}, u32[]{:S(2)}, u32[]{:S(2)}) %all-to-all-start) | async-done | bytes 196640 | tf_op jit(solution)/shard_map/rhs/all_to_all | solution.py:127
  42.5 1.8 reshape.145
  45.9 1.8 bitcast_multiply_fusion
  50.3 1.4 fusion.4
  60.4 1.4 fusion.5
  69.0 1.5 fusion.8
  71.9 2.2 fusion.7
  75.4 1.3 collective-permute-start.18
  76.7 28.6 %collective-permute-done.17 = bf16[16,1536]{1,0:T(8,128)(2,1)S(1)} collective-permute-done((bf16[16,1536]{1,0:T(8,128)(2,1)}, bf16[16,1536]{1,0:T(8,128)(2,1)S(1)}, u32[]{:S(2)}, u32[]{:S(2)}) %collective-permute-start.17) | collective-permute-done | bytes 49184 | tf_op jit(solution)/shard_map/root/ppermute | solution.py:32
  105.3 4.9 %collective-permute-done.18 = bf16[16,1536]{1,0:T(8,128)(2,1)} collective-permute-done((bf16[16,1536]{1,0:T(8,128)(2,1)}, bf16[16,1536]{1,0:T(8,128)(2,1)}, u32[]{:S(2)}, u32[]{:S(2)}) %collective-permute-start.18) | collective-permute-done | bytes 49184 | tf_op jit(solution)/shard_map/root/ppermute | solution.py:32
  111.9 1.3 collective-permute-start.19
  113.2 1.3 collective-permute-start.20
  114.5 1.9 collective-permute-start.21
  116.5 3.7 %collective-permute-done.21 = bf16[16,1536]{1,0:T(8,128)(2,1)S(1)} collective-permute-done((bf16[16,1536]{1,0:T(8,128)(2,1)S(1)}, bf16[16,1536]{1,0:T(8,128)(2,1)S(1)}, u32[]{:S(2)}, u32[]{:S(2)}) %collective-permute-start.21) | collective-permute-done | bytes 49184 | tf_op jit(solution)/shard_map/root/ppermute | solution.py:32
  120.2 1.3 collective-permute-start.22
  121.5 1.5 collective-permute-done.22
  123.0 15.6 %all_to_all.19 = bf16[16,8,768]{2,1,0:T(8,128)(2,1)S(1)} all-to-all(bf16[16,8,768]{2,1,0:T(8,128)(2,1)S(1)} %bitcast.104), channel_id=1, replica_groups={{0,8,16,24,128,136,144,152,256,264,272,280,384,392,400,408},{32,40,48,5..., dimensions={0} | all-to-all | bytes 393216 | tf_op jit(solution)/shard_map/coupling/all_to_all | solution.py:156
  138.8 2.6 convolution_convert_fusion
  141.4 1.3 collective-permute-start.23
  142.7 1.3 collective-permute-start.24
  144.0 1.3 collective-permute-start.25
  145.3 9.5 %collective-permute-done.23 = bf16[64,1024]{1,0:T(8,128)(2,1)S(1)} collective-permute-done((bf16[64,1024]{1,0:T(8,128)(2,1)S(1)}, bf16[64,1024]{1,0:T(8,128)(2,1)S(1)}, u32[]{:S(2)}, u32[]{:S(2)}) %collective-permute-start.23) | collective-permute-done | bytes 131104 | tf_op jit(solution)/shard_map/coupling/ppermute | solution.py:32
  156.3 1.7 convolution_convert_fusion.7
  159.7 1.5 fusion.13
  163.5 1.7 convolution_convert_fusion.5
  165.7 1.5 fusion.32
  170.0 1.5 fusion.14
  173.6 1.7 convolution_convert_fusion.3
  175.9 1.5 fusion.26
  180.1 1.5 fusion.16
  181.7 1.3 collective-permute-start.40
  184.3 42.3 %collective-permute-done.40 = bf16[64,1024]{1,0:T(8,128)(2,1)S(1)} collective-permute-done((bf16[64,1024]{1,0:T(8,128)(2,1)S(1)}, bf16[64,1024]{1,0:T(8,128)(2,1)S(1)}, u32[]{:S(2)}, u32[]{:S(2)}) %collective-permute-start.40) | collective-permute-done | bytes 131104 | tf_op jit(solution)/shard_map/child/ppermute | solution.py:32
  226.6 4.9 %collective-permute-done.41 = bf16[64,1024]{1,0:T(8,128)(2,1)S(1)} collective-permute-done((bf16[64,1024]{1,0:T(8,128)(2,1)S(1)}, bf16[64,1024]{1,0:T(8,128)(2,1)S(1)}, u32[]{:S(2)}, u32[]{:S(2)}) %collective-permute-start.41) | collective-permute-done | bytes 131104 | tf_op jit(solution)/shard_map/child/ppermute | solution.py:32
  231.5 1.7 convolution_convert_fusion.1
  233.7 1.3 collective-permute-start.42
  235.0 1.3 collective-permute-start.43
  236.3 1.9 collective-permute-start.44
  238.8 3.4 %collective-permute-done.44 = bf16[64,1024]{1,0:T(8,128)(2,1)S(1)} collective-permute-done((bf16[64,1024]{1,0:T(8,128)(2,1)S(1)}, bf16[64,1024]{1,0:T(8,128)(2,1)S(1)}, u32[]{:S(2)}, u32[]{:S(2)}) %collective-permute-start.44) | collective-permute-done | bytes 131104 | tf_op jit(solution)/shard_map/child/ppermute | solution.py:32
  242.3 1.3 collective-permute-start.45
  244.3 9.8 %all-to-all-start.2 = ((bf16[8,16,768]{2,1,0:T(8,128)(2,1)}), bf16[8,16,768]{2,1,0:T(8,128)(2,1)S(1)}, u32[]{:S(2)}, u32[]{:S(2)}) async-start(bf16[8,16,768]{2,1,0:T(8,128)(2,1)} %bitcast.13), calls=%async_computation.2 | async-start | bytes 393216 | tf_op jit(solution)/shard_map/root_out/all_to_all | solution.py:184
  254.2 1.9 collective-permute-start.46
  256.2 3.9 %all-to-all-done.2 = bf16[8,16,768]{2,1,0:T(8,128)(2,1)S(1)} async-done(((bf16[8,16,768]{2,1,0:T(8,128)(2,1)}), bf16[8,16,768]{2,1,0:T(8,128)(2,1)S(1)}, u32[]{:S(2)}, u32[]{:S(2)}) %all-to-all-start.2) | async-done | bytes 196640 | tf_op jit(solution)/shard_map/root_out/all_to_all | solution.py:184
  (178 shorter events, 44.9 us)
Async XLA Ops:
  11.6 34.1 %collective-permute-start.1 = (bf16[768,1536]{0,1:T(8,128)(2,1)}, bf16[768,1536]{0,1:T(8,128)(2,1)}, u32[]{:S(2)}, u32[]{:S(2)}) collective-permute-start(bf16[768,1536]{0,1:T(8,128)(2,1)} %copy.26), channel_id=1, source_target_pairs={{0,8},{8,0},{16,24},{24,16},{32,40},{40,32},{48,56},{56,48},{64,72... | collective-permute-start | bytes 7077896 | tf_op jit(solution)/shard_map/mask/ppermute | solution.py:108
  20.4 24.9 %collective-permute-start = (bf16[512,1024]{1,0:T(8,128)(2,1)S(1)}, bf16[512,1024]{1,0:T(8,128)(2,1)}, u32[]{:S(2)}, u32[]{:S(2)}) collective-permute-start(bf16[512,1024]{1,0:T(8,128)(2,1)S(1)} %bitcast.102), channel_id=1, source_target_pairs={{0,8},{8,0},{16,24},{24,16},{32,40},{40,32},{48,56},{56,48},{64,72... | collective-permute-start | bytes 3145736 | tf_op jit(solution)/shard_map/mask/ppermute | solution.py:120
  22.3 10.4 %collective-permute-start.2 = (s32[3,6]{1,0:T(4,128)S(1)}, s32[3,6]{1,0:T(4,128)S(1)}, u32[]{:S(2)}, u32[]{:S(2)}) collective-permute-start(s32[3,6]{1,0:T(4,128)S(1)} %copy-done.16), channel_id=1, source_target_pairs={{0,8},{8,0},{16,24},{24,16},{32,40},{40,32},{48,56},{56,48},{64,72... | collective-permute-start | bytes 224 | tf_op jit(solution)/shard_map/mask/ppermute | solution.py:109
  25.5 17.0 %all-to-all-start = ((bf16[64,12,128]{2,1,0:T(8,128)(2,1)}), bf16[64,12,128]{2,1,0:T(8,128)(2,1)}, u32[]{:S(2)}, u32[]{:S(2)}) async-start(bf16[64,12,128]{2,1,0:T(8,128)(2,1)} %bitcast.2), calls=%async_computation | async-start | bytes 524288 | tf_op jit(solution)/shard_map/rhs/all_to_all | solution.py:127
  30.6 108.2 %all-gather.2.cloned.1.call-start = ((), (), s32[]{:S(2)}) async-start(), calls=%async_computation.3 | async-start | bytes 3932160 | tf_op jit(solution)/shard_map/gather/all_gather | solution.py:137
  48.2 1.3 collective-permute-start.3
  51.7 2.7 %collective-permute-start.5 = (bf16[16,1536]{1,0:T(8,128)(2,1)}, bf16[16,1536]{1,0:T(8,128)(2,1)S(1)}, u32[]{:S(2)}, u32[]{:S(2)}) collective-permute-start(bf16[16,1536]{1,0:T(8,128)(2,1)} %fusion.4), channel_id=1, source_target_pairs={{100,68},{101,69},{108,76},{109,77},{116,84},{117,85},{124,92},{12... | collective-permute-start | bytes 147464 | tf_op jit(solution)/shard_map/root/ppermute | solution.py:32
  52.3 2.1 collective-permute-start.6
  53.6 2.5 collective-permute-start.7
  56.9 2.7 %collective-permute-start.8 = (bf16[16,1536]{1,0:T(8,128)(2,1)S(1)}, bf16[16,1536]{1,0:T(8,128)(2,1)S(1)}, u32[]{:S(2)}, u32[]{:S(2)}) collective-permute-start(bf16[16,1536]{1,0:T(8,128)(2,1)S(1)} %add_convert_fusion.12), channel_id=1, source_target_pairs={{68,66},{69,67},{76,74},{77,75},{84,82},{85,83},{92,90},{93,91},{9... | collective-permute-start | bytes 147464 | tf_op jit(solution)/shard_map/root/ppermute | solution.py:32
  57.6 2.1 collective-permute-start.9
  58.9 1.5 collective-permute-start.10
  61.8 3.4 %collective-permute-start.11 = (bf16[16,1536]{1,0:T(8,128)(2,1)}, bf16[16,1536]{1,0:T(8,128)(2,1)}, u32[]{:S(2)}, u32[]{:S(2)}) collective-permute-start(bf16[16,1536]{1,0:T(8,128)(2,1)} %fusion.5), channel_id=1, source_target_pairs={{66,34},{67,35},{74,42},{75,43},{82,50},{83,51},{90,58},{91,59},{9... | collective-permute-start | bytes 147464 | tf_op jit(solution)/shard_map/root/ppermute | solution.py:32
  63.0 2.1 collective-permute-start.12
  64.3 2.5 collective-permute-start.13
  66.9 4.3 %collective-permute-start.14 = (bf16[16,1536]{1,0:T(8,128)(2,1)S(1)}, bf16[16,1536]{1,0:T(8,128)(2,1)S(1)}, u32[]{:S(2)}, u32[]{:S(2)}) collective-permute-start(bf16[16,1536]{1,0:T(8,128)(2,1)S(1)} %add_convert_fusion.10), channel_id=1, source_target_pairs={{34,32},{35,33},{42,40},{43,41},{50,48},{51,49},{58,56},{59,57},{6... | collective-permute-start | bytes 147464 | tf_op jit(solution)/shard_map/root/ppermute | solution.py:32
  67.6 3.6 %collective-permute-start.15 = (bf16[16,1536]{1,0:T(8,128)(2,1)S(1)}, bf16[16,1536]{1,0:T(8,128)(2,1)S(1)}, u32[]{:S(2)}, u32[]{:S(2)}) collective-permute-start(bf16[16,1536]{1,0:T(8,128)(2,1)S(1)} %add_convert_fusion.10), channel_id=1, source_target_pairs={{34,33},{35,32},{42,41},{43,40},{50,49},{51,48},{58,57},{59,56},{6... | collective-permute-start | bytes 147464 | tf_op jit(solution)/shard_map/root/ppermute | solution.py:32
  70.5 1.5 collective-permute-start.16
  74.1 31.2 %collective-permute-start.17 = (bf16[16,1536]{1,0:T(8,128)(2,1)}, bf16[16,1536]{1,0:T(8,128)(2,1)S(1)}, u32[]{:S(2)}, u32[]{:S(2)}) collective-permute-start(bf16[16,1536]{1,0:T(8,128)(2,1)} %fusion.7), channel_id=1, source_target_pairs={{32,0},{33,1},{40,8},{41,9},{48,16},{49,17},{56,24},{57,25},{160,1... | collective-permute-start | bytes 147464 | tf_op jit(solution)/shard_map/root/ppermute | solution.py:32
  75.4 34.8 %collective-permute-start.18 = (bf16[16,1536]{1,0:T(8,128)(2,1)}, bf16[16,1536]{1,0:T(8,128)(2,1)}, u32[]{:S(2)}, u32[]{:S(2)}) collective-permute-start(bf16[16,1536]{1,0:T(8,128)(2,1)} %fusion.7), channel_id=1, source_target_pairs={{32,16},{33,17},{40,24},{41,25},{48,0},{49,1},{56,8},{57,9},{160,1... | collective-permute-start | bytes 147464 | tf_op jit(solution)/shard_map/root/ppermute | solution.py:32
  111.9 4.5 %collective-permute-start.19 = (bf16[16,1536]{1,0:T(8,128)(2,1)S(1)}, bf16[16,1536]{1,0:T(8,128)(2,1)S(1)}, u32[]{:S(2)}, u32[]{:S(2)}) collective-permute-start(bf16[16,1536]{1,0:T(8,128)(2,1)S(1)} %maximum_select_fusion.7), channel_id=1, source_target_pairs={{0,6},{1,7},{8,14},{9,15},{16,22},{17,23},{24,30},{25,31},{32,38},... | collective-permute-start | bytes 147464 | tf_op jit(solution)/shard_map/root/ppermute | solution.py:32
  113.2 3.2 %collective-permute-start.20 = (bf16[16,1536]{1,0:T(8,128)(2,1)S(1)}, bf16[16,1536]{1,0:T(8,128)(2,1)S(1)}, u32[]{:S(2)}, u32[]{:S(2)}) collective-permute-start(bf16[16,1536]{1,0:T(8,128)(2,1)S(1)} %maximum_select_fusion.7), channel_id=1, source_target_pairs={{0,7},{1,6},{8,15},{9,14},{16,23},{17,22},{24,31},{25,30},{34,35},... | collective-permute-start | bytes 147464 | tf_op jit(solution)/shard_map/root/ppermute | solution.py:32
  114.5 5.6 %collective-permute-start.21 = (bf16[16,1536]{1,0:T(8,128)(2,1)S(1)}, bf16[16,1536]{1,0:T(8,128)(2,1)S(1)}, u32[]{:S(2)}, u32[]{:S(2)}) collective-permute-start(bf16[16,1536]{1,0:T(8,128)(2,1)S(1)} %maximum_select_fusion.7), channel_id=1, source_target_pairs={{0,1},{1,0},{8,9},{9,8},{16,17},{17,16},{24,25},{25,24},{128,129},... | collective-permute-start | bytes 147464 | tf_op jit(solution)/shard_map/root/ppermute | solution.py:32
  120.2 2.8 %collective-permute-start.22 = (bf16[16,1536]{1,0:T(8,128)(2,1)S(1)}, bf16[16,1536]{1,0:T(8,128)(2,1)S(1)}, u32[]{:S(2)}, u32[]{:S(2)}) collective-permute-start(bf16[16,1536]{1,0:T(8,128)(2,1)S(1)} %add_convert_fusion.8), channel_id=1, source_target_pairs={{0,2},{1,3},{8,10},{9,11},{16,18},{17,19},{24,26},{25,27},{6,4},{7... | collective-permute-start | bytes 147464 | tf_op jit(solution)/shard_map/root/ppermute | solution.py:32
  141.4 13.4 %collective-permute-start.23 = (bf16[64,1024]{1,0:T(8,128)(2,1)S(1)}, bf16[64,1024]{1,0:T(8,128)(2,1)S(1)}, u32[]{:S(2)}, u32[]{:S(2)}) collective-permute-start(bf16[64,1024]{1,0:T(8,128)(2,1)S(1)} %convolution_convert_fusion), channel_id=1, source_target_pairs={{32,0},{33,1},{40,8},{41,9},{48,16},{49,17},{56,24},{57,25},{66,34... | collective-permute-start | bytes 393224 | tf_op jit(solution)/shard_map/coupling/ppermute | solution.py:32
  142.7 12.1 %collective-permute-start.24 = (bf16[64,1024]{1,0:T(8,128)(2,1)S(1)}, bf16[64,1024]{1,0:T(8,128)(2,1)S(1)}, u32[]{:S(2)}, u32[]{:S(2)}) collective-permute-start(bf16[64,1024]{1,0:T(8,128)(2,1)S(1)} %convolution_convert_fusion), channel_id=1, source_target_pairs={{64,0},{65,1},{72,8},{73,9},{80,16},{81,17},{88,24},{89,25},{98,34... | collective-permute-start | bytes 393224 | tf_op jit(solution)/shard_map/coupling/ppermute | solution.py:32
  144.0 11.7 %collective-permute-start.25 = (bf16[64,1024]{1,0:T(8,128)(2,1)S(1)}, bf16[64,1024]{1,0:T(8,128)(2,1)S(1)}, u32[]{:S(2)}, u32[]{:S(2)}) collective-permute-start(bf16[64,1024]{1,0:T(8,128)(2,1)S(1)} %convolution_convert_fusion), channel_id=1, source_target_pairs={{96,0},{97,1},{104,8},{105,9},{112,16},{113,17},{120,24},{121,25},... | collective-permute-start | bytes 393224 | tf_op jit(solution)/shard_map/coupling/ppermute | solution.py:32
  158.0 1.4 collective-permute-start.26
  161.2 2.2 collective-permute-start.28
  161.9 1.6 collective-permute-start.29
  162.8 2.9 %collective-permute-start.30 = (bf16[64,1024]{1,0:T(8,128)(2,1)S(1)}, bf16[64,1024]{1,0:T(8,128)(2,1)S(1)}, u32[]{:S(2)}, u32[]{:S(2)}) collective-permute-start(bf16[64,1024]{1,0:T(8,128)(2,1)S(1)} %add_convert_fusion.6), channel_id=1, source_target_pairs={{100,98},{101,99},{108,106},{109,107},{116,114},{117,115},{124,122... | collective-permute-start | bytes 393224 | tf_op jit(solution)/shard_map/child/ppermute | solution.py:32
  167.2 2.3 collective-permute-start.31
  167.9 1.7 collective-permute-start.32
  168.9 1.1 collective-permute-start.33
  171.5 2.1 collective-permute-start.34
  172.2 1.4 collective-permute-start.35
  172.9 2.9 %collective-permute-start.36 = (bf16[64,1024]{1,0:T(8,128)(2,1)S(1)}, bf16[64,1024]{1,0:T(8,128)(2,1)S(1)}, u32[]{:S(2)}, u32[]{:S(2)}) collective-permute-start(bf16[64,1024]{1,0:T(8,128)(2,1)S(1)} %add_convert_fusion.4), channel_id=1, source_target_pairs={{66,64},{67,65},{74,72},{75,73},{82,80},{83,81},{90,88},{91,89},{1... | collective-permute-start | bytes 393224 | tf_op jit(solution)/shard_map/child/ppermute | solution.py:32
  177.4 2.4 collective-permute-start.37
  178.1 1.7 collective-permute-start.38
  179.1 1.1 collective-permute-start.39
  181.7 44.9 %collective-permute-start.40 = (bf16[64,1024]{1,0:T(8,128)(2,1)S(1)}, bf16[64,1024]{1,0:T(8,128)(2,1)S(1)}, u32[]{:S(2)}, u32[]{:S(2)}) collective-permute-start(bf16[64,1024]{1,0:T(8,128)(2,1)S(1)} %fusion.16), channel_id=1, source_target_pairs={{32,0},{33,1},{40,8},{41,9},{48,16},{49,17},{56,24},{57,25},{160,1... | collective-permute-start | bytes 393224 | tf_op jit(solution)/shard_map/child/ppermute | solution.py:32
  183.0 48.5 %collective-permute-start.41 = (bf16[64,1024]{1,0:T(8,128)(2,1)S(1)}, bf16[64,1024]{1,0:T(8,128)(2,1)S(1)}, u32[]{:S(2)}, u32[]{:S(2)}) collective-permute-start(bf16[64,1024]{1,0:T(8,128)(2,1)S(1)} %fusion.16), channel_id=1, source_target_pairs={{32,16},{33,17},{40,24},{41,25},{48,0},{49,1},{56,8},{57,9},{160,1... | collective-permute-start | bytes 393224 | tf_op jit(solution)/shard_map/child/ppermute | solution.py:32
  233.7 4.5 %collective-permute-start.42 = (bf16[64,1024]{1,0:T(8,128)(2,1)S(1)}, bf16[64,1024]{1,0:T(8,128)(2,1)S(1)}, u32[]{:S(2)}, u32[]{:S(2)}) collective-permute-start(bf16[64,1024]{1,0:T(8,128)(2,1)S(1)} %maximum_select_fusion.2), channel_id=1, source_target_pairs={{0,6},{1,7},{8,14},{9,15},{16,22},{17,23},{24,30},{25,31},{32,38},... | collective-permute-start | bytes 393224 | tf_op jit(solution)/shard_map/child/ppermute | solution.py:32
  235.0 3.8 %collective-permute-start.43 = (bf16[64,1024]{1,0:T(8,128)(2,1)S(1)}, bf16[64,1024]{1,0:T(8,128)(2,1)S(1)}, u32[]{:S(2)}, u32[]{:S(2)}) collective-permute-start(bf16[64,1024]{1,0:T(8,128)(2,1)S(1)} %maximum_select_fusion.2), channel_id=1, source_target_pairs={{0,7},{1,6},{8,15},{9,14},{16,23},{17,22},{24,31},{25,30},{34,35},... | collective-permute-start | bytes 393224 | tf_op jit(solution)/shard_map/child/ppermute | solution.py:32
  236.3 6.0 %collective-permute-start.44 = (bf16[64,1024]{1,0:T(8,128)(2,1)S(1)}, bf16[64,1024]{1,0:T(8,128)(2,1)S(1)}, u32[]{:S(2)}, u32[]{:S(2)}) collective-permute-start(bf16[64,1024]{1,0:T(8,128)(2,1)S(1)} %maximum_select_fusion.2), channel_id=1, source_target_pairs={{0,1},{1,0},{8,9},{9,8},{16,17},{17,16},{24,25},{25,24},{128,129},... | collective-permute-start | bytes 393224 | tf_op jit(solution)/shard_map/child/ppermute | solution.py:32
  242.3 11.8 %collective-permute-start.45 = (bf16[64,1024]{1,0:T(8,128)(2,1)S(1)}, bf16[64,1024]{1,0:T(8,128)(2,1)S(1)}, u32[]{:S(2)}, u32[]{:S(2)}) collective-permute-start(bf16[64,1024]{1,0:T(8,128)(2,1)S(1)} %add_convert_fusion.1), channel_id=1, source_target_pairs={{0,2},{1,3},{8,10},{9,11},{16,18},{17,19},{24,26},{25,27},{6,4},{7... | collective-permute-start | bytes 393224 | tf_op jit(solution)/shard_map/child/ppermute | solution.py:32
  244.3 15.7 %all-to-all-start.2 = ((bf16[8,16,768]{2,1,0:T(8,128)(2,1)}), bf16[8,16,768]{2,1,0:T(8,128)(2,1)S(1)}, u32[]{:S(2)}, u32[]{:S(2)}) async-start(bf16[8,16,768]{2,1,0:T(8,128)(2,1)} %bitcast.13), calls=%async_computation.2 | async-start | bytes 393216 | tf_op jit(solution)/shard_map/root_out/all_to_all | solution.py:184
  254.2 6.6 %collective-permute-start.46 = (bf16[64,512]{1,0:T(8,128)(2,1)S(1)}, bf16[64,512]{1,0:T(8,128)(2,1)S(1)}, u32[]{:S(2)}, u32[]{:S(2)}) collective-permute-start(bf16[64,512]{1,0:T(8,128)(2,1)S(1)} %get-tuple-element.13), channel_id=1, source_target_pairs={{0,8},{8,0},{16,24},{24,16},{32,40},{40,32},{48,56},{56,48},{64,72... | collective-permute-start | bytes 196616 | tf_op jit(solution)/shard_map/child/ppermute | solution.py:176
  (19 other events, 136.9 us)
Sparse Core Ops, SparseCore 0:
  64.4 63.8 all-gather.1

commit v4 on v1

--- a/solution.py
+++ b/solution.py
@@ -32,10 +32,18 @@
     return lax.ppermute(value, GRID, pairs).astype(F32)
 
 
-def sweep(rhs, forward, diagonal, width, split_rows):
+def sweep(rhs, own, other, split_rows):
+    rows = own.shape[0]
+
+    def forward(x):
+        return dot(x[:, :rows], own) + dot(x[:, rows:], other)
+
+    def diagonal(x):
+        return jnp.concatenate([dot_t(x, own), dot_t(x, other)], 1)
+
     row_panel = lax.axis_index("row") // GROUP
     col_panel = lax.axis_index("col") // PAIR
-    current = jnp.zeros((rhs.shape[0], width), BF16)
+    current = jnp.zeros((rhs.shape[0], 2 * rows), BF16)
     carried = jnp.zeros(rhs.shape, F32)
     totals = jnp.zeros(rhs.shape, F32)
     for r in range(PANELS - 1, -1, -1):
@@ -78,7 +86,7 @@
             current = (current.astype(F32) + received).astype(BF16)
             received = send(current, [(0, 0, 0, 0, 1, 0), (0, 0, 0, 3, 2, 0), (1, 1, 0, 3, 2, 0)])
             current = (current.astype(F32) + received).astype(BF16)
-    return current
+    return current[:, :rows], current[:, rows:]
 
 
 def per_device(root_factor, partials, pattern, coupling, child_factor, child_bits):
@@ -88,22 +96,25 @@
     col_index = lax.axis_index("col")
     core = row_index % 2
     quarters = [[s * GROUP + j for j in range(GROUP)] for s in range(PANELS)]
-    across = [[s * GROUP + j for s in range(PANELS)] for j in range(GROUP)]
+    opposite = [[s * GROUP + k, s * GROUP + 2 + k] for s in range(PANELS) for k in range(2)]
     chips = [
         [g * ROWS + 2 * y + k for g in range(layers) for k in range(2)] for y in range(ROWS // 2)
     ]
 
     with jax.named_scope("mask"):
+        swap = [(i, i ^ 1) for i in range(ROWS)]
+        partner_factor = lax.ppermute(root_factor, "row", swap)
+        partner_pattern = lax.ppermute(pattern, "row", swap)
         block = rows_here // pattern.shape[0]
-        expanded = jnp.repeat(jnp.repeat(pattern, block, 0), block, 1)
         on_diagonal = row_index // GROUP == col_index // PAIR
-        masked_root = root_factor * jnp.where(on_diagonal, 1, expanded).astype(BF16)
-        partner_root = lax.ppermute(masked_root, "row", [(i, i ^ 1) for i in range(ROWS)])
 
-    with jax.named_scope("child_gather"):
-        child_panel = lax.all_gather(
-            child_factor[0], "row", axis=0, tiled=True, axis_index_groups=quarters
-        )
+        def masked(factor, blocks):
+            expanded = jnp.repeat(jnp.repeat(blocks, block, 0), block, 1)
+            return factor * jnp.where(on_diagonal, 1, expanded).astype(BF16)
+
+        masked_root = masked(root_factor, pattern)
+        partner_root = masked(partner_factor, partner_pattern)
+
 
     with jax.named_scope("rhs"):
         probes_here = partials.shape[1]
@@ -113,44 +124,42 @@
         pieces = lax.all_to_all(
             pieces.reshape(layers * ROWS, 12, lanes), ("gz", "row"), 0, 0, tiled=True
         )
-        root_rhs = jnp.sum(pieces.astype(F32).reshape(layers, ROWS, 12 * lanes), 0)
-        root_rhs = root_rhs.astype(BF16).astype(F32)
+        root_rhs = jnp.sum(pieces.astype(F32).reshape(layers, ROWS, 12, lanes), 0)
+        root_rhs = root_rhs.astype(BF16).reshape(ROWS, 12 * lanes).astype(F32)
+
+    with jax.named_scope("child_gather"):
+        child_own = lax.all_gather(
+            child_factor[0], "row", axis=0, tiled=True, axis_index_groups=opposite
+        )
 
     with jax.named_scope("root"):
-        root_rows = sweep(
-            root_rhs,
-            lambda x: dot(x[:, :rows_here], masked_root) + dot(x[:, rows_here:], partner_root),
-            lambda x: jnp.concatenate([dot_t(x, masked_root), dot_t(x, partner_root)], 1),
-            2 * rows_here,
-            True,
-        )
+        own, other = sweep(root_rhs, masked_root, partner_root, True)
 
     with jax.named_scope("coupling"):
-        own, other = root_rows[:, :rows_here], root_rows[:, rows_here:]
         by_core = jnp.stack([jnp.where(core == k, own, other) for k in range(2)])
+        by_core, child_own = lax.optimization_barrier((by_core, child_own))
+        child_other = lax.ppermute(child_own, "row", swap)
         shared = jnp.broadcast_to(by_core[None], (layers,) + by_core.shape)
         shared = shared.reshape(layers * 2 * ROWS, rows_here)
         shared = lax.all_to_all(shared, ("gz", "row"), 0, 0, tiled=True, axis_index_groups=chips)
         root_all = shared.reshape(layers * 2, ROWS, rows_here).transpose(1, 0, 2)
         root_all = root_all.reshape(layers * 2 * ROWS, rows_here)
-        coupled = dot(root_all[:, : rows_here // 2], coupling[0]).astype(BF16)
-        coupled = lax.all_to_all(coupled, "row", 0, 0, tiled=True, axis_index_groups=quarters)
-        share = coupled.shape[0] // GROUP
-        coupled = jnp.sum(coupled.reshape(GROUP, share, -1).astype(F32), 0).astype(BF16)
-        coupled = lax.all_gather(coupled, "row", axis=0, axis_index_groups=across)
-        coupled = jnp.sum(coupled.astype(F32), 0)
+        terms = dot(root_all[:, : rows_here // 2], coupling[0]).astype(BF16)
+        terms = lax.all_to_all(terms, "row", 0, 0, tiled=True, axis_index_groups=quarters)
+        share = terms.shape[0] // GROUP
+        terms = jnp.sum(terms.reshape(GROUP, share, -1).astype(F32), 0).astype(BF16)
+        coupled = terms.astype(F32)
+        for d in range(1, PANELS):
+            coupled = coupled + send(terms, [((p + d) % PANELS, p, 0, p, p, 0) for p in range(PANELS)])
         bits = lax.dynamic_slice_in_dim(child_bits[0], row_index % GROUP * share, share, 0)
         child_rhs = (2 * bits - 1).astype(F32) - coupled
 
     with jax.named_scope("child"):
-        child_rows = sweep(
-            child_rhs,
-            lambda x: dot(x, child_panel),
-            lambda x: dot_t(x, child_panel),
-            child_panel.shape[0],
-            False,
+        own, other = sweep(child_rhs, child_own, child_other, False)
+        blocks = jnp.stack(
+            [jnp.where(core == k, own, other).reshape(share, 2, -1) for k in range(2)], 2
         )
-        child_rows = child_rows.reshape(share, GROUP, -1).transpose(1, 0, 2)
+        child_rows = blocks.reshape(share, GROUP, -1).transpose(1, 0, 2)
         child_rows = child_rows.reshape(GROUP * share, -1)
         child_rows = lax.all_to_all(child_rows, "row", 0, 0, tiled=True, axis_index_groups=quarters)
     return (root_all, child_rows[None])

time: 251 us -> 270 us (1.076)
  waiting for transfers between devices: 90 us -> 118 us
  blocking collectives: 42.3 us -> 30.8 us
  starting transfers between devices: 52.6 us -> 55.8 us
    all_gather x1, waiting for transfers between devices: 0.02 us -> 22.3 us  [per_device(): lax.all_gather(child_factor[0], 'row', axis=0, tiled=True, axis_index_gro...]
    ppermute x37 -> x40, waiting for transfers between devices: 72.9 us -> 86.2 us  [send(): return lax.ppermute(value, GRID, pairs).astype(F32)]
    all_gather x1 -> x0, blocking collectives: 11.5 us -> none  [per_device(): coupled = lax.all_gather(coupled, 'row', axis=0, axis_index_groups=across)]
    all_to_all x0 -> x1, blocking collectives: none -> 8.34 us  [per_device(): lax.all_to_all(terms, 'row', 0, 0, tiled=True, axis_index_groups=quarters)]
    all_to_all x1 -> x0, waiting for transfers between devices: 5.17 us -> none  [per_device(): lax.all_to_all(coupled, 'row', 0, 0, tiled=True, axis_index_groups=quarters)]
    all_to_all x1, blocking collectives: 15 us -> 10.1 us  [per_device(): lax.all_to_all(shared, ('gz', 'row'), 0, 0, tiled=True, axis_index_groups...]
    ppermute x1 -> x3, starting transfers between devices: 8.79 us -> 13.4 us  [the longest x1 8.78 us: per_device(): partner_factor = lax.ppermute(root_factor, 'row', swap)]
    all_to_all x1 -> x0, starting transfers between devices: 4.32 us -> none  [per_device(): lax.all_to_all(coupled, 'row', 0, 0, tiled=True, axis_index_groups=quarters)]
  transfers between devices with their start and end apart: 41 -> 45, of which waited for: 11 -> 14; matrix products, arithmetic and copies ran while one was open for 10% -> 9% of each run, Pallas kernels for 0% -> 0%
where the time goes in v4:
time: 270 us; the launch traced here: 268 us
  waiting for transfers between devices  118 us (44%)
  starting transfers between devices  55.8 us (21%)
  matrix products  35.7 us (13%)
  blocking collectives  30.8 us (11%)
  between operations  15.1 us (6%)
  local copies, waits for them, and re-layouts  7.14 us (3%)
  other arithmetic  5.5 us (2%)
    ppermute x40, waiting for transfers between devices, send(): return lax.ppermute(value, GRID, pairs).astype(F32)  86.2 us
    ppermute x40, starting transfers between devices, send(): return lax.ppermute(value, GRID, pairs).astype(F32)  37.2 us
    all_gather x1, waiting for transfers between devices, per_device(): lax.all_gather(child_factor[0], 'row', axis=0, tiled=True, axis_index_gro...  22.3 us
    dot_general x21, matrix products, dot(): return jnp.dot(a, b, preferred_element_type=F32)  20.2 us
    dot_general x16, matrix products, dot_t(): lax.dot_general(a, b, (((1,), (1,)), ((), ())), preferred_element_type=F32)  15.5 us
    all_to_all x1, blocking collectives, per_device(): lax.all_to_all(child_rows, 'row', 0, 0, tiled=True, axis_index_groups=qua...  12.4 us
    all_to_all x1, blocking collectives, per_device(): lax.all_to_all(shared, ('gz', 'row'), 0, 0, tiled=True, axis_index_groups...  10.1 us
    all_to_all x1, waiting for transfers between devices, per_device(): lax.all_to_all(pieces.reshape(layers * ROWS, 12, lanes), ('gz', 'row'), 0...  9.66 us
  transfers between devices with their start and end apart: 45, of which 14 were waited for; matrix products, arithmetic and copies ran while one was open for 9% of the time, Pallas kernels for 0%

profile of v4, /device:TPU:1, one launch (start us, length us, event | category | flops | bytes accessed | tf_op | source)
XLA Modules:
  0.0 268.3 jit_solution(12371874890397919368)
XLA Ops:
  7.2 4.3 %copy.51 = bf16[768,1536]{0,1:T(8,128)(2,1)} copy(bf16[768,1536]{1,0:T(8,128)(2,1)} %param.6) | data formatting | bytes 4718592 | tf_op args[0]
  11.5 8.8 %collective-permute-start = (bf16[768,1536]{0,1:T(8,128)(2,1)}, bf16[768,1536]{0,1:T(8,128)(2,1)}, u32[]{:S(2)}, u32[]{:S(2)}) collective-permute-start(bf16[768,1536]{0,1:T(8,128)(2,1)} %copy.51), channel_id=1, source_target_pairs={{0,8},{8,0},{16,24},{24,16},{32,40},{40,32},{48,56},{56,48},{64,72... | collective-permute-start | bytes 7077896 | tf_op jit(solution)/shard_map/mask/ppermute | solution.py:106
  20.3 1.9 collective-permute-start.1
  23.1 5.2 %all-to-all-start = ((bf16[64,12,128]{2,1,0:T(8,128)(2,1)}), bf16[64,12,128]{2,1,0:T(8,128)(2,1)S(1)}, u32[]{:S(2)}, u32[]{:S(2)}) async-start(bf16[64,12,128]{2,1,0:T(8,128)(2,1)} %bitcast), calls=%async_computation | async-start | bytes 524288 | tf_op jit(solution)/shard_map/rhs/all_to_all | solution.py:124
  28.6 1.8 bitcast_multiply_fusion.1
  30.7 9.7 %all-to-all-done = bf16[64,12,128]{2,1,0:T(8,128)(2,1)S(1)} async-done(((bf16[64,12,128]{2,1,0:T(8,128)(2,1)}), bf16[64,12,128]{2,1,0:T(8,128)(2,1)S(1)}, u32[]{:S(2)}, u32[]{:S(2)}) %all-to-all-start) | async-done | bytes 196640 | tf_op jit(solution)/shard_map/rhs/all_to_all | solution.py:124
  40.8 1.8 bitcast_multiply_fusion
  47.3 0.8 collective-permute-start.6
  62.8 1.3 collective-permute-start.16
  64.1 1.3 collective-permute-start.17
  65.4 28.8 %collective-permute-done.16 = bf16[16,1536]{1,0:T(8,128)(2,1)S(1)} collective-permute-done((bf16[16,1536]{1,0:T(8,128)(2,1)S(1)}, bf16[16,1536]{1,0:T(8,128)(2,1)S(1)}, u32[]{:S(2)}, u32[]{:S(2)}) %collective-permute-start.16) | collective-permute-done | bytes 49184 | tf_op jit(solution)/shard_map/root/ppermute | solution.py:32
  94.2 3.1 %collective-permute-done.17 = bf16[16,1536]{1,0:T(8,128)(2,1)S(1)} collective-permute-done((bf16[16,1536]{1,0:T(8,128)(2,1)S(1)}, bf16[16,1536]{1,0:T(8,128)(2,1)S(1)}, u32[]{:S(2)}, u32[]{:S(2)}) %collective-permute-start.17) | collective-permute-done | bytes 49184 | tf_op jit(solution)/shard_map/root/ppermute | solution.py:32
  98.2 1.3 collective-permute-start.18
  99.5 1.3 collective-permute-start.19
  100.8 1.9 collective-permute-start.20
  102.7 3.2 %collective-permute-done.20 = bf16[16,1536]{1,0:T(8,128)(2,1)S(1)} collective-permute-done((bf16[16,1536]{1,0:T(8,128)(2,1)S(1)}, bf16[16,1536]{1,0:T(8,128)(2,1)S(1)}, u32[]{:S(2)}, u32[]{:S(2)}) %collective-permute-start.20) | collective-permute-done | bytes 49184 | tf_op jit(solution)/shard_map/root/ppermute | solution.py:32
  105.9 1.3 collective-permute-start.21
  107.2 1.1 collective-permute-done.21
  108.4 22.3 %all-gather.3.cloned.1.call-done = bf16[1,1024,1024]{2,1,0:T(8,128)(2,1)} async-done(((bf16[1,512,1024]{2,1,0:T(8,128)(2,1)}), bf16[1,1024,1024]{2,1,0:T(8,128)(2,1)}) %all-gather.3.cloned.1.call-update) | async-done | bytes 2097168 | tf_op jit(solution)/shard_map/child_gather/all_gather | solution.py:131
  130.8 2.7 %collective-permute-start.25 = (bf16[1024,1024]{1,0:T(8,128)(2,1)}, bf16[1024,1024]{1,0:T(8,128)(2,1)}, u32[]{:S(2)}, u32[]{:S(2)}) collective-permute-start(bf16[1024,1024]{1,0:T(8,128)(2,1)} %bitcast.88), channel_id=1, source_target_pairs={{0,8},{8,0},{16,24},{24,16},{32,40},{40,32},{48,56},{56,48},{64,72... | collective-permute-start | bytes 6291464 | tf_op jit(solution)/shard_map/coupling/ppermute | solution.py:141
  133.5 10.1 %all_to_all.29 = bf16[8,16,768]{2,1,0:T(8,128)(2,1)S(1)} all-to-all(bf16[8,16,768]{2,1,0:T(8,128)(2,1)S(1)} %bitcast.105), channel_id=1, replica_groups={{0,8,128,136,256,264,384,392},{16,24,144,152,272,280,400,408},{32,40,16..., dimensions={0} | all-to-all | bytes 393216 | tf_op jit(solution)/shard_map/coupling/all_to_all | solution.py:144
  143.9 8.3 %all_to_all.30 = bf16[4,32,1024]{2,1,0:T(8,128)(2,1)S(1)} all-to-all(bf16[4,32,1024]{2,1,0:T(8,128)(2,1)S(1)} %bitcast.104), channel_id=1, replica_groups={{0,8,16,24},{32,40,48,56},{64,72,80,88},{96,104,112,120},{1,9,17,25},{3..., dimensions={0} | all-to-all | bytes 524288 | tf_op jit(solution)/shard_map/coupling/all_to_all | solution.py:148
  152.3 1.3 collective-permute-start.22
  153.6 1.3 collective-permute-start.23
  154.9 1.3 collective-permute-start.24
  156.2 3.7 %collective-permute-done.22 = bf16[32,1024]{1,0:T(8,128)(2,1)S(1)} collective-permute-done((bf16[32,1024]{1,0:T(8,128)(2,1)S(1)}, bf16[32,1024]{1,0:T(8,128)(2,1)S(1)}, u32[]{:S(2)}, u32[]{:S(2)}) %collective-permute-start.22) | collective-permute-done | bytes 65568 | tf_op jit(solution)/shard_map/coupling/ppermute | solution.py:32
  160.0 2.8 %collective-permute-done.23 = bf16[32,1024]{1,0:T(8,128)(2,1)S(1)} collective-permute-done((bf16[32,1024]{1,0:T(8,128)(2,1)S(1)}, bf16[32,1024]{1,0:T(8,128)(2,1)S(1)}, u32[]{:S(2)}, u32[]{:S(2)}) %collective-permute-start.23) | collective-permute-done | bytes 65568 | tf_op jit(solution)/shard_map/coupling/ppermute | solution.py:32
  162.8 1.0 bitcast_subtract_fusion
  164.6 2.3 convolution_convert_fusion.7
  168.8 2.1 fusion.13
  171.6 0.8 collective-permute-start.29
  173.2 2.3 convolution_convert_fusion.5
  176.9 2.1 fusion.31
  180.7 2.1 fusion.14
  184.9 2.3 convolution_convert_fusion.3
  188.6 2.1 fusion.25
  192.4 2.1 fusion.16
  194.5 1.3 collective-permute-start.38
  195.8 37.6 %collective-permute-done.38 = bf16[32,1024]{1,0:T(8,128)(2,1)S(1)} collective-permute-done((bf16[32,1024]{1,0:T(8,128)(2,1)S(1)}, bf16[32,1024]{1,0:T(8,128)(2,1)S(1)}, u32[]{:S(2)}, u32[]{:S(2)}) %collective-permute-start.38) | collective-permute-done | bytes 65568 | tf_op jit(solution)/shard_map/child/ppermute | solution.py:32
  234.1 2.3 convolution_convert_fusion.1
  236.5 1.3 collective-permute-start.39
  237.8 1.3 collective-permute-start.40
  239.1 1.9 collective-permute-start.41
  241.7 1.4 collective-permute-done.40
  243.1 1.6 collective-permute-done.41
  244.9 1.3 collective-permute-start.42
  246.2 1.9 collective-permute-done.42
  248.3 12.4 %all_to_all.31 = bf16[4,32,512]{2,1,0:T(8,128)(2,1)S(1)} all-to-all(bf16[4,32,512]{2,1,0:T(8,128)(2,1)S(1)} %bitcast.106), channel_id=1, replica_groups={{0,8,16,24},{32,40,48,56},{64,72,80,88},{96,104,112,120},{1,9,17,25},{3..., dimensions={0} | all-to-all | bytes 262144 | tf_op jit(solution)/shard_map/child/all_to_all | solution.py:164
  (149 shorter events, 36.9 us)
Async XLA Ops:
  7.2 136.5 %copy-start = (bf16[1,384,1024]{2,1,0:T(8,128)(2,1)S(1)}, bf16[1,384,1024]{2,1,0:T(8,128)(2,1)}, u32[]{:S(2)}) copy-start(bf16[1,384,1024]{2,1,0:T(8,128)(2,1)} %param.9) | copy-start | bytes 2359300
  11.5 29.2 %collective-permute-start = (bf16[768,1536]{0,1:T(8,128)(2,1)}, bf16[768,1536]{0,1:T(8,128)(2,1)}, u32[]{:S(2)}, u32[]{:S(2)}) collective-permute-start(bf16[768,1536]{0,1:T(8,128)(2,1)} %copy.51), channel_id=1, source_target_pairs={{0,8},{8,0},{16,24},{24,16},{32,40},{40,32},{48,56},{56,48},{64,72... | collective-permute-start | bytes 7077896 | tf_op jit(solution)/shard_map/mask/ppermute | solution.py:106
  20.3 10.1 %collective-permute-start.1 = (s32[3,6]{1,0:T(4,128)S(1)}, s32[3,6]{1,0:T(4,128)S(1)}, u32[]{:S(2)}, u32[]{:S(2)}) collective-permute-start(s32[3,6]{1,0:T(4,128)S(1)} %copy-done.8), channel_id=1, source_target_pairs={{0,8},{8,0},{16,24},{24,16},{32,40},{40,32},{48,56},{56,48},{64,72... | collective-permute-start | bytes 224 | tf_op jit(solution)/shard_map/mask/ppermute | solution.py:107
  23.1 17.2 %all-to-all-start = ((bf16[64,12,128]{2,1,0:T(8,128)(2,1)}), bf16[64,12,128]{2,1,0:T(8,128)(2,1)S(1)}, u32[]{:S(2)}, u32[]{:S(2)}) async-start(bf16[64,12,128]{2,1,0:T(8,128)(2,1)} %bitcast), calls=%async_computation | async-start | bytes 524288 | tf_op jit(solution)/shard_map/rhs/all_to_all | solution.py:124
  28.3 102.4 %all-gather.3.cloned.1.call-start = ((), (), s32[]{:S(2)}) async-start(), calls=%async_computation.4 | async-start | bytes 3145728 | tf_op jit(solution)/shard_map/child_gather/all_gather | solution.py:131
  43.1 1.3 collective-permute-start.2
  43.7 0.7 collective-permute-start.3
  45.9 2.2 collective-permute-start.4
  46.6 1.5 collective-permute-start.5
  47.3 2.1 collective-permute-start.6
  50.1 2.7 %collective-permute-start.7 = (bf16[16,1536]{1,0:T(8,128)(2,1)S(1)}, bf16[16,1536]{1,0:T(8,128)(2,1)S(1)}, u32[]{:S(2)}, u32[]{:S(2)}) collective-permute-start(bf16[16,1536]{1,0:T(8,128)(2,1)S(1)} %add_convert_fusion.12), channel_id=1, source_target_pairs={{68,66},{69,67},{76,74},{77,75},{84,82},{85,83},{92,90},{93,91},{9... | collective-permute-start | bytes 147464 | tf_op jit(solution)/shard_map/root/ppermute | solution.py:32
  50.8 2.1 collective-permute-start.8
  52.2 1.4 collective-permute-start.9
  54.3 2.2 collective-permute-start.10
  55.0 1.5 collective-permute-start.11
  55.7 2.1 collective-permute-start.12
  58.5 2.7 %collective-permute-start.13 = (bf16[16,1536]{1,0:T(8,128)(2,1)S(1)}, bf16[16,1536]{1,0:T(8,128)(2,1)S(1)}, u32[]{:S(2)}, u32[]{:S(2)}) collective-permute-start(bf16[16,1536]{1,0:T(8,128)(2,1)S(1)} %add_convert_fusion.10), channel_id=1, source_target_pairs={{34,32},{35,33},{42,40},{43,41},{50,48},{51,49},{58,56},{59,57},{6... | collective-permute-start | bytes 147464 | tf_op jit(solution)/shard_map/root/ppermute | solution.py:32
  59.2 2.1 collective-permute-start.14
  60.6 1.4 collective-permute-start.15
  62.8 31.4 %collective-permute-start.16 = (bf16[16,1536]{1,0:T(8,128)(2,1)S(1)}, bf16[16,1536]{1,0:T(8,128)(2,1)S(1)}, u32[]{:S(2)}, u32[]{:S(2)}) collective-permute-start(bf16[16,1536]{1,0:T(8,128)(2,1)S(1)} %fusion.7), channel_id=1, source_target_pairs={{32,0},{33,1},{40,8},{41,9},{48,16},{49,17},{56,24},{57,25},{160,1... | collective-permute-start | bytes 147464 | tf_op jit(solution)/shard_map/root/ppermute | solution.py:32
  64.1 33.2 %collective-permute-start.17 = (bf16[16,1536]{1,0:T(8,128)(2,1)S(1)}, bf16[16,1536]{1,0:T(8,128)(2,1)S(1)}, u32[]{:S(2)}, u32[]{:S(2)}) collective-permute-start(bf16[16,1536]{1,0:T(8,128)(2,1)S(1)} %fusion.7), channel_id=1, source_target_pairs={{32,16},{33,17},{40,24},{41,25},{48,0},{49,1},{56,8},{57,9},{160,1... | collective-permute-start | bytes 147464 | tf_op jit(solution)/shard_map/root/ppermute | solution.py:32
  65.4 32.3 %copy-start.4 = (bf16[768,1536]{0,1:T(8,128)(2,1)S(1)}, bf16[768,1536]{0,1:T(8,128)(2,1)}, u32[]{:S(2)}) copy-start(bf16[768,1536]{0,1:T(8,128)(2,1)} %copy-done.1) | copy-start | bytes 7077892
  98.2 4.5 %collective-permute-start.18 = (bf16[16,1536]{1,0:T(8,128)(2,1)S(1)}, bf16[16,1536]{1,0:T(8,128)(2,1)S(1)}, u32[]{:S(2)}, u32[]{:S(2)}) collective-permute-start(bf16[16,1536]{1,0:T(8,128)(2,1)S(1)} %maximum_select_fusion.7), channel_id=1, source_target_pairs={{0,6},{1,7},{8,14},{9,15},{16,22},{17,23},{24,30},{25,31},{32,38},... | collective-permute-start | bytes 147464 | tf_op jit(solution)/shard_map/root/ppermute | solution.py:32
  99.5 3.2 %collective-permute-start.19 = (bf16[16,1536]{1,0:T(8,128)(2,1)S(1)}, bf16[16,1536]{1,0:T(8,128)(2,1)S(1)}, u32[]{:S(2)}, u32[]{:S(2)}) collective-permute-start(bf16[16,1536]{1,0:T(8,128)(2,1)S(1)} %maximum_select_fusion.7), channel_id=1, source_target_pairs={{0,7},{1,6},{8,15},{9,14},{16,23},{17,22},{24,31},{25,30},{34,35},... | collective-permute-start | bytes 147464 | tf_op jit(solution)/shard_map/root/ppermute | solution.py:32
  100.8 5.1 %collective-permute-start.20 = (bf16[16,1536]{1,0:T(8,128)(2,1)S(1)}, bf16[16,1536]{1,0:T(8,128)(2,1)S(1)}, u32[]{:S(2)}, u32[]{:S(2)}) collective-permute-start(bf16[16,1536]{1,0:T(8,128)(2,1)S(1)} %maximum_select_fusion.7), channel_id=1, source_target_pairs={{0,1},{1,0},{8,9},{9,8},{16,17},{17,16},{24,25},{25,24},{128,129},... | collective-permute-start | bytes 147464 | tf_op jit(solution)/shard_map/root/ppermute | solution.py:32
  105.9 2.5 collective-permute-start.21
  130.8 33.1 %copy-start.5 = (bf16[1,1024,1024]{2,1,0:T(8,128)(2,1)S(1)}, bf16[1,1024,1024]{2,1,0:T(8,128)(2,1)}, u32[]{:S(2)}) copy-start(bf16[1,1024,1024]{2,1,0:T(8,128)(2,1)} %all-gather.3.cloned.1.call-done) | copy-start | bytes 6291460
  130.8 33.8 %collective-permute-start.25 = (bf16[1024,1024]{1,0:T(8,128)(2,1)}, bf16[1024,1024]{1,0:T(8,128)(2,1)}, u32[]{:S(2)}, u32[]{:S(2)}) collective-permute-start(bf16[1024,1024]{1,0:T(8,128)(2,1)} %bitcast.88), channel_id=1, source_target_pairs={{0,8},{8,0},{16,24},{24,16},{32,40},{40,32},{48,56},{56,48},{64,72... | collective-permute-start | bytes 6291464 | tf_op jit(solution)/shard_map/coupling/ppermute | solution.py:141
  152.3 7.6 %collective-permute-start.22 = (bf16[32,1024]{1,0:T(8,128)(2,1)S(1)}, bf16[32,1024]{1,0:T(8,128)(2,1)S(1)}, u32[]{:S(2)}, u32[]{:S(2)}) collective-permute-start(bf16[32,1024]{1,0:T(8,128)(2,1)S(1)} %reduce_sum.22), channel_id=1, source_target_pairs={{32,0},{33,1},{40,8},{41,9},{48,16},{49,17},{56,24},{57,25},{66,34... | collective-permute-start | bytes 196616 | tf_op jit(solution)/shard_map/coupling/ppermute | solution.py:32
  153.6 9.1 %collective-permute-start.23 = (bf16[32,1024]{1,0:T(8,128)(2,1)S(1)}, bf16[32,1024]{1,0:T(8,128)(2,1)S(1)}, u32[]{:S(2)}, u32[]{:S(2)}) collective-permute-start(bf16[32,1024]{1,0:T(8,128)(2,1)S(1)} %reduce_sum.22), channel_id=1, source_target_pairs={{64,0},{65,1},{72,8},{73,9},{80,16},{81,17},{88,24},{89,25},{98,34... | collective-permute-start | bytes 196616 | tf_op jit(solution)/shard_map/coupling/ppermute | solution.py:32
  154.9 7.9 %collective-permute-start.24 = (bf16[32,1024]{1,0:T(8,128)(2,1)S(1)}, bf16[32,1024]{1,0:T(8,128)(2,1)S(1)}, u32[]{:S(2)}, u32[]{:S(2)}) collective-permute-start(bf16[32,1024]{1,0:T(8,128)(2,1)S(1)} %reduce_sum.22), channel_id=1, source_target_pairs={{96,0},{97,1},{104,8},{105,9},{112,16},{113,17},{120,24},{121,25},... | collective-permute-start | bytes 196616 | tf_op jit(solution)/shard_map/coupling/ppermute | solution.py:32
  166.9 1.4 collective-permute-start.26
  167.6 0.7 collective-permute-start.27
  170.9 1.5 collective-permute-start.28
  171.6 3.9 %collective-permute-start.29 = (bf16[32,2048]{1,0:T(8,128)(2,1)S(1)}, bf16[32,2048]{1,0:T(8,128)(2,1)S(1)}, u32[]{:S(2)}, u32[]{:S(2)}) collective-permute-start(bf16[32,2048]{1,0:T(8,128)(2,1)S(1)} %add_convert_fusion.6), channel_id=1, source_target_pairs={{100,98},{101,99},{108,106},{109,107},{116,114},{117,115},{124,122... | collective-permute-start | bytes 393224 | tf_op jit(solution)/shard_map/child/ppermute | solution.py:32
  175.6 4.6 %collective-permute-start.30 = (bf16[32,2048]{1,0:T(8,128)(2,1)S(1)}, bf16[32,2048]{1,0:T(8,128)(2,1)S(1)}, u32[]{:S(2)}, u32[]{:S(2)}) collective-permute-start(bf16[32,2048]{1,0:T(8,128)(2,1)S(1)} %add_convert_fusion.5), channel_id=1, source_target_pairs={{68,66},{69,67},{76,74},{77,75},{84,82},{85,83},{92,90},{93,91},{9... | collective-permute-start | bytes 393224 | tf_op jit(solution)/shard_map/child/ppermute | solution.py:32
  176.2 3.9 %collective-permute-start.31 = (bf16[32,2048]{1,0:T(8,128)(2,1)S(1)}, bf16[32,2048]{1,0:T(8,128)(2,1)S(1)}, u32[]{:S(2)}, u32[]{:S(2)}) collective-permute-start(bf16[32,2048]{1,0:T(8,128)(2,1)S(1)} %add_convert_fusion.5), channel_id=1, source_target_pairs={{68,67},{69,66},{76,75},{77,74},{84,83},{85,82},{92,91},{93,90},{1... | collective-permute-start | bytes 393224 | tf_op jit(solution)/shard_map/child/ppermute | solution.py:32
  179.5 1.2 collective-permute-start.32
  182.8 1.4 collective-permute-start.33
  183.5 3.7 %collective-permute-start.34 = (bf16[32,2048]{1,0:T(8,128)(2,1)S(1)}, bf16[32,2048]{1,0:T(8,128)(2,1)S(1)}, u32[]{:S(2)}, u32[]{:S(2)}) collective-permute-start(bf16[32,2048]{1,0:T(8,128)(2,1)S(1)} %add_convert_fusion.4), channel_id=1, source_target_pairs={{66,64},{67,65},{74,72},{75,73},{82,80},{83,81},{90,88},{91,89},{1... | collective-permute-start | bytes 393224 | tf_op jit(solution)/shard_map/child/ppermute | solution.py:32
  187.3 4.6 %collective-permute-start.35 = (bf16[32,2048]{1,0:T(8,128)(2,1)S(1)}, bf16[32,2048]{1,0:T(8,128)(2,1)S(1)}, u32[]{:S(2)}, u32[]{:S(2)}) collective-permute-start(bf16[32,2048]{1,0:T(8,128)(2,1)S(1)} %add_convert_fusion.3), channel_id=1, source_target_pairs={{34,32},{35,33},{42,40},{43,41},{50,48},{51,49},{58,56},{59,57},{6... | collective-permute-start | bytes 393224 | tf_op jit(solution)/shard_map/child/ppermute | solution.py:32
  187.9 3.9 %collective-permute-start.36 = (bf16[32,2048]{1,0:T(8,128)(2,1)S(1)}, bf16[32,2048]{1,0:T(8,128)(2,1)S(1)}, u32[]{:S(2)}, u32[]{:S(2)}) collective-permute-start(bf16[32,2048]{1,0:T(8,128)(2,1)S(1)} %add_convert_fusion.3), channel_id=1, source_target_pairs={{34,33},{35,32},{42,41},{43,40},{50,49},{51,48},{58,57},{59,56},{6... | collective-permute-start | bytes 393224 | tf_op jit(solution)/shard_map/child/ppermute | solution.py:32
  191.2 1.2 collective-permute-start.37
  194.5 38.9 %collective-permute-start.38 = (bf16[32,1024]{1,0:T(8,128)(2,1)S(1)}, bf16[32,1024]{1,0:T(8,128)(2,1)S(1)}, u32[]{:S(2)}, u32[]{:S(2)}) collective-permute-start(bf16[32,1024]{1,0:T(8,128)(2,1)S(1)} %fusion.16), channel_id=1, source_target_pairs={{32,0},{33,1},{40,8},{41,9},{48,16},{49,17},{56,24},{57,25},{160,1... | collective-permute-start | bytes 196616 | tf_op jit(solution)/shard_map/child/ppermute | solution.py:32
  236.5 5.3 %collective-permute-start.39 = (bf16[32,2048]{1,0:T(8,128)(2,1)S(1)}, bf16[32,2048]{1,0:T(8,128)(2,1)S(1)}, u32[]{:S(2)}, u32[]{:S(2)}) collective-permute-start(bf16[32,2048]{1,0:T(8,128)(2,1)S(1)} %maximum_select_fusion.3), channel_id=1, source_target_pairs={{0,6},{1,7},{8,14},{9,15},{16,22},{17,23},{24,30},{25,31},{32,38},... | collective-permute-start | bytes 393224 | tf_op jit(solution)/shard_map/child/ppermute | solution.py:32
  237.8 5.4 %collective-permute-start.40 = (bf16[32,2048]{1,0:T(8,128)(2,1)S(1)}, bf16[32,2048]{1,0:T(8,128)(2,1)S(1)}, u32[]{:S(2)}, u32[]{:S(2)}) collective-permute-start(bf16[32,2048]{1,0:T(8,128)(2,1)S(1)} %maximum_select_fusion.3), channel_id=1, source_target_pairs={{0,7},{1,6},{8,15},{9,14},{16,23},{17,22},{24,31},{25,30},{34,35},... | collective-permute-start | bytes 393224 | tf_op jit(solution)/shard_map/child/ppermute | solution.py:32
  239.1 5.7 %collective-permute-start.41 = (bf16[32,2048]{1,0:T(8,128)(2,1)S(1)}, bf16[32,2048]{1,0:T(8,128)(2,1)S(1)}, u32[]{:S(2)}, u32[]{:S(2)}) collective-permute-start(bf16[32,2048]{1,0:T(8,128)(2,1)S(1)} %maximum_select_fusion.3), channel_id=1, source_target_pairs={{0,1},{1,0},{8,9},{9,8},{16,17},{17,16},{24,25},{25,24},{128,129},... | collective-permute-start | bytes 393224 | tf_op jit(solution)/shard_map/child/ppermute | solution.py:32
  244.9 3.2 %collective-permute-start.42 = (bf16[32,2048]{1,0:T(8,128)(2,1)S(1)}, bf16[32,2048]{1,0:T(8,128)(2,1)S(1)}, u32[]{:S(2)}, u32[]{:S(2)}) collective-permute-start(bf16[32,2048]{1,0:T(8,128)(2,1)S(1)} %add_convert_fusion.1), channel_id=1, source_target_pairs={{0,2},{1,3},{8,10},{9,11},{16,18},{17,19},{24,26},{25,27},{6,4},{7... | collective-permute-start | bytes 393224 | tf_op jit(solution)/shard_map/child/ppermute | solution.py:32
  (6 other events, 55.1 us)
Sparse Core Ops, SparseCore 0:
  65.5 65.1 all-gather.2

commit v5 on v4

--- a/solution.py
+++ b/solution.py
@@ -32,24 +32,24 @@
     return lax.ppermute(value, GRID, pairs).astype(F32)
 
 
-def sweep(rhs, own, other, split_rows):
-    rows = own.shape[0]
+def sweep(rhs, blocks, split_rows, beside=lambda r, value: value):
+    rows = blocks[0].shape[0]
 
     def forward(x):
-        return dot(x[:, :rows], own) + dot(x[:, rows:], other)
+        return sum(dot(x[:, i * rows : (i + 1) * rows], block) for i, block in enumerate(blocks))
 
     def diagonal(x):
-        return jnp.concatenate([dot_t(x, own), dot_t(x, other)], 1)
+        return jnp.concatenate([dot_t(x, block) for block in blocks], 1)
 
     row_panel = lax.axis_index("row") // GROUP
     col_panel = lax.axis_index("col") // PAIR
-    current = jnp.zeros((rhs.shape[0], 2 * rows), BF16)
+    current = jnp.zeros((rhs.shape[0], len(blocks) * rows), BF16)
     carried = jnp.zeros(rhs.shape, F32)
     totals = jnp.zeros(rhs.shape, F32)
     for r in range(PANELS - 1, -1, -1):
         ahead = None
         if r < PANELS - 1:
-            terms = (forward(current) + carried).astype(BF16)
+            terms = beside(r, (forward(current) + carried).astype(BF16))
             down = [(r + 1, r, 0, r, r, 0)]
             if r == 1:
                 down.append((3, 2, 0, 0, 0, 0))
@@ -62,6 +62,8 @@
             carried = carried + first
         residual = (rhs - totals).astype(BF16)
         piece = diagonal(residual).astype(BF16)
+        if r == PANELS - 1:
+            piece = beside(r, piece)
         current = jnp.where((row_panel == r) & (col_panel == r), piece, current)
         if ahead is not None:
             current = (current.astype(F32) + ahead).astype(BF16)
@@ -86,7 +88,7 @@
             current = (current.astype(F32) + received).astype(BF16)
             received = send(current, [(0, 0, 0, 0, 1, 0), (0, 0, 0, 3, 2, 0), (1, 1, 0, 3, 2, 0)])
             current = (current.astype(F32) + received).astype(BF16)
-    return current[:, :rows], current[:, rows:]
+    return current
 
 
 def per_device(root_factor, partials, pattern, coupling, child_factor, child_bits):
@@ -96,7 +98,6 @@
     col_index = lax.axis_index("col")
     core = row_index % 2
     quarters = [[s * GROUP + j for j in range(GROUP)] for s in range(PANELS)]
-    opposite = [[s * GROUP + k, s * GROUP + 2 + k] for s in range(PANELS) for k in range(2)]
     chips = [
         [g * ROWS + 2 * y + k for g in range(layers) for k in range(2)] for y in range(ROWS // 2)
     ]
@@ -127,18 +128,35 @@
         root_rhs = jnp.sum(pieces.astype(F32).reshape(layers, ROWS, 12, lanes), 0)
         root_rhs = root_rhs.astype(BF16).reshape(ROWS, 12 * lanes).astype(F32)
 
-    with jax.named_scope("child_gather"):
-        child_own = lax.all_gather(
-            child_factor[0], "row", axis=0, tiled=True, axis_index_groups=opposite
-        )
+    child_here = child_factor[0]
+    moved = {}
+
+    def rows_of(half, flip):
+        first = half * ROWS // 2
+        return [(i, i ^ flip) for i in range(first, first + ROWS // 2)]
+
+    def move_children(r, value):
+        if r == 1:
+            value, moved[0, 1], there = lax.optimization_barrier((value, moved[0, 1], moved[0, 2]))
+            moved[0, 2] = there
+            moved[0, 3] = lax.ppermute(there, "row", rows_of(0, 1))
+        if r == 0:
+            value, moved[0, 3] = lax.optimization_barrier((value, moved[0, 3]))
+        if r == 3 or r == 0:
+            half = 0 if r == 3 else 1
+            value, here = lax.optimization_barrier((value, child_here))
+            moved[half, 2] = lax.ppermute(here, "row", rows_of(half, 2))
+            moved[half, 1] = lax.ppermute(here, "row", rows_of(half, 1))
+        return value
 
     with jax.named_scope("root"):
-        own, other = sweep(root_rhs, masked_root, partner_root, True)
+        root_rows = sweep(root_rhs, [masked_root, partner_root], True, move_children)
 
     with jax.named_scope("coupling"):
+        root_rows, there = lax.optimization_barrier((root_rows, moved[1, 2]))
+        moved[1, 3] = lax.ppermute(there, "row", rows_of(1, 1))
+        own, other = root_rows[:, :rows_here], root_rows[:, rows_here:]
         by_core = jnp.stack([jnp.where(core == k, own, other) for k in range(2)])
-        by_core, child_own = lax.optimization_barrier((by_core, child_own))
-        child_other = lax.ppermute(child_own, "row", swap)
         shared = jnp.broadcast_to(by_core[None], (layers,) + by_core.shape)
         shared = shared.reshape(layers * 2 * ROWS, rows_here)
         shared = lax.all_to_all(shared, ("gz", "row"), 0, 0, tiled=True, axis_index_groups=chips)
@@ -155,11 +173,11 @@
         child_rhs = (2 * bits - 1).astype(F32) - coupled
 
     with jax.named_scope("child"):
-        own, other = sweep(child_rhs, child_own, child_other, False)
-        blocks = jnp.stack(
-            [jnp.where(core == k, own, other).reshape(share, 2, -1) for k in range(2)], 2
-        )
-        child_rows = blocks.reshape(share, GROUP, -1).transpose(1, 0, 2)
+        blocks = [child_here] + [moved[0, flip] + moved[1, flip] for flip in (1, 2, 3)]
+        child_rows = sweep(child_rhs, blocks, False).reshape(share, 2, 2, -1)
+        child_rows = jnp.where(core == 1, child_rows[:, :, ::-1], child_rows)
+        child_rows = jnp.where(row_index % GROUP // 2 == 1, child_rows[:, ::-1], child_rows)
+        child_rows = child_rows.reshape(share, GROUP, -1).transpose(1, 0, 2)
         child_rows = child_rows.reshape(GROUP * share, -1)
         child_rows = lax.all_to_all(child_rows, "row", 0, 0, tiled=True, axis_index_groups=quarters)
     return (root_all, child_rows[None])

time: 270 us -> 241 us (0.89)
  waiting for transfers between devices: 118 us -> 95.4 us
  between operations: 15.1 us -> 1.85 us
  starting transfers between devices: 55.8 us -> 66.5 us
  matrix products: 35.7 us -> 28.8 us
  other arithmetic: 5.5 us -> 11.1 us
    all_gather x1 -> x0, waiting for transfers between devices: 22.3 us -> none  [per_device(): lax.all_gather(child_factor[0], 'row', axis=0, tiled=True, axis_index_gro...]
    ppermute x40, waiting for transfers between devices: 86.2 us -> 73.2 us  [send(): return lax.ppermute(value, GRID, pairs).astype(F32)]
    ppermute x1 -> x6, waiting for transfers between devices: 0.01 us -> 12.5 us  [the longest x2 12.5 us: move_children(): moved[half, 2] = lax.ppermute(here, 'row', rows_of(half, 2))]
    ppermute x1 -> x6, starting transfers between devices: 2.7 us -> 12.1 us  [the longest x2 4.78 us: move_children(): moved[half, 2] = lax.ppermute(here, 'row', rows_of(half, 2))]
    dot_general x21 -> x31, matrix products: 20.2 us -> 13.4 us  [dot(): return jnp.dot(a, b, preferred_element_type=F32)]
    add x0 -> x3, other arithmetic: none -> 5.25 us  [per_device(): moved[0, flip] + moved[1, flip]]
    all_to_all x1, blocking collectives: 12.4 us -> 8.13 us  [per_device(): lax.all_to_all(child_rows, 'row', 0, 0, tiled=True, axis_index_groups=qua...]
    all_to_all x1, blocking collectives: 10.1 us -> 13 us  [per_device(): lax.all_to_all(shared, ('gz', 'row'), 0, 0, tiled=True, axis_index_groups...]
  transfers between devices with their start and end apart: 45 -> 49, of which waited for: 14 -> 12; matrix products, arithmetic and copies ran while one was open for 9% -> 13% of each run, Pallas kernels for 0% -> 0%
where the time goes in v5:
time: 241 us; the launch traced here: 240 us
  waiting for transfers between devices  95.4 us (40%)
  starting transfers between devices  66.5 us (28%)
  blocking collectives  29.5 us (12%)
  matrix products  28.8 us (12%)
  other arithmetic  11.1 us (5%)
  local copies, waits for them, and re-layouts  7.14 us (3%)
    ppermute x40, waiting for transfers between devices, send(): return lax.ppermute(value, GRID, pairs).astype(F32)  73.2 us
    ppermute x40, starting transfers between devices, send(): return lax.ppermute(value, GRID, pairs).astype(F32)  38.4 us
    dot_general x24, matrix products, dot_t(): lax.dot_general(a, b, (((1,), (1,)), ((), ())), preferred_element_type=F32)  15.4 us
    dot_general x31, matrix products, dot(): return jnp.dot(a, b, preferred_element_type=F32)  13.4 us
    all_to_all x1, blocking collectives, per_device(): lax.all_to_all(shared, ('gz', 'row'), 0, 0, tiled=True, axis_index_groups...  13 us
    ppermute x2, waiting for transfers between devices, move_children(): moved[half, 2] = lax.ppermute(here, 'row', rows_of(half, 2))  12.5 us
    all_to_all x1, waiting for transfers between devices, per_device(): lax.all_to_all(pieces.reshape(layers * ROWS, 12, lanes), ('gz', 'row'), 0...  9.71 us
    ppermute x1, starting transfers between devices, per_device(): partner_factor = lax.ppermute(root_factor, 'row', swap)  8.78 us
  transfers between devices with their start and end apart: 49, of which 12 were waited for; matrix products, arithmetic and copies ran while one was open for 13% of the time, Pallas kernels for 0%

profile of v5, /device:TPU:1, one launch (start us, length us, event | category | flops | bytes accessed | tf_op | source)
XLA Modules:
  0.0 240.2 jit_solution(3358105484329201760)
XLA Ops:
  0.7 4.4 %copy.47 = bf16[768,1536]{0,1:T(8,128)(2,1)} copy(bf16[768,1536]{1,0:T(8,128)(2,1)} %param.6) | data formatting | bytes 4718592 | tf_op args[0]
  5.0 8.8 %collective-permute-start = (bf16[768,1536]{0,1:T(8,128)(2,1)}, bf16[768,1536]{0,1:T(8,128)(2,1)}, u32[]{:S(2)}, u32[]{:S(2)}) collective-permute-start(bf16[768,1536]{0,1:T(8,128)(2,1)} %copy.47), channel_id=1, source_target_pairs={{0,8},{8,0},{16,24},{24,16},{32,40},{40,32},{48,56},{56,48},{64,72... | collective-permute-start | bytes 7077896 | tf_op jit(solution)/shard_map/mask/ppermute | solution.py:107
  13.8 1.9 collective-permute-start.1
  15.8 0.7 broadcast_in_dim.40
  16.5 5.2 %all-to-all-start = ((bf16[64,12,128]{2,1,0:T(8,128)(2,1)}), bf16[64,12,128]{2,1,0:T(8,128)(2,1)S(1)}, u32[]{:S(2)}, u32[]{:S(2)}) async-start(bf16[64,12,128]{2,1,0:T(8,128)(2,1)} %bitcast), calls=%async_computation | async-start | bytes 524288 | tf_op jit(solution)/shard_map/rhs/all_to_all | solution.py:125
  22.0 1.8 bitcast_multiply_fusion.1
  24.1 9.7 %all-to-all-done = bf16[64,12,128]{2,1,0:T(8,128)(2,1)S(1)} async-done(((bf16[64,12,128]{2,1,0:T(8,128)(2,1)}), bf16[64,12,128]{2,1,0:T(8,128)(2,1)S(1)}, u32[]{:S(2)}, u32[]{:S(2)}) %all-to-all-start) | async-done | bytes 196640 | tf_op jit(solution)/shard_map/rhs/all_to_all | solution.py:125
  34.3 1.8 bitcast_multiply_fusion
  40.8 3.1 %collective-permute-start.11 = (bf16[512,1024]{1,0:T(8,128)(2,1)}, bf16[512,1024]{1,0:T(8,128)(2,1)}, u32[]{:S(2)}, u32[]{:S(2)}) collective-permute-start(bf16[512,1024]{1,0:T(8,128)(2,1)} %bitcast.132), channel_id=1, source_target_pairs={{0,16},{8,24},{16,0},{24,8},{32,48},{40,56},{48,32},{56,40},{1,17}... | collective-permute-start | bytes 3145736 | tf_op jit(solution)/shard_map/root/ppermute | solution.py:148
  43.9 2.5 %collective-permute-start.10 = (bf16[512,1024]{1,0:T(8,128)(2,1)}, bf16[512,1024]{1,0:T(8,128)(2,1)}, u32[]{:S(2)}, u32[]{:S(2)}) collective-permute-start(bf16[512,1024]{1,0:T(8,128)(2,1)} %bitcast.133), channel_id=1, source_target_pairs={{0,8},{8,0},{16,24},{24,16},{32,40},{40,32},{48,56},{56,48},{1,9},... | collective-permute-start | bytes 3145736 | tf_op jit(solution)/shard_map/root/ppermute | solution.py:149
  47.1 2.2 convolution_convert_fusion.21
  54.8 12.5 %collective-permute-done.11 = bf16[512,1024]{1,0:T(8,128)(2,1)} collective-permute-done((bf16[512,1024]{1,0:T(8,128)(2,1)}, bf16[512,1024]{1,0:T(8,128)(2,1)}, u32[]{:S(2)}, u32[]{:S(2)}) %collective-permute-start.11) | collective-permute-done | bytes 1048608 | tf_op jit(solution)/shard_map/root/ppermute | solution.py:148
  69.3 3.2 %collective-permute-start.18 = (bf16[512,1024]{1,0:T(8,128)(2,1)}, bf16[512,1024]{1,0:T(8,128)(2,1)}, u32[]{:S(2)}, u32[]{:S(2)}) collective-permute-start(bf16[512,1024]{1,0:T(8,128)(2,1)} %collective-permute-done.11), channel_id=1, source_target_pairs={{0,8},{8,0},{16,24},{24,16},{32,40},{40,32},{48,56},{56,48},{1,9},... | collective-permute-start | bytes 3145736 | tf_op jit(solution)/shard_map/root/ppermute | solution.py:142
  72.5 2.2 convolution_convert_fusion.19
  79.5 0.7 fusion.7
  80.2 1.3 collective-permute-start.20
  81.5 1.3 collective-permute-start.19
  82.8 1.7 collective-permute-start.25
  84.5 9.7 %collective-permute-done.20 = bf16[16,1536]{1,0:T(8,128)(2,1)S(1)} collective-permute-done((bf16[16,1536]{1,0:T(8,128)(2,1)S(1)}, bf16[16,1536]{1,0:T(8,128)(2,1)S(1)}, u32[]{:S(2)}, u32[]{:S(2)}) %collective-permute-start.20) | collective-permute-done | bytes 49184 | tf_op jit(solution)/shard_map/root/ppermute | solution.py:32
  94.2 2.2 collective-permute-done.19
  96.4 2.1 convolution_convert_fusion.17
  98.9 3.7 %collective-permute-start.23 = (bf16[16,1536]{1,0:T(8,128)(2,1)S(1)}, bf16[16,1536]{1,0:T(8,128)(2,1)S(1)}, u32[]{:S(2)}, u32[]{:S(2)}) collective-permute-start(bf16[16,1536]{1,0:T(8,128)(2,1)S(1)} %maximum_select_fusion.6), channel_id=1, source_target_pairs={{0,1},{1,0},{8,9},{9,8},{16,17},{17,16},{24,25},{25,24},{128,129},... | collective-permute-start | bytes 147464 | tf_op jit(solution)/shard_map/root/ppermute | solution.py:32
  102.6 1.3 collective-permute-start.22
  103.9 1.3 collective-permute-start.21
  105.2 1.2 collective-permute-done.21
  106.5 1.3 collective-permute-start.24
  109.1 13.0 %all_to_all.29 = bf16[8,16,768]{2,1,0:T(8,128)(2,1)S(1)} all-to-all(bf16[8,16,768]{2,1,0:T(8,128)(2,1)S(1)} %bitcast.143), channel_id=1, replica_groups={{0,8,128,136,256,264,384,392},{16,24,144,152,272,280,400,408},{32,40,16..., dimensions={0} | all-to-all | bytes 393216 | tf_op jit(solution)/shard_map/coupling/all_to_all | solution.py:162
  122.5 8.3 %all_to_all.30 = bf16[4,32,1024]{2,1,0:T(8,128)(2,1)S(1)} all-to-all(bf16[4,32,1024]{2,1,0:T(8,128)(2,1)S(1)} %bitcast.142), channel_id=1, replica_groups={{0,8,16,24},{32,40,48,56},{64,72,80,88},{96,104,112,120},{1,9,17,25},{3..., dimensions={0} | all-to-all | bytes 524288 | tf_op jit(solution)/shard_map/coupling/all_to_all | solution.py:166
  130.9 1.3 collective-permute-start.28
  132.2 1.3 collective-permute-start.27
  133.5 1.3 collective-permute-start.26
  134.8 0.9 collective-permute-start.30
  135.7 1.9 add.251
  137.7 1.7 add.250
  139.4 1.7 collective-permute-done.27
  141.8 1.0 fusion.88
  144.1 1.6 add.252
  164.1 1.3 collective-permute-start.43
  165.4 46.0 %collective-permute-done.43 = bf16[32,1024]{1,0:T(8,128)(2,1)S(1)} collective-permute-done((bf16[32,1024]{1,0:T(8,128)(2,1)S(1)}, bf16[32,1024]{1,0:T(8,128)(2,1)S(1)}, u32[]{:S(2)}, u32[]{:S(2)}) %collective-permute-start.43) | collective-permute-done | bytes 65568 | tf_op jit(solution)/shard_map/child/ppermute | solution.py:32
  213.2 1.9 collective-permute-start.46
  215.1 1.3 collective-permute-start.45
  216.4 1.3 collective-permute-start.44
  217.7 1.2 collective-permute-done.46
  218.9 8.1 %collective-permute-done.44 = bf16[32,2048]{1,0:T(8,128)(2,1)S(1)} collective-permute-done((bf16[32,2048]{1,0:T(8,128)(2,1)S(1)}, bf16[32,2048]{1,0:T(8,128)(2,1)S(1)}, u32[]{:S(2)}, u32[]{:S(2)}) %collective-permute-start.44) | collective-permute-done | bytes 131104 | tf_op jit(solution)/shard_map/child/ppermute | solution.py:32
  227.0 1.3 collective-permute-start.47
  228.4 1.9 collective-permute-done.47
  230.4 0.7 rev.6
  231.4 8.1 %all_to_all.31 = bf16[4,32,512]{2,1,0:T(8,128)(2,1)S(1)} all-to-all(bf16[4,32,512]{2,1,0:T(8,128)(2,1)S(1)} %bitcast.144), channel_id=1, replica_groups={{0,8,16,24},{32,40,48,56},{64,72,80,88},{96,104,112,120},{1,9,17,25},{3..., dimensions={0} | all-to-all | bytes 262144 | tf_op jit(solution)/shard_map/child/all_to_all | solution.py:182
  (178 shorter events, 43.3 us)
Async XLA Ops:
  5.0 29.2 %collective-permute-start = (bf16[768,1536]{0,1:T(8,128)(2,1)}, bf16[768,1536]{0,1:T(8,128)(2,1)}, u32[]{:S(2)}, u32[]{:S(2)}) collective-permute-start(bf16[768,1536]{0,1:T(8,128)(2,1)} %copy.47), channel_id=1, source_target_pairs={{0,8},{8,0},{16,24},{24,16},{32,40},{40,32},{48,56},{56,48},{64,72... | collective-permute-start | bytes 7077896 | tf_op jit(solution)/shard_map/mask/ppermute | solution.py:107
  13.8 10.1 %collective-permute-start.1 = (s32[3,6]{1,0:T(4,128)S(1)}, s32[3,6]{1,0:T(4,128)S(1)}, u32[]{:S(2)}, u32[]{:S(2)}) collective-permute-start(s32[3,6]{1,0:T(4,128)S(1)} %copy-done.7), channel_id=1, source_target_pairs={{0,8},{8,0},{16,24},{24,16},{32,40},{40,32},{48,56},{56,48},{64,72... | collective-permute-start | bytes 224 | tf_op jit(solution)/shard_map/mask/ppermute | solution.py:108
  16.5 17.2 %all-to-all-start = ((bf16[64,12,128]{2,1,0:T(8,128)(2,1)}), bf16[64,12,128]{2,1,0:T(8,128)(2,1)S(1)}, u32[]{:S(2)}, u32[]{:S(2)}) async-start(bf16[64,12,128]{2,1,0:T(8,128)(2,1)} %bitcast), calls=%async_computation | async-start | bytes 524288 | tf_op jit(solution)/shard_map/rhs/all_to_all | solution.py:125
  36.5 1.3 collective-permute-start.2
  39.4 7.7 %collective-permute-start.5 = (bf16[16,1536]{1,0:T(8,128)(2,1)S(1)}, bf16[16,1536]{1,0:T(8,128)(2,1)S(1)}, u32[]{:S(2)}, u32[]{:S(2)}) collective-permute-start(bf16[16,1536]{1,0:T(8,128)(2,1)S(1)} %fusion.4), channel_id=1, source_target_pairs={{100,84},{101,85},{108,92},{109,93},{116,68},{117,69},{124,76},{12... | collective-permute-start | bytes 147464 | tf_op jit(solution)/shard_map/root/ppermute | solution.py:32
  40.1 7.0 %collective-permute-start.4 = (bf16[16,1536]{1,0:T(8,128)(2,1)S(1)}, bf16[16,1536]{1,0:T(8,128)(2,1)S(1)}, u32[]{:S(2)}, u32[]{:S(2)}) collective-permute-start(bf16[16,1536]{1,0:T(8,128)(2,1)S(1)} %fusion.4), channel_id=1, source_target_pairs={{100,68},{101,69},{108,76},{109,77},{116,84},{117,85},{124,92},{12... | collective-permute-start | bytes 147464 | tf_op jit(solution)/shard_map/root/ppermute | solution.py:32
  40.8 26.5 %collective-permute-start.11 = (bf16[512,1024]{1,0:T(8,128)(2,1)}, bf16[512,1024]{1,0:T(8,128)(2,1)}, u32[]{:S(2)}, u32[]{:S(2)}) collective-permute-start(bf16[512,1024]{1,0:T(8,128)(2,1)} %bitcast.132), channel_id=1, source_target_pairs={{0,16},{8,24},{16,0},{24,8},{32,48},{40,56},{48,32},{56,40},{1,17}... | collective-permute-start | bytes 3145736 | tf_op jit(solution)/shard_map/root/ppermute | solution.py:148
  43.9 23.4 %collective-permute-start.10 = (bf16[512,1024]{1,0:T(8,128)(2,1)}, bf16[512,1024]{1,0:T(8,128)(2,1)}, u32[]{:S(2)}, u32[]{:S(2)}) collective-permute-start(bf16[512,1024]{1,0:T(8,128)(2,1)} %bitcast.133), channel_id=1, source_target_pairs={{0,8},{8,0},{16,24},{24,16},{32,40},{40,32},{48,56},{56,48},{1,9},... | collective-permute-start | bytes 3145736 | tf_op jit(solution)/shard_map/root/ppermute | solution.py:149
  46.4 3.4 %collective-permute-start.6 = (bf16[16,1536]{1,0:T(8,128)(2,1)S(1)}, bf16[16,1536]{1,0:T(8,128)(2,1)S(1)}, u32[]{:S(2)}, u32[]{:S(2)}) collective-permute-start(bf16[16,1536]{1,0:T(8,128)(2,1)S(1)} %add_convert_fusion.13), channel_id=1, source_target_pairs={{100,98},{101,99},{108,106},{109,107},{116,114},{117,115},{124,122... | collective-permute-start | bytes 147464 | tf_op jit(solution)/shard_map/root/ppermute | solution.py:32
  49.8 3.5 %collective-permute-start.8 = (bf16[16,1536]{1,0:T(8,128)(2,1)S(1)}, bf16[16,1536]{1,0:T(8,128)(2,1)S(1)}, u32[]{:S(2)}, u32[]{:S(2)}) collective-permute-start(bf16[16,1536]{1,0:T(8,128)(2,1)S(1)} %add_convert_fusion.12), channel_id=1, source_target_pairs={{68,67},{69,66},{76,75},{77,74},{84,83},{85,82},{92,91},{93,90},{1... | collective-permute-start | bytes 147464 | tf_op jit(solution)/shard_map/root/ppermute | solution.py:32
  50.5 2.8 %collective-permute-start.7 = (bf16[16,1536]{1,0:T(8,128)(2,1)S(1)}, bf16[16,1536]{1,0:T(8,128)(2,1)S(1)}, u32[]{:S(2)}, u32[]{:S(2)}) collective-permute-start(bf16[16,1536]{1,0:T(8,128)(2,1)S(1)} %add_convert_fusion.12), channel_id=1, source_target_pairs={{68,66},{69,67},{76,74},{77,75},{84,82},{85,83},{92,90},{93,91},{9... | collective-permute-start | bytes 147464 | tf_op jit(solution)/shard_map/root/ppermute | solution.py:32
  52.6 1.4 collective-permute-start.9
  67.3 5.2 %collective-permute-start.13 = (bf16[16,1536]{1,0:T(8,128)(2,1)S(1)}, bf16[16,1536]{1,0:T(8,128)(2,1)S(1)}, u32[]{:S(2)}, u32[]{:S(2)}) collective-permute-start(bf16[16,1536]{1,0:T(8,128)(2,1)S(1)} %fusion.5), channel_id=1, source_target_pairs={{66,50},{67,51},{74,58},{75,59},{82,34},{83,35},{90,42},{91,43},{1... | collective-permute-start | bytes 147464 | tf_op jit(solution)/shard_map/root/ppermute | solution.py:32
  67.9 4.6 %collective-permute-start.12 = (bf16[16,1536]{1,0:T(8,128)(2,1)S(1)}, bf16[16,1536]{1,0:T(8,128)(2,1)S(1)}, u32[]{:S(2)}, u32[]{:S(2)}) collective-permute-start(bf16[16,1536]{1,0:T(8,128)(2,1)S(1)} %fusion.5), channel_id=1, source_target_pairs={{66,34},{67,35},{74,42},{75,43},{82,50},{83,51},{90,58},{91,59},{9... | collective-permute-start | bytes 147464 | tf_op jit(solution)/shard_map/root/ppermute | solution.py:32
  68.6 6.6 %collective-permute-start.14 = (bf16[16,1536]{1,0:T(8,128)(2,1)S(1)}, bf16[16,1536]{1,0:T(8,128)(2,1)S(1)}, u32[]{:S(2)}, u32[]{:S(2)}) collective-permute-start(bf16[16,1536]{1,0:T(8,128)(2,1)S(1)} %add_convert_fusion.11), channel_id=1, source_target_pairs={{66,64},{67,65},{74,72},{75,73},{82,80},{83,81},{90,88},{91,89},{1... | collective-permute-start | bytes 147464 | tf_op jit(solution)/shard_map/root/ppermute | solution.py:32
  69.3 10.9 %collective-permute-start.18 = (bf16[512,1024]{1,0:T(8,128)(2,1)}, bf16[512,1024]{1,0:T(8,128)(2,1)}, u32[]{:S(2)}, u32[]{:S(2)}) collective-permute-start(bf16[512,1024]{1,0:T(8,128)(2,1)} %collective-permute-done.11), channel_id=1, source_target_pairs={{0,8},{8,0},{16,24},{24,16},{32,40},{40,32},{48,56},{56,48},{1,9},... | collective-permute-start | bytes 3145736 | tf_op jit(solution)/shard_map/root/ppermute | solution.py:142
  75.2 3.5 %collective-permute-start.16 = (bf16[16,1536]{1,0:T(8,128)(2,1)S(1)}, bf16[16,1536]{1,0:T(8,128)(2,1)S(1)}, u32[]{:S(2)}, u32[]{:S(2)}) collective-permute-start(bf16[16,1536]{1,0:T(8,128)(2,1)S(1)} %add_convert_fusion.10), channel_id=1, source_target_pairs={{34,33},{35,32},{42,41},{43,40},{50,49},{51,48},{58,57},{59,56},{6... | collective-permute-start | bytes 147464 | tf_op jit(solution)/shard_map/root/ppermute | solution.py:32
  75.9 2.8 %collective-permute-start.15 = (bf16[16,1536]{1,0:T(8,128)(2,1)S(1)}, bf16[16,1536]{1,0:T(8,128)(2,1)S(1)}, u32[]{:S(2)}, u32[]{:S(2)}) collective-permute-start(bf16[16,1536]{1,0:T(8,128)(2,1)S(1)} %add_convert_fusion.10), channel_id=1, source_target_pairs={{34,32},{35,33},{42,40},{43,41},{50,48},{51,49},{58,56},{59,57},{6... | collective-permute-start | bytes 147464 | tf_op jit(solution)/shard_map/root/ppermute | solution.py:32
  78.0 1.4 collective-permute-start.17
  80.2 13.9 %collective-permute-start.20 = (bf16[16,1536]{1,0:T(8,128)(2,1)S(1)}, bf16[16,1536]{1,0:T(8,128)(2,1)S(1)}, u32[]{:S(2)}, u32[]{:S(2)}) collective-permute-start(bf16[16,1536]{1,0:T(8,128)(2,1)S(1)} %fusion.7), channel_id=1, source_target_pairs={{32,16},{33,17},{40,24},{41,25},{48,0},{49,1},{56,8},{57,9},{160,1... | collective-permute-start | bytes 147464 | tf_op jit(solution)/shard_map/root/ppermute | solution.py:32
  81.5 14.9 %collective-permute-start.19 = (bf16[16,1536]{1,0:T(8,128)(2,1)S(1)}, bf16[16,1536]{1,0:T(8,128)(2,1)S(1)}, u32[]{:S(2)}, u32[]{:S(2)}) collective-permute-start(bf16[16,1536]{1,0:T(8,128)(2,1)S(1)} %fusion.7), channel_id=1, source_target_pairs={{32,0},{33,1},{40,8},{41,9},{48,16},{49,17},{56,24},{57,25},{160,1... | collective-permute-start | bytes 147464 | tf_op jit(solution)/shard_map/root/ppermute | solution.py:32
  82.8 26.2 %collective-permute-start.25 = (bf16[512,1024]{1,0:T(8,128)(2,1)}, bf16[512,1024]{1,0:T(8,128)(2,1)}, u32[]{:S(2)}, u32[]{:S(2)}) collective-permute-start(bf16[512,1024]{1,0:T(8,128)(2,1)} %bitcast.134), channel_id=1, source_target_pairs={{64,80},{72,88},{80,64},{88,72},{96,112},{104,120},{112,96},{120,1... | collective-permute-start | bytes 3145736 | tf_op jit(solution)/shard_map/root/ppermute | solution.py:148
  98.9 6.3 %collective-permute-start.23 = (bf16[16,1536]{1,0:T(8,128)(2,1)S(1)}, bf16[16,1536]{1,0:T(8,128)(2,1)S(1)}, u32[]{:S(2)}, u32[]{:S(2)}) collective-permute-start(bf16[16,1536]{1,0:T(8,128)(2,1)S(1)} %maximum_select_fusion.6), channel_id=1, source_target_pairs={{0,1},{1,0},{8,9},{9,8},{16,17},{17,16},{24,25},{25,24},{128,129},... | collective-permute-start | bytes 147464 | tf_op jit(solution)/shard_map/root/ppermute | solution.py:32
  102.6 2.6 %collective-permute-start.22 = (bf16[16,1536]{1,0:T(8,128)(2,1)S(1)}, bf16[16,1536]{1,0:T(8,128)(2,1)S(1)}, u32[]{:S(2)}, u32[]{:S(2)}) collective-permute-start(bf16[16,1536]{1,0:T(8,128)(2,1)S(1)} %maximum_select_fusion.6), channel_id=1, source_target_pairs={{0,7},{1,6},{8,15},{9,14},{16,23},{17,22},{24,31},{25,30},{34,35},... | collective-permute-start | bytes 147464 | tf_op jit(solution)/shard_map/root/ppermute | solution.py:32
  103.9 2.6 %collective-permute-start.21 = (bf16[16,1536]{1,0:T(8,128)(2,1)S(1)}, bf16[16,1536]{1,0:T(8,128)(2,1)S(1)}, u32[]{:S(2)}, u32[]{:S(2)}) collective-permute-start(bf16[16,1536]{1,0:T(8,128)(2,1)S(1)} %maximum_select_fusion.6), channel_id=1, source_target_pairs={{0,6},{1,7},{8,14},{9,15},{16,22},{17,23},{24,30},{25,31},{32,38},... | collective-permute-start | bytes 147464 | tf_op jit(solution)/shard_map/root/ppermute | solution.py:32
  106.5 2.5 %collective-permute-start.24 = (bf16[16,1536]{1,0:T(8,128)(2,1)S(1)}, bf16[16,1536]{1,0:T(8,128)(2,1)S(1)}, u32[]{:S(2)}, u32[]{:S(2)}) collective-permute-start(bf16[16,1536]{1,0:T(8,128)(2,1)S(1)} %add_convert_fusion.8), channel_id=1, source_target_pairs={{0,2},{1,3},{8,10},{9,11},{16,18},{17,19},{24,26},{25,27},{6,4},{7... | collective-permute-start | bytes 147464 | tf_op jit(solution)/shard_map/root/ppermute | solution.py:32
  107.8 29.8 %collective-permute-start.29 = (bf16[512,1024]{1,0:T(8,128)(2,1)}, bf16[512,1024]{1,0:T(8,128)(2,1)S(1)}, u32[]{:S(2)}, u32[]{:S(2)}) collective-permute-start(bf16[512,1024]{1,0:T(8,128)(2,1)} %bitcast.135), channel_id=1, source_target_pairs={{64,72},{72,64},{80,88},{88,80},{96,104},{104,96},{112,120},{120,1... | collective-permute-start | bytes 3145736 | tf_op jit(solution)/shard_map/root/ppermute | solution.py:149
  130.9 8.5 %collective-permute-start.28 = (bf16[32,1024]{1,0:T(8,128)(2,1)S(1)}, bf16[32,1024]{1,0:T(8,128)(2,1)S(1)}, u32[]{:S(2)}, u32[]{:S(2)}) collective-permute-start(bf16[32,1024]{1,0:T(8,128)(2,1)S(1)} %reduce_sum.22), channel_id=1, source_target_pairs={{96,0},{97,1},{104,8},{105,9},{112,16},{113,17},{120,24},{121,25},... | collective-permute-start | bytes 196616 | tf_op jit(solution)/shard_map/coupling/ppermute | solution.py:32
  132.2 8.9 %collective-permute-start.27 = (bf16[32,1024]{1,0:T(8,128)(2,1)S(1)}, bf16[32,1024]{1,0:T(8,128)(2,1)S(1)}, u32[]{:S(2)}, u32[]{:S(2)}) collective-permute-start(bf16[32,1024]{1,0:T(8,128)(2,1)S(1)} %reduce_sum.22), channel_id=1, source_target_pairs={{64,0},{65,1},{72,8},{73,9},{80,16},{81,17},{88,24},{89,25},{98,34... | collective-permute-start | bytes 196616 | tf_op jit(solution)/shard_map/coupling/ppermute | solution.py:32
  133.5 8.3 %collective-permute-start.26 = (bf16[32,1024]{1,0:T(8,128)(2,1)S(1)}, bf16[32,1024]{1,0:T(8,128)(2,1)S(1)}, u32[]{:S(2)}, u32[]{:S(2)}) collective-permute-start(bf16[32,1024]{1,0:T(8,128)(2,1)S(1)} %reduce_sum.22), channel_id=1, source_target_pairs={{32,0},{33,1},{40,8},{41,9},{48,16},{49,17},{56,24},{57,25},{66,34... | collective-permute-start | bytes 196616 | tf_op jit(solution)/shard_map/coupling/ppermute | solution.py:32
  134.8 9.3 %collective-permute-start.30 = (bf16[512,1024]{1,0:T(8,128)(2,1)}, bf16[512,1024]{1,0:T(8,128)(2,1)S(1)}, u32[]{:S(2)}, u32[]{:S(2)}) collective-permute-start(bf16[512,1024]{1,0:T(8,128)(2,1)} %collective-permute-done.25), channel_id=1, source_target_pairs={{64,72},{72,64},{80,88},{88,80},{96,104},{104,96},{112,120},{120,1... | collective-permute-start | bytes 3145736 | tf_op jit(solution)/shard_map/coupling/ppermute | solution.py:157
  146.2 1.4 collective-permute-start.32
  146.8 0.7 collective-permute-start.31
  148.8 1.4 collective-permute-start.33
  149.5 2.4 %collective-permute-start.34 = (bf16[32,2048]{1,0:T(8,128)(2,1)S(1)}, bf16[32,2048]{1,0:T(8,128)(2,1)S(1)}, u32[]{:S(2)}, u32[]{:S(2)}) collective-permute-start(bf16[32,2048]{1,0:T(8,128)(2,1)S(1)} %add_convert_fusion.6), channel_id=1, source_target_pairs={{100,98},{101,99},{108,106},{109,107},{116,114},{117,115},{124,122... | collective-permute-start | bytes 393224 | tf_op jit(solution)/shard_map/child/ppermute | solution.py:32
  152.5 2.6 %collective-permute-start.36 = (bf16[32,2048]{1,0:T(8,128)(2,1)S(1)}, bf16[32,2048]{1,0:T(8,128)(2,1)S(1)}, u32[]{:S(2)}, u32[]{:S(2)}) collective-permute-start(bf16[32,2048]{1,0:T(8,128)(2,1)S(1)} %add_convert_fusion.5), channel_id=1, source_target_pairs={{68,67},{69,66},{76,75},{77,74},{84,83},{85,82},{92,91},{93,90},{1... | collective-permute-start | bytes 393224 | tf_op jit(solution)/shard_map/child/ppermute | solution.py:32
  153.2 2.0 collective-permute-start.35
  154.5 1.6 collective-permute-start.37
  156.4 1.4 collective-permute-start.38
  157.1 2.4 %collective-permute-start.39 = (bf16[32,2048]{1,0:T(8,128)(2,1)S(1)}, bf16[32,2048]{1,0:T(8,128)(2,1)S(1)}, u32[]{:S(2)}, u32[]{:S(2)}) collective-permute-start(bf16[32,2048]{1,0:T(8,128)(2,1)S(1)} %add_convert_fusion.4), channel_id=1, source_target_pairs={{66,64},{67,65},{74,72},{75,73},{82,80},{83,81},{90,88},{91,89},{1... | collective-permute-start | bytes 393224 | tf_op jit(solution)/shard_map/child/ppermute | solution.py:32
  160.2 2.6 %collective-permute-start.41 = (bf16[32,2048]{1,0:T(8,128)(2,1)S(1)}, bf16[32,2048]{1,0:T(8,128)(2,1)S(1)}, u32[]{:S(2)}, u32[]{:S(2)}) collective-permute-start(bf16[32,2048]{1,0:T(8,128)(2,1)S(1)} %add_convert_fusion.3), channel_id=1, source_target_pairs={{34,33},{35,32},{42,41},{43,40},{50,49},{51,48},{58,57},{59,56},{6... | collective-permute-start | bytes 393224 | tf_op jit(solution)/shard_map/child/ppermute | solution.py:32
  160.9 2.0 collective-permute-start.40
  162.1 1.6 collective-permute-start.42
  164.1 47.3 %collective-permute-start.43 = (bf16[32,1024]{1,0:T(8,128)(2,1)S(1)}, bf16[32,1024]{1,0:T(8,128)(2,1)S(1)}, u32[]{:S(2)}, u32[]{:S(2)}) collective-permute-start(bf16[32,1024]{1,0:T(8,128)(2,1)S(1)} %fusion.19), channel_id=1, source_target_pairs={{32,0},{33,1},{40,8},{41,9},{48,16},{49,17},{56,24},{57,25},{160,1... | collective-permute-start | bytes 196616 | tf_op jit(solution)/shard_map/child/ppermute | solution.py:32
  213.2 5.7 %collective-permute-start.46 = (bf16[32,2048]{1,0:T(8,128)(2,1)S(1)}, bf16[32,2048]{1,0:T(8,128)(2,1)S(1)}, u32[]{:S(2)}, u32[]{:S(2)}) collective-permute-start(bf16[32,2048]{1,0:T(8,128)(2,1)S(1)} %maximum_select_fusion.3), channel_id=1, source_target_pairs={{0,1},{1,0},{8,9},{9,8},{16,17},{17,16},{24,25},{25,24},{128,129},... | collective-permute-start | bytes 393224 | tf_op jit(solution)/shard_map/child/ppermute | solution.py:32
  215.1 3.8 %collective-permute-start.45 = (bf16[32,2048]{1,0:T(8,128)(2,1)S(1)}, bf16[32,2048]{1,0:T(8,128)(2,1)S(1)}, u32[]{:S(2)}, u32[]{:S(2)}) collective-permute-start(bf16[32,2048]{1,0:T(8,128)(2,1)S(1)} %maximum_select_fusion.3), channel_id=1, source_target_pairs={{0,7},{1,6},{8,15},{9,14},{16,23},{17,22},{24,31},{25,30},{34,35},... | collective-permute-start | bytes 393224 | tf_op jit(solution)/shard_map/child/ppermute | solution.py:32
  216.4 10.5 %collective-permute-start.44 = (bf16[32,2048]{1,0:T(8,128)(2,1)S(1)}, bf16[32,2048]{1,0:T(8,128)(2,1)S(1)}, u32[]{:S(2)}, u32[]{:S(2)}) collective-permute-start(bf16[32,2048]{1,0:T(8,128)(2,1)S(1)} %maximum_select_fusion.3), channel_id=1, source_target_pairs={{0,6},{1,7},{8,14},{9,15},{16,22},{17,23},{24,30},{25,31},{32,38},... | collective-permute-start | bytes 393224 | tf_op jit(solution)/shard_map/child/ppermute | solution.py:32
  227.0 3.2 %collective-permute-start.47 = (bf16[32,2048]{1,0:T(8,128)(2,1)S(1)}, bf16[32,2048]{1,0:T(8,128)(2,1)S(1)}, u32[]{:S(2)}, u32[]{:S(2)}) collective-permute-start(bf16[32,2048]{1,0:T(8,128)(2,1)S(1)} %add_convert_fusion.1), channel_id=1, source_target_pairs={{0,2},{1,3},{8,10},{9,11},{16,18},{17,19},{24,26},{25,27},{6,4},{7... | collective-permute-start | bytes 393224 | tf_op jit(solution)/shard_map/child/ppermute | solution.py:32
  (9 other events, 181.8 us)

commit v6 on v5

--- a/solution.py
+++ b/solution.py
@@ -1,6 +1,8 @@
 import jax
 import jax.numpy as jnp
 from jax import lax
+from jax.experimental import pallas as pl
+from jax.experimental.pallas import tpu as pltpu
 from jax.sharding import PartitionSpec as P
 
 PANELS = 4
@@ -29,44 +31,101 @@
                 source = (rows * GROUP + j) * COLS + cols * PAIR + q
                 target = (to_rows * GROUP + (j ^ row_flip)) * COLS + to_cols * PAIR + (q ^ col_flip)
                 pairs.append((source, target))
-    return lax.ppermute(value, GRID, pairs).astype(F32)
-
-
-def sweep(rhs, blocks, split_rows, beside=lambda r, value: value):
-    rows = blocks[0].shape[0]
-
-    def forward(x):
-        return sum(dot(x[:, i * rows : (i + 1) * rows], block) for i, block in enumerate(blocks))
-
-    def diagonal(x):
-        return jnp.concatenate([dot_t(x, block) for block in blocks], 1)
-
+    return lax.ppermute(value, GRID, pairs)
+
+
+def terms_kernel(keep_own, keep_other, x, own, other, carried, terms, total):
+    step = pl.program_id(0)
+    block = own.shape[0]
+
+    @pl.when(step == 0)
+    def _():
+        total[...] = carried[...]
+
+    for c in range(own.shape[1] // block):
+        cols = slice(c * block, (c + 1) * block)
+        total[:, cols] += keep_own[step, c] * dot(x[0], own[:, cols])
+        total[:, cols] += keep_other[step, c] * dot(x[1], other[:, cols])
+
+    @pl.when(step == pl.num_programs(0) - 1)
+    def _():
+        terms[...] = total[...].astype(BF16)
+
+
+def root_terms(keep, factors, current, carried):
+    steps, probes, (rows, cols) = keep[0].shape[0], current.shape[1], factors[0].shape
+    factor_spec = pl.BlockSpec((rows // steps, cols), lambda i: (i, 0))
+    whole = pl.BlockSpec((probes, cols), lambda i: (0, 0))
+    return pl.pallas_call(
+        terms_kernel,
+        grid=(steps,),
+        in_specs=[pl.BlockSpec(memory_space=pltpu.SMEM)] * 2
+        + [pl.BlockSpec((2, probes, rows // steps), lambda i: (0, 0, i))]
+        + [factor_spec] * 2
+        + [whole],
+        out_specs=whole,
+        out_shape=jax.ShapeDtypeStruct((probes, cols), BF16),
+        scratch_shapes=[pltpu.VMEM((probes, cols), F32)],
+        compiler_params=pltpu.CompilerParams(vmem_limit_bytes=8 * 2**20),
+        cost_estimate=pl.CostEstimate(
+            flops=4 * probes * rows * cols, bytes_accessed=4 * rows * cols, transcendentals=0
+        ),
+    )(*keep, *([current] + list(factors) + [carried]))
+
+
+def pieces_kernel(solving, rhs, first, second, own, other, current, out, residual):
+    @pl.when(pl.program_id(0) == 0)
+    def _():
+        totals = first[...].astype(F32) + second[...].astype(F32)
+        residual[...] = (rhs[...] - totals).astype(BF16)
+
+    for k, factor in enumerate((own, other)):
+        piece = dot_t(residual[...], factor[...])
+        out[k] = jnp.where(solving[0] == 1, piece, current[k].astype(F32)).astype(BF16)
+
+
+def root_pieces(solving, rhs, first, second, factors, current):
+    (rows, cols), probes, steps = factors[0].shape, rhs.shape[0], 3
+    factor_spec = pl.BlockSpec((rows // steps, cols), lambda i: (i, 0))
+    whole = pl.BlockSpec((probes, cols), lambda i: (0, 0))
+    part = pl.BlockSpec((2, probes, rows // steps), lambda i: (0, 0, i))
+    return pl.pallas_call(
+        pieces_kernel,
+        grid=(steps,),
+        in_specs=[pl.BlockSpec(memory_space=pltpu.SMEM)] + [whole] * 3 + [factor_spec] * 2 + [part],
+        out_specs=part,
+        out_shape=jax.ShapeDtypeStruct(current.shape, BF16),
+        scratch_shapes=[pltpu.VMEM((probes, cols), BF16)],
+        compiler_params=pltpu.CompilerParams(vmem_limit_bytes=8 * 2**20),
+        cost_estimate=pl.CostEstimate(
+            flops=4 * probes * rows * cols, bytes_accessed=4 * rows * cols, transcendentals=0
+        ),
+    )(solving.astype(jnp.int32).reshape(1), rhs, first, second, *factors, current)
+
+
+def sweep(rhs, current, forward, solve, split_rows, beside=lambda r, value: value):
     row_panel = lax.axis_index("row") // GROUP
     col_panel = lax.axis_index("col") // PAIR
-    current = jnp.zeros((rhs.shape[0], len(blocks) * rows), BF16)
     carried = jnp.zeros(rhs.shape, F32)
-    totals = jnp.zeros(rhs.shape, F32)
+    first = second = jnp.zeros(rhs.shape, BF16)
     for r in range(PANELS - 1, -1, -1):
         ahead = None
         if r < PANELS - 1:
-            terms = beside(r, (forward(current) + carried).astype(BF16))
+            terms = beside(r, forward(current, carried))
             down = [(r + 1, r, 0, r, r, 0)]
             if r == 1:
                 down.append((3, 2, 0, 0, 0, 0))
             first = send(terms, down)
-            totals = first
             if split_rows:
-                totals = totals + send(terms, [(r + 1, r, 2, r, r, 0)])
+                second = send(terms, [(r + 1, r, 2, r, r, 0)])
             if r >= 1:
                 ahead = send(current, [(r + 1, r + 1, 0, r, r - 1, 0)])
-            carried = carried + first
-        residual = (rhs - totals).astype(BF16)
-        piece = diagonal(residual).astype(BF16)
+            carried = carried + first.astype(F32)
+        current = solve((row_panel == r) & (col_panel == r), rhs, first, second, current)
         if r == PANELS - 1:
-            piece = beside(r, piece)
-        current = jnp.where((row_panel == r) & (col_panel == r), piece, current)
+            current = beside(r, current)
         if ahead is not None:
-            current = (current.astype(F32) + ahead).astype(BF16)
+            current = (current.astype(F32) + ahead.astype(F32)).astype(BF16)
         if r >= 1:
             straight = [(r, r, 0, r, r - 1, 0)]
             crossed = [(r, r, 0, r, r - 1, 1)]
@@ -76,18 +135,20 @@
             if r == 1:
                 straight.append((2, 2, 0, 0, 3, 0))
                 crossed.append((2, 2, 0, 2, 2, 1))
-            received = send(current, straight) + send(current, crossed)
+            received = send(current, straight).astype(F32) + send(current, crossed).astype(F32)
             if r < PANELS - 1:
-                terms = (forward(current) + carried).astype(BF16)
-                carried = carried + send(terms, [(r + 1, r, 0, r - 1, r - 1, 0)])
+                terms = forward(current, carried)
+                carried = carried + send(terms, [(r + 1, r, 0, r - 1, r - 1, 0)]).astype(F32)
             current = (current.astype(F32) + received).astype(BF16)
         else:
-            received = send(current, [(0, 0, 0, 0, 3, 0), (1, 1, 0, 0, 3, 0)])
-            received = received + send(current, [(0, 0, 0, 0, 3, 1), (1, 1, 0, 1, 1, 1)])
-            received = received + send(current, [(0, 0, 0, 0, 0, 1)])
-            current = (current.astype(F32) + received).astype(BF16)
+            received = [
+                send(current, [(0, 0, 0, 0, 3, 0), (1, 1, 0, 0, 3, 0)]),
+                send(current, [(0, 0, 0, 0, 3, 1), (1, 1, 0, 1, 1, 1)]),
+                send(current, [(0, 0, 0, 0, 0, 1)]),
+            ]
+            current = sum([part.astype(F32) for part in received], current.astype(F32)).astype(BF16)
             received = send(current, [(0, 0, 0, 0, 1, 0), (0, 0, 0, 3, 2, 0), (1, 1, 0, 3, 2, 0)])
-            current = (current.astype(F32) + received).astype(BF16)
+            current = (current.astype(F32) + received.astype(F32)).astype(BF16)
     return current
 
 
@@ -106,16 +167,9 @@
         swap = [(i, i ^ 1) for i in range(ROWS)]
         partner_factor = lax.ppermute(root_factor, "row", swap)
         partner_pattern = lax.ppermute(pattern, "row", swap)
-        block = rows_here // pattern.shape[0]
         on_diagonal = row_index // GROUP == col_index // PAIR
-
-        def masked(factor, blocks):
-            expanded = jnp.repeat(jnp.repeat(blocks, block, 0), block, 1)
-            return factor * jnp.where(on_diagonal, 1, expanded).astype(BF16)
-
-        masked_root = masked(root_factor, pattern)
-        partner_root = masked(partner_factor, partner_pattern)
-
+        keep = [jnp.where(on_diagonal, 1, p).astype(F32) for p in (pattern, partner_pattern)]
+        factors = [root_factor, partner_factor]
 
     with jax.named_scope("rhs"):
         probes_here = partials.shape[1]
@@ -150,12 +204,21 @@
         return value
 
     with jax.named_scope("root"):
-        root_rows = sweep(root_rhs, [masked_root, partner_root], True, move_children)
+        root_rows = sweep(
+            root_rhs,
+            jnp.zeros((2, root_rhs.shape[0], rows_here), BF16),
+            lambda current, carried: root_terms(keep, factors, current, carried),
+            lambda solving, rhs, first, second, current: root_pieces(
+                solving, rhs, first, second, factors, current
+            ),
+            True,
+            move_children,
+        )
 
     with jax.named_scope("coupling"):
         root_rows, there = lax.optimization_barrier((root_rows, moved[1, 2]))
         moved[1, 3] = lax.ppermute(there, "row", rows_of(1, 1))
-        own, other = root_rows[:, :rows_here], root_rows[:, rows_here:]
+        own, other = root_rows[0], root_rows[1]
         by_core = jnp.stack([jnp.where(core == k, own, other) for k in range(2)])
         shared = jnp.broadcast_to(by_core[None], (layers,) + by_core.shape)
         shared = shared.reshape(layers * 2 * ROWS, rows_here)
@@ -168,13 +231,28 @@
         terms = jnp.sum(terms.reshape(GROUP, share, -1).astype(F32), 0).astype(BF16)
         coupled = terms.astype(F32)
         for d in range(1, PANELS):
-            coupled = coupled + send(terms, [((p + d) % PANELS, p, 0, p, p, 0) for p in range(PANELS)])
+            parts = [((p + d) % PANELS, p, 0, p, p, 0) for p in range(PANELS)]
+            coupled = coupled + send(terms, parts).astype(F32)
         bits = lax.dynamic_slice_in_dim(child_bits[0], row_index % GROUP * share, share, 0)
         child_rhs = (2 * bits - 1).astype(F32) - coupled
 
     with jax.named_scope("child"):
         blocks = [child_here] + [moved[0, flip] + moved[1, flip] for flip in (1, 2, 3)]
-        child_rows = sweep(child_rhs, blocks, False).reshape(share, 2, 2, -1)
+        rows = child_here.shape[0]
+
+        def child_terms(current, carried):
+            for i, block in enumerate(blocks):
+                carried = carried + dot(current[:, i * rows : (i + 1) * rows], block)
+            return carried.astype(BF16)
+
+        def child_pieces(solving, rhs, first, second, current):
+            residual = (rhs - first.astype(F32)).astype(BF16)
+            piece = jnp.concatenate([dot_t(residual, block) for block in blocks], 1).astype(BF16)
+            return jnp.where(solving, piece, current)
+
+        child_rows = jnp.zeros((share, GROUP * rows), BF16)
+        child_rows = sweep(child_rhs, child_rows, child_terms, child_pieces, False)
+        child_rows = child_rows.reshape(share, 2, 2, -1)
         child_rows = jnp.where(core == 1, child_rows[:, :, ::-1], child_rows)
         child_rows = jnp.where(row_index % GROUP // 2 == 1, child_rows[:, ::-1], child_rows)
         child_rows = child_rows.reshape(share, GROUP, -1).transpose(1, 0, 2)

time: 241 us -> 251 us (1.041)
  Pallas kernels: 0 us -> 14.6 us
  local copies, waits for them, and re-layouts: 7.14 us -> 12.9 us
  matrix products: 28.8 us -> 23.9 us
  other arithmetic: 11.1 us -> 7.79 us
    pallas_call x0 -> x9, Pallas kernels: none -> 14.6 us  [the longest x5 8.29 us: root_terms(): pl.pallas_call(terms_kernel, grid=(steps,), in_specs=[pl.BlockSpec(memory...]
    unnamed x22 -> x29, local copies, waits for them, and re-layouts: 5.22 us -> 10.4 us
    ppermute x2, waiting for transfers between devices: 12.5 us -> 8.32 us  [move_children(): moved[half, 2] = lax.ppermute(here, 'row', rows_of(half, 2))]
    dot_general x24 -> x16, matrix products: 15.4 us -> 11.7 us  [dot_t(): lax.dot_general(a, b, (((1,), (1,)), ((), ())), preferred_element_type=F32)]
    mul x2 -> x0, other arithmetic: 3.66 us -> none  [masked(): return factor * jnp.where(on_diagonal, 1, expanded).astype(BF16)]
    ppermute x40, waiting for transfers between devices: 73.2 us -> 76 us  [send(): return lax.ppermute(value, GRID, pairs)]
    dot_general x31 -> x21, matrix products: 13.4 us -> 12.3 us  [dot(): return jnp.dot(a, b, preferred_element_type=F32)]
  transfers between devices with their start and end apart: 49 -> 49, of which waited for: 12 -> 13; matrix products, arithmetic and copies ran while one was open for 13% -> 9% of each run, Pallas kernels for 0% -> 6%
where the time goes in v6:
time: 251 us; the launch traced here: 249 us
  waiting for transfers between devices  93.8 us (37%)
  starting transfers between devices  65.7 us (26%)
  blocking collectives  28.8 us (11%)
  matrix products  23.9 us (10%)
  Pallas kernels  14.6 us (6%)
  local copies, waits for them, and re-layouts  12.9 us (5%)
  other arithmetic  7.79 us (3%)
    ppermute x40, waiting for transfers between devices, send(): return lax.ppermute(value, GRID, pairs)  76 us
    ppermute x40, starting transfers between devices, send(): return lax.ppermute(value, GRID, pairs)  37.4 us
    all_to_all x1, blocking collectives, per_device(): lax.all_to_all(shared, ('gz', 'row'), 0, 0, tiled=True, axis_index_groups...  12.3 us
    dot_general x21, matrix products, dot(): return jnp.dot(a, b, preferred_element_type=F32)  12.3 us
    dot_general x16, matrix products, dot_t(): lax.dot_general(a, b, (((1,), (1,)), ((), ())), preferred_element_type=F32)  11.7 us
    unnamed x29, local copies, waits for them, and re-layouts  10.4 us
    all_to_all x1, waiting for transfers between devices, per_device(): lax.all_to_all(pieces.reshape(layers * ROWS, 12, lanes), ('gz', 'row'), 0...  9.41 us
    ppermute x1, starting transfers between devices, per_device(): partner_factor = lax.ppermute(root_factor, 'row', swap)  8.92 us
  transfers between devices with their start and end apart: 49, of which 13 were waited for; matrix products, arithmetic and copies ran while one was open for 9% of the time, Pallas kernels for 6%

profile of v6, /device:TPU:1, one launch (start us, length us, event | category | flops | bytes accessed | tf_op | source)
XLA Modules:
  0.0 249.4 jit_solution(17989045630890140992)
XLA Ops:
  0.6 8.9 %collective-permute-start.1 = (bf16[768,1536]{1,0:T(8,128)(2,1)}, bf16[768,1536]{1,0:T(8,128)(2,1)S(1)}, u32[]{:S(2)}, u32[]{:S(2)}) collective-permute-start(bf16[768,1536]{1,0:T(8,128)(2,1)} %own.17), channel_id=1, source_target_pairs={{0,8},{8,0},{16,24},{24,16},{32,40},{40,32},{48,56},{56,48},{64,72... | collective-permute-start | bytes 7077896 | tf_op jit(solution)/shard_map/mask/ppermute | solution.py:168
  11.1 5.1 %all-to-all-start = ((bf16[64,12,128]{2,1,0:T(8,128)(2,1)}), bf16[64,12,128]{2,1,0:T(8,128)(2,1)}, u32[]{:S(2)}, u32[]{:S(2)}) async-start(bf16[64,12,128]{2,1,0:T(8,128)(2,1)} %bitcast.1), calls=%async_computation | async-start | bytes 524288 | tf_op jit(solution)/shard_map/rhs/all_to_all | solution.py:179
  16.2 2.4 collective-permute-start
  18.7 9.4 %all-to-all-done = bf16[64,12,128]{2,1,0:T(8,128)(2,1)} async-done(((bf16[64,12,128]{2,1,0:T(8,128)(2,1)}), bf16[64,12,128]{2,1,0:T(8,128)(2,1)}, u32[]{:S(2)}, u32[]{:S(2)}) %all-to-all-start) | async-done | bytes 196640 | tf_op jit(solution)/shard_map/rhs/all_to_all | solution.py:179
  29.1 1.4 copy-done.3
  30.5 1.7 copy-done.1
  32.2 1.7 copy-done.4
  33.9 1.6 root.9
  36.8 3.1 %collective-permute-start.11 = (bf16[512,1024]{1,0:T(8,128)(2,1)}, bf16[512,1024]{1,0:T(8,128)(2,1)}, u32[]{:S(2)}, u32[]{:S(2)}) collective-permute-start(bf16[512,1024]{1,0:T(8,128)(2,1)} %bitcast.6), channel_id=1, source_target_pairs={{0,16},{8,24},{16,0},{24,8},{32,48},{40,56},{48,32},{56,40},{1,17}... | collective-permute-start | bytes 3145736 | tf_op jit(solution)/shard_map/root/ppermute | solution.py:202
  39.9 2.5 %collective-permute-start.10 = (bf16[512,1024]{1,0:T(8,128)(2,1)}, bf16[512,1024]{1,0:T(8,128)(2,1)}, u32[]{:S(2)}, u32[]{:S(2)}) collective-permute-start(bf16[512,1024]{1,0:T(8,128)(2,1)} %bitcast.6), channel_id=1, source_target_pairs={{0,8},{8,0},{16,24},{24,16},{32,40},{40,32},{48,56},{56,48},{1,9},... | collective-permute-start | bytes 3145736 | tf_op jit(solution)/shard_map/root/ppermute | solution.py:203
  42.5 1.7 root.10
  46.2 1.7 copy-done.6
  47.9 1.6 root.11
  50.9 1.7 root.12
  53.3 1.7 root.13
  55.0 8.3 %collective-permute-done.11 = bf16[512,1024]{1,0:T(8,128)(2,1)} collective-permute-done((bf16[512,1024]{1,0:T(8,128)(2,1)}, bf16[512,1024]{1,0:T(8,128)(2,1)}, u32[]{:S(2)}, u32[]{:S(2)}) %collective-permute-start.11) | collective-permute-done | bytes 1048608 | tf_op jit(solution)/shard_map/root/ppermute | solution.py:202
  65.9 3.2 %collective-permute-start.18 = (bf16[512,1024]{1,0:T(8,128)(2,1)}, bf16[512,1024]{1,0:T(8,128)(2,1)S(1)}, u32[]{:S(2)}, u32[]{:S(2)}) collective-permute-start(bf16[512,1024]{1,0:T(8,128)(2,1)} %collective-permute-done.11), channel_id=1, source_target_pairs={{0,8},{8,0},{16,24},{24,16},{32,40},{40,32},{48,56},{56,48},{1,9},... | collective-permute-start | bytes 3145736 | tf_op jit(solution)/shard_map/root/ppermute | solution.py:196
  69.2 1.7 copy-done.8
  70.8 1.6 root.14
  74.6 1.7 root.15
  77.0 1.7 root.16
  78.7 1.7 collective-permute-start.25
  83.0 12.2 %collective-permute-done.20.second = bf16[16,1536]{1,0:T(8,128)(2,1)S(1)} collective-permute-done((bf16[16,1536]{1,0:T(8,128)(2,1)S(1)}, bf16[16,1536]{1,0:T(8,128)(2,1)S(1)}, u32[]{:S(2)}, u32[]{:S(2)}) %collective-permute-start.20) | collective-permute-done | bytes 49184 | tf_op jit(solution)/shard_map/root/ppermute | solution.py:34
  95.2 4.9 %collective-permute-done.19.first = bf16[16,1536]{1,0:T(8,128)(2,1)S(1)} collective-permute-done((bf16[16,1536]{1,0:T(8,128)(2,1)S(1)}, bf16[16,1536]{1,0:T(8,128)(2,1)S(1)}, u32[]{:S(2)}, u32[]{:S(2)}) %collective-permute-start.19) | collective-permute-done | bytes 49184 | tf_op jit(solution)/shard_map/root/ppermute | solution.py:34
  100.1 1.7 copy-done.10
  101.7 1.6 root.17
  103.3 1.9 collective-permute-start.23
  108.2 1.5 collective-permute-done.21
  112.2 12.3 %all_to_all.29 = bf16[8,16,768]{2,1,0:T(8,128)(2,1)S(1)} all-to-all(bf16[8,16,768]{2,1,0:T(8,128)(2,1)S(1)} %bitcast.91), channel_id=1, replica_groups={{0,8,128,136,256,264,384,392},{16,24,144,152,272,280,400,408},{32,40,16..., dimensions={0} | all-to-all | bytes 393216 | tf_op jit(solution)/shard_map/coupling/all_to_all | solution.py:225
  124.9 8.3 %all_to_all.30 = bf16[4,32,1024]{2,1,0:T(8,128)(2,1)S(1)} all-to-all(bf16[4,32,1024]{2,1,0:T(8,128)(2,1)S(1)} %bitcast.90), channel_id=1, replica_groups={{0,8,16,24},{32,40,48,56},{64,72,80,88},{96,104,112,120},{1,9,17,25},{3..., dimensions={0} | all-to-all | bytes 524288 | tf_op jit(solution)/shard_map/coupling/all_to_all | solution.py:229
  138.0 1.9 add.203
  139.9 1.6 add.202
  141.6 2.0 collective-permute-done.27
  145.2 1.6 convolution_convert_fusion.16
  150.3 1.5 fusion.53
  155.3 1.6 convolution_convert_fusion.12
  159.2 1.5 fusion.12
  162.4 1.5 fusion.11
  166.6 1.6 convolution_convert_fusion.8
  170.6 1.5 fusion.10
  173.4 1.5 fusion.26
  176.5 42.8 %collective-permute-done.43 = bf16[32,1024]{1,0:T(8,128)(2,1)S(1)} collective-permute-done((bf16[32,1024]{1,0:T(8,128)(2,1)S(1)}, bf16[32,1024]{1,0:T(8,128)(2,1)S(1)}, u32[]{:S(2)}, u32[]{:S(2)}) %collective-permute-start.43) | collective-permute-done | bytes 65568 | tf_op jit(solution)/shard_map/child/ppermute | solution.py:34
  220.7 1.6 convolution_convert_fusion.4
  222.4 1.9 collective-permute-start.46
  228.1 8.1 %collective-permute-done.44 = bf16[32,2048]{1,0:T(8,128)(2,1)S(1)} collective-permute-done((bf16[32,2048]{1,0:T(8,128)(2,1)S(1)}, bf16[32,2048]{1,0:T(8,128)(2,1)S(1)}, u32[]{:S(2)}, u32[]{:S(2)}) %collective-permute-start.44) | collective-permute-done | bytes 131104 | tf_op jit(solution)/shard_map/child/ppermute | solution.py:34
  236.2 1.3 collective-permute-start.47
  237.5 1.9 collective-permute-done.47
  240.6 8.1 %all_to_all.31 = bf16[4,32,512]{2,1,0:T(8,128)(2,1)S(1)} all-to-all(bf16[4,32,512]{2,1,0:T(8,128)(2,1)S(1)} %bitcast.92), channel_id=1, replica_groups={{0,8,16,24},{32,40,48,56},{64,72,80,88},{96,104,112,120},{1,9,17,25},{3..., dimensions={0} | all-to-all | bytes 262144 | tf_op jit(solution)/shard_map/child/all_to_all | solution.py:260
  (174 shorter events, 53.7 us)
Async XLA Ops:
  0.6 28.5 %collective-permute-start.1 = (bf16[768,1536]{1,0:T(8,128)(2,1)}, bf16[768,1536]{1,0:T(8,128)(2,1)S(1)}, u32[]{:S(2)}, u32[]{:S(2)}) collective-permute-start(bf16[768,1536]{1,0:T(8,128)(2,1)} %own.17), channel_id=1, source_target_pairs={{0,8},{8,0},{16,24},{24,16},{32,40},{40,32},{48,56},{56,48},{64,72... | collective-permute-start | bytes 7077896 | tf_op jit(solution)/shard_map/mask/ppermute | solution.py:168
  11.1 17.0 %all-to-all-start = ((bf16[64,12,128]{2,1,0:T(8,128)(2,1)}), bf16[64,12,128]{2,1,0:T(8,128)(2,1)}, u32[]{:S(2)}, u32[]{:S(2)}) async-start(bf16[64,12,128]{2,1,0:T(8,128)(2,1)} %bitcast.1), calls=%async_computation | async-start | bytes 524288 | tf_op jit(solution)/shard_map/rhs/all_to_all | solution.py:179
  16.2 20.6 %collective-permute-start = (s32[3,6]{1,0:T(4,128)}, s32[3,6]{1,0:T(4,128)S(1)}, u32[]{:S(2)}, u32[]{:S(2)}) collective-permute-start(s32[3,6]{1,0:T(4,128)} %param.8), channel_id=1, source_target_pairs={{0,8},{8,0},{16,24},{24,16},{32,40},{40,32},{48,56},{56,48},{64,72... | collective-permute-start | bytes 224 | tf_op jit(solution)/shard_map/mask/ppermute | solution.py:169
  35.4 7.0 %collective-permute-start.3 = (bf16[2,16,768]{2,1,0:T(8,128)(2,1)S(1)}, bf16[2,16,768]{2,1,0:T(8,128)(2,1)S(1)}, u32[]{:S(2)}, u32[]{:S(2)}) collective-permute-start(bf16[2,16,768]{2,1,0:T(8,128)(2,1)S(1)} %root.9), channel_id=1, source_target_pairs={{102,101},{103,100},{110,109},{111,108},{118,117},{119,116},{126,1... | collective-permute-start | bytes 147464 | tf_op jit(solution)/shard_map/root/ppermute | solution.py:34
  36.1 6.3 %collective-permute-start.2 = (bf16[2,16,768]{2,1,0:T(8,128)(2,1)S(1)}, bf16[2,16,768]{2,1,0:T(8,128)(2,1)S(1)}, u32[]{:S(2)}, u32[]{:S(2)}) collective-permute-start(bf16[2,16,768]{2,1,0:T(8,128)(2,1)S(1)} %root.9), channel_id=1, source_target_pairs={{102,100},{103,101},{110,108},{111,109},{118,116},{119,117},{126,1... | collective-permute-start | bytes 147464 | tf_op jit(solution)/shard_map/root/ppermute | solution.py:34
  36.8 26.5 %collective-permute-start.11 = (bf16[512,1024]{1,0:T(8,128)(2,1)}, bf16[512,1024]{1,0:T(8,128)(2,1)}, u32[]{:S(2)}, u32[]{:S(2)}) collective-permute-start(bf16[512,1024]{1,0:T(8,128)(2,1)} %bitcast.6), channel_id=1, source_target_pairs={{0,16},{8,24},{16,0},{24,8},{32,48},{40,56},{48,32},{56,40},{1,17}... | collective-permute-start | bytes 3145736 | tf_op jit(solution)/shard_map/root/ppermute | solution.py:202
  39.9 23.4 %collective-permute-start.10 = (bf16[512,1024]{1,0:T(8,128)(2,1)}, bf16[512,1024]{1,0:T(8,128)(2,1)}, u32[]{:S(2)}, u32[]{:S(2)}) collective-permute-start(bf16[512,1024]{1,0:T(8,128)(2,1)} %bitcast.6), channel_id=1, source_target_pairs={{0,8},{8,0},{16,24},{24,16},{32,40},{40,32},{48,56},{56,48},{1,9},... | collective-permute-start | bytes 3145736 | tf_op jit(solution)/shard_map/root/ppermute | solution.py:203
  44.2 2.0 collective-permute-start.5
  44.9 1.4 collective-permute-start.4
  45.5 4.0 %collective-permute-start.6 = (bf16[2,16,768]{2,1,0:T(8,128)(2,1)S(1)}, bf16[2,16,768]{2,1,0:T(8,128)(2,1)S(1)}, u32[]{:S(2)}, u32[]{:S(2)}) collective-permute-start(bf16[2,16,768]{2,1,0:T(8,128)(2,1)S(1)} %add_convert_fusion.14.x.current), channel_id=1, source_target_pairs={{100,98},{101,99},{108,106},{109,107},{116,114},{117,115},{124,122... | collective-permute-start | bytes 147464 | tf_op jit(solution)/shard_map/root/ppermute | solution.py:34
  49.5 3.7 %collective-permute-start.8 = (bf16[2,16,768]{2,1,0:T(8,128)(2,1)S(1)}, bf16[2,16,768]{2,1,0:T(8,128)(2,1)S(1)}, u32[]{:S(2)}, u32[]{:S(2)}) collective-permute-start(bf16[2,16,768]{2,1,0:T(8,128)(2,1)S(1)} %add_convert_fusion.13.x), channel_id=1, source_target_pairs={{68,67},{69,66},{76,75},{77,74},{84,83},{85,82},{92,91},{93,90},{1... | collective-permute-start | bytes 147464 | tf_op jit(solution)/shard_map/root/ppermute | solution.py:34
  50.2 3.0 %collective-permute-start.7 = (bf16[2,16,768]{2,1,0:T(8,128)(2,1)S(1)}, bf16[2,16,768]{2,1,0:T(8,128)(2,1)S(1)}, u32[]{:S(2)}, u32[]{:S(2)}) collective-permute-start(bf16[2,16,768]{2,1,0:T(8,128)(2,1)S(1)} %add_convert_fusion.13.x), channel_id=1, source_target_pairs={{68,66},{69,67},{76,74},{77,75},{84,82},{85,83},{92,90},{93,91},{9... | collective-permute-start | bytes 147464 | tf_op jit(solution)/shard_map/root/ppermute | solution.py:34
  52.6 0.7 collective-permute-start.9
  63.3 5.8 %collective-permute-start.13 = (bf16[16,1536]{1,0:T(8,128)(2,1)S(1)}, bf16[16,1536]{1,0:T(8,128)(2,1)S(1)}, u32[]{:S(2)}, u32[]{:S(2)}) collective-permute-start(bf16[16,1536]{1,0:T(8,128)(2,1)S(1)} %root.13), channel_id=1, source_target_pairs={{66,50},{67,51},{74,58},{75,59},{82,34},{83,35},{90,42},{91,43},{1... | collective-permute-start | bytes 147464 | tf_op jit(solution)/shard_map/root/ppermute | solution.py:34
  64.0 5.2 %collective-permute-start.12 = (bf16[16,1536]{1,0:T(8,128)(2,1)S(1)}, bf16[16,1536]{1,0:T(8,128)(2,1)S(1)}, u32[]{:S(2)}, u32[]{:S(2)}) collective-permute-start(bf16[16,1536]{1,0:T(8,128)(2,1)S(1)} %root.13), channel_id=1, source_target_pairs={{66,34},{67,35},{74,42},{75,43},{82,50},{83,51},{90,58},{91,59},{9... | collective-permute-start | bytes 147464 | tf_op jit(solution)/shard_map/root/ppermute | solution.py:34
  64.7 7.8 %collective-permute-start.14 = (bf16[2,16,768]{2,1,0:T(8,128)(2,1)S(1)}, bf16[2,16,768]{2,1,0:T(8,128)(2,1)}, u32[]{:S(2)}, u32[]{:S(2)}) collective-permute-start(bf16[2,16,768]{2,1,0:T(8,128)(2,1)S(1)} %add_convert_fusion.12.x.current), channel_id=1, source_target_pairs={{66,64},{67,65},{74,72},{75,73},{82,80},{83,81},{90,88},{91,89},{1... | collective-permute-start | bytes 147464 | tf_op jit(solution)/shard_map/root/ppermute | solution.py:34
  65.9 12.8 %collective-permute-start.18 = (bf16[512,1024]{1,0:T(8,128)(2,1)}, bf16[512,1024]{1,0:T(8,128)(2,1)S(1)}, u32[]{:S(2)}, u32[]{:S(2)}) collective-permute-start(bf16[512,1024]{1,0:T(8,128)(2,1)} %collective-permute-done.11), channel_id=1, source_target_pairs={{0,8},{8,0},{16,24},{24,16},{32,40},{40,32},{48,56},{56,48},{1,9},... | collective-permute-start | bytes 3145736 | tf_op jit(solution)/shard_map/root/ppermute | solution.py:196
  73.2 3.7 %collective-permute-start.16 = (bf16[2,16,768]{2,1,0:T(8,128)(2,1)S(1)}, bf16[2,16,768]{2,1,0:T(8,128)(2,1)S(1)}, u32[]{:S(2)}, u32[]{:S(2)}) collective-permute-start(bf16[2,16,768]{2,1,0:T(8,128)(2,1)S(1)} %add_convert_fusion.11.x), channel_id=1, source_target_pairs={{34,33},{35,32},{42,41},{43,40},{50,49},{51,48},{58,57},{59,56},{6... | collective-permute-start | bytes 147464 | tf_op jit(solution)/shard_map/root/ppermute | solution.py:34
  73.9 3.1 %collective-permute-start.15 = (bf16[2,16,768]{2,1,0:T(8,128)(2,1)S(1)}, bf16[2,16,768]{2,1,0:T(8,128)(2,1)S(1)}, u32[]{:S(2)}, u32[]{:S(2)}) collective-permute-start(bf16[2,16,768]{2,1,0:T(8,128)(2,1)S(1)} %add_convert_fusion.11.x), channel_id=1, source_target_pairs={{34,32},{35,33},{42,40},{43,41},{50,48},{51,49},{58,56},{59,57},{6... | collective-permute-start | bytes 147464 | tf_op jit(solution)/shard_map/root/ppermute | solution.py:34
  76.3 0.7 collective-permute-start.17
  78.7 33.4 %collective-permute-start.25 = (bf16[512,1024]{1,0:T(8,128)(2,1)}, bf16[512,1024]{1,0:T(8,128)(2,1)}, u32[]{:S(2)}, u32[]{:S(2)}) collective-permute-start(bf16[512,1024]{1,0:T(8,128)(2,1)} %bitcast.6), channel_id=1, source_target_pairs={{64,80},{72,88},{80,64},{88,72},{96,112},{104,120},{112,96},{120,1... | collective-permute-start | bytes 3145736 | tf_op jit(solution)/shard_map/root/ppermute | solution.py:202
  80.4 14.8 %collective-permute-start.20 = (bf16[16,1536]{1,0:T(8,128)(2,1)S(1)}, bf16[16,1536]{1,0:T(8,128)(2,1)S(1)}, u32[]{:S(2)}, u32[]{:S(2)}) collective-permute-start(bf16[16,1536]{1,0:T(8,128)(2,1)S(1)} %root.16), channel_id=1, source_target_pairs={{32,16},{33,17},{40,24},{41,25},{48,0},{49,1},{56,8},{57,9},{160,1... | collective-permute-start | bytes 147464 | tf_op jit(solution)/shard_map/root/ppermute | solution.py:34
  81.7 18.4 %collective-permute-start.19 = (bf16[16,1536]{1,0:T(8,128)(2,1)S(1)}, bf16[16,1536]{1,0:T(8,128)(2,1)S(1)}, u32[]{:S(2)}, u32[]{:S(2)}) collective-permute-start(bf16[16,1536]{1,0:T(8,128)(2,1)S(1)} %root.16), channel_id=1, source_target_pairs={{32,0},{33,1},{40,8},{41,9},{48,16},{49,17},{56,24},{57,25},{160,1... | collective-permute-start | bytes 147464 | tf_op jit(solution)/shard_map/root/ppermute | solution.py:34
  103.3 4.8 %collective-permute-start.23 = (bf16[2,16,768]{2,1,0:T(8,128)(2,1)S(1)}, bf16[2,16,768]{2,1,0:T(8,128)(2,1)S(1)}, u32[]{:S(2)}, u32[]{:S(2)}) collective-permute-start(bf16[2,16,768]{2,1,0:T(8,128)(2,1)S(1)} %root.17), channel_id=1, source_target_pairs={{0,1},{1,0},{8,9},{9,8},{16,17},{17,16},{24,25},{25,24},{128,129},... | collective-permute-start | bytes 147464 | tf_op jit(solution)/shard_map/root/ppermute | solution.py:34
  105.3 2.9 %collective-permute-start.22 = (bf16[2,16,768]{2,1,0:T(8,128)(2,1)S(1)}, bf16[2,16,768]{2,1,0:T(8,128)(2,1)S(1)}, u32[]{:S(2)}, u32[]{:S(2)}) collective-permute-start(bf16[2,16,768]{2,1,0:T(8,128)(2,1)S(1)} %root.17), channel_id=1, source_target_pairs={{0,7},{1,6},{8,15},{9,14},{16,23},{17,22},{24,31},{25,30},{34,35},... | collective-permute-start | bytes 147464 | tf_op jit(solution)/shard_map/root/ppermute | solution.py:34
  106.6 3.1 %collective-permute-start.21 = (bf16[2,16,768]{2,1,0:T(8,128)(2,1)S(1)}, bf16[2,16,768]{2,1,0:T(8,128)(2,1)S(1)}, u32[]{:S(2)}, u32[]{:S(2)}) collective-permute-start(bf16[2,16,768]{2,1,0:T(8,128)(2,1)S(1)} %root.17), channel_id=1, source_target_pairs={{0,6},{1,7},{8,14},{9,15},{16,22},{17,23},{24,30},{25,31},{32,38},... | collective-permute-start | bytes 147464 | tf_op jit(solution)/shard_map/root/ppermute | solution.py:34
  109.7 2.5 collective-permute-start.24
  111.0 28.9 %collective-permute-start.29 = (bf16[512,1024]{1,0:T(8,128)(2,1)}, bf16[512,1024]{1,0:T(8,128)(2,1)S(1)}, u32[]{:S(2)}, u32[]{:S(2)}) collective-permute-start(bf16[512,1024]{1,0:T(8,128)(2,1)} %bitcast.6), channel_id=1, source_target_pairs={{64,72},{72,64},{80,88},{88,80},{96,104},{104,96},{112,120},{120,1... | collective-permute-start | bytes 3145736 | tf_op jit(solution)/shard_map/root/ppermute | solution.py:203
  133.3 8.2 %collective-permute-start.28 = (bf16[32,1024]{1,0:T(8,128)(2,1)S(1)}, bf16[32,1024]{1,0:T(8,128)(2,1)S(1)}, u32[]{:S(2)}, u32[]{:S(2)}) collective-permute-start(bf16[32,1024]{1,0:T(8,128)(2,1)S(1)} %reduce_sum.22), channel_id=1, source_target_pairs={{96,0},{97,1},{104,8},{105,9},{112,16},{113,17},{120,24},{121,25},... | collective-permute-start | bytes 196616 | tf_op jit(solution)/shard_map/coupling/ppermute | solution.py:34
  134.6 8.9 %collective-permute-start.27 = (bf16[32,1024]{1,0:T(8,128)(2,1)S(1)}, bf16[32,1024]{1,0:T(8,128)(2,1)S(1)}, u32[]{:S(2)}, u32[]{:S(2)}) collective-permute-start(bf16[32,1024]{1,0:T(8,128)(2,1)S(1)} %reduce_sum.22), channel_id=1, source_target_pairs={{64,0},{65,1},{72,8},{73,9},{80,16},{81,17},{88,24},{89,25},{98,34... | collective-permute-start | bytes 196616 | tf_op jit(solution)/shard_map/coupling/ppermute | solution.py:34
  135.9 8.3 %collective-permute-start.26 = (bf16[32,1024]{1,0:T(8,128)(2,1)S(1)}, bf16[32,1024]{1,0:T(8,128)(2,1)S(1)}, u32[]{:S(2)}, u32[]{:S(2)}) collective-permute-start(bf16[32,1024]{1,0:T(8,128)(2,1)S(1)} %reduce_sum.22), channel_id=1, source_target_pairs={{32,0},{33,1},{40,8},{41,9},{48,16},{49,17},{56,24},{57,25},{66,34... | collective-permute-start | bytes 196616 | tf_op jit(solution)/shard_map/coupling/ppermute | solution.py:34
  137.2 10.5 %collective-permute-start.30 = (bf16[512,1024]{1,0:T(8,128)(2,1)}, bf16[512,1024]{1,0:T(8,128)(2,1)S(1)}, u32[]{:S(2)}, u32[]{:S(2)}) collective-permute-start(bf16[512,1024]{1,0:T(8,128)(2,1)} %collective-permute-done.25), channel_id=1, source_target_pairs={{64,72},{72,64},{80,88},{88,80},{96,104},{104,96},{112,120},{120,1... | collective-permute-start | bytes 3145736 | tf_op jit(solution)/shard_map/coupling/ppermute | solution.py:220
  148.6 1.4 collective-permute-start.32
  152.4 1.5 collective-permute-start.33
  153.1 3.8 %collective-permute-start.34 = (bf16[32,2048]{1,0:T(8,128)(2,1)S(1)}, bf16[32,2048]{1,0:T(8,128)(2,1)S(1)}, u32[]{:S(2)}, u32[]{:S(2)}) collective-permute-start(bf16[32,2048]{1,0:T(8,128)(2,1)S(1)} %add_convert_fusion.6), channel_id=1, source_target_pairs={{100,98},{101,99},{108,106},{109,107},{116,114},{117,115},{124,122... | collective-permute-start | bytes 393224 | tf_op jit(solution)/shard_map/child/ppermute | solution.py:34
  157.9 3.6 %collective-permute-start.37 = (bf16[32,2048]{1,0:T(8,128)(2,1)S(1)}, bf16[32,2048]{1,0:T(8,128)(2,1)S(1)}, u32[]{:S(2)}, u32[]{:S(2)}) collective-permute-start(bf16[32,2048]{1,0:T(8,128)(2,1)S(1)} %add_convert_fusion.5), channel_id=1, source_target_pairs={{68,67},{69,66},{76,75},{77,74},{84,83},{85,82},{92,91},{93,90},{1... | collective-permute-start | bytes 393224 | tf_op jit(solution)/shard_map/child/ppermute | solution.py:34
  158.6 2.9 %collective-permute-start.36 = (bf16[32,2048]{1,0:T(8,128)(2,1)S(1)}, bf16[32,2048]{1,0:T(8,128)(2,1)S(1)}, u32[]{:S(2)}, u32[]{:S(2)}) collective-permute-start(bf16[32,2048]{1,0:T(8,128)(2,1)S(1)} %add_convert_fusion.5), channel_id=1, source_target_pairs={{68,66},{69,67},{76,74},{77,75},{84,82},{85,83},{92,90},{93,91},{9... | collective-permute-start | bytes 393224 | tf_op jit(solution)/shard_map/child/ppermute | solution.py:34
  160.8 1.6 collective-permute-start.35
  163.9 1.4 collective-permute-start.38
  164.6 3.6 %collective-permute-start.39 = (bf16[32,2048]{1,0:T(8,128)(2,1)S(1)}, bf16[32,2048]{1,0:T(8,128)(2,1)S(1)}, u32[]{:S(2)}, u32[]{:S(2)}) collective-permute-start(bf16[32,2048]{1,0:T(8,128)(2,1)S(1)} %add_convert_fusion.4), channel_id=1, source_target_pairs={{66,64},{67,65},{74,72},{75,73},{82,80},{83,81},{90,88},{91,89},{1... | collective-permute-start | bytes 393224 | tf_op jit(solution)/shard_map/child/ppermute | solution.py:34
  169.2 3.6 %collective-permute-start.42 = (bf16[32,2048]{1,0:T(8,128)(2,1)S(1)}, bf16[32,2048]{1,0:T(8,128)(2,1)S(1)}, u32[]{:S(2)}, u32[]{:S(2)}) collective-permute-start(bf16[32,2048]{1,0:T(8,128)(2,1)S(1)} %add_convert_fusion.3), channel_id=1, source_target_pairs={{34,33},{35,32},{42,41},{43,40},{50,49},{51,48},{58,57},{59,56},{6... | collective-permute-start | bytes 393224 | tf_op jit(solution)/shard_map/child/ppermute | solution.py:34
  169.9 2.9 %collective-permute-start.41 = (bf16[32,2048]{1,0:T(8,128)(2,1)S(1)}, bf16[32,2048]{1,0:T(8,128)(2,1)S(1)}, u32[]{:S(2)}, u32[]{:S(2)}) collective-permute-start(bf16[32,2048]{1,0:T(8,128)(2,1)S(1)} %add_convert_fusion.3), channel_id=1, source_target_pairs={{34,32},{35,33},{42,40},{43,41},{50,48},{51,49},{58,56},{59,57},{6... | collective-permute-start | bytes 393224 | tf_op jit(solution)/shard_map/child/ppermute | solution.py:34
  172.1 2.9 %collective-permute-start.40 = (bf16[32,1024]{1,0:T(8,128)(2,1)S(1)}, bf16[32,1024]{1,0:T(8,128)(2,1)S(1)}, u32[]{:S(2)}, u32[]{:S(2)}) collective-permute-start(bf16[32,1024]{1,0:T(8,128)(2,1)S(1)} %fusion.10), channel_id=1, source_target_pairs={{64,32},{65,33},{72,40},{73,41},{80,48},{81,49},{88,56},{89,57},{1... | collective-permute-start | bytes 196616 | tf_op jit(solution)/shard_map/child/ppermute | solution.py:34
  175.2 44.1 %collective-permute-start.43 = (bf16[32,1024]{1,0:T(8,128)(2,1)S(1)}, bf16[32,1024]{1,0:T(8,128)(2,1)S(1)}, u32[]{:S(2)}, u32[]{:S(2)}) collective-permute-start(bf16[32,1024]{1,0:T(8,128)(2,1)S(1)} %add_convert_fusion.7), channel_id=1, source_target_pairs={{32,0},{33,1},{40,8},{41,9},{48,16},{49,17},{56,24},{57,25},{160,1... | collective-permute-start | bytes 196616 | tf_op jit(solution)/shard_map/child/ppermute | solution.py:34
  222.4 5.7 %collective-permute-start.46 = (bf16[32,2048]{1,0:T(8,128)(2,1)S(1)}, bf16[32,2048]{1,0:T(8,128)(2,1)S(1)}, u32[]{:S(2)}, u32[]{:S(2)}) collective-permute-start(bf16[32,2048]{1,0:T(8,128)(2,1)S(1)} %maximum_select_fusion.3), channel_id=1, source_target_pairs={{0,1},{1,0},{8,9},{9,8},{16,17},{17,16},{24,25},{25,24},{128,129},... | collective-permute-start | bytes 393224 | tf_op jit(solution)/shard_map/child/ppermute | solution.py:34
  224.3 3.8 %collective-permute-start.45 = (bf16[32,2048]{1,0:T(8,128)(2,1)S(1)}, bf16[32,2048]{1,0:T(8,128)(2,1)S(1)}, u32[]{:S(2)}, u32[]{:S(2)}) collective-permute-start(bf16[32,2048]{1,0:T(8,128)(2,1)S(1)} %maximum_select_fusion.3), channel_id=1, source_target_pairs={{0,7},{1,6},{8,15},{9,14},{16,23},{17,22},{24,31},{25,30},{34,35},... | collective-permute-start | bytes 393224 | tf_op jit(solution)/shard_map/child/ppermute | solution.py:34
  225.6 10.5 %collective-permute-start.44 = (bf16[32,2048]{1,0:T(8,128)(2,1)S(1)}, bf16[32,2048]{1,0:T(8,128)(2,1)S(1)}, u32[]{:S(2)}, u32[]{:S(2)}) collective-permute-start(bf16[32,2048]{1,0:T(8,128)(2,1)S(1)} %maximum_select_fusion.3), channel_id=1, source_target_pairs={{0,6},{1,7},{8,14},{9,15},{16,22},{17,23},{24,30},{25,31},{32,38},... | collective-permute-start | bytes 393224 | tf_op jit(solution)/shard_map/child/ppermute | solution.py:34
  236.2 3.2 %collective-permute-start.47 = (bf16[32,2048]{1,0:T(8,128)(2,1)S(1)}, bf16[32,2048]{1,0:T(8,128)(2,1)S(1)}, u32[]{:S(2)}, u32[]{:S(2)}) collective-permute-start(bf16[32,2048]{1,0:T(8,128)(2,1)S(1)} %add_convert_fusion.1), channel_id=1, source_target_pairs={{0,2},{1,3},{8,10},{9,11},{16,18},{17,19},{24,26},{25,27},{6,4},{7... | collective-permute-start | bytes 393224 | tf_op jit(solution)/shard_map/child/ppermute | solution.py:34
  (15 other events, 181.7 us)

commit v7 on v6

--- a/solution.py
+++ b/solution.py
@@ -66,7 +66,7 @@
         out_specs=whole,
         out_shape=jax.ShapeDtypeStruct((probes, cols), BF16),
         scratch_shapes=[pltpu.VMEM((probes, cols), F32)],
-        compiler_params=pltpu.CompilerParams(vmem_limit_bytes=8 * 2**20),
+        compiler_params=pltpu.CompilerParams(vmem_limit_bytes=56 * 2**20),
         cost_estimate=pl.CostEstimate(
             flops=4 * probes * rows * cols, bytes_accessed=4 * rows * cols, transcendentals=0
         ),
@@ -96,7 +96,7 @@
         out_specs=part,
         out_shape=jax.ShapeDtypeStruct(current.shape, BF16),
         scratch_shapes=[pltpu.VMEM((probes, cols), BF16)],
-        compiler_params=pltpu.CompilerParams(vmem_limit_bytes=8 * 2**20),
+        compiler_params=pltpu.CompilerParams(vmem_limit_bytes=56 * 2**20),
         cost_estimate=pl.CostEstimate(
             flops=4 * probes * rows * cols, bytes_accessed=4 * rows * cols, transcendentals=0
         ),

time: 251 us -> 280 us (1.12)
  Pallas kernels: 14.6 us -> 40.5 us
  other arithmetic: 7.79 us -> 19.5 us
  local copies, waits for them, and re-layouts: 12.9 us -> 8.04 us
    pallas_call x5, Pallas kernels: 8.29 us -> 21.6 us  [root_terms(): pl.pallas_call(terms_kernel, grid=(steps,), in_specs=[pl.BlockSpec(memory...]
    pallas_call x4, Pallas kernels: 6.36 us -> 19 us  [root_pieces(): pl.pallas_call(pieces_kernel, grid=(steps,), in_specs=[pl.BlockSpec(memor...]
    ppermute x2, waiting for transfers between devices: 8.32 us -> 0.01 us  [move_children(): moved[half, 2] = lax.ppermute(here, 'row', rows_of(half, 2))]
    unnamed x29 -> x35, local copies, waits for them, and re-layouts: 10.4 us -> 3.54 us
    ppermute x40, waiting for transfers between devices: 76 us -> 82.5 us  [send(): return lax.ppermute(value, GRID, pairs)]
    convert_element_type x6, other arithmetic: 0.23 us -> 4.49 us  [sweep(): current = (current.astype(F32) + received).astype(BF16)]
  transfers between devices with their start and end apart: 49 -> 49, of which waited for: 13 -> 11; matrix products, arithmetic and copies ran while one was open for 9% -> 13% of each run, Pallas kernels for 6% -> 15%
where the time goes in v7:
time: 280 us; the launch traced here: 278 us
  waiting for transfers between devices  91.5 us (33%)
  starting transfers between devices  65.4 us (23%)
  Pallas kernels  40.5 us (14%)
  blocking collectives  27 us (10%)
  matrix products  23.9 us (9%)
  other arithmetic  19.5 us (7%)
  local copies, waits for them, and re-layouts  8.04 us (3%)
    ppermute x40, waiting for transfers between devices, send(): return lax.ppermute(value, GRID, pairs)  82.5 us
    ppermute x40, starting transfers between devices, send(): return lax.ppermute(value, GRID, pairs)  36.8 us
    pallas_call x5, Pallas kernels, root_terms(): pl.pallas_call(terms_kernel, grid=(steps,), in_specs=[pl.BlockSpec(memory...  21.6 us
    pallas_call x4, Pallas kernels, root_pieces(): pl.pallas_call(pieces_kernel, grid=(steps,), in_specs=[pl.BlockSpec(memor...  19 us
    dot_general x21, matrix products, dot(): return jnp.dot(a, b, preferred_element_type=F32)  12.3 us
    dot_general x16, matrix products, dot_t(): lax.dot_general(a, b, (((1,), (1,)), ((), ())), preferred_element_type=F32)  11.7 us
    all_to_all x1, blocking collectives, per_device(): lax.all_to_all(shared, ('gz', 'row'), 0, 0, tiled=True, axis_index_groups...  10.5 us
    all_to_all x1, waiting for transfers between devices, per_device(): lax.all_to_all(pieces.reshape(layers * ROWS, 12, lanes), ('gz', 'row'), 0...  9 us
  transfers between devices with their start and end apart: 49, of which 11 were waited for; matrix products, arithmetic and copies ran while one was open for 13% of the time, Pallas kernels for 15%

profile of v7, /device:TPU:1, one launch (start us, length us, event | category | flops | bytes accessed | tf_op | source)
XLA Modules:
  0.0 277.7 jit_solution(17679191788863850002)
XLA Ops:
  0.6 8.9 %collective-permute-start.1 = (bf16[768,1536]{1,0:T(8,128)(2,1)}, bf16[768,1536]{1,0:T(8,128)(2,1)S(1)}, u32[]{:S(2)}, u32[]{:S(2)}) collective-permute-start(bf16[768,1536]{1,0:T(8,128)(2,1)} %own.17), channel_id=1, source_target_pairs={{0,8},{8,0},{16,24},{24,16},{32,40},{40,32},{48,56},{56,48},{64,72... | collective-permute-start | bytes 7077896 | tf_op jit(solution)/shard_map/mask/ppermute | solution.py:168
  11.1 4.9 %all-to-all-start = ((bf16[64,12,128]{2,1,0:T(8,128)(2,1)}), bf16[64,12,128]{2,1,0:T(8,128)(2,1)S(1)}, u32[]{:S(2)}, u32[]{:S(2)}) async-start(bf16[64,12,128]{2,1,0:T(8,128)(2,1)} %bitcast.91), calls=%async_computation | async-start | bytes 524288 | tf_op jit(solution)/shard_map/rhs/all_to_all | solution.py:179
  16.0 2.4 collective-permute-start
  19.0 9.0 %all-to-all-done = bf16[64,12,128]{2,1,0:T(8,128)(2,1)S(1)} async-done(((bf16[64,12,128]{2,1,0:T(8,128)(2,1)}), bf16[64,12,128]{2,1,0:T(8,128)(2,1)S(1)}, u32[]{:S(2)}, u32[]{:S(2)}) %all-to-all-start) | async-done | bytes 196640 | tf_op jit(solution)/shard_map/rhs/all_to_all | solution.py:179
  30.1 4.9 %root.9 = bf16[2,16,768]{2,1,0:T(8,128)(2,1)} custom-call(s32[1]{0:T(128)} %bitcast.5.solving, f32[16,1536]{1,0:T(8,128)} %copy_bitcast_fusion.1.rhs, bf16[16,1536]{1,0:T(8,128)(2,1)} %broadcast_in_dim.36.first.second, bf16[16,1536]{1,0:T(8,128)(2,1)} %broadcast_in_dim.36.first.second, bf16[768,1536]{1,0:T(8,128)(2,1)} %own.17, bf16[768,1536]{1,0:T(8,128)(2,1)} %copy-done.1, ...), custom_call_target="tpu_custom_call" | custom-call | flops 75497472 | bytes 4718592 | tf_op jit(solution)/shard_map/root/pallas_call | solution.py:92
  36.9 3.1 %collective-permute-start.11 = (bf16[512,1024]{1,0:T(8,128)(2,1)}, bf16[512,1024]{1,0:T(8,128)(2,1)S(1)}, u32[]{:S(2)}, u32[]{:S(2)}) collective-permute-start(bf16[512,1024]{1,0:T(8,128)(2,1)} %bitcast.6), channel_id=1, source_target_pairs={{0,16},{8,24},{16,0},{24,8},{32,48},{40,56},{48,32},{56,40},{1,17}... | collective-permute-start | bytes 3145736 | tf_op jit(solution)/shard_map/root/ppermute | solution.py:202
  40.0 2.5 collective-permute-start.10
  42.5 1.4 add_convert_fusion.14.x.current
  44.6 4.3 %root.10 = bf16[16,1536]{1,0:T(8,128)(2,1)} custom-call(f32[3,6]{1,0:T(4,128)} %select_convert_fusion.1.keep_own, f32[3,6]{1,0:T(4,128)} %select_convert_fusion.keep_other, bf16[2,16,768]{2,1,0:T(8,128)(2,1)} %add_convert_fusion.14.x.current, bf16[768,1536]{1,0:T(8,128)(2,1)} %own.17, bf16[768,1536]{1,0:T(8,128)(2,1)} %copy-done.1, ...), custom_call_target="tpu_custom_call" | custom-call | flops 75497472 | bytes 4718592 | tf_op jit(solution)/shard_map/root/pallas_call | solution.py:59
  51.6 4.7 %root.11 = bf16[2,16,768]{2,1,0:T(8,128)(2,1)} custom-call(s32[1]{0:T(128)} %bitcast.4.solving, f32[16,1536]{1,0:T(8,128)} %copy_bitcast_fusion.1.rhs, bf16[16,1536]{1,0:T(8,128)(2,1)} %copy-done.5, bf16[16,1536]{1,0:T(8,128)(2,1)} %copy-done.15, bf16[768,1536]{1,0:T(8,128)(2,1)} %own.17, bf16[768,1536]{1,0:T(8,128)(2,1)} %copy-done.1, ...), custom_call_target="tpu_custom_call" | custom-call | flops 75497472 | bytes 4718592 | tf_op jit(solution)/shard_map/root/pallas_call | solution.py:92
  58.5 1.4 convert_element_type.276.carried
  59.9 4.3 %root.12 = bf16[16,1536]{1,0:T(8,128)(2,1)} custom-call(f32[3,6]{1,0:T(4,128)} %select_convert_fusion.1.keep_own, f32[3,6]{1,0:T(4,128)} %select_convert_fusion.keep_other, bf16[2,16,768]{2,1,0:T(8,128)(2,1)} %copy-done.8, bf16[768,1536]{1,0:T(8,128)(2,1)} %own.17, bf16[768,1536]{1,0:T(8,128)(2,1)} %copy-done.1, f32[16,1536]{1,0:T(8,128)} %convert_element_type.276.carried), custom_call_target="tpu_custom_call" | custom-call | flops 75497472 | bytes 4718592 | tf_op jit(solution)/shard_map/root/pallas_call | solution.py:59
  64.9 1.4 add_convert_fusion.12.x.current
  67.0 4.3 %root.13 = bf16[16,1536]{1,0:T(8,128)(2,1)} custom-call(f32[3,6]{1,0:T(4,128)} %select_convert_fusion.1.keep_own, f32[3,6]{1,0:T(4,128)} %select_convert_fusion.keep_other, bf16[2,16,768]{2,1,0:T(8,128)(2,1)} %add_convert_fusion.12.x.current, bf16[768,1536]{1,0:T(8,128)(2,1)} %own.17, bf16[768,1536]{1,0:T(8,128)(2,1)} %copy-done.1, ...), custom_call_target="tpu_custom_call" | custom-call | flops 75497472 | bytes 4718592 | tf_op jit(solution)/shard_map/root/pallas_call | solution.py:59
  73.4 1.9 collective-permute-start.18
  75.9 4.7 %root.14 = bf16[2,16,768]{2,1,0:T(8,128)(2,1)} custom-call(s32[1]{0:T(128)} %bitcast.3.solving, f32[16,1536]{1,0:T(8,128)} %copy_bitcast_fusion.1.rhs, bf16[16,1536]{1,0:T(8,128)(2,1)} %copy-done.12, bf16[16,1536]{1,0:T(8,128)(2,1)} %copy-done.13, bf16[768,1536]{1,0:T(8,128)(2,1)} %own.17, bf16[768,1536]{1,0:T(8,128)(2,1)} %copy-done.1, ...), custom_call_target="tpu_custom_call" | custom-call | flops 75497472 | bytes 4718592 | tf_op jit(solution)/shard_map/root/pallas_call | solution.py:92
  82.8 1.5 convert_add_fusion.3.carried
  84.3 4.3 %root.15 = bf16[16,1536]{1,0:T(8,128)(2,1)} custom-call(f32[3,6]{1,0:T(4,128)} %select_convert_fusion.1.keep_own, f32[3,6]{1,0:T(4,128)} %select_convert_fusion.keep_other, bf16[2,16,768]{2,1,0:T(8,128)(2,1)} %copy-done.7, bf16[768,1536]{1,0:T(8,128)(2,1)} %own.17, bf16[768,1536]{1,0:T(8,128)(2,1)} %copy-done.1, f32[16,1536]{1,0:T(8,128)} %convert_add_fusion.3.carried), custom_call_target="tpu_custom_call" | custom-call | flops 75497472 | bytes 4718592 | tf_op jit(solution)/shard_map/root/pallas_call | solution.py:59
  89.3 1.4 add_convert_fusion.10.x.current
  91.4 4.3 %root.16 = bf16[16,1536]{1,0:T(8,128)(2,1)} custom-call(f32[3,6]{1,0:T(4,128)} %select_convert_fusion.1.keep_own, f32[3,6]{1,0:T(4,128)} %select_convert_fusion.keep_other, bf16[2,16,768]{2,1,0:T(8,128)(2,1)} %add_convert_fusion.10.x.current, bf16[768,1536]{1,0:T(8,128)(2,1)} %own.17, bf16[768,1536]{1,0:T(8,128)(2,1)} %copy-done.1, ...), custom_call_target="tpu_custom_call" | custom-call | flops 75497472 | bytes 4718592 | tf_op jit(solution)/shard_map/root/pallas_call | solution.py:59
  96.7 1.6 collective-permute-start.25
  100.9 14.0 %collective-permute-done.20.second = bf16[16,1536]{1,0:T(8,128)(2,1)S(1)} collective-permute-done((bf16[16,1536]{1,0:T(8,128)(2,1)}, bf16[16,1536]{1,0:T(8,128)(2,1)S(1)}, u32[]{:S(2)}, u32[]{:S(2)}) %collective-permute-start.20) | collective-permute-done | bytes 49184 | tf_op jit(solution)/shard_map/root/ppermute | solution.py:34
  115.0 5.6 %collective-permute-done.19.first = bf16[16,1536]{1,0:T(8,128)(2,1)S(1)} collective-permute-done((bf16[16,1536]{1,0:T(8,128)(2,1)}, bf16[16,1536]{1,0:T(8,128)(2,1)S(1)}, u32[]{:S(2)}, u32[]{:S(2)}) %collective-permute-start.19) | collective-permute-done | bytes 49184 | tf_op jit(solution)/shard_map/root/ppermute | solution.py:34
  121.2 4.7 %root.17 = bf16[2,16,768]{2,1,0:T(8,128)(2,1)} custom-call(s32[1]{0:T(128)} %bitcast.solving, f32[16,1536]{1,0:T(8,128)} %copy_bitcast_fusion.1.rhs, bf16[16,1536]{1,0:T(8,128)(2,1)} %copy-done.16, bf16[16,1536]{1,0:T(8,128)(2,1)} %copy-done.14, bf16[768,1536]{1,0:T(8,128)(2,1)} %own.17, bf16[768,1536]{1,0:T(8,128)(2,1)} %copy-done.1, ...), custom_call_target="tpu_custom_call" | custom-call | flops 75497472 | bytes 4718592 | tf_op jit(solution)/shard_map/root/pallas_call | solution.py:92
  125.9 1.9 collective-permute-start.23
  130.9 2.6 collective-permute-done.21
  135.7 1.7 collective-permute-start.29
  137.4 10.5 %all_to_all.29 = bf16[8,16,768]{2,1,0:T(8,128)(2,1)S(1)} all-to-all(bf16[8,16,768]{2,1,0:T(8,128)(2,1)S(1)} %bitcast.93), channel_id=1, replica_groups={{0,8,128,136,256,264,384,392},{16,24,144,152,272,280,400,408},{32,40,16..., dimensions={0} | all-to-all | bytes 393216 | tf_op jit(solution)/shard_map/coupling/all_to_all | solution.py:225
  148.3 8.3 %all_to_all.30 = bf16[4,32,1024]{2,1,0:T(8,128)(2,1)S(1)} all-to-all(bf16[4,32,1024]{2,1,0:T(8,128)(2,1)S(1)} %bitcast.92), channel_id=1, replica_groups={{0,8,16,24},{32,40,48,56},{64,72,80,88},{96,104,112,120},{1,9,17,25},{3..., dimensions={0} | all-to-all | bytes 524288 | tf_op jit(solution)/shard_map/coupling/all_to_all | solution.py:229
  160.6 1.7 collective-permute-start.30
  162.3 1.6 add.203
  163.9 1.6 add.202
  165.6 1.3 collective-permute-done.27
  168.6 1.6 convolution_convert_fusion.16
  171.1 1.6 add.204
  174.9 1.5 fusion.53
  179.9 1.6 convolution_convert_fusion.12
  183.9 1.5 fusion.12
  187.0 1.5 fusion.11
  191.2 1.6 convolution_convert_fusion.8
  195.2 1.5 fusion.10
  198.0 1.5 fusion.26
  201.2 46.5 %collective-permute-done.43 = bf16[32,1024]{1,0:T(8,128)(2,1)S(1)} collective-permute-done((bf16[32,1024]{1,0:T(8,128)(2,1)S(1)}, bf16[32,1024]{1,0:T(8,128)(2,1)S(1)}, u32[]{:S(2)}, u32[]{:S(2)}) %collective-permute-start.43) | collective-permute-done | bytes 65568 | tf_op jit(solution)/shard_map/child/ppermute | solution.py:34
  248.9 1.6 convolution_convert_fusion.4
  250.6 1.9 collective-permute-start.46
  256.3 8.1 %collective-permute-done.44 = bf16[32,2048]{1,0:T(8,128)(2,1)S(1)} collective-permute-done((bf16[32,2048]{1,0:T(8,128)(2,1)S(1)}, bf16[32,2048]{1,0:T(8,128)(2,1)S(1)}, u32[]{:S(2)}, u32[]{:S(2)}) %collective-permute-start.44) | collective-permute-done | bytes 131104 | tf_op jit(solution)/shard_map/child/ppermute | solution.py:34
  265.8 1.9 collective-permute-done.47
  268.9 8.1 %all_to_all.31 = bf16[4,32,512]{2,1,0:T(8,128)(2,1)S(1)} all-to-all(bf16[4,32,512]{2,1,0:T(8,128)(2,1)S(1)} %bitcast.94), channel_id=1, replica_groups={{0,8,16,24},{32,40,48,56},{64,72,80,88},{96,104,112,120},{1,9,17,25},{3..., dimensions={0} | all-to-all | bytes 262144 | tf_op jit(solution)/shard_map/child/all_to_all | solution.py:260
  (180 shorter events, 60.7 us)
Async XLA Ops:
  0.6 28.0 %collective-permute-start.1 = (bf16[768,1536]{1,0:T(8,128)(2,1)}, bf16[768,1536]{1,0:T(8,128)(2,1)S(1)}, u32[]{:S(2)}, u32[]{:S(2)}) collective-permute-start(bf16[768,1536]{1,0:T(8,128)(2,1)} %own.17), channel_id=1, source_target_pairs={{0,8},{8,0},{16,24},{24,16},{32,40},{40,32},{48,56},{56,48},{64,72... | collective-permute-start | bytes 7077896 | tf_op jit(solution)/shard_map/mask/ppermute | solution.py:168
  11.1 16.9 %all-to-all-start = ((bf16[64,12,128]{2,1,0:T(8,128)(2,1)}), bf16[64,12,128]{2,1,0:T(8,128)(2,1)S(1)}, u32[]{:S(2)}, u32[]{:S(2)}) async-start(bf16[64,12,128]{2,1,0:T(8,128)(2,1)} %bitcast.91), calls=%async_computation | async-start | bytes 524288 | tf_op jit(solution)/shard_map/rhs/all_to_all | solution.py:179
  16.0 20.3 %collective-permute-start = (s32[3,6]{1,0:T(4,128)}, s32[3,6]{1,0:T(4,128)S(1)}, u32[]{:S(2)}, u32[]{:S(2)}) collective-permute-start(s32[3,6]{1,0:T(4,128)} %param.8), channel_id=1, source_target_pairs={{0,8},{8,0},{16,24},{24,16},{32,40},{40,32},{48,56},{56,48},{64,72... | collective-permute-start | bytes 224 | tf_op jit(solution)/shard_map/mask/ppermute | solution.py:169
  35.0 7.5 %collective-permute-start.3 = (bf16[2,16,768]{2,1,0:T(8,128)(2,1)}, bf16[2,16,768]{2,1,0:T(8,128)(2,1)S(1)}, u32[]{:S(2)}, u32[]{:S(2)}) collective-permute-start(bf16[2,16,768]{2,1,0:T(8,128)(2,1)} %root.9), channel_id=1, source_target_pairs={{102,101},{103,100},{110,109},{111,108},{118,117},{119,116},{126,1... | collective-permute-start | bytes 147464 | tf_op jit(solution)/shard_map/root/ppermute | solution.py:34
  35.6 6.9 %collective-permute-start.2 = (bf16[2,16,768]{2,1,0:T(8,128)(2,1)}, bf16[2,16,768]{2,1,0:T(8,128)(2,1)S(1)}, u32[]{:S(2)}, u32[]{:S(2)}) collective-permute-start(bf16[2,16,768]{2,1,0:T(8,128)(2,1)} %root.9), channel_id=1, source_target_pairs={{102,100},{103,101},{110,108},{111,109},{118,116},{119,117},{126,1... | collective-permute-start | bytes 147464 | tf_op jit(solution)/shard_map/root/ppermute | solution.py:34
  36.9 34.4 %collective-permute-start.11 = (bf16[512,1024]{1,0:T(8,128)(2,1)}, bf16[512,1024]{1,0:T(8,128)(2,1)S(1)}, u32[]{:S(2)}, u32[]{:S(2)}) collective-permute-start(bf16[512,1024]{1,0:T(8,128)(2,1)} %bitcast.6), channel_id=1, source_target_pairs={{0,16},{8,24},{16,0},{24,8},{32,48},{40,56},{48,32},{56,40},{1,17}... | collective-permute-start | bytes 3145736 | tf_op jit(solution)/shard_map/root/ppermute | solution.py:202
  40.0 31.3 %collective-permute-start.10 = (bf16[512,1024]{1,0:T(8,128)(2,1)}, bf16[512,1024]{1,0:T(8,128)(2,1)S(1)}, u32[]{:S(2)}, u32[]{:S(2)}) collective-permute-start(bf16[512,1024]{1,0:T(8,128)(2,1)} %bitcast.6), channel_id=1, source_target_pairs={{0,8},{8,0},{16,24},{24,16},{32,40},{40,32},{48,56},{56,48},{1,9},... | collective-permute-start | bytes 3145736 | tf_op jit(solution)/shard_map/root/ppermute | solution.py:203
  48.9 2.0 collective-permute-start.5
  49.6 1.4 collective-permute-start.4
  50.3 6.0 %collective-permute-start.6 = (bf16[2,16,768]{2,1,0:T(8,128)(2,1)S(1)}, bf16[2,16,768]{2,1,0:T(8,128)(2,1)S(1)}, u32[]{:S(2)}, u32[]{:S(2)}) collective-permute-start(bf16[2,16,768]{2,1,0:T(8,128)(2,1)S(1)} %copy-done.11), channel_id=1, source_target_pairs={{100,98},{101,99},{108,106},{109,107},{116,114},{117,115},{124,122... | collective-permute-start | bytes 147464 | tf_op jit(solution)/shard_map/root/ppermute | solution.py:34
  57.1 7.8 %collective-permute-start.8 = (bf16[2,16,768]{2,1,0:T(8,128)(2,1)S(1)}, bf16[2,16,768]{2,1,0:T(8,128)(2,1)S(1)}, u32[]{:S(2)}, u32[]{:S(2)}) collective-permute-start(bf16[2,16,768]{2,1,0:T(8,128)(2,1)S(1)} %add_convert_fusion.13.x), channel_id=1, source_target_pairs={{68,67},{69,66},{76,75},{77,74},{84,83},{85,82},{92,91},{93,90},{1... | collective-permute-start | bytes 147464 | tf_op jit(solution)/shard_map/root/ppermute | solution.py:34
  57.8 7.1 %collective-permute-start.7 = (bf16[2,16,768]{2,1,0:T(8,128)(2,1)S(1)}, bf16[2,16,768]{2,1,0:T(8,128)(2,1)S(1)}, u32[]{:S(2)}, u32[]{:S(2)}) collective-permute-start(bf16[2,16,768]{2,1,0:T(8,128)(2,1)S(1)} %add_convert_fusion.13.x), channel_id=1, source_target_pairs={{68,66},{69,67},{76,74},{77,75},{84,82},{85,83},{92,90},{93,91},{9... | collective-permute-start | bytes 147464 | tf_op jit(solution)/shard_map/root/ppermute | solution.py:34
  64.2 2.1 collective-permute-start.9
  71.3 4.0 %collective-permute-start.13 = (bf16[16,1536]{1,0:T(8,128)(2,1)}, bf16[16,1536]{1,0:T(8,128)(2,1)S(1)}, u32[]{:S(2)}, u32[]{:S(2)}) collective-permute-start(bf16[16,1536]{1,0:T(8,128)(2,1)} %root.13), channel_id=1, source_target_pairs={{66,50},{67,51},{74,58},{75,59},{82,34},{83,35},{90,42},{91,43},{1... | collective-permute-start | bytes 147464 | tf_op jit(solution)/shard_map/root/ppermute | solution.py:34
  72.0 3.3 %collective-permute-start.12 = (bf16[16,1536]{1,0:T(8,128)(2,1)}, bf16[16,1536]{1,0:T(8,128)(2,1)S(1)}, u32[]{:S(2)}, u32[]{:S(2)}) collective-permute-start(bf16[16,1536]{1,0:T(8,128)(2,1)} %root.13), channel_id=1, source_target_pairs={{66,34},{67,35},{74,42},{75,43},{82,50},{83,51},{90,58},{91,59},{9... | collective-permute-start | bytes 147464 | tf_op jit(solution)/shard_map/root/ppermute | solution.py:34
  72.7 8.0 %collective-permute-start.14 = (bf16[2,16,768]{2,1,0:T(8,128)(2,1)S(1)}, bf16[2,16,768]{2,1,0:T(8,128)(2,1)S(1)}, u32[]{:S(2)}, u32[]{:S(2)}) collective-permute-start(bf16[2,16,768]{2,1,0:T(8,128)(2,1)S(1)} %copy-done.10), channel_id=1, source_target_pairs={{66,64},{67,65},{74,72},{75,73},{82,80},{83,81},{90,88},{91,89},{1... | collective-permute-start | bytes 147464 | tf_op jit(solution)/shard_map/root/ppermute | solution.py:34
  73.4 22.3 %collective-permute-start.18 = (bf16[512,1024]{1,0:T(8,128)(2,1)S(1)}, bf16[512,1024]{1,0:T(8,128)(2,1)S(1)}, u32[]{:S(2)}, u32[]{:S(2)}) collective-permute-start(bf16[512,1024]{1,0:T(8,128)(2,1)S(1)} %collective-permute-done.11), channel_id=1, source_target_pairs={{0,8},{8,0},{16,24},{24,16},{32,40},{40,32},{48,56},{56,48},{1,9},... | collective-permute-start | bytes 3145736 | tf_op jit(solution)/shard_map/root/ppermute | solution.py:196
  81.5 7.8 %collective-permute-start.16 = (bf16[2,16,768]{2,1,0:T(8,128)(2,1)S(1)}, bf16[2,16,768]{2,1,0:T(8,128)(2,1)S(1)}, u32[]{:S(2)}, u32[]{:S(2)}) collective-permute-start(bf16[2,16,768]{2,1,0:T(8,128)(2,1)S(1)} %add_convert_fusion.11.x), channel_id=1, source_target_pairs={{34,33},{35,32},{42,41},{43,40},{50,49},{51,48},{58,57},{59,56},{6... | collective-permute-start | bytes 147464 | tf_op jit(solution)/shard_map/root/ppermute | solution.py:34
  82.1 7.1 %collective-permute-start.15 = (bf16[2,16,768]{2,1,0:T(8,128)(2,1)S(1)}, bf16[2,16,768]{2,1,0:T(8,128)(2,1)S(1)}, u32[]{:S(2)}, u32[]{:S(2)}) collective-permute-start(bf16[2,16,768]{2,1,0:T(8,128)(2,1)S(1)} %add_convert_fusion.11.x), channel_id=1, source_target_pairs={{34,32},{35,33},{42,40},{43,41},{50,48},{51,49},{58,56},{59,57},{6... | collective-permute-start | bytes 147464 | tf_op jit(solution)/shard_map/root/ppermute | solution.py:34
  88.6 2.1 collective-permute-start.17
  96.7 40.6 %collective-permute-start.25 = (bf16[512,1024]{1,0:T(8,128)(2,1)}, bf16[512,1024]{1,0:T(8,128)(2,1)}, u32[]{:S(2)}, u32[]{:S(2)}) collective-permute-start(bf16[512,1024]{1,0:T(8,128)(2,1)} %bitcast.6), channel_id=1, source_target_pairs={{64,80},{72,88},{80,64},{88,72},{96,112},{104,120},{112,96},{120,1... | collective-permute-start | bytes 3145736 | tf_op jit(solution)/shard_map/root/ppermute | solution.py:202
  98.3 16.6 %collective-permute-start.20 = (bf16[16,1536]{1,0:T(8,128)(2,1)}, bf16[16,1536]{1,0:T(8,128)(2,1)S(1)}, u32[]{:S(2)}, u32[]{:S(2)}) collective-permute-start(bf16[16,1536]{1,0:T(8,128)(2,1)} %root.16), channel_id=1, source_target_pairs={{32,16},{33,17},{40,24},{41,25},{48,0},{49,1},{56,8},{57,9},{160,1... | collective-permute-start | bytes 147464 | tf_op jit(solution)/shard_map/root/ppermute | solution.py:34
  99.6 20.9 %collective-permute-start.19 = (bf16[16,1536]{1,0:T(8,128)(2,1)}, bf16[16,1536]{1,0:T(8,128)(2,1)S(1)}, u32[]{:S(2)}, u32[]{:S(2)}) collective-permute-start(bf16[16,1536]{1,0:T(8,128)(2,1)} %root.16), channel_id=1, source_target_pairs={{32,0},{33,1},{40,8},{41,9},{48,16},{49,17},{56,24},{57,25},{160,1... | collective-permute-start | bytes 147464 | tf_op jit(solution)/shard_map/root/ppermute | solution.py:34
  125.9 5.0 %collective-permute-start.23 = (bf16[2,16,768]{2,1,0:T(8,128)(2,1)}, bf16[2,16,768]{2,1,0:T(8,128)(2,1)S(1)}, u32[]{:S(2)}, u32[]{:S(2)}) collective-permute-start(bf16[2,16,768]{2,1,0:T(8,128)(2,1)} %root.17), channel_id=1, source_target_pairs={{0,1},{1,0},{8,9},{9,8},{16,17},{17,16},{24,25},{25,24},{128,129},... | collective-permute-start | bytes 147464 | tf_op jit(solution)/shard_map/root/ppermute | solution.py:34
  127.8 3.1 %collective-permute-start.22 = (bf16[2,16,768]{2,1,0:T(8,128)(2,1)}, bf16[2,16,768]{2,1,0:T(8,128)(2,1)S(1)}, u32[]{:S(2)}, u32[]{:S(2)}) collective-permute-start(bf16[2,16,768]{2,1,0:T(8,128)(2,1)} %root.17), channel_id=1, source_target_pairs={{0,7},{1,6},{8,15},{9,14},{16,23},{17,22},{24,31},{25,30},{34,35},... | collective-permute-start | bytes 147464 | tf_op jit(solution)/shard_map/root/ppermute | solution.py:34
  129.1 4.4 %collective-permute-start.21 = (bf16[2,16,768]{2,1,0:T(8,128)(2,1)}, bf16[2,16,768]{2,1,0:T(8,128)(2,1)S(1)}, u32[]{:S(2)}, u32[]{:S(2)}) collective-permute-start(bf16[2,16,768]{2,1,0:T(8,128)(2,1)} %root.17), channel_id=1, source_target_pairs={{0,6},{1,7},{8,14},{9,15},{16,22},{17,23},{24,30},{25,31},{32,38},... | collective-permute-start | bytes 147464 | tf_op jit(solution)/shard_map/root/ppermute | solution.py:34
  134.4 3.0 %collective-permute-start.24 = (bf16[2,16,768]{2,1,0:T(8,128)(2,1)S(1)}, bf16[2,16,768]{2,1,0:T(8,128)(2,1)S(1)}, u32[]{:S(2)}, u32[]{:S(2)}) collective-permute-start(bf16[2,16,768]{2,1,0:T(8,128)(2,1)S(1)} %add_convert_fusion.9), channel_id=1, source_target_pairs={{0,2},{1,3},{8,10},{9,11},{16,18},{17,19},{24,26},{25,27},{6,4},{7... | collective-permute-start | bytes 147464 | tf_op jit(solution)/shard_map/root/ppermute | solution.py:34
  135.7 28.3 %collective-permute-start.29 = (bf16[512,1024]{1,0:T(8,128)(2,1)}, bf16[512,1024]{1,0:T(8,128)(2,1)}, u32[]{:S(2)}, u32[]{:S(2)}) collective-permute-start(bf16[512,1024]{1,0:T(8,128)(2,1)} %bitcast.6), channel_id=1, source_target_pairs={{64,72},{72,64},{80,88},{88,80},{96,104},{104,96},{112,120},{120,1... | collective-permute-start | bytes 3145736 | tf_op jit(solution)/shard_map/root/ppermute | solution.py:203
  156.7 8.9 %collective-permute-start.28 = (bf16[32,1024]{1,0:T(8,128)(2,1)S(1)}, bf16[32,1024]{1,0:T(8,128)(2,1)S(1)}, u32[]{:S(2)}, u32[]{:S(2)}) collective-permute-start(bf16[32,1024]{1,0:T(8,128)(2,1)S(1)} %reduce_sum.22), channel_id=1, source_target_pairs={{96,0},{97,1},{104,8},{105,9},{112,16},{113,17},{120,24},{121,25},... | collective-permute-start | bytes 196616 | tf_op jit(solution)/shard_map/coupling/ppermute | solution.py:34
  158.0 8.9 %collective-permute-start.27 = (bf16[32,1024]{1,0:T(8,128)(2,1)S(1)}, bf16[32,1024]{1,0:T(8,128)(2,1)S(1)}, u32[]{:S(2)}, u32[]{:S(2)}) collective-permute-start(bf16[32,1024]{1,0:T(8,128)(2,1)S(1)} %reduce_sum.22), channel_id=1, source_target_pairs={{64,0},{65,1},{72,8},{73,9},{80,16},{81,17},{88,24},{89,25},{98,34... | collective-permute-start | bytes 196616 | tf_op jit(solution)/shard_map/coupling/ppermute | solution.py:34
  159.3 8.3 %collective-permute-start.26 = (bf16[32,1024]{1,0:T(8,128)(2,1)S(1)}, bf16[32,1024]{1,0:T(8,128)(2,1)S(1)}, u32[]{:S(2)}, u32[]{:S(2)}) collective-permute-start(bf16[32,1024]{1,0:T(8,128)(2,1)S(1)} %reduce_sum.22), channel_id=1, source_target_pairs={{32,0},{33,1},{40,8},{41,9},{48,16},{49,17},{56,24},{57,25},{66,34... | collective-permute-start | bytes 196616 | tf_op jit(solution)/shard_map/coupling/ppermute | solution.py:34
  160.6 10.5 %collective-permute-start.30 = (bf16[512,1024]{1,0:T(8,128)(2,1)}, bf16[512,1024]{1,0:T(8,128)(2,1)}, u32[]{:S(2)}, u32[]{:S(2)}) collective-permute-start(bf16[512,1024]{1,0:T(8,128)(2,1)} %collective-permute-done.25), channel_id=1, source_target_pairs={{64,72},{72,64},{80,88},{88,80},{96,104},{104,96},{112,120},{120,1... | collective-permute-start | bytes 3145736 | tf_op jit(solution)/shard_map/coupling/ppermute | solution.py:220
  173.2 1.4 collective-permute-start.32
  177.1 1.5 collective-permute-start.33
  177.7 3.8 %collective-permute-start.34 = (bf16[32,2048]{1,0:T(8,128)(2,1)S(1)}, bf16[32,2048]{1,0:T(8,128)(2,1)S(1)}, u32[]{:S(2)}, u32[]{:S(2)}) collective-permute-start(bf16[32,2048]{1,0:T(8,128)(2,1)S(1)} %add_convert_fusion.6), channel_id=1, source_target_pairs={{100,98},{101,99},{108,106},{109,107},{116,114},{117,115},{124,122... | collective-permute-start | bytes 393224 | tf_op jit(solution)/shard_map/child/ppermute | solution.py:34
  182.5 3.6 %collective-permute-start.37 = (bf16[32,2048]{1,0:T(8,128)(2,1)S(1)}, bf16[32,2048]{1,0:T(8,128)(2,1)S(1)}, u32[]{:S(2)}, u32[]{:S(2)}) collective-permute-start(bf16[32,2048]{1,0:T(8,128)(2,1)S(1)} %add_convert_fusion.5), channel_id=1, source_target_pairs={{68,67},{69,66},{76,75},{77,74},{84,83},{85,82},{92,91},{93,90},{1... | collective-permute-start | bytes 393224 | tf_op jit(solution)/shard_map/child/ppermute | solution.py:34
  183.2 2.9 %collective-permute-start.36 = (bf16[32,2048]{1,0:T(8,128)(2,1)S(1)}, bf16[32,2048]{1,0:T(8,128)(2,1)S(1)}, u32[]{:S(2)}, u32[]{:S(2)}) collective-permute-start(bf16[32,2048]{1,0:T(8,128)(2,1)S(1)} %add_convert_fusion.5), channel_id=1, source_target_pairs={{68,66},{69,67},{76,74},{77,75},{84,82},{85,83},{92,90},{93,91},{9... | collective-permute-start | bytes 393224 | tf_op jit(solution)/shard_map/child/ppermute | solution.py:34
  185.4 1.6 collective-permute-start.35
  188.6 1.4 collective-permute-start.38
  189.2 3.6 %collective-permute-start.39 = (bf16[32,2048]{1,0:T(8,128)(2,1)S(1)}, bf16[32,2048]{1,0:T(8,128)(2,1)S(1)}, u32[]{:S(2)}, u32[]{:S(2)}) collective-permute-start(bf16[32,2048]{1,0:T(8,128)(2,1)S(1)} %add_convert_fusion.4), channel_id=1, source_target_pairs={{66,64},{67,65},{74,72},{75,73},{82,80},{83,81},{90,88},{91,89},{1... | collective-permute-start | bytes 393224 | tf_op jit(solution)/shard_map/child/ppermute | solution.py:34
  193.8 3.6 %collective-permute-start.42 = (bf16[32,2048]{1,0:T(8,128)(2,1)S(1)}, bf16[32,2048]{1,0:T(8,128)(2,1)S(1)}, u32[]{:S(2)}, u32[]{:S(2)}) collective-permute-start(bf16[32,2048]{1,0:T(8,128)(2,1)S(1)} %add_convert_fusion.3), channel_id=1, source_target_pairs={{34,33},{35,32},{42,41},{43,40},{50,49},{51,48},{58,57},{59,56},{6... | collective-permute-start | bytes 393224 | tf_op jit(solution)/shard_map/child/ppermute | solution.py:34
  194.5 2.9 %collective-permute-start.41 = (bf16[32,2048]{1,0:T(8,128)(2,1)S(1)}, bf16[32,2048]{1,0:T(8,128)(2,1)S(1)}, u32[]{:S(2)}, u32[]{:S(2)}) collective-permute-start(bf16[32,2048]{1,0:T(8,128)(2,1)S(1)} %add_convert_fusion.3), channel_id=1, source_target_pairs={{34,32},{35,33},{42,40},{43,41},{50,48},{51,49},{58,56},{59,57},{6... | collective-permute-start | bytes 393224 | tf_op jit(solution)/shard_map/child/ppermute | solution.py:34
  196.7 2.9 %collective-permute-start.40 = (bf16[32,1024]{1,0:T(8,128)(2,1)S(1)}, bf16[32,1024]{1,0:T(8,128)(2,1)S(1)}, u32[]{:S(2)}, u32[]{:S(2)}) collective-permute-start(bf16[32,1024]{1,0:T(8,128)(2,1)S(1)} %fusion.10), channel_id=1, source_target_pairs={{64,32},{65,33},{72,40},{73,41},{80,48},{81,49},{88,56},{89,57},{1... | collective-permute-start | bytes 196616 | tf_op jit(solution)/shard_map/child/ppermute | solution.py:34
  199.9 47.8 %collective-permute-start.43 = (bf16[32,1024]{1,0:T(8,128)(2,1)S(1)}, bf16[32,1024]{1,0:T(8,128)(2,1)S(1)}, u32[]{:S(2)}, u32[]{:S(2)}) collective-permute-start(bf16[32,1024]{1,0:T(8,128)(2,1)S(1)} %add_convert_fusion.7), channel_id=1, source_target_pairs={{32,0},{33,1},{40,8},{41,9},{48,16},{49,17},{56,24},{57,25},{160,1... | collective-permute-start | bytes 196616 | tf_op jit(solution)/shard_map/child/ppermute | solution.py:34
  250.6 5.7 %collective-permute-start.46 = (bf16[32,2048]{1,0:T(8,128)(2,1)S(1)}, bf16[32,2048]{1,0:T(8,128)(2,1)S(1)}, u32[]{:S(2)}, u32[]{:S(2)}) collective-permute-start(bf16[32,2048]{1,0:T(8,128)(2,1)S(1)} %maximum_select_fusion.3), channel_id=1, source_target_pairs={{0,1},{1,0},{8,9},{9,8},{16,17},{17,16},{24,25},{25,24},{128,129},... | collective-permute-start | bytes 393224 | tf_op jit(solution)/shard_map/child/ppermute | solution.py:34
  252.6 3.8 %collective-permute-start.45 = (bf16[32,2048]{1,0:T(8,128)(2,1)S(1)}, bf16[32,2048]{1,0:T(8,128)(2,1)S(1)}, u32[]{:S(2)}, u32[]{:S(2)}) collective-permute-start(bf16[32,2048]{1,0:T(8,128)(2,1)S(1)} %maximum_select_fusion.3), channel_id=1, source_target_pairs={{0,7},{1,6},{8,15},{9,14},{16,23},{17,22},{24,31},{25,30},{34,35},... | collective-permute-start | bytes 393224 | tf_op jit(solution)/shard_map/child/ppermute | solution.py:34
  253.9 10.5 %collective-permute-start.44 = (bf16[32,2048]{1,0:T(8,128)(2,1)S(1)}, bf16[32,2048]{1,0:T(8,128)(2,1)S(1)}, u32[]{:S(2)}, u32[]{:S(2)}) collective-permute-start(bf16[32,2048]{1,0:T(8,128)(2,1)S(1)} %maximum_select_fusion.3), channel_id=1, source_target_pairs={{0,6},{1,7},{8,14},{9,15},{16,22},{17,23},{24,30},{25,31},{32,38},... | collective-permute-start | bytes 393224 | tf_op jit(solution)/shard_map/child/ppermute | solution.py:34
  264.5 3.2 %collective-permute-start.47 = (bf16[32,2048]{1,0:T(8,128)(2,1)S(1)}, bf16[32,2048]{1,0:T(8,128)(2,1)S(1)}, u32[]{:S(2)}, u32[]{:S(2)}) collective-permute-start(bf16[32,2048]{1,0:T(8,128)(2,1)S(1)} %add_convert_fusion.1), channel_id=1, source_target_pairs={{0,2},{1,3},{8,10},{9,11},{16,18},{17,19},{24,26},{25,27},{6,4},{7... | collective-permute-start | bytes 393224 | tf_op jit(solution)/shard_map/child/ppermute | solution.py:34
  (18 other events, 210.5 us)

commit v8 on v6

--- a/solution.py
+++ b/solution.py
@@ -1,3 +1,5 @@
+import functools
+
 import jax
 import jax.numpy as jnp
 from jax import lax
@@ -34,94 +36,108 @@
     return lax.ppermute(value, GRID, pairs)
 
 
-def terms_kernel(keep_own, keep_other, x, own, other, carried, terms, total):
+def terms_kernel(count, masked, *refs):
+    keep, refs = refs[: count * masked], refs[count * masked :]
+    x, factors, (carried, terms, total) = refs[0], refs[1 : 1 + count], refs[1 + count :]
     step = pl.program_id(0)
-    block = own.shape[0]
+    rows, cols = factors[0].shape
+    width = rows if masked else cols
 
     @pl.when(step == 0)
     def _():
         total[...] = carried[...]
 
-    for c in range(own.shape[1] // block):
-        cols = slice(c * block, (c + 1) * block)
-        total[:, cols] += keep_own[step, c] * dot(x[0], own[:, cols])
-        total[:, cols] += keep_other[step, c] * dot(x[1], other[:, cols])
+    for c in range(cols // width):
+        part = slice(c * width, (c + 1) * width)
+        for k in range(count):
+            product = dot(x[k], factors[k][:, part])
+            total[:, part] += keep[k][step, c] * product if masked else product
 
     @pl.when(step == pl.num_programs(0) - 1)
     def _():
         terms[...] = total[...].astype(BF16)
 
 
-def root_terms(keep, factors, current, carried):
-    steps, probes, (rows, cols) = keep[0].shape[0], current.shape[1], factors[0].shape
+def terms_of(keep, steps, factors, current, carried):
+    count, probes, (rows, cols) = len(factors), current.shape[1], factors[0].shape
     factor_spec = pl.BlockSpec((rows // steps, cols), lambda i: (i, 0))
     whole = pl.BlockSpec((probes, cols), lambda i: (0, 0))
     return pl.pallas_call(
-        terms_kernel,
+        functools.partial(terms_kernel, count, len(keep) > 0),
         grid=(steps,),
-        in_specs=[pl.BlockSpec(memory_space=pltpu.SMEM)] * 2
-        + [pl.BlockSpec((2, probes, rows // steps), lambda i: (0, 0, i))]
-        + [factor_spec] * 2
+        in_specs=[pl.BlockSpec(memory_space=pltpu.SMEM)] * len(keep)
+        + [pl.BlockSpec((count, probes, rows // steps), lambda i: (0, 0, i))]
+        + [factor_spec] * count
         + [whole],
         out_specs=whole,
         out_shape=jax.ShapeDtypeStruct((probes, cols), BF16),
         scratch_shapes=[pltpu.VMEM((probes, cols), F32)],
         compiler_params=pltpu.CompilerParams(vmem_limit_bytes=8 * 2**20),
         cost_estimate=pl.CostEstimate(
-            flops=4 * probes * rows * cols, bytes_accessed=4 * rows * cols, transcendentals=0
+            flops=2 * count * probes * rows * cols,
+            bytes_accessed=2 * count * rows * cols,
+            transcendentals=0,
         ),
-    )(*keep, *([current] + list(factors) + [carried]))
-
-
-def pieces_kernel(solving, rhs, first, second, own, other, current, out, residual):
+    )(*keep, current, *factors, carried)
+
+
+def pieces_kernel(r, count, *refs):
+    solving, rhs, refs = refs[0], refs[1], refs[2:]
+    sums, factors = refs[: -count - 3], refs[-count - 3 : -3]
+    current, out, residual = refs[-3:]
+
     @pl.when(pl.program_id(0) == 0)
     def _():
-        totals = first[...].astype(F32) + second[...].astype(F32)
-        residual[...] = (rhs[...] - totals).astype(BF16)
-
-    for k, factor in enumerate((own, other)):
+        left = rhs[...]
+        if sums:
+            left = left - sum([part[...].astype(F32) for part in sums[1:]], sums[0][...].astype(F32))
+        residual[...] = left.astype(BF16)
+
+    for k, factor in enumerate(factors):
         piece = dot_t(residual[...], factor[...])
-        out[k] = jnp.where(solving[0] == 1, piece, current[k].astype(F32)).astype(BF16)
-
-
-def root_pieces(solving, rhs, first, second, factors, current):
-    (rows, cols), probes, steps = factors[0].shape, rhs.shape[0], 3
+        out[k] = jnp.where(solving[r] == 1, piece, current[k].astype(F32)).astype(BF16)
+
+
+def pieces_of(solving, steps, factors, r, rhs, sums, current):
+    (rows, cols), probes, count = factors[0].shape, rhs.shape[0], len(factors)
     factor_spec = pl.BlockSpec((rows // steps, cols), lambda i: (i, 0))
     whole = pl.BlockSpec((probes, cols), lambda i: (0, 0))
-    part = pl.BlockSpec((2, probes, rows // steps), lambda i: (0, 0, i))
+    part = pl.BlockSpec((count, probes, rows // steps), lambda i: (0, 0, i))
     return pl.pallas_call(
-        pieces_kernel,
+        functools.partial(pieces_kernel, r, count),
         grid=(steps,),
-        in_specs=[pl.BlockSpec(memory_space=pltpu.SMEM)] + [whole] * 3 + [factor_spec] * 2 + [part],
+        in_specs=[pl.BlockSpec(memory_space=pltpu.SMEM)]
+        + [whole] * (1 + len(sums))
+        + [factor_spec] * count
+        + [part],
         out_specs=part,
         out_shape=jax.ShapeDtypeStruct(current.shape, BF16),
         scratch_shapes=[pltpu.VMEM((probes, cols), BF16)],
         compiler_params=pltpu.CompilerParams(vmem_limit_bytes=8 * 2**20),
         cost_estimate=pl.CostEstimate(
-            flops=4 * probes * rows * cols, bytes_accessed=4 * rows * cols, transcendentals=0
+            flops=2 * count * probes * rows * cols,
+            bytes_accessed=2 * count * rows * cols,
+            transcendentals=0,
         ),
-    )(solving.astype(jnp.int32).reshape(1), rhs, first, second, *factors, current)
+    )(solving, rhs, *sums, *factors, current)
 
 
 def sweep(rhs, current, forward, solve, split_rows, beside=lambda r, value: value):
-    row_panel = lax.axis_index("row") // GROUP
-    col_panel = lax.axis_index("col") // PAIR
     carried = jnp.zeros(rhs.shape, F32)
-    first = second = jnp.zeros(rhs.shape, BF16)
     for r in range(PANELS - 1, -1, -1):
-        ahead = None
+        ahead, sums = None, []
         if r < PANELS - 1:
             terms = beside(r, forward(current, carried))
             down = [(r + 1, r, 0, r, r, 0)]
             if r == 1:
                 down.append((3, 2, 0, 0, 0, 0))
-            first = send(terms, down)
+            sums = [send(terms, down)]
             if split_rows:
-                second = send(terms, [(r + 1, r, 2, r, r, 0)])
+                sums.append(send(terms, [(r + 1, r, 2, r, r, 0)]))
             if r >= 1:
                 ahead = send(current, [(r + 1, r + 1, 0, r, r - 1, 0)])
-            carried = carried + first.astype(F32)
-        current = solve((row_panel == r) & (col_panel == r), rhs, first, second, current)
+            carried = carried + sums[0].astype(F32)
+        current = solve(r, rhs, sums, current)
         if r == PANELS - 1:
             current = beside(r, current)
         if ahead is not None:
@@ -170,9 +186,11 @@
         on_diagonal = row_index // GROUP == col_index // PAIR
         keep = [jnp.where(on_diagonal, 1, p).astype(F32) for p in (pattern, partner_pattern)]
         factors = [root_factor, partner_factor]
+        panel = jnp.arange(PANELS)
+        solving = (panel == row_index // GROUP) & (panel == col_index // PAIR)
+        solving = solving.astype(jnp.int32)
 
     with jax.named_scope("rhs"):
-        probes_here = partials.shape[1]
         lanes = cols_here // 12
         pieces = partials[0].reshape(layers, 1, 2, 12, lanes)
         pieces = jnp.broadcast_to(pieces, (layers, ROWS // 2, 2, 12, lanes))
@@ -207,10 +225,8 @@
         root_rows = sweep(
             root_rhs,
             jnp.zeros((2, root_rhs.shape[0], rows_here), BF16),
-            lambda current, carried: root_terms(keep, factors, current, carried),
-            lambda solving, rhs, first, second, current: root_pieces(
-                solving, rhs, first, second, factors, current
-            ),
+            functools.partial(terms_of, keep, pattern.shape[0], factors),
+            functools.partial(pieces_of, solving, pattern.shape[0], factors),
             True,
             move_children,
         )
@@ -238,24 +254,16 @@
 
     with jax.named_scope("child"):
         blocks = [child_here] + [moved[0, flip] + moved[1, flip] for flip in (1, 2, 3)]
-        rows = child_here.shape[0]
-
-        def child_terms(current, carried):
-            for i, block in enumerate(blocks):
-                carried = carried + dot(current[:, i * rows : (i + 1) * rows], block)
-            return carried.astype(BF16)
-
-        def child_pieces(solving, rhs, first, second, current):
-            residual = (rhs - first.astype(F32)).astype(BF16)
-            piece = jnp.concatenate([dot_t(residual, block) for block in blocks], 1).astype(BF16)
-            return jnp.where(solving, piece, current)
-
-        child_rows = jnp.zeros((share, GROUP * rows), BF16)
-        child_rows = sweep(child_rhs, child_rows, child_terms, child_pieces, False)
-        child_rows = child_rows.reshape(share, 2, 2, -1)
-        child_rows = jnp.where(core == 1, child_rows[:, :, ::-1], child_rows)
-        child_rows = jnp.where(row_index % GROUP // 2 == 1, child_rows[:, ::-1], child_rows)
-        child_rows = child_rows.reshape(share, GROUP, -1).transpose(1, 0, 2)
+        child_rows = sweep(
+            child_rhs,
+            jnp.zeros((GROUP, share, child_here.shape[0]), BF16),
+            functools.partial(terms_of, [], 2, blocks),
+            functools.partial(pieces_of, solving, 2, blocks),
+            False,
+        )
+        child_rows = child_rows.reshape(2, 2, share, -1)
+        child_rows = jnp.where(core == 1, child_rows[:, ::-1], child_rows)
+        child_rows = jnp.where(row_index % GROUP // 2 == 1, child_rows[::-1], child_rows)
         child_rows = child_rows.reshape(GROUP * share, -1)
         child_rows = lax.all_to_all(child_rows, "row", 0, 0, tiled=True, axis_index_groups=quarters)
     return (root_all, child_rows[None])

time: 251 us -> 245 us (0.976)
  matrix products: 23.9 us -> 0.31 us
  Pallas kernels: 14.6 us -> 37.4 us
  blocking collectives: 28.8 us -> 16.6 us
  waiting for transfers between devices: 93.8 us -> 105 us
  local copies, waits for them, and re-layouts: 12.9 us -> 4.68 us
  starting transfers between devices: 65.7 us -> 71.4 us
    pallas_call x9 -> x18, Pallas kernels: 14.6 us -> 37.4 us  [the longest x8 18.9 us: pieces_of(): pl.pallas_call(functools.partial(pieces_kernel, r, count), grid=(steps,),...]
    all_to_all x1 -> x0, blocking collectives: 12.3 us -> none  [per_device(): lax.all_to_all(shared, ('gz', 'row'), 0, 0, tiled=True, axis_index_groups...]
    dot_general x21 -> x1, matrix products: 12.3 us -> 0.31 us  [dot(): return jnp.dot(a, b, preferred_element_type=F32)]
    dot_general x16 -> x0, matrix products: 11.7 us -> none  [dot_t(): lax.dot_general(a, b, (((1,), (1,)), ((), ())), preferred_element_type=F32)]
    unnamed x29 -> x21, local copies, waits for them, and re-layouts: 10.4 us -> 2.38 us
    ppermute x40, waiting for transfers between devices: 76 us -> 81.3 us  [send(): return lax.ppermute(value, GRID, pairs)]
    all_to_all x0 -> x1, starting transfers between devices: none -> 4.69 us  [per_device(): lax.all_to_all(shared, ('gz', 'row'), 0, 0, tiled=True, axis_index_groups...]
    all_to_all x0 -> x1, waiting for transfers between devices: none -> 4.26 us  [per_device(): lax.all_to_all(shared, ('gz', 'row'), 0, 0, tiled=True, axis_index_groups...]
  transfers between devices with their start and end apart: 49 -> 50, of which waited for: 13 -> 13; matrix products, arithmetic and copies ran while one was open for 9% -> 3% of each run, Pallas kernels for 6% -> 10%
where the time goes in v8:
time: 245 us; the launch traced here: 243 us
  waiting for transfers between devices  105 us (43%)
  starting transfers between devices  71.4 us (29%)
  Pallas kernels  37.4 us (15%)
  blocking collectives  16.6 us (7%)
  other arithmetic  6.61 us (3%)
  local copies, waits for them, and re-layouts  4.68 us (2%)
    ppermute x40, waiting for transfers between devices, send(): return lax.ppermute(value, GRID, pairs)  81.3 us
    ppermute x40, starting transfers between devices, send(): return lax.ppermute(value, GRID, pairs)  36.8 us
    pallas_call x8, Pallas kernels, pieces_of(): pl.pallas_call(functools.partial(pieces_kernel, r, count), grid=(steps,),...  18.9 us
    pallas_call x10, Pallas kernels, terms_of(): pl.pallas_call(functools.partial(terms_kernel, count, len(keep) > 0), gri...  18.4 us
    all_to_all x1, waiting for transfers between devices, per_device(): lax.all_to_all(pieces.reshape(layers * ROWS, 12, lanes), ('gz', 'row'), 0...  9.56 us
    ppermute x2, waiting for transfers between devices, move_children(): moved[half, 2] = lax.ppermute(here, 'row', rows_of(half, 2))  9.32 us
    ppermute x1, starting transfers between devices, per_device(): partner_factor = lax.ppermute(root_factor, 'row', swap)  8.92 us
    all_to_all x1, blocking collectives, per_device(): lax.all_to_all(terms, 'row', 0, 0, tiled=True, axis_index_groups=quarters)  8.47 us
  transfers between devices with their start and end apart: 50, of which 13 were waited for; matrix products, arithmetic and copies ran while one was open for 3% of the time, Pallas kernels for 10%

profile of v8, /device:TPU:1, one launch (start us, length us, event | category | flops | bytes accessed | tf_op | source)
XLA Modules:
  0.0 243.4 jit_solution(10634474369465016333)
XLA Ops:
  0.6 8.9 %collective-permute-start.1 = (bf16[768,1536]{1,0:T(8,128)(2,1)}, bf16[768,1536]{1,0:T(8,128)(2,1)S(1)}, u32[]{:S(2)}, u32[]{:S(2)}) collective-permute-start(bf16[768,1536]{1,0:T(8,128)(2,1)} %refs_4_.5), channel_id=1, source_target_pairs={{0,8},{8,0},{16,24},{24,16},{32,40},{40,32},{48,56},{56,48},{64,72... | collective-permute-start | bytes 7077896 | tf_op jit(solution)/shard_map/mask/ppermute | solution.py:184
  11.1 4.9 %all-to-all-start = ((bf16[64,12,128]{2,1,0:T(8,128)(2,1)}), bf16[64,12,128]{2,1,0:T(8,128)(2,1)S(1)}, u32[]{:S(2)}, u32[]{:S(2)}) async-start(bf16[64,12,128]{2,1,0:T(8,128)(2,1)} %bitcast.24), calls=%async_computation | async-start | bytes 524288 | tf_op jit(solution)/shard_map/rhs/all_to_all | solution.py:197
  15.9 2.4 collective-permute-start
  18.4 9.6 %all-to-all-done = bf16[64,12,128]{2,1,0:T(8,128)(2,1)S(1)} async-done(((bf16[64,12,128]{2,1,0:T(8,128)(2,1)}), bf16[64,12,128]{2,1,0:T(8,128)(2,1)S(1)}, u32[]{:S(2)}, u32[]{:S(2)}) %all-to-all-start) | async-done | bytes 196640 | tf_op jit(solution)/shard_map/rhs/all_to_all | solution.py:197
  28.1 1.7 copy-done.1
  29.7 2.1 root.9
  33.2 3.1 %collective-permute-start.11 = (bf16[512,1024]{1,0:T(8,128)(2,1)}, bf16[512,1024]{1,0:T(8,128)(2,1)S(1)}, u32[]{:S(2)}, u32[]{:S(2)}) collective-permute-start(bf16[512,1024]{1,0:T(8,128)(2,1)} %bitcast.2.refs_2_.refs_1_.refs_3_), channel_id=1, source_target_pairs={{0,16},{8,24},{16,0},{24,8},{32,48},{40,56},{48,32},{56,40},{1,17}... | collective-permute-start | bytes 3145736 | tf_op jit(solution)/shard_map/root/ppermute | solution.py:220
  36.3 2.5 %collective-permute-start.10 = (bf16[512,1024]{1,0:T(8,128)(2,1)}, bf16[512,1024]{1,0:T(8,128)(2,1)S(1)}, u32[]{:S(2)}, u32[]{:S(2)}) collective-permute-start(bf16[512,1024]{1,0:T(8,128)(2,1)} %bitcast.2.refs_2_.refs_1_.refs_3_), channel_id=1, source_target_pairs={{0,8},{8,0},{16,24},{24,16},{32,40},{40,32},{48,56},{56,48},{1,9},... | collective-permute-start | bytes 3145736 | tf_op jit(solution)/shard_map/root/ppermute | solution.py:221
  38.9 1.7 root.10
  42.6 2.2 root.11
  46.2 1.7 root.12
  48.6 1.7 root.13
  50.3 9.3 %collective-permute-done.11 = bf16[512,1024]{1,0:T(8,128)(2,1)S(1)} collective-permute-done((bf16[512,1024]{1,0:T(8,128)(2,1)}, bf16[512,1024]{1,0:T(8,128)(2,1)S(1)}, u32[]{:S(2)}, u32[]{:S(2)}) %collective-permute-start.11) | collective-permute-done | bytes 1048608 | tf_op jit(solution)/shard_map/root/ppermute | solution.py:220
  61.6 3.2 %collective-permute-start.18 = (bf16[512,1024]{1,0:T(8,128)(2,1)S(1)}, bf16[512,1024]{1,0:T(8,128)(2,1)S(1)}, u32[]{:S(2)}, u32[]{:S(2)}) collective-permute-start(bf16[512,1024]{1,0:T(8,128)(2,1)S(1)} %collective-permute-done.11), channel_id=1, source_target_pairs={{0,8},{8,0},{16,24},{24,16},{32,40},{40,32},{48,56},{56,48},{1,9},... | collective-permute-start | bytes 3145736 | tf_op jit(solution)/shard_map/root/ppermute | solution.py:214
  64.9 2.2 root.14
  68.5 1.7 root.15
  70.9 1.7 root.16
  72.6 1.6 collective-permute-start.25
  76.8 11.7 %collective-permute-done.20.refs_3_ = bf16[16,1536]{1,0:T(8,128)(2,1)S(1)} collective-permute-done((bf16[16,1536]{1,0:T(8,128)(2,1)S(1)}, bf16[16,1536]{1,0:T(8,128)(2,1)S(1)}, u32[]{:S(2)}, u32[]{:S(2)}) %collective-permute-start.20) | collective-permute-done | bytes 49184 | tf_op jit(solution)/shard_map/root/ppermute | solution.py:36
  88.5 6.4 %collective-permute-done.19.refs_2_ = bf16[16,1536]{1,0:T(8,128)(2,1)S(1)} collective-permute-done((bf16[16,1536]{1,0:T(8,128)(2,1)S(1)}, bf16[16,1536]{1,0:T(8,128)(2,1)S(1)}, u32[]{:S(2)}, u32[]{:S(2)}) %collective-permute-start.19) | collective-permute-done | bytes 49184 | tf_op jit(solution)/shard_map/root/ppermute | solution.py:36
  94.9 2.2 root.17
  97.1 2.1 collective-permute-start.23
  102.1 2.5 %collective-permute-done.21 = bf16[2,16,768]{2,1,0:T(8,128)(2,1)S(1)} collective-permute-done((bf16[2,16,768]{2,1,0:T(8,128)(2,1)S(1)}, bf16[2,16,768]{2,1,0:T(8,128)(2,1)S(1)}, u32[]{:S(2)}, u32[]{:S(2)}) %collective-permute-start.21) | collective-permute-done | bytes 49184 | tf_op jit(solution)/shard_map/root/ppermute | solution.py:36
  105.9 1.7 collective-permute-start.29
  108.3 4.7 %all-to-all-start.1 = ((bf16[8,16,768]{2,1,0:T(8,128)(2,1)}), bf16[8,16,768]{2,1,0:T(8,128)(2,1)S(1)}, u32[]{:S(2)}, u32[]{:S(2)}) async-start(bf16[8,16,768]{2,1,0:T(8,128)(2,1)} %bitcast.3), calls=%async_computation.1 | async-start | bytes 393216 | tf_op jit(solution)/shard_map/coupling/all_to_all | solution.py:241
  113.0 1.6 collective-permute-start.30
  114.7 4.3 %all-to-all-done.1 = bf16[8,16,768]{2,1,0:T(8,128)(2,1)S(1)} async-done(((bf16[8,16,768]{2,1,0:T(8,128)(2,1)}), bf16[8,16,768]{2,1,0:T(8,128)(2,1)S(1)}, u32[]{:S(2)}, u32[]{:S(2)}) %all-to-all-start.1) | async-done | bytes 196640 | tf_op jit(solution)/shard_map/coupling/all_to_all | solution.py:241
  119.4 8.5 %all_to_all.32 = bf16[4,32,1024]{2,1,0:T(8,128)(2,1)S(1)} all-to-all(bf16[4,32,1024]{2,1,0:T(8,128)(2,1)S(1)} %bitcast.25), channel_id=1, replica_groups={{0,8,16,24},{32,40,48,56},{64,72,80,88},{96,104,112,120},{1,9,17,25},{3..., dimensions={0} | all-to-all | bytes 524288 | tf_op jit(solution)/shard_map/coupling/all_to_all | solution.py:245
  131.8 1.6 add.146.refs_4_.refs_3_.refs_5_
  133.5 1.7 add.145.refs_3_.refs_2_.refs_4_
  135.2 2.9 %collective-permute-done.27 = bf16[32,1024]{1,0:T(8,128)(2,1)S(1)} collective-permute-done((bf16[32,1024]{1,0:T(8,128)(2,1)S(1)}, bf16[32,1024]{1,0:T(8,128)(2,1)S(1)}, u32[]{:S(2)}, u32[]{:S(2)}) %collective-permute-start.27) | collective-permute-done | bytes 65568 | tf_op jit(solution)/shard_map/coupling/ppermute | solution.py:36
  139.8 1.5 add.147.refs_5_.refs_4_.refs_6_
  141.3 2.6 %child.9 = bf16[4,32,512]{2,1,0:T(8,128)(2,1)S(1)} custom-call(s32[4]{0:T(128)S(1)} %and_convert_fusion.refs_0_, f32[32,1024]{1,0:T(8,128)S(1)} %bitcast_subtract_fusion.refs_1_, bf16[512,1024]{1,0:T(8,128)(2,1)} %bitcast.2.refs_2_.refs_1_.refs_3_, bf16[512,1024]{1,0:T(8,128)(2,1)S(1)} %add.145.refs_3_.refs_2_.refs_4_, ...), custom_call_target="tpu_custom_call" | custom-call | flops 134217728 | bytes 4194304 | tf_op jit(solution)/shard_map/child/pallas_call | solution.py:106
  146.0 2.0 child.10
  148.8 2.6 %child.11 = bf16[4,32,512]{2,1,0:T(8,128)(2,1)S(1)} custom-call(s32[4]{0:T(128)S(1)} %and_convert_fusion.refs_0_, f32[32,1024]{1,0:T(8,128)S(1)} %bitcast_subtract_fusion.refs_1_, bf16[32,1024]{1,0:T(8,128)(2,1)S(1)} %collective-permute-done.33.refs_2_, bf16[512,1024]{1,0:T(8,128)(2,1)} %bitcast.2.refs_2_.refs_1_.refs_3_, ...), custom_call_target="tpu_custom_call" | custom-call | flops 134217728 | bytes 4194304 | tf_op jit(solution)/shard_map/child/pallas_call | solution.py:106
  151.4 2.0 child.12
  155.6 2.0 child.13
  159.0 2.6 %child.14 = bf16[4,32,512]{2,1,0:T(8,128)(2,1)S(1)} custom-call(s32[4]{0:T(128)S(1)} %and_convert_fusion.refs_0_, f32[32,1024]{1,0:T(8,128)S(1)} %bitcast_subtract_fusion.refs_1_, bf16[32,1024]{1,0:T(8,128)(2,1)S(1)} %collective-permute-done.38.refs_2_, bf16[512,1024]{1,0:T(8,128)(2,1)} %bitcast.2.refs_2_.refs_1_.refs_3_, ...), custom_call_target="tpu_custom_call" | custom-call | flops 134217728 | bytes 4194304 | tf_op jit(solution)/shard_map/child/pallas_call | solution.py:106
  161.7 2.0 child.15
  165.8 2.0 child.16
  169.2 45.7 %collective-permute-done.43.refs_2_ = bf16[32,1024]{1,0:T(8,128)(2,1)S(1)} collective-permute-done((bf16[32,1024]{1,0:T(8,128)(2,1)S(1)}, bf16[32,1024]{1,0:T(8,128)(2,1)S(1)}, u32[]{:S(2)}, u32[]{:S(2)}) %collective-permute-start.43) | collective-permute-done | bytes 65568 | tf_op jit(solution)/shard_map/child/ppermute | solution.py:36
  214.8 2.6 %child.17 = bf16[4,32,512]{2,1,0:T(8,128)(2,1)S(1)} custom-call(s32[4]{0:T(128)S(1)} %and_convert_fusion.refs_0_, f32[32,1024]{1,0:T(8,128)S(1)} %bitcast_subtract_fusion.refs_1_, bf16[32,1024]{1,0:T(8,128)(2,1)S(1)} %collective-permute-done.43.refs_2_, bf16[512,1024]{1,0:T(8,128)(2,1)} %bitcast.2.refs_2_.refs_1_.refs_3_, ...), custom_call_target="tpu_custom_call" | custom-call | flops 134217728 | bytes 4194304 | tf_op jit(solution)/shard_map/child/pallas_call | solution.py:106
  217.4 1.9 collective-permute-start.46
  219.3 1.3 collective-permute-start.45
  220.6 1.3 collective-permute-start.44
  223.1 8.0 %collective-permute-done.44 = bf16[4,32,512]{2,1,0:T(8,128)(2,1)S(1)} collective-permute-done((bf16[4,32,512]{2,1,0:T(8,128)(2,1)S(1)}, bf16[4,32,512]{2,1,0:T(8,128)(2,1)S(1)}, u32[]{:S(2)}, u32[]{:S(2)}) %collective-permute-start.44) | collective-permute-done | bytes 131104 | tf_op jit(solution)/shard_map/child/ppermute | solution.py:36
  232.5 1.9 collective-permute-done.47
  234.5 8.2 %all_to_all.33 = bf16[4,32,512]{2,1,0:T(8,128)(2,1)S(1)} all-to-all(bf16[4,32,512]{2,1,0:T(8,128)(2,1)S(1)} %bitcast.27), channel_id=1, replica_groups={{0,8,16,24},{32,40,48,56},{64,72,80,88},{96,104,112,120},{1,9,17,25},{3..., dimensions={0} | all-to-all | bytes 262144 | tf_op jit(solution)/shard_map/child/all_to_all | solution.py:268
  (138 shorter events, 37.6 us)
Async XLA Ops:
  0.6 27.4 %collective-permute-start.1 = (bf16[768,1536]{1,0:T(8,128)(2,1)}, bf16[768,1536]{1,0:T(8,128)(2,1)S(1)}, u32[]{:S(2)}, u32[]{:S(2)}) collective-permute-start(bf16[768,1536]{1,0:T(8,128)(2,1)} %refs_4_.5), channel_id=1, source_target_pairs={{0,8},{8,0},{16,24},{24,16},{32,40},{40,32},{48,56},{56,48},{64,72... | collective-permute-start | bytes 7077896 | tf_op jit(solution)/shard_map/mask/ppermute | solution.py:184
  11.1 16.9 %all-to-all-start = ((bf16[64,12,128]{2,1,0:T(8,128)(2,1)}), bf16[64,12,128]{2,1,0:T(8,128)(2,1)S(1)}, u32[]{:S(2)}, u32[]{:S(2)}) async-start(bf16[64,12,128]{2,1,0:T(8,128)(2,1)} %bitcast.24), calls=%async_computation | async-start | bytes 524288 | tf_op jit(solution)/shard_map/rhs/all_to_all | solution.py:197
  15.9 17.3 %collective-permute-start = (s32[3,6]{1,0:T(4,128)}, s32[3,6]{1,0:T(4,128)S(1)}, u32[]{:S(2)}, u32[]{:S(2)}) collective-permute-start(s32[3,6]{1,0:T(4,128)} %param.8), channel_id=1, source_target_pairs={{0,8},{8,0},{16,24},{24,16},{32,40},{40,32},{48,56},{56,48},{64,72... | collective-permute-start | bytes 224 | tf_op jit(solution)/shard_map/mask/ppermute | solution.py:185
  31.9 7.0 %collective-permute-start.3 = (bf16[2,16,768]{2,1,0:T(8,128)(2,1)S(1)}, bf16[2,16,768]{2,1,0:T(8,128)(2,1)S(1)}, u32[]{:S(2)}, u32[]{:S(2)}) collective-permute-start(bf16[2,16,768]{2,1,0:T(8,128)(2,1)S(1)} %root.9), channel_id=1, source_target_pairs={{102,101},{103,100},{110,109},{111,108},{118,117},{119,116},{126,1... | collective-permute-start | bytes 147464 | tf_op jit(solution)/shard_map/root/ppermute | solution.py:36
  32.5 6.3 %collective-permute-start.2 = (bf16[2,16,768]{2,1,0:T(8,128)(2,1)S(1)}, bf16[2,16,768]{2,1,0:T(8,128)(2,1)S(1)}, u32[]{:S(2)}, u32[]{:S(2)}) collective-permute-start(bf16[2,16,768]{2,1,0:T(8,128)(2,1)S(1)} %root.9), channel_id=1, source_target_pairs={{102,100},{103,101},{110,108},{111,109},{118,116},{119,117},{126,1... | collective-permute-start | bytes 147464 | tf_op jit(solution)/shard_map/root/ppermute | solution.py:36
  33.2 26.4 %collective-permute-start.11 = (bf16[512,1024]{1,0:T(8,128)(2,1)}, bf16[512,1024]{1,0:T(8,128)(2,1)S(1)}, u32[]{:S(2)}, u32[]{:S(2)}) collective-permute-start(bf16[512,1024]{1,0:T(8,128)(2,1)} %bitcast.2.refs_2_.refs_1_.refs_3_), channel_id=1, source_target_pairs={{0,16},{8,24},{16,0},{24,8},{32,48},{40,56},{48,32},{56,40},{1,17}... | collective-permute-start | bytes 3145736 | tf_op jit(solution)/shard_map/root/ppermute | solution.py:220
  36.3 23.3 %collective-permute-start.10 = (bf16[512,1024]{1,0:T(8,128)(2,1)}, bf16[512,1024]{1,0:T(8,128)(2,1)S(1)}, u32[]{:S(2)}, u32[]{:S(2)}) collective-permute-start(bf16[512,1024]{1,0:T(8,128)(2,1)} %bitcast.2.refs_2_.refs_1_.refs_3_), channel_id=1, source_target_pairs={{0,8},{8,0},{16,24},{24,16},{32,40},{40,32},{48,56},{56,48},{1,9},... | collective-permute-start | bytes 3145736 | tf_op jit(solution)/shard_map/root/ppermute | solution.py:221
  40.6 2.0 collective-permute-start.5
  41.3 1.4 collective-permute-start.4
  41.9 2.9 %collective-permute-start.6 = (bf16[2,16,768]{2,1,0:T(8,128)(2,1)S(1)}, bf16[2,16,768]{2,1,0:T(8,128)(2,1)S(1)}, u32[]{:S(2)}, u32[]{:S(2)}) collective-permute-start(bf16[2,16,768]{2,1,0:T(8,128)(2,1)S(1)} %add_convert_fusion.13.refs_2_.refs_6_), channel_id=1, source_target_pairs={{100,98},{101,99},{108,106},{109,107},{116,114},{117,115},{124,122... | collective-permute-start | bytes 147464 | tf_op jit(solution)/shard_map/root/ppermute | solution.py:36
  44.9 3.7 %collective-permute-start.8 = (bf16[2,16,768]{2,1,0:T(8,128)(2,1)S(1)}, bf16[2,16,768]{2,1,0:T(8,128)(2,1)S(1)}, u32[]{:S(2)}, u32[]{:S(2)}) collective-permute-start(bf16[2,16,768]{2,1,0:T(8,128)(2,1)S(1)} %add_convert_fusion.12.refs_2_), channel_id=1, source_target_pairs={{68,67},{69,66},{76,75},{77,74},{84,83},{85,82},{92,91},{93,90},{1... | collective-permute-start | bytes 147464 | tf_op jit(solution)/shard_map/root/ppermute | solution.py:36
  45.5 3.0 %collective-permute-start.7 = (bf16[2,16,768]{2,1,0:T(8,128)(2,1)S(1)}, bf16[2,16,768]{2,1,0:T(8,128)(2,1)S(1)}, u32[]{:S(2)}, u32[]{:S(2)}) collective-permute-start(bf16[2,16,768]{2,1,0:T(8,128)(2,1)S(1)} %add_convert_fusion.12.refs_2_), channel_id=1, source_target_pairs={{68,66},{69,67},{76,74},{77,75},{84,82},{85,83},{92,90},{93,91},{9... | collective-permute-start | bytes 147464 | tf_op jit(solution)/shard_map/root/ppermute | solution.py:36
  47.9 0.7 collective-permute-start.9
  59.6 5.2 %collective-permute-start.13 = (bf16[16,1536]{1,0:T(8,128)(2,1)S(1)}, bf16[16,1536]{1,0:T(8,128)(2,1)S(1)}, u32[]{:S(2)}, u32[]{:S(2)}) collective-permute-start(bf16[16,1536]{1,0:T(8,128)(2,1)S(1)} %root.13), channel_id=1, source_target_pairs={{66,50},{67,51},{74,58},{75,59},{82,34},{83,35},{90,42},{91,43},{1... | collective-permute-start | bytes 147464 | tf_op jit(solution)/shard_map/root/ppermute | solution.py:36
  60.3 4.6 %collective-permute-start.12 = (bf16[16,1536]{1,0:T(8,128)(2,1)S(1)}, bf16[16,1536]{1,0:T(8,128)(2,1)S(1)}, u32[]{:S(2)}, u32[]{:S(2)}) collective-permute-start(bf16[16,1536]{1,0:T(8,128)(2,1)S(1)} %root.13), channel_id=1, source_target_pairs={{66,34},{67,35},{74,42},{75,43},{82,50},{83,51},{90,58},{91,59},{9... | collective-permute-start | bytes 147464 | tf_op jit(solution)/shard_map/root/ppermute | solution.py:36
  61.0 6.1 %collective-permute-start.14 = (bf16[2,16,768]{2,1,0:T(8,128)(2,1)S(1)}, bf16[2,16,768]{2,1,0:T(8,128)(2,1)S(1)}, u32[]{:S(2)}, u32[]{:S(2)}) collective-permute-start(bf16[2,16,768]{2,1,0:T(8,128)(2,1)S(1)} %add_convert_fusion.11.refs_2_.refs_6_), channel_id=1, source_target_pairs={{66,64},{67,65},{74,72},{75,73},{82,80},{83,81},{90,88},{91,89},{1... | collective-permute-start | bytes 147464 | tf_op jit(solution)/shard_map/root/ppermute | solution.py:36
  61.6 10.9 %collective-permute-start.18 = (bf16[512,1024]{1,0:T(8,128)(2,1)S(1)}, bf16[512,1024]{1,0:T(8,128)(2,1)S(1)}, u32[]{:S(2)}, u32[]{:S(2)}) collective-permute-start(bf16[512,1024]{1,0:T(8,128)(2,1)S(1)} %collective-permute-done.11), channel_id=1, source_target_pairs={{0,8},{8,0},{16,24},{24,16},{32,40},{40,32},{48,56},{56,48},{1,9},... | collective-permute-start | bytes 3145736 | tf_op jit(solution)/shard_map/root/ppermute | solution.py:214
  67.1 3.7 %collective-permute-start.16 = (bf16[2,16,768]{2,1,0:T(8,128)(2,1)S(1)}, bf16[2,16,768]{2,1,0:T(8,128)(2,1)S(1)}, u32[]{:S(2)}, u32[]{:S(2)}) collective-permute-start(bf16[2,16,768]{2,1,0:T(8,128)(2,1)S(1)} %add_convert_fusion.10.refs_2_), channel_id=1, source_target_pairs={{34,33},{35,32},{42,41},{43,40},{50,49},{51,48},{58,57},{59,56},{6... | collective-permute-start | bytes 147464 | tf_op jit(solution)/shard_map/root/ppermute | solution.py:36
  67.8 3.0 %collective-permute-start.15 = (bf16[2,16,768]{2,1,0:T(8,128)(2,1)S(1)}, bf16[2,16,768]{2,1,0:T(8,128)(2,1)S(1)}, u32[]{:S(2)}, u32[]{:S(2)}) collective-permute-start(bf16[2,16,768]{2,1,0:T(8,128)(2,1)S(1)} %add_convert_fusion.10.refs_2_), channel_id=1, source_target_pairs={{34,32},{35,33},{42,40},{43,41},{50,48},{51,49},{58,56},{59,57},{6... | collective-permute-start | bytes 147464 | tf_op jit(solution)/shard_map/root/ppermute | solution.py:36
  70.2 0.7 collective-permute-start.17
  72.6 35.0 %collective-permute-start.25 = (bf16[512,1024]{1,0:T(8,128)(2,1)}, bf16[512,1024]{1,0:T(8,128)(2,1)}, u32[]{:S(2)}, u32[]{:S(2)}) collective-permute-start(bf16[512,1024]{1,0:T(8,128)(2,1)} %bitcast.2.refs_2_.refs_1_.refs_3_), channel_id=1, source_target_pairs={{64,80},{72,88},{80,64},{88,72},{96,112},{104,120},{112,96},{120,1... | collective-permute-start | bytes 3145736 | tf_op jit(solution)/shard_map/root/ppermute | solution.py:220
  74.2 14.3 %collective-permute-start.20 = (bf16[16,1536]{1,0:T(8,128)(2,1)S(1)}, bf16[16,1536]{1,0:T(8,128)(2,1)S(1)}, u32[]{:S(2)}, u32[]{:S(2)}) collective-permute-start(bf16[16,1536]{1,0:T(8,128)(2,1)S(1)} %root.16), channel_id=1, source_target_pairs={{32,16},{33,17},{40,24},{41,25},{48,0},{49,1},{56,8},{57,9},{160,1... | collective-permute-start | bytes 147464 | tf_op jit(solution)/shard_map/root/ppermute | solution.py:36
  75.5 19.4 %collective-permute-start.19 = (bf16[16,1536]{1,0:T(8,128)(2,1)S(1)}, bf16[16,1536]{1,0:T(8,128)(2,1)S(1)}, u32[]{:S(2)}, u32[]{:S(2)}) collective-permute-start(bf16[16,1536]{1,0:T(8,128)(2,1)S(1)} %root.16), channel_id=1, source_target_pairs={{32,0},{33,1},{40,8},{41,9},{48,16},{49,17},{56,24},{57,25},{160,1... | collective-permute-start | bytes 147464 | tf_op jit(solution)/shard_map/root/ppermute | solution.py:36
  97.1 5.0 %collective-permute-start.23 = (bf16[2,16,768]{2,1,0:T(8,128)(2,1)S(1)}, bf16[2,16,768]{2,1,0:T(8,128)(2,1)S(1)}, u32[]{:S(2)}, u32[]{:S(2)}) collective-permute-start(bf16[2,16,768]{2,1,0:T(8,128)(2,1)S(1)} %root.17), channel_id=1, source_target_pairs={{0,1},{1,0},{8,9},{9,8},{16,17},{17,16},{24,25},{25,24},{128,129},... | collective-permute-start | bytes 147464 | tf_op jit(solution)/shard_map/root/ppermute | solution.py:36
  99.2 2.9 %collective-permute-start.22 = (bf16[2,16,768]{2,1,0:T(8,128)(2,1)S(1)}, bf16[2,16,768]{2,1,0:T(8,128)(2,1)S(1)}, u32[]{:S(2)}, u32[]{:S(2)}) collective-permute-start(bf16[2,16,768]{2,1,0:T(8,128)(2,1)S(1)} %root.17), channel_id=1, source_target_pairs={{0,7},{1,6},{8,15},{9,14},{16,23},{17,22},{24,31},{25,30},{34,35},... | collective-permute-start | bytes 147464 | tf_op jit(solution)/shard_map/root/ppermute | solution.py:36
  100.5 4.1 %collective-permute-start.21 = (bf16[2,16,768]{2,1,0:T(8,128)(2,1)S(1)}, bf16[2,16,768]{2,1,0:T(8,128)(2,1)S(1)}, u32[]{:S(2)}, u32[]{:S(2)}) collective-permute-start(bf16[2,16,768]{2,1,0:T(8,128)(2,1)S(1)} %root.17), channel_id=1, source_target_pairs={{0,6},{1,7},{8,14},{9,15},{16,22},{17,23},{24,30},{25,31},{32,38},... | collective-permute-start | bytes 147464 | tf_op jit(solution)/shard_map/root/ppermute | solution.py:36
  104.6 3.0 %collective-permute-start.24 = (bf16[2,16,768]{2,1,0:T(8,128)(2,1)S(1)}, bf16[2,16,768]{2,1,0:T(8,128)(2,1)S(1)}, u32[]{:S(2)}, u32[]{:S(2)}) collective-permute-start(bf16[2,16,768]{2,1,0:T(8,128)(2,1)S(1)} %add_convert_fusion.8), channel_id=1, source_target_pairs={{0,2},{1,3},{8,10},{9,11},{16,18},{17,19},{24,26},{25,27},{6,4},{7... | collective-permute-start | bytes 147464 | tf_op jit(solution)/shard_map/root/ppermute | solution.py:36
  105.9 27.5 %collective-permute-start.29 = (bf16[512,1024]{1,0:T(8,128)(2,1)}, bf16[512,1024]{1,0:T(8,128)(2,1)}, u32[]{:S(2)}, u32[]{:S(2)}) collective-permute-start(bf16[512,1024]{1,0:T(8,128)(2,1)} %bitcast.2.refs_2_.refs_1_.refs_3_), channel_id=1, source_target_pairs={{64,72},{72,64},{80,88},{88,80},{96,104},{104,96},{112,120},{120,1... | collective-permute-start | bytes 3145736 | tf_op jit(solution)/shard_map/root/ppermute | solution.py:221
  108.3 10.6 %all-to-all-start.1 = ((bf16[8,16,768]{2,1,0:T(8,128)(2,1)}), bf16[8,16,768]{2,1,0:T(8,128)(2,1)S(1)}, u32[]{:S(2)}, u32[]{:S(2)}) async-start(bf16[8,16,768]{2,1,0:T(8,128)(2,1)} %bitcast.3), calls=%async_computation.1 | async-start | bytes 393216 | tf_op jit(solution)/shard_map/coupling/all_to_all | solution.py:241
  113.0 26.7 %collective-permute-start.30 = (bf16[512,1024]{1,0:T(8,128)(2,1)}, bf16[512,1024]{1,0:T(8,128)(2,1)}, u32[]{:S(2)}, u32[]{:S(2)}) collective-permute-start(bf16[512,1024]{1,0:T(8,128)(2,1)} %collective-permute-done.25), channel_id=1, source_target_pairs={{64,72},{72,64},{80,88},{88,80},{96,104},{104,96},{112,120},{120,1... | collective-permute-start | bytes 3145736 | tf_op jit(solution)/shard_map/coupling/ppermute | solution.py:236
  127.9 7.3 %collective-permute-start.28 = (bf16[32,1024]{1,0:T(8,128)(2,1)S(1)}, bf16[32,1024]{1,0:T(8,128)(2,1)S(1)}, u32[]{:S(2)}, u32[]{:S(2)}) collective-permute-start(bf16[32,1024]{1,0:T(8,128)(2,1)S(1)} %reduce_sum.22), channel_id=1, source_target_pairs={{96,0},{97,1},{104,8},{105,9},{112,16},{113,17},{120,24},{121,25},... | collective-permute-start | bytes 196616 | tf_op jit(solution)/shard_map/coupling/ppermute | solution.py:36
  129.2 8.9 %collective-permute-start.27 = (bf16[32,1024]{1,0:T(8,128)(2,1)S(1)}, bf16[32,1024]{1,0:T(8,128)(2,1)S(1)}, u32[]{:S(2)}, u32[]{:S(2)}) collective-permute-start(bf16[32,1024]{1,0:T(8,128)(2,1)S(1)} %reduce_sum.22), channel_id=1, source_target_pairs={{64,0},{65,1},{72,8},{73,9},{80,16},{81,17},{88,24},{89,25},{98,34... | collective-permute-start | bytes 196616 | tf_op jit(solution)/shard_map/coupling/ppermute | solution.py:36
  130.5 8.3 %collective-permute-start.26 = (bf16[32,1024]{1,0:T(8,128)(2,1)S(1)}, bf16[32,1024]{1,0:T(8,128)(2,1)S(1)}, u32[]{:S(2)}, u32[]{:S(2)}) collective-permute-start(bf16[32,1024]{1,0:T(8,128)(2,1)S(1)} %reduce_sum.22), channel_id=1, source_target_pairs={{32,0},{33,1},{40,8},{41,9},{48,16},{49,17},{56,24},{57,25},{66,34... | collective-permute-start | bytes 196616 | tf_op jit(solution)/shard_map/coupling/ppermute | solution.py:36
  143.9 1.4 collective-permute-start.32
  145.3 6.0 %collective-permute-start.34 = (bf16[4,32,512]{2,1,0:T(8,128)(2,1)S(1)}, bf16[4,32,512]{2,1,0:T(8,128)(2,1)S(1)}, u32[]{:S(2)}, u32[]{:S(2)}) collective-permute-start(bf16[4,32,512]{2,1,0:T(8,128)(2,1)S(1)} %add_convert_fusion.6.refs_0_.refs_7_), channel_id=1, source_target_pairs={{100,98},{101,99},{108,106},{109,107},{116,114},{117,115},{124,122... | collective-permute-start | bytes 393224 | tf_op jit(solution)/shard_map/child/ppermute | solution.py:36
  153.4 2.0 collective-permute-start.37
  154.1 1.4 collective-permute-start.36
  154.8 0.7 collective-permute-start.35
  157.6 1.4 collective-permute-start.38
  158.3 3.3 %collective-permute-start.39 = (bf16[4,32,512]{2,1,0:T(8,128)(2,1)S(1)}, bf16[4,32,512]{2,1,0:T(8,128)(2,1)S(1)}, u32[]{:S(2)}, u32[]{:S(2)}) collective-permute-start(bf16[4,32,512]{2,1,0:T(8,128)(2,1)S(1)} %add_convert_fusion.4.refs_0_.refs_7_), channel_id=1, source_target_pairs={{66,64},{67,65},{74,72},{75,73},{82,80},{83,81},{90,88},{91,89},{1... | collective-permute-start | bytes 393224 | tf_op jit(solution)/shard_map/child/ppermute | solution.py:36
  163.7 2.0 collective-permute-start.42
  164.4 1.4 collective-permute-start.41
  165.0 0.7 collective-permute-start.40
  167.9 47.0 %collective-permute-start.43 = (bf16[32,1024]{1,0:T(8,128)(2,1)S(1)}, bf16[32,1024]{1,0:T(8,128)(2,1)S(1)}, u32[]{:S(2)}, u32[]{:S(2)}) collective-permute-start(bf16[32,1024]{1,0:T(8,128)(2,1)S(1)} %child.16), channel_id=1, source_target_pairs={{32,0},{33,1},{40,8},{41,9},{48,16},{49,17},{56,24},{57,25},{160,1... | collective-permute-start | bytes 196616 | tf_op jit(solution)/shard_map/child/ppermute | solution.py:36
  217.4 5.7 %collective-permute-start.46 = (bf16[4,32,512]{2,1,0:T(8,128)(2,1)S(1)}, bf16[4,32,512]{2,1,0:T(8,128)(2,1)S(1)}, u32[]{:S(2)}, u32[]{:S(2)}) collective-permute-start(bf16[4,32,512]{2,1,0:T(8,128)(2,1)S(1)} %child.17), channel_id=1, source_target_pairs={{0,1},{1,0},{8,9},{9,8},{16,17},{17,16},{24,25},{25,24},{128,129},... | collective-permute-start | bytes 393224 | tf_op jit(solution)/shard_map/child/ppermute | solution.py:36
  219.3 3.8 %collective-permute-start.45 = (bf16[4,32,512]{2,1,0:T(8,128)(2,1)S(1)}, bf16[4,32,512]{2,1,0:T(8,128)(2,1)S(1)}, u32[]{:S(2)}, u32[]{:S(2)}) collective-permute-start(bf16[4,32,512]{2,1,0:T(8,128)(2,1)S(1)} %child.17), channel_id=1, source_target_pairs={{0,7},{1,6},{8,15},{9,14},{16,23},{17,22},{24,31},{25,30},{34,35},... | collective-permute-start | bytes 393224 | tf_op jit(solution)/shard_map/child/ppermute | solution.py:36
  220.6 10.5 %collective-permute-start.44 = (bf16[4,32,512]{2,1,0:T(8,128)(2,1)S(1)}, bf16[4,32,512]{2,1,0:T(8,128)(2,1)S(1)}, u32[]{:S(2)}, u32[]{:S(2)}) collective-permute-start(bf16[4,32,512]{2,1,0:T(8,128)(2,1)S(1)} %child.17), channel_id=1, source_target_pairs={{0,6},{1,7},{8,14},{9,15},{16,22},{17,23},{24,30},{25,31},{32,38},... | collective-permute-start | bytes 393224 | tf_op jit(solution)/shard_map/child/ppermute | solution.py:36
  231.2 3.2 %collective-permute-start.47 = (bf16[4,32,512]{2,1,0:T(8,128)(2,1)S(1)}, bf16[4,32,512]{2,1,0:T(8,128)(2,1)S(1)}, u32[]{:S(2)}, u32[]{:S(2)}) collective-permute-start(bf16[4,32,512]{2,1,0:T(8,128)(2,1)S(1)} %add_convert_fusion.1), channel_id=1, source_target_pairs={{0,2},{1,3},{8,10},{9,11},{16,18},{17,19},{24,26},{25,27},{6,4},{7... | collective-permute-start | bytes 393224 | tf_op jit(solution)/shard_map/child/ppermute | solution.py:36
  (12 other events, 239.9 us)

commit v9 on v8

--- a/solution.py
+++ b/solution.py
@@ -134,6 +134,8 @@
             sums = [send(terms, down)]
             if split_rows:
                 sums.append(send(terms, [(r + 1, r, 2, r, r, 0)]))
+            elif r < PANELS - 2:
+                sums.append(send(terms, [(r + 2, r, 0, r, r, 0)]))
             if r >= 1:
                 ahead = send(current, [(r + 1, r + 1, 0, r, r - 1, 0)])
             carried = carried + sums[0].astype(F32)
@@ -152,7 +154,7 @@
                 straight.append((2, 2, 0, 0, 3, 0))
                 crossed.append((2, 2, 0, 2, 2, 1))
             received = send(current, straight).astype(F32) + send(current, crossed).astype(F32)
-            if r < PANELS - 1:
+            if r < PANELS - 1 and split_rows:
                 terms = forward(current, carried)
                 carried = carried + send(terms, [(r + 1, r, 0, r - 1, r - 1, 0)]).astype(F32)
             current = (current.astype(F32) + received).astype(BF16)
@@ -254,13 +256,24 @@
 
     with jax.named_scope("child"):
         blocks = [child_here] + [moved[0, flip] + moved[1, flip] for flip in (1, 2, 3)]
-        child_rows = sweep(
-            child_rhs,
-            jnp.zeros((GROUP, share, child_here.shape[0]), BF16),
-            functools.partial(terms_of, [], 2, blocks),
-            functools.partial(pieces_of, solving, 2, blocks),
-            False,
-        )
+        rows = child_here.shape[0]
+        solves = (row_index // GROUP, col_index // PAIR)
+
+        def child_terms(current, carried):
+            for i, block in enumerate(blocks):
+                carried = carried + dot(current[:, i * rows : (i + 1) * rows], block)
+            return carried.astype(BF16)
+
+        def child_pieces(r, rhs, sums, current):
+            for part in sums:
+                rhs = rhs - part.astype(F32)
+            residual = rhs.astype(BF16)
+            piece = jnp.concatenate([dot_t(residual, block) for block in blocks], 1).astype(BF16)
+            return jnp.where((solves[0] == r) & (solves[1] == r), piece, current)
+
+        child_rows = jnp.zeros((share, GROUP * rows), BF16)
+        child_rows = sweep(child_rhs, child_rows, child_terms, child_pieces, False)
+        child_rows = child_rows.reshape(share, GROUP, rows).transpose(1, 0, 2)
         child_rows = child_rows.reshape(2, 2, share, -1)
         child_rows = jnp.where(core == 1, child_rows[:, ::-1], child_rows)
         child_rows = jnp.where(row_index % GROUP // 2 == 1, child_rows[::-1], child_rows)

time: 245 us -> 249 us (1.016)
  matrix products: 0.31 us -> 22.8 us
  Pallas kernels: 37.4 us -> 16.9 us
  blocking collectives: 16.6 us -> 26.1 us
  waiting for transfers between devices: 105 us -> 99.4 us
  starting transfers between devices: 71.4 us -> 67.6 us
    dot_general x0 -> x16, matrix products: none -> 15.3 us  [dot_t(): lax.dot_general(a, b, (((1,), (1,)), ((), ())), preferred_element_type=F32)]
    pallas_call x8 -> x4, Pallas kernels: 18.9 us -> 8.66 us  [pieces_of(): pl.pallas_call(functools.partial(pieces_kernel, r, count), grid=(steps,),...]
    pallas_call x10 -> x5, Pallas kernels: 18.4 us -> 8.29 us  [terms_of(): pl.pallas_call(functools.partial(terms_kernel, count, len(keep) > 0), gri...]
    all_to_all x0 -> x1, blocking collectives: none -> 9.68 us  [per_device(): lax.all_to_all(shared, ('gz', 'row'), 0, 0, tiled=True, axis_index_groups...]
    dot_general x1 -> x13, matrix products: 0.31 us -> 7.47 us  [dot(): return jnp.dot(a, b, preferred_element_type=F32)]
    all_to_all x1 -> x0, starting transfers between devices: 4.69 us -> none  [per_device(): lax.all_to_all(shared, ('gz', 'row'), 0, 0, tiled=True, axis_index_groups...]
    all_to_all x1 -> x0, waiting for transfers between devices: 4.26 us -> none  [per_device(): lax.all_to_all(shared, ('gz', 'row'), 0, 0, tiled=True, axis_index_groups...]
  transfers between devices with their start and end apart: 50 -> 49, of which waited for: 13 -> 13; matrix products, arithmetic and copies ran while one was open for 3% -> 7% of each run, Pallas kernels for 10% -> 7%
where the time goes in v9:
time: 249 us; the launch traced here: 247 us
  waiting for transfers between devices  99.4 us (40%)
  starting transfers between devices  67.6 us (27%)
  blocking collectives  26.1 us (10%)
  matrix products  22.8 us (9%)
  Pallas kernels  16.9 us (7%)
  other arithmetic  7.29 us (3%)
  local copies, waits for them, and re-layouts  4.92 us (2%)
    ppermute x40, waiting for transfers between devices, send(): return lax.ppermute(value, GRID, pairs)  80.5 us
    ppermute x40, starting transfers between devices, send(): return lax.ppermute(value, GRID, pairs)  37.7 us
    dot_general x16, matrix products, dot_t(): lax.dot_general(a, b, (((1,), (1,)), ((), ())), preferred_element_type=F32)  15.3 us
    all_to_all x1, blocking collectives, per_device(): lax.all_to_all(shared, ('gz', 'row'), 0, 0, tiled=True, axis_index_groups...  9.68 us
    all_to_all x1, waiting for transfers between devices, per_device(): lax.all_to_all(pieces.reshape(layers * ROWS, 12, lanes), ('gz', 'row'), 0...  9.56 us
    ppermute x2, waiting for transfers between devices, move_children(): moved[half, 2] = lax.ppermute(here, 'row', rows_of(half, 2))  9.32 us
    ppermute x1, starting transfers between devices, per_device(): partner_factor = lax.ppermute(root_factor, 'row', swap)  8.92 us
    pallas_call x4, Pallas kernels, pieces_of(): pl.pallas_call(functools.partial(pieces_kernel, r, count), grid=(steps,),...  8.66 us
  transfers between devices with their start and end apart: 49, of which 13 were waited for; matrix products, arithmetic and copies ran while one was open for 7% of the time, Pallas kernels for 7%

profile of v9, /device:TPU:1, one launch (start us, length us, event | category | flops | bytes accessed | tf_op | source)
XLA Modules:
  0.0 247.0 jit_solution(16999748880942103752)
XLA Ops:
  0.6 8.9 %collective-permute-start.1 = (bf16[768,1536]{1,0:T(8,128)(2,1)}, bf16[768,1536]{1,0:T(8,128)(2,1)S(1)}, u32[]{:S(2)}, u32[]{:S(2)}) collective-permute-start(bf16[768,1536]{1,0:T(8,128)(2,1)} %refs_4_.5), channel_id=1, source_target_pairs={{0,8},{8,0},{16,24},{24,16},{32,40},{40,32},{48,56},{56,48},{64,72... | collective-permute-start | bytes 7077896 | tf_op jit(solution)/shard_map/mask/ppermute | solution.py:186
  11.1 4.9 %all-to-all-start = ((bf16[64,12,128]{2,1,0:T(8,128)(2,1)}), bf16[64,12,128]{2,1,0:T(8,128)(2,1)S(1)}, u32[]{:S(2)}, u32[]{:S(2)}) async-start(bf16[64,12,128]{2,1,0:T(8,128)(2,1)} %bitcast.78), calls=%async_computation | async-start | bytes 524288 | tf_op jit(solution)/shard_map/rhs/all_to_all | solution.py:199
  15.9 2.4 collective-permute-start
  18.4 9.6 %all-to-all-done = bf16[64,12,128]{2,1,0:T(8,128)(2,1)S(1)} async-done(((bf16[64,12,128]{2,1,0:T(8,128)(2,1)}), bf16[64,12,128]{2,1,0:T(8,128)(2,1)S(1)}, u32[]{:S(2)}, u32[]{:S(2)}) %all-to-all-start) | async-done | bytes 196640 | tf_op jit(solution)/shard_map/rhs/all_to_all | solution.py:199
  28.1 1.7 copy-done.1
  29.7 2.1 root.9
  33.2 3.1 %collective-permute-start.11 = (bf16[512,1024]{1,0:T(8,128)(2,1)}, bf16[512,1024]{1,0:T(8,128)(2,1)S(1)}, u32[]{:S(2)}, u32[]{:S(2)}) collective-permute-start(bf16[512,1024]{1,0:T(8,128)(2,1)} %bitcast.2), channel_id=1, source_target_pairs={{0,16},{8,24},{16,0},{24,8},{32,48},{40,56},{48,32},{56,40},{1,17}... | collective-permute-start | bytes 3145736 | tf_op jit(solution)/shard_map/root/ppermute | solution.py:222
  36.3 2.5 %collective-permute-start.10 = (bf16[512,1024]{1,0:T(8,128)(2,1)}, bf16[512,1024]{1,0:T(8,128)(2,1)S(1)}, u32[]{:S(2)}, u32[]{:S(2)}) collective-permute-start(bf16[512,1024]{1,0:T(8,128)(2,1)} %bitcast.2), channel_id=1, source_target_pairs={{0,8},{8,0},{16,24},{24,16},{32,40},{40,32},{48,56},{56,48},{1,9},... | collective-permute-start | bytes 3145736 | tf_op jit(solution)/shard_map/root/ppermute | solution.py:223
  38.9 1.7 root.10
  42.6 2.2 root.11
  46.2 1.7 root.12
  48.6 1.7 root.13
  50.3 9.3 %collective-permute-done.11 = bf16[512,1024]{1,0:T(8,128)(2,1)S(1)} collective-permute-done((bf16[512,1024]{1,0:T(8,128)(2,1)}, bf16[512,1024]{1,0:T(8,128)(2,1)S(1)}, u32[]{:S(2)}, u32[]{:S(2)}) %collective-permute-start.11) | collective-permute-done | bytes 1048608 | tf_op jit(solution)/shard_map/root/ppermute | solution.py:222
  61.6 3.2 %collective-permute-start.18 = (bf16[512,1024]{1,0:T(8,128)(2,1)S(1)}, bf16[512,1024]{1,0:T(8,128)(2,1)S(1)}, u32[]{:S(2)}, u32[]{:S(2)}) collective-permute-start(bf16[512,1024]{1,0:T(8,128)(2,1)S(1)} %collective-permute-done.11), channel_id=1, source_target_pairs={{0,8},{8,0},{16,24},{24,16},{32,40},{40,32},{48,56},{56,48},{1,9},... | collective-permute-start | bytes 3145736 | tf_op jit(solution)/shard_map/root/ppermute | solution.py:216
  64.9 2.2 root.14
  68.5 1.7 root.15
  70.9 1.7 root.16
  72.6 1.6 collective-permute-start.25
  76.8 11.7 %collective-permute-done.20.refs_3_ = bf16[16,1536]{1,0:T(8,128)(2,1)S(1)} collective-permute-done((bf16[16,1536]{1,0:T(8,128)(2,1)S(1)}, bf16[16,1536]{1,0:T(8,128)(2,1)S(1)}, u32[]{:S(2)}, u32[]{:S(2)}) %collective-permute-start.20) | collective-permute-done | bytes 49184 | tf_op jit(solution)/shard_map/root/ppermute | solution.py:36
  88.5 6.4 %collective-permute-done.19.refs_2_ = bf16[16,1536]{1,0:T(8,128)(2,1)S(1)} collective-permute-done((bf16[16,1536]{1,0:T(8,128)(2,1)S(1)}, bf16[16,1536]{1,0:T(8,128)(2,1)S(1)}, u32[]{:S(2)}, u32[]{:S(2)}) %collective-permute-start.19) | collective-permute-done | bytes 49184 | tf_op jit(solution)/shard_map/root/ppermute | solution.py:36
  94.9 2.2 root.17
  97.1 2.1 collective-permute-start.23
  102.1 2.5 %collective-permute-done.21 = bf16[2,16,768]{2,1,0:T(8,128)(2,1)S(1)} collective-permute-done((bf16[2,16,768]{2,1,0:T(8,128)(2,1)S(1)}, bf16[2,16,768]{2,1,0:T(8,128)(2,1)S(1)}, u32[]{:S(2)}, u32[]{:S(2)}) %collective-permute-start.21) | collective-permute-done | bytes 49184 | tf_op jit(solution)/shard_map/root/ppermute | solution.py:36
  105.9 1.7 collective-permute-start.29
  107.7 9.7 %all_to_all.32 = bf16[8,16,768]{2,1,0:T(8,128)(2,1)S(1)} all-to-all(bf16[8,16,768]{2,1,0:T(8,128)(2,1)S(1)} %bitcast.80), channel_id=1, replica_groups={{0,8,128,136,256,264,384,392},{16,24,144,152,272,280,400,408},{32,40,16..., dimensions={0} | all-to-all | bytes 393216 | tf_op jit(solution)/shard_map/coupling/all_to_all | solution.py:243
  117.7 8.3 %all_to_all.33 = bf16[4,32,1024]{2,1,0:T(8,128)(2,1)S(1)} all-to-all(bf16[4,32,1024]{2,1,0:T(8,128)(2,1)S(1)} %bitcast.79), channel_id=1, replica_groups={{0,8,16,24},{32,40,48,56},{64,72,80,88},{96,104,112,120},{1,9,17,25},{3..., dimensions={0} | all-to-all | bytes 524288 | tf_op jit(solution)/shard_map/coupling/all_to_all | solution.py:247
  130.0 1.6 collective-permute-start.30
  131.7 1.6 add.173
  133.3 1.9 add.172
  138.0 1.6 convolution_convert_fusion.16
  140.6 1.6 add.174
  144.4 1.5 fusion.37
  147.9 1.6 convolution_convert_fusion.9
  150.4 1.6 convolution_convert_fusion.12
  154.6 1.5 fusion.4
  158.2 1.6 convolution_convert_fusion.5
  160.7 1.6 convolution_convert_fusion.8
  164.6 1.5 fusion.24
  169.0 35.4 %collective-permute-done.43 = bf16[32,1024]{1,0:T(8,128)(2,1)S(1)} collective-permute-done((bf16[32,1024]{1,0:T(8,128)(2,1)S(1)}, bf16[32,1024]{1,0:T(8,128)(2,1)S(1)}, u32[]{:S(2)}, u32[]{:S(2)}) %collective-permute-start.43) | collective-permute-done | bytes 65568 | tf_op jit(solution)/shard_map/child/ppermute | solution.py:36
  204.5 11.2 %collective-permute-done.42 = bf16[32,1024]{1,0:T(8,128)(2,1)S(1)} collective-permute-done((bf16[32,1024]{1,0:T(8,128)(2,1)S(1)}, bf16[32,1024]{1,0:T(8,128)(2,1)S(1)}, u32[]{:S(2)}, u32[]{:S(2)}) %collective-permute-start.42) | collective-permute-done | bytes 65568 | tf_op jit(solution)/shard_map/child/ppermute | solution.py:36
  215.7 1.6 convolution_convert_fusion.1
  218.2 1.6 convolution_convert_fusion.4
  219.9 1.9 collective-permute-start.46
  221.8 1.3 collective-permute-start.45
  223.1 1.3 collective-permute-start.44
  225.6 8.1 %collective-permute-done.44 = bf16[32,2048]{1,0:T(8,128)(2,1)S(1)} collective-permute-done((bf16[32,2048]{1,0:T(8,128)(2,1)S(1)}, bf16[32,2048]{1,0:T(8,128)(2,1)S(1)}, u32[]{:S(2)}, u32[]{:S(2)}) %collective-permute-start.44) | collective-permute-done | bytes 131104 | tf_op jit(solution)/shard_map/child/ppermute | solution.py:36
  235.1 1.9 collective-permute-done.47
  238.2 8.1 %all_to_all.34 = bf16[4,32,512]{2,1,0:T(8,128)(2,1)S(1)} all-to-all(bf16[4,32,512]{2,1,0:T(8,128)(2,1)S(1)} %bitcast.82), channel_id=1, replica_groups={{0,8,16,24},{32,40,48,56},{64,72,80,88},{96,104,112,120},{1,9,17,25},{3..., dimensions={0} | all-to-all | bytes 262144 | tf_op jit(solution)/shard_map/child/all_to_all | solution.py:281
  (163 shorter events, 46.6 us)
Async XLA Ops:
  0.6 27.4 %collective-permute-start.1 = (bf16[768,1536]{1,0:T(8,128)(2,1)}, bf16[768,1536]{1,0:T(8,128)(2,1)S(1)}, u32[]{:S(2)}, u32[]{:S(2)}) collective-permute-start(bf16[768,1536]{1,0:T(8,128)(2,1)} %refs_4_.5), channel_id=1, source_target_pairs={{0,8},{8,0},{16,24},{24,16},{32,40},{40,32},{48,56},{56,48},{64,72... | collective-permute-start | bytes 7077896 | tf_op jit(solution)/shard_map/mask/ppermute | solution.py:186
  11.1 16.9 %all-to-all-start = ((bf16[64,12,128]{2,1,0:T(8,128)(2,1)}), bf16[64,12,128]{2,1,0:T(8,128)(2,1)S(1)}, u32[]{:S(2)}, u32[]{:S(2)}) async-start(bf16[64,12,128]{2,1,0:T(8,128)(2,1)} %bitcast.78), calls=%async_computation | async-start | bytes 524288 | tf_op jit(solution)/shard_map/rhs/all_to_all | solution.py:199
  15.9 17.3 %collective-permute-start = (s32[3,6]{1,0:T(4,128)}, s32[3,6]{1,0:T(4,128)S(1)}, u32[]{:S(2)}, u32[]{:S(2)}) collective-permute-start(s32[3,6]{1,0:T(4,128)} %param.8), channel_id=1, source_target_pairs={{0,8},{8,0},{16,24},{24,16},{32,40},{40,32},{48,56},{56,48},{64,72... | collective-permute-start | bytes 224 | tf_op jit(solution)/shard_map/mask/ppermute | solution.py:187
  31.9 7.0 %collective-permute-start.3 = (bf16[2,16,768]{2,1,0:T(8,128)(2,1)S(1)}, bf16[2,16,768]{2,1,0:T(8,128)(2,1)S(1)}, u32[]{:S(2)}, u32[]{:S(2)}) collective-permute-start(bf16[2,16,768]{2,1,0:T(8,128)(2,1)S(1)} %root.9), channel_id=1, source_target_pairs={{102,101},{103,100},{110,109},{111,108},{118,117},{119,116},{126,1... | collective-permute-start | bytes 147464 | tf_op jit(solution)/shard_map/root/ppermute | solution.py:36
  32.5 6.3 %collective-permute-start.2 = (bf16[2,16,768]{2,1,0:T(8,128)(2,1)S(1)}, bf16[2,16,768]{2,1,0:T(8,128)(2,1)S(1)}, u32[]{:S(2)}, u32[]{:S(2)}) collective-permute-start(bf16[2,16,768]{2,1,0:T(8,128)(2,1)S(1)} %root.9), channel_id=1, source_target_pairs={{102,100},{103,101},{110,108},{111,109},{118,116},{119,117},{126,1... | collective-permute-start | bytes 147464 | tf_op jit(solution)/shard_map/root/ppermute | solution.py:36
  33.2 26.4 %collective-permute-start.11 = (bf16[512,1024]{1,0:T(8,128)(2,1)}, bf16[512,1024]{1,0:T(8,128)(2,1)S(1)}, u32[]{:S(2)}, u32[]{:S(2)}) collective-permute-start(bf16[512,1024]{1,0:T(8,128)(2,1)} %bitcast.2), channel_id=1, source_target_pairs={{0,16},{8,24},{16,0},{24,8},{32,48},{40,56},{48,32},{56,40},{1,17}... | collective-permute-start | bytes 3145736 | tf_op jit(solution)/shard_map/root/ppermute | solution.py:222
  36.3 23.3 %collective-permute-start.10 = (bf16[512,1024]{1,0:T(8,128)(2,1)}, bf16[512,1024]{1,0:T(8,128)(2,1)S(1)}, u32[]{:S(2)}, u32[]{:S(2)}) collective-permute-start(bf16[512,1024]{1,0:T(8,128)(2,1)} %bitcast.2), channel_id=1, source_target_pairs={{0,8},{8,0},{16,24},{24,16},{32,40},{40,32},{48,56},{56,48},{1,9},... | collective-permute-start | bytes 3145736 | tf_op jit(solution)/shard_map/root/ppermute | solution.py:223
  40.6 2.0 collective-permute-start.5
  41.3 1.4 collective-permute-start.4
  41.9 2.9 %collective-permute-start.6 = (bf16[2,16,768]{2,1,0:T(8,128)(2,1)S(1)}, bf16[2,16,768]{2,1,0:T(8,128)(2,1)S(1)}, u32[]{:S(2)}, u32[]{:S(2)}) collective-permute-start(bf16[2,16,768]{2,1,0:T(8,128)(2,1)S(1)} %add_convert_fusion.13.refs_2_.refs_6_), channel_id=1, source_target_pairs={{100,98},{101,99},{108,106},{109,107},{116,114},{117,115},{124,122... | collective-permute-start | bytes 147464 | tf_op jit(solution)/shard_map/root/ppermute | solution.py:36
  44.9 3.7 %collective-permute-start.8 = (bf16[2,16,768]{2,1,0:T(8,128)(2,1)S(1)}, bf16[2,16,768]{2,1,0:T(8,128)(2,1)S(1)}, u32[]{:S(2)}, u32[]{:S(2)}) collective-permute-start(bf16[2,16,768]{2,1,0:T(8,128)(2,1)S(1)} %add_convert_fusion.12.refs_2_), channel_id=1, source_target_pairs={{68,67},{69,66},{76,75},{77,74},{84,83},{85,82},{92,91},{93,90},{1... | collective-permute-start | bytes 147464 | tf_op jit(solution)/shard_map/root/ppermute | solution.py:36
  45.5 3.0 %collective-permute-start.7 = (bf16[2,16,768]{2,1,0:T(8,128)(2,1)S(1)}, bf16[2,16,768]{2,1,0:T(8,128)(2,1)S(1)}, u32[]{:S(2)}, u32[]{:S(2)}) collective-permute-start(bf16[2,16,768]{2,1,0:T(8,128)(2,1)S(1)} %add_convert_fusion.12.refs_2_), channel_id=1, source_target_pairs={{68,66},{69,67},{76,74},{77,75},{84,82},{85,83},{92,90},{93,91},{9... | collective-permute-start | bytes 147464 | tf_op jit(solution)/shard_map/root/ppermute | solution.py:36
  47.9 0.7 collective-permute-start.9
  59.6 5.2 %collective-permute-start.13 = (bf16[16,1536]{1,0:T(8,128)(2,1)S(1)}, bf16[16,1536]{1,0:T(8,128)(2,1)S(1)}, u32[]{:S(2)}, u32[]{:S(2)}) collective-permute-start(bf16[16,1536]{1,0:T(8,128)(2,1)S(1)} %root.13), channel_id=1, source_target_pairs={{66,50},{67,51},{74,58},{75,59},{82,34},{83,35},{90,42},{91,43},{1... | collective-permute-start | bytes 147464 | tf_op jit(solution)/shard_map/root/ppermute | solution.py:36
  60.3 4.6 %collective-permute-start.12 = (bf16[16,1536]{1,0:T(8,128)(2,1)S(1)}, bf16[16,1536]{1,0:T(8,128)(2,1)S(1)}, u32[]{:S(2)}, u32[]{:S(2)}) collective-permute-start(bf16[16,1536]{1,0:T(8,128)(2,1)S(1)} %root.13), channel_id=1, source_target_pairs={{66,34},{67,35},{74,42},{75,43},{82,50},{83,51},{90,58},{91,59},{9... | collective-permute-start | bytes 147464 | tf_op jit(solution)/shard_map/root/ppermute | solution.py:36
  61.0 6.1 %collective-permute-start.14 = (bf16[2,16,768]{2,1,0:T(8,128)(2,1)S(1)}, bf16[2,16,768]{2,1,0:T(8,128)(2,1)S(1)}, u32[]{:S(2)}, u32[]{:S(2)}) collective-permute-start(bf16[2,16,768]{2,1,0:T(8,128)(2,1)S(1)} %add_convert_fusion.11.refs_2_.refs_6_), channel_id=1, source_target_pairs={{66,64},{67,65},{74,72},{75,73},{82,80},{83,81},{90,88},{91,89},{1... | collective-permute-start | bytes 147464 | tf_op jit(solution)/shard_map/root/ppermute | solution.py:36
  61.6 10.9 %collective-permute-start.18 = (bf16[512,1024]{1,0:T(8,128)(2,1)S(1)}, bf16[512,1024]{1,0:T(8,128)(2,1)S(1)}, u32[]{:S(2)}, u32[]{:S(2)}) collective-permute-start(bf16[512,1024]{1,0:T(8,128)(2,1)S(1)} %collective-permute-done.11), channel_id=1, source_target_pairs={{0,8},{8,0},{16,24},{24,16},{32,40},{40,32},{48,56},{56,48},{1,9},... | collective-permute-start | bytes 3145736 | tf_op jit(solution)/shard_map/root/ppermute | solution.py:216
  67.1 3.7 %collective-permute-start.16 = (bf16[2,16,768]{2,1,0:T(8,128)(2,1)S(1)}, bf16[2,16,768]{2,1,0:T(8,128)(2,1)S(1)}, u32[]{:S(2)}, u32[]{:S(2)}) collective-permute-start(bf16[2,16,768]{2,1,0:T(8,128)(2,1)S(1)} %add_convert_fusion.10.refs_2_), channel_id=1, source_target_pairs={{34,33},{35,32},{42,41},{43,40},{50,49},{51,48},{58,57},{59,56},{6... | collective-permute-start | bytes 147464 | tf_op jit(solution)/shard_map/root/ppermute | solution.py:36
  67.8 3.0 %collective-permute-start.15 = (bf16[2,16,768]{2,1,0:T(8,128)(2,1)S(1)}, bf16[2,16,768]{2,1,0:T(8,128)(2,1)S(1)}, u32[]{:S(2)}, u32[]{:S(2)}) collective-permute-start(bf16[2,16,768]{2,1,0:T(8,128)(2,1)S(1)} %add_convert_fusion.10.refs_2_), channel_id=1, source_target_pairs={{34,32},{35,33},{42,40},{43,41},{50,48},{51,49},{58,56},{59,57},{6... | collective-permute-start | bytes 147464 | tf_op jit(solution)/shard_map/root/ppermute | solution.py:36
  70.2 0.7 collective-permute-start.17
  72.6 35.0 %collective-permute-start.25 = (bf16[512,1024]{1,0:T(8,128)(2,1)}, bf16[512,1024]{1,0:T(8,128)(2,1)}, u32[]{:S(2)}, u32[]{:S(2)}) collective-permute-start(bf16[512,1024]{1,0:T(8,128)(2,1)} %bitcast.2), channel_id=1, source_target_pairs={{64,80},{72,88},{80,64},{88,72},{96,112},{104,120},{112,96},{120,1... | collective-permute-start | bytes 3145736 | tf_op jit(solution)/shard_map/root/ppermute | solution.py:222
  74.2 14.3 %collective-permute-start.20 = (bf16[16,1536]{1,0:T(8,128)(2,1)S(1)}, bf16[16,1536]{1,0:T(8,128)(2,1)S(1)}, u32[]{:S(2)}, u32[]{:S(2)}) collective-permute-start(bf16[16,1536]{1,0:T(8,128)(2,1)S(1)} %root.16), channel_id=1, source_target_pairs={{32,16},{33,17},{40,24},{41,25},{48,0},{49,1},{56,8},{57,9},{160,1... | collective-permute-start | bytes 147464 | tf_op jit(solution)/shard_map/root/ppermute | solution.py:36
  75.5 19.4 %collective-permute-start.19 = (bf16[16,1536]{1,0:T(8,128)(2,1)S(1)}, bf16[16,1536]{1,0:T(8,128)(2,1)S(1)}, u32[]{:S(2)}, u32[]{:S(2)}) collective-permute-start(bf16[16,1536]{1,0:T(8,128)(2,1)S(1)} %root.16), channel_id=1, source_target_pairs={{32,0},{33,1},{40,8},{41,9},{48,16},{49,17},{56,24},{57,25},{160,1... | collective-permute-start | bytes 147464 | tf_op jit(solution)/shard_map/root/ppermute | solution.py:36
  97.1 5.0 %collective-permute-start.23 = (bf16[2,16,768]{2,1,0:T(8,128)(2,1)S(1)}, bf16[2,16,768]{2,1,0:T(8,128)(2,1)S(1)}, u32[]{:S(2)}, u32[]{:S(2)}) collective-permute-start(bf16[2,16,768]{2,1,0:T(8,128)(2,1)S(1)} %root.17), channel_id=1, source_target_pairs={{0,1},{1,0},{8,9},{9,8},{16,17},{17,16},{24,25},{25,24},{128,129},... | collective-permute-start | bytes 147464 | tf_op jit(solution)/shard_map/root/ppermute | solution.py:36
  99.1 2.9 %collective-permute-start.22 = (bf16[2,16,768]{2,1,0:T(8,128)(2,1)S(1)}, bf16[2,16,768]{2,1,0:T(8,128)(2,1)S(1)}, u32[]{:S(2)}, u32[]{:S(2)}) collective-permute-start(bf16[2,16,768]{2,1,0:T(8,128)(2,1)S(1)} %root.17), channel_id=1, source_target_pairs={{0,7},{1,6},{8,15},{9,14},{16,23},{17,22},{24,31},{25,30},{34,35},... | collective-permute-start | bytes 147464 | tf_op jit(solution)/shard_map/root/ppermute | solution.py:36
  100.4 4.1 %collective-permute-start.21 = (bf16[2,16,768]{2,1,0:T(8,128)(2,1)S(1)}, bf16[2,16,768]{2,1,0:T(8,128)(2,1)S(1)}, u32[]{:S(2)}, u32[]{:S(2)}) collective-permute-start(bf16[2,16,768]{2,1,0:T(8,128)(2,1)S(1)} %root.17), channel_id=1, source_target_pairs={{0,6},{1,7},{8,14},{9,15},{16,22},{17,23},{24,30},{25,31},{32,38},... | collective-permute-start | bytes 147464 | tf_op jit(solution)/shard_map/root/ppermute | solution.py:36
  104.6 3.0 %collective-permute-start.24 = (bf16[2,16,768]{2,1,0:T(8,128)(2,1)S(1)}, bf16[2,16,768]{2,1,0:T(8,128)(2,1)S(1)}, u32[]{:S(2)}, u32[]{:S(2)}) collective-permute-start(bf16[2,16,768]{2,1,0:T(8,128)(2,1)S(1)} %add_convert_fusion.8), channel_id=1, source_target_pairs={{0,2},{1,3},{8,10},{9,11},{16,18},{17,19},{24,26},{25,27},{6,4},{7... | collective-permute-start | bytes 147464 | tf_op jit(solution)/shard_map/root/ppermute | solution.py:36
  105.9 27.4 %collective-permute-start.29 = (bf16[512,1024]{1,0:T(8,128)(2,1)}, bf16[512,1024]{1,0:T(8,128)(2,1)}, u32[]{:S(2)}, u32[]{:S(2)}) collective-permute-start(bf16[512,1024]{1,0:T(8,128)(2,1)} %bitcast.2), channel_id=1, source_target_pairs={{64,72},{72,64},{80,88},{88,80},{96,104},{104,96},{112,120},{120,1... | collective-permute-start | bytes 3145736 | tf_op jit(solution)/shard_map/root/ppermute | solution.py:223
  126.1 9.2 %collective-permute-start.28 = (bf16[32,1024]{1,0:T(8,128)(2,1)S(1)}, bf16[32,1024]{1,0:T(8,128)(2,1)S(1)}, u32[]{:S(2)}, u32[]{:S(2)}) collective-permute-start(bf16[32,1024]{1,0:T(8,128)(2,1)S(1)} %reduce_sum.22), channel_id=1, source_target_pairs={{96,0},{97,1},{104,8},{105,9},{112,16},{113,17},{120,24},{121,25},... | collective-permute-start | bytes 196616 | tf_op jit(solution)/shard_map/coupling/ppermute | solution.py:36
  127.4 8.9 %collective-permute-start.27 = (bf16[32,1024]{1,0:T(8,128)(2,1)S(1)}, bf16[32,1024]{1,0:T(8,128)(2,1)S(1)}, u32[]{:S(2)}, u32[]{:S(2)}) collective-permute-start(bf16[32,1024]{1,0:T(8,128)(2,1)S(1)} %reduce_sum.22), channel_id=1, source_target_pairs={{64,0},{65,1},{72,8},{73,9},{80,16},{81,17},{88,24},{89,25},{98,34... | collective-permute-start | bytes 196616 | tf_op jit(solution)/shard_map/coupling/ppermute | solution.py:36
  128.7 8.3 %collective-permute-start.26 = (bf16[32,1024]{1,0:T(8,128)(2,1)S(1)}, bf16[32,1024]{1,0:T(8,128)(2,1)S(1)}, u32[]{:S(2)}, u32[]{:S(2)}) collective-permute-start(bf16[32,1024]{1,0:T(8,128)(2,1)S(1)} %reduce_sum.22), channel_id=1, source_target_pairs={{32,0},{33,1},{40,8},{41,9},{48,16},{49,17},{56,24},{57,25},{66,34... | collective-permute-start | bytes 196616 | tf_op jit(solution)/shard_map/coupling/ppermute | solution.py:36
  130.0 10.5 %collective-permute-start.30 = (bf16[512,1024]{1,0:T(8,128)(2,1)}, bf16[512,1024]{1,0:T(8,128)(2,1)}, u32[]{:S(2)}, u32[]{:S(2)}) collective-permute-start(bf16[512,1024]{1,0:T(8,128)(2,1)} %collective-permute-done.25), channel_id=1, source_target_pairs={{64,72},{72,64},{80,88},{88,80},{96,104},{104,96},{112,120},{120,1... | collective-permute-start | bytes 3145736 | tf_op jit(solution)/shard_map/coupling/ppermute | solution.py:238
  142.6 1.4 collective-permute-start.32
  143.3 0.7 collective-permute-start.31
  146.5 1.4 collective-permute-start.33
  147.2 4.9 %collective-permute-start.34 = (bf16[32,2048]{1,0:T(8,128)(2,1)S(1)}, bf16[32,2048]{1,0:T(8,128)(2,1)S(1)}, u32[]{:S(2)}, u32[]{:S(2)}) collective-permute-start(bf16[32,2048]{1,0:T(8,128)(2,1)S(1)} %add_convert_fusion.6), channel_id=1, source_target_pairs={{100,98},{101,99},{108,106},{109,107},{116,114},{117,115},{124,122... | collective-permute-start | bytes 393224 | tf_op jit(solution)/shard_map/child/ppermute | solution.py:36
  152.1 1.5 collective-permute-start.36
  152.8 0.9 collective-permute-start.35
  156.1 2.0 collective-permute-start.38
  156.8 1.4 collective-permute-start.37
  157.5 4.9 %collective-permute-start.39 = (bf16[32,2048]{1,0:T(8,128)(2,1)S(1)}, bf16[32,2048]{1,0:T(8,128)(2,1)S(1)}, u32[]{:S(2)}, u32[]{:S(2)}) collective-permute-start(bf16[32,2048]{1,0:T(8,128)(2,1)S(1)} %add_convert_fusion.4), channel_id=1, source_target_pairs={{66,64},{67,65},{74,72},{75,73},{82,80},{83,81},{90,88},{91,89},{1... | collective-permute-start | bytes 393224 | tf_op jit(solution)/shard_map/child/ppermute | solution.py:36
  162.5 1.5 collective-permute-start.41
  166.4 38.0 %collective-permute-start.43 = (bf16[32,1024]{1,0:T(8,128)(2,1)S(1)}, bf16[32,1024]{1,0:T(8,128)(2,1)S(1)}, u32[]{:S(2)}, u32[]{:S(2)}) collective-permute-start(bf16[32,1024]{1,0:T(8,128)(2,1)S(1)} %fusion.14), channel_id=1, source_target_pairs={{64,0},{65,1},{72,8},{73,9},{80,16},{81,17},{88,24},{89,25},{192,1... | collective-permute-start | bytes 196616 | tf_op jit(solution)/shard_map/child/ppermute | solution.py:36
  167.7 47.9 %collective-permute-start.42 = (bf16[32,1024]{1,0:T(8,128)(2,1)S(1)}, bf16[32,1024]{1,0:T(8,128)(2,1)S(1)}, u32[]{:S(2)}, u32[]{:S(2)}) collective-permute-start(bf16[32,1024]{1,0:T(8,128)(2,1)S(1)} %fusion.14), channel_id=1, source_target_pairs={{32,0},{33,1},{40,8},{41,9},{48,16},{49,17},{56,24},{57,25},{160,1... | collective-permute-start | bytes 196616 | tf_op jit(solution)/shard_map/child/ppermute | solution.py:36
  219.9 5.7 %collective-permute-start.46 = (bf16[32,2048]{1,0:T(8,128)(2,1)S(1)}, bf16[32,2048]{1,0:T(8,128)(2,1)S(1)}, u32[]{:S(2)}, u32[]{:S(2)}) collective-permute-start(bf16[32,2048]{1,0:T(8,128)(2,1)S(1)} %maximum_select_fusion.3), channel_id=1, source_target_pairs={{0,1},{1,0},{8,9},{9,8},{16,17},{17,16},{24,25},{25,24},{128,129},... | collective-permute-start | bytes 393224 | tf_op jit(solution)/shard_map/child/ppermute | solution.py:36
  221.8 3.8 %collective-permute-start.45 = (bf16[32,2048]{1,0:T(8,128)(2,1)S(1)}, bf16[32,2048]{1,0:T(8,128)(2,1)S(1)}, u32[]{:S(2)}, u32[]{:S(2)}) collective-permute-start(bf16[32,2048]{1,0:T(8,128)(2,1)S(1)} %maximum_select_fusion.3), channel_id=1, source_target_pairs={{0,7},{1,6},{8,15},{9,14},{16,23},{17,22},{24,31},{25,30},{34,35},... | collective-permute-start | bytes 393224 | tf_op jit(solution)/shard_map/child/ppermute | solution.py:36
  223.1 10.5 %collective-permute-start.44 = (bf16[32,2048]{1,0:T(8,128)(2,1)S(1)}, bf16[32,2048]{1,0:T(8,128)(2,1)S(1)}, u32[]{:S(2)}, u32[]{:S(2)}) collective-permute-start(bf16[32,2048]{1,0:T(8,128)(2,1)S(1)} %maximum_select_fusion.3), channel_id=1, source_target_pairs={{0,6},{1,7},{8,14},{9,15},{16,22},{17,23},{24,30},{25,31},{32,38},... | collective-permute-start | bytes 393224 | tf_op jit(solution)/shard_map/child/ppermute | solution.py:36
  233.7 3.2 %collective-permute-start.47 = (bf16[32,2048]{1,0:T(8,128)(2,1)S(1)}, bf16[32,2048]{1,0:T(8,128)(2,1)S(1)}, u32[]{:S(2)}, u32[]{:S(2)}) collective-permute-start(bf16[32,2048]{1,0:T(8,128)(2,1)S(1)} %add_convert_fusion.1), channel_id=1, source_target_pairs={{0,2},{1,3},{8,10},{9,11},{16,18},{17,19},{24,26},{25,27},{6,4},{7... | collective-permute-start | bytes 393224 | tf_op jit(solution)/shard_map/child/ppermute | solution.py:36
  (13 other events, 235.5 us)

commit v10 on v9

--- a/solution.py
+++ b/solution.py
@@ -257,7 +257,6 @@
     with jax.named_scope("child"):
         blocks = [child_here] + [moved[0, flip] + moved[1, flip] for flip in (1, 2, 3)]
         rows = child_here.shape[0]
-        solves = (row_index // GROUP, col_index // PAIR)
 
         def child_terms(current, carried):
             for i, block in enumerate(blocks):
@@ -269,7 +268,7 @@
                 rhs = rhs - part.astype(F32)
             residual = rhs.astype(BF16)
             piece = jnp.concatenate([dot_t(residual, block) for block in blocks], 1).astype(BF16)
-            return jnp.where((solves[0] == r) & (solves[1] == r), piece, current)
+            return jnp.where(solving[r : r + 1].reshape(1, 1) == 1, piece, current)
 
         child_rows = jnp.zeros((share, GROUP * rows), BF16)
         child_rows = sweep(child_rhs, child_rows, child_terms, child_pieces, False)

time: 249 us -> 245 us (0.984)
  blocking collectives: 26.1 us -> 17.9 us
  starting transfers between devices: 67.6 us -> 71.8 us
  matrix products: 22.8 us -> 19.9 us
    all_to_all x1 -> x0, blocking collectives: 8.34 us -> none  [per_device(): lax.all_to_all(terms, 'row', 0, 0, tiled=True, axis_index_groups=quarters)]
    all_to_all x0 -> x1, starting transfers between devices: none -> 4.32 us  [per_device(): lax.all_to_all(terms, 'row', 0, 0, tiled=True, axis_index_groups=quarters)]
    dot_general x16, matrix products: 15.3 us -> 11.7 us  [dot_t(): lax.dot_general(a, b, (((1,), (1,)), ((), ())), preferred_element_type=F32)]
    all_to_all x0 -> x1, waiting for transfers between devices: none -> 3.51 us  [per_device(): lax.all_to_all(terms, 'row', 0, 0, tiled=True, axis_index_groups=quarters)]
    ppermute x40, waiting for transfers between devices: 80.5 us -> 78 us  [send(): return lax.ppermute(value, GRID, pairs)]
  transfers between devices with their start and end apart: 49 -> 50, of which waited for: 13 -> 14; matrix products, arithmetic and copies ran while one was open for 7% -> 7% of each run, Pallas kernels for 7% -> 7%
where the time goes in v10:
time: 245 us; the launch traced here: 244 us
  waiting for transfers between devices  100 us (41%)
  starting transfers between devices  71.8 us (29%)
  matrix products  19.9 us (8%)
  blocking collectives  17.9 us (7%)
  Pallas kernels  16.9 us (7%)
  other arithmetic  6.97 us (3%)
  local copies, waits for them, and re-layouts  5.55 us (2%)
  between operations  4.32 us (2%)
    ppermute x40, waiting for transfers between devices, send(): return lax.ppermute(value, GRID, pairs)  78 us
    ppermute x40, starting transfers between devices, send(): return lax.ppermute(value, GRID, pairs)  37.6 us
    dot_general x16, matrix products, dot_t(): lax.dot_general(a, b, (((1,), (1,)), ((), ())), preferred_element_type=F32)  11.7 us
    all_to_all x1, blocking collectives, per_device(): lax.all_to_all(shared, ('gz', 'row'), 0, 0, tiled=True, axis_index_groups...  9.68 us
    all_to_all x1, waiting for transfers between devices, per_device(): lax.all_to_all(pieces.reshape(layers * ROWS, 12, lanes), ('gz', 'row'), 0...  9.56 us
    ppermute x2, waiting for transfers between devices, move_children(): moved[half, 2] = lax.ppermute(here, 'row', rows_of(half, 2))  9.32 us
    ppermute x1, starting transfers between devices, per_device(): partner_factor = lax.ppermute(root_factor, 'row', swap)  8.92 us
    pallas_call x4, Pallas kernels, pieces_of(): pl.pallas_call(functools.partial(pieces_kernel, r, count), grid=(steps,),...  8.66 us
  transfers between devices with their start and end apart: 50, of which 14 were waited for; matrix products, arithmetic and copies ran while one was open for 7% of the time, Pallas kernels for 7%

profile of v10, /device:TPU:1, one launch (start us, length us, event | category | flops | bytes accessed | tf_op | source)
XLA Modules:
  0.0 243.7 jit_solution(7190983916708765207)
XLA Ops:
  0.6 8.9 %collective-permute-start.1 = (bf16[768,1536]{1,0:T(8,128)(2,1)}, bf16[768,1536]{1,0:T(8,128)(2,1)S(1)}, u32[]{:S(2)}, u32[]{:S(2)}) collective-permute-start(bf16[768,1536]{1,0:T(8,128)(2,1)} %refs_4_.5), channel_id=1, source_target_pairs={{0,8},{8,0},{16,24},{24,16},{32,40},{40,32},{48,56},{56,48},{64,72... | collective-permute-start | bytes 7077896 | tf_op jit(solution)/shard_map/mask/ppermute | solution.py:186
  11.1 4.9 %all-to-all-start = ((bf16[64,12,128]{2,1,0:T(8,128)(2,1)}), bf16[64,12,128]{2,1,0:T(8,128)(2,1)S(1)}, u32[]{:S(2)}, u32[]{:S(2)}) async-start(bf16[64,12,128]{2,1,0:T(8,128)(2,1)} %bitcast.82), calls=%async_computation | async-start | bytes 524288 | tf_op jit(solution)/shard_map/rhs/all_to_all | solution.py:199
  16.0 2.4 collective-permute-start
  18.4 9.6 %all-to-all-done = bf16[64,12,128]{2,1,0:T(8,128)(2,1)S(1)} async-done(((bf16[64,12,128]{2,1,0:T(8,128)(2,1)}), bf16[64,12,128]{2,1,0:T(8,128)(2,1)S(1)}, u32[]{:S(2)}, u32[]{:S(2)}) %all-to-all-start) | async-done | bytes 196640 | tf_op jit(solution)/shard_map/rhs/all_to_all | solution.py:199
  28.1 1.7 copy-done.1
  29.7 2.1 root.9
  33.2 3.1 %collective-permute-start.11 = (bf16[512,1024]{1,0:T(8,128)(2,1)}, bf16[512,1024]{1,0:T(8,128)(2,1)S(1)}, u32[]{:S(2)}, u32[]{:S(2)}) collective-permute-start(bf16[512,1024]{1,0:T(8,128)(2,1)} %bitcast.2), channel_id=1, source_target_pairs={{0,16},{8,24},{16,0},{24,8},{32,48},{40,56},{48,32},{56,40},{1,17}... | collective-permute-start | bytes 3145736 | tf_op jit(solution)/shard_map/root/ppermute | solution.py:222
  36.3 2.5 %collective-permute-start.10 = (bf16[512,1024]{1,0:T(8,128)(2,1)}, bf16[512,1024]{1,0:T(8,128)(2,1)S(1)}, u32[]{:S(2)}, u32[]{:S(2)}) collective-permute-start(bf16[512,1024]{1,0:T(8,128)(2,1)} %bitcast.2), channel_id=1, source_target_pairs={{0,8},{8,0},{16,24},{24,16},{32,40},{40,32},{48,56},{56,48},{1,9},... | collective-permute-start | bytes 3145736 | tf_op jit(solution)/shard_map/root/ppermute | solution.py:223
  38.9 1.7 root.10
  42.6 2.2 root.11
  46.2 1.7 root.12
  48.6 1.7 root.13
  50.3 9.3 %collective-permute-done.11 = bf16[512,1024]{1,0:T(8,128)(2,1)S(1)} collective-permute-done((bf16[512,1024]{1,0:T(8,128)(2,1)}, bf16[512,1024]{1,0:T(8,128)(2,1)S(1)}, u32[]{:S(2)}, u32[]{:S(2)}) %collective-permute-start.11) | collective-permute-done | bytes 1048608 | tf_op jit(solution)/shard_map/root/ppermute | solution.py:222
  61.6 3.2 %collective-permute-start.18 = (bf16[512,1024]{1,0:T(8,128)(2,1)S(1)}, bf16[512,1024]{1,0:T(8,128)(2,1)S(1)}, u32[]{:S(2)}, u32[]{:S(2)}) collective-permute-start(bf16[512,1024]{1,0:T(8,128)(2,1)S(1)} %collective-permute-done.11), channel_id=1, source_target_pairs={{0,8},{8,0},{16,24},{24,16},{32,40},{40,32},{48,56},{56,48},{1,9},... | collective-permute-start | bytes 3145736 | tf_op jit(solution)/shard_map/root/ppermute | solution.py:216
  64.9 2.2 root.14
  68.5 1.7 root.15
  70.9 1.7 root.16
  72.6 1.7 collective-permute-start.25
  76.8 11.7 %collective-permute-done.20.refs_3_ = bf16[16,1536]{1,0:T(8,128)(2,1)S(1)} collective-permute-done((bf16[16,1536]{1,0:T(8,128)(2,1)S(1)}, bf16[16,1536]{1,0:T(8,128)(2,1)S(1)}, u32[]{:S(2)}, u32[]{:S(2)}) %collective-permute-start.20) | collective-permute-done | bytes 49184 | tf_op jit(solution)/shard_map/root/ppermute | solution.py:36
  88.5 6.4 %collective-permute-done.19.refs_2_ = bf16[16,1536]{1,0:T(8,128)(2,1)S(1)} collective-permute-done((bf16[16,1536]{1,0:T(8,128)(2,1)S(1)}, bf16[16,1536]{1,0:T(8,128)(2,1)S(1)}, u32[]{:S(2)}, u32[]{:S(2)}) %collective-permute-start.19) | collective-permute-done | bytes 49184 | tf_op jit(solution)/shard_map/root/ppermute | solution.py:36
  94.9 2.2 root.17
  97.1 2.1 collective-permute-start.23
  102.1 2.5 %collective-permute-done.21 = bf16[2,16,768]{2,1,0:T(8,128)(2,1)S(1)} collective-permute-done((bf16[2,16,768]{2,1,0:T(8,128)(2,1)S(1)}, bf16[2,16,768]{2,1,0:T(8,128)(2,1)S(1)}, u32[]{:S(2)}, u32[]{:S(2)}) %collective-permute-start.21) | collective-permute-done | bytes 49184 | tf_op jit(solution)/shard_map/root/ppermute | solution.py:36
  105.9 1.7 collective-permute-start.29
  107.7 9.7 %all_to_all.32 = bf16[8,16,768]{2,1,0:T(8,128)(2,1)S(1)} all-to-all(bf16[8,16,768]{2,1,0:T(8,128)(2,1)S(1)} %bitcast.83), channel_id=1, replica_groups={{0,8,128,136,256,264,384,392},{16,24,144,152,272,280,400,408},{32,40,16..., dimensions={0} | all-to-all | bytes 393216 | tf_op jit(solution)/shard_map/coupling/all_to_all | solution.py:243
  118.5 4.3 %all-to-all-start.2 = ((bf16[4,32,1024]{2,1,0:T(8,128)(2,1)}), bf16[4,32,1024]{2,1,0:T(8,128)(2,1)S(1)}, u32[]{:S(2)}, u32[]{:S(2)}) async-start(bf16[4,32,1024]{2,1,0:T(8,128)(2,1)} %bitcast.10), calls=%async_computation.2 | async-start | bytes 524288 | tf_op jit(solution)/shard_map/coupling/all_to_all | solution.py:247
  122.8 1.7 collective-permute-start.30
  124.5 3.5 %all-to-all-done.2 = bf16[4,32,1024]{2,1,0:T(8,128)(2,1)S(1)} async-done(((bf16[4,32,1024]{2,1,0:T(8,128)(2,1)}), bf16[4,32,1024]{2,1,0:T(8,128)(2,1)S(1)}, u32[]{:S(2)}, u32[]{:S(2)}) %all-to-all-start.2) | async-done | bytes 262176 | tf_op jit(solution)/shard_map/coupling/all_to_all | solution.py:247
  133.1 1.6 add.173
  134.8 1.6 add.172
  136.4 1.8 collective-permute-done.27
  138.2 1.6 collective-permute-done.26
  140.8 1.6 convolution_convert_fusion.16
  143.3 1.6 add.174
  147.1 1.5 fusion.37
  152.6 1.6 convolution_convert_fusion.12
  156.8 1.5 fusion.4
  162.3 1.6 convolution_convert_fusion.8
  166.1 1.5 fusion.24
  171.1 35.0 %collective-permute-done.43 = bf16[32,1024]{1,0:T(8,128)(2,1)S(1)} collective-permute-done((bf16[32,1024]{1,0:T(8,128)(2,1)S(1)}, bf16[32,1024]{1,0:T(8,128)(2,1)S(1)}, u32[]{:S(2)}, u32[]{:S(2)}) %collective-permute-start.43) | collective-permute-done | bytes 65568 | tf_op jit(solution)/shard_map/child/ppermute | solution.py:36
  206.1 7.5 %collective-permute-done.42 = bf16[32,1024]{1,0:T(8,128)(2,1)S(1)} collective-permute-done((bf16[32,1024]{1,0:T(8,128)(2,1)S(1)}, bf16[32,1024]{1,0:T(8,128)(2,1)S(1)}, u32[]{:S(2)}, u32[]{:S(2)}) %collective-permute-start.42) | collective-permute-done | bytes 65568 | tf_op jit(solution)/shard_map/child/ppermute | solution.py:36
  214.9 1.6 convolution_convert_fusion.4
  216.6 1.9 collective-permute-start.46
  218.6 1.3 collective-permute-start.45
  219.9 1.3 collective-permute-start.44
  222.4 8.0 %collective-permute-done.44 = bf16[32,2048]{1,0:T(8,128)(2,1)S(1)} collective-permute-done((bf16[32,2048]{1,0:T(8,128)(2,1)S(1)}, bf16[32,2048]{1,0:T(8,128)(2,1)S(1)}, u32[]{:S(2)}, u32[]{:S(2)}) %collective-permute-start.44) | collective-permute-done | bytes 131104 | tf_op jit(solution)/shard_map/child/ppermute | solution.py:36
  231.8 1.9 collective-permute-done.47
  234.9 8.2 %all_to_all.33 = bf16[4,32,512]{2,1,0:T(8,128)(2,1)S(1)} all-to-all(bf16[4,32,512]{2,1,0:T(8,128)(2,1)S(1)} %bitcast.85), channel_id=1, replica_groups={{0,8,16,24},{32,40,48,56},{64,72,80,88},{96,104,112,120},{1,9,17,25},{3..., dimensions={0} | all-to-all | bytes 262144 | tf_op jit(solution)/shard_map/child/all_to_all | solution.py:280
  (161 shorter events, 47.4 us)
Async XLA Ops:
  0.6 27.4 %collective-permute-start.1 = (bf16[768,1536]{1,0:T(8,128)(2,1)}, bf16[768,1536]{1,0:T(8,128)(2,1)S(1)}, u32[]{:S(2)}, u32[]{:S(2)}) collective-permute-start(bf16[768,1536]{1,0:T(8,128)(2,1)} %refs_4_.5), channel_id=1, source_target_pairs={{0,8},{8,0},{16,24},{24,16},{32,40},{40,32},{48,56},{56,48},{64,72... | collective-permute-start | bytes 7077896 | tf_op jit(solution)/shard_map/mask/ppermute | solution.py:186
  11.1 16.9 %all-to-all-start = ((bf16[64,12,128]{2,1,0:T(8,128)(2,1)}), bf16[64,12,128]{2,1,0:T(8,128)(2,1)S(1)}, u32[]{:S(2)}, u32[]{:S(2)}) async-start(bf16[64,12,128]{2,1,0:T(8,128)(2,1)} %bitcast.82), calls=%async_computation | async-start | bytes 524288 | tf_op jit(solution)/shard_map/rhs/all_to_all | solution.py:199
  16.0 17.3 %collective-permute-start = (s32[3,6]{1,0:T(4,128)}, s32[3,6]{1,0:T(4,128)S(1)}, u32[]{:S(2)}, u32[]{:S(2)}) collective-permute-start(s32[3,6]{1,0:T(4,128)} %param.8), channel_id=1, source_target_pairs={{0,8},{8,0},{16,24},{24,16},{32,40},{40,32},{48,56},{56,48},{64,72... | collective-permute-start | bytes 224 | tf_op jit(solution)/shard_map/mask/ppermute | solution.py:187
  31.9 7.0 %collective-permute-start.3 = (bf16[2,16,768]{2,1,0:T(8,128)(2,1)S(1)}, bf16[2,16,768]{2,1,0:T(8,128)(2,1)S(1)}, u32[]{:S(2)}, u32[]{:S(2)}) collective-permute-start(bf16[2,16,768]{2,1,0:T(8,128)(2,1)S(1)} %root.9), channel_id=1, source_target_pairs={{102,101},{103,100},{110,109},{111,108},{118,117},{119,116},{126,1... | collective-permute-start | bytes 147464 | tf_op jit(solution)/shard_map/root/ppermute | solution.py:36
  32.5 6.3 %collective-permute-start.2 = (bf16[2,16,768]{2,1,0:T(8,128)(2,1)S(1)}, bf16[2,16,768]{2,1,0:T(8,128)(2,1)S(1)}, u32[]{:S(2)}, u32[]{:S(2)}) collective-permute-start(bf16[2,16,768]{2,1,0:T(8,128)(2,1)S(1)} %root.9), channel_id=1, source_target_pairs={{102,100},{103,101},{110,108},{111,109},{118,116},{119,117},{126,1... | collective-permute-start | bytes 147464 | tf_op jit(solution)/shard_map/root/ppermute | solution.py:36
  33.2 26.4 %collective-permute-start.11 = (bf16[512,1024]{1,0:T(8,128)(2,1)}, bf16[512,1024]{1,0:T(8,128)(2,1)S(1)}, u32[]{:S(2)}, u32[]{:S(2)}) collective-permute-start(bf16[512,1024]{1,0:T(8,128)(2,1)} %bitcast.2), channel_id=1, source_target_pairs={{0,16},{8,24},{16,0},{24,8},{32,48},{40,56},{48,32},{56,40},{1,17}... | collective-permute-start | bytes 3145736 | tf_op jit(solution)/shard_map/root/ppermute | solution.py:222
  36.3 23.3 %collective-permute-start.10 = (bf16[512,1024]{1,0:T(8,128)(2,1)}, bf16[512,1024]{1,0:T(8,128)(2,1)S(1)}, u32[]{:S(2)}, u32[]{:S(2)}) collective-permute-start(bf16[512,1024]{1,0:T(8,128)(2,1)} %bitcast.2), channel_id=1, source_target_pairs={{0,8},{8,0},{16,24},{24,16},{32,40},{40,32},{48,56},{56,48},{1,9},... | collective-permute-start | bytes 3145736 | tf_op jit(solution)/shard_map/root/ppermute | solution.py:223
  40.6 2.0 collective-permute-start.5
  41.3 1.4 collective-permute-start.4
  41.9 2.9 %collective-permute-start.6 = (bf16[2,16,768]{2,1,0:T(8,128)(2,1)S(1)}, bf16[2,16,768]{2,1,0:T(8,128)(2,1)S(1)}, u32[]{:S(2)}, u32[]{:S(2)}) collective-permute-start(bf16[2,16,768]{2,1,0:T(8,128)(2,1)S(1)} %add_convert_fusion.13.refs_2_.refs_6_), channel_id=1, source_target_pairs={{100,98},{101,99},{108,106},{109,107},{116,114},{117,115},{124,122... | collective-permute-start | bytes 147464 | tf_op jit(solution)/shard_map/root/ppermute | solution.py:36
  44.9 3.7 %collective-permute-start.8 = (bf16[2,16,768]{2,1,0:T(8,128)(2,1)S(1)}, bf16[2,16,768]{2,1,0:T(8,128)(2,1)S(1)}, u32[]{:S(2)}, u32[]{:S(2)}) collective-permute-start(bf16[2,16,768]{2,1,0:T(8,128)(2,1)S(1)} %add_convert_fusion.12.refs_2_), channel_id=1, source_target_pairs={{68,67},{69,66},{76,75},{77,74},{84,83},{85,82},{92,91},{93,90},{1... | collective-permute-start | bytes 147464 | tf_op jit(solution)/shard_map/root/ppermute | solution.py:36
  45.5 3.0 %collective-permute-start.7 = (bf16[2,16,768]{2,1,0:T(8,128)(2,1)S(1)}, bf16[2,16,768]{2,1,0:T(8,128)(2,1)S(1)}, u32[]{:S(2)}, u32[]{:S(2)}) collective-permute-start(bf16[2,16,768]{2,1,0:T(8,128)(2,1)S(1)} %add_convert_fusion.12.refs_2_), channel_id=1, source_target_pairs={{68,66},{69,67},{76,74},{77,75},{84,82},{85,83},{92,90},{93,91},{9... | collective-permute-start | bytes 147464 | tf_op jit(solution)/shard_map/root/ppermute | solution.py:36
  47.9 0.7 collective-permute-start.9
  59.6 5.2 %collective-permute-start.13 = (bf16[16,1536]{1,0:T(8,128)(2,1)S(1)}, bf16[16,1536]{1,0:T(8,128)(2,1)S(1)}, u32[]{:S(2)}, u32[]{:S(2)}) collective-permute-start(bf16[16,1536]{1,0:T(8,128)(2,1)S(1)} %root.13), channel_id=1, source_target_pairs={{66,50},{67,51},{74,58},{75,59},{82,34},{83,35},{90,42},{91,43},{1... | collective-permute-start | bytes 147464 | tf_op jit(solution)/shard_map/root/ppermute | solution.py:36
  60.3 4.6 %collective-permute-start.12 = (bf16[16,1536]{1,0:T(8,128)(2,1)S(1)}, bf16[16,1536]{1,0:T(8,128)(2,1)S(1)}, u32[]{:S(2)}, u32[]{:S(2)}) collective-permute-start(bf16[16,1536]{1,0:T(8,128)(2,1)S(1)} %root.13), channel_id=1, source_target_pairs={{66,34},{67,35},{74,42},{75,43},{82,50},{83,51},{90,58},{91,59},{9... | collective-permute-start | bytes 147464 | tf_op jit(solution)/shard_map/root/ppermute | solution.py:36
  61.0 6.1 %collective-permute-start.14 = (bf16[2,16,768]{2,1,0:T(8,128)(2,1)S(1)}, bf16[2,16,768]{2,1,0:T(8,128)(2,1)S(1)}, u32[]{:S(2)}, u32[]{:S(2)}) collective-permute-start(bf16[2,16,768]{2,1,0:T(8,128)(2,1)S(1)} %add_convert_fusion.11.refs_2_.refs_6_), channel_id=1, source_target_pairs={{66,64},{67,65},{74,72},{75,73},{82,80},{83,81},{90,88},{91,89},{1... | collective-permute-start | bytes 147464 | tf_op jit(solution)/shard_map/root/ppermute | solution.py:36
  61.6 10.9 %collective-permute-start.18 = (bf16[512,1024]{1,0:T(8,128)(2,1)S(1)}, bf16[512,1024]{1,0:T(8,128)(2,1)S(1)}, u32[]{:S(2)}, u32[]{:S(2)}) collective-permute-start(bf16[512,1024]{1,0:T(8,128)(2,1)S(1)} %collective-permute-done.11), channel_id=1, source_target_pairs={{0,8},{8,0},{16,24},{24,16},{32,40},{40,32},{48,56},{56,48},{1,9},... | collective-permute-start | bytes 3145736 | tf_op jit(solution)/shard_map/root/ppermute | solution.py:216
  67.1 3.7 %collective-permute-start.16 = (bf16[2,16,768]{2,1,0:T(8,128)(2,1)S(1)}, bf16[2,16,768]{2,1,0:T(8,128)(2,1)S(1)}, u32[]{:S(2)}, u32[]{:S(2)}) collective-permute-start(bf16[2,16,768]{2,1,0:T(8,128)(2,1)S(1)} %add_convert_fusion.10.refs_2_), channel_id=1, source_target_pairs={{34,33},{35,32},{42,41},{43,40},{50,49},{51,48},{58,57},{59,56},{6... | collective-permute-start | bytes 147464 | tf_op jit(solution)/shard_map/root/ppermute | solution.py:36
  67.8 3.0 %collective-permute-start.15 = (bf16[2,16,768]{2,1,0:T(8,128)(2,1)S(1)}, bf16[2,16,768]{2,1,0:T(8,128)(2,1)S(1)}, u32[]{:S(2)}, u32[]{:S(2)}) collective-permute-start(bf16[2,16,768]{2,1,0:T(8,128)(2,1)S(1)} %add_convert_fusion.10.refs_2_), channel_id=1, source_target_pairs={{34,32},{35,33},{42,40},{43,41},{50,48},{51,49},{58,56},{59,57},{6... | collective-permute-start | bytes 147464 | tf_op jit(solution)/shard_map/root/ppermute | solution.py:36
  70.2 0.7 collective-permute-start.17
  72.6 35.0 %collective-permute-start.25 = (bf16[512,1024]{1,0:T(8,128)(2,1)}, bf16[512,1024]{1,0:T(8,128)(2,1)}, u32[]{:S(2)}, u32[]{:S(2)}) collective-permute-start(bf16[512,1024]{1,0:T(8,128)(2,1)} %bitcast.2), channel_id=1, source_target_pairs={{64,80},{72,88},{80,64},{88,72},{96,112},{104,120},{112,96},{120,1... | collective-permute-start | bytes 3145736 | tf_op jit(solution)/shard_map/root/ppermute | solution.py:222
  74.2 14.3 %collective-permute-start.20 = (bf16[16,1536]{1,0:T(8,128)(2,1)S(1)}, bf16[16,1536]{1,0:T(8,128)(2,1)S(1)}, u32[]{:S(2)}, u32[]{:S(2)}) collective-permute-start(bf16[16,1536]{1,0:T(8,128)(2,1)S(1)} %root.16), channel_id=1, source_target_pairs={{32,16},{33,17},{40,24},{41,25},{48,0},{49,1},{56,8},{57,9},{160,1... | collective-permute-start | bytes 147464 | tf_op jit(solution)/shard_map/root/ppermute | solution.py:36
  75.5 19.4 %collective-permute-start.19 = (bf16[16,1536]{1,0:T(8,128)(2,1)S(1)}, bf16[16,1536]{1,0:T(8,128)(2,1)S(1)}, u32[]{:S(2)}, u32[]{:S(2)}) collective-permute-start(bf16[16,1536]{1,0:T(8,128)(2,1)S(1)} %root.16), channel_id=1, source_target_pairs={{32,0},{33,1},{40,8},{41,9},{48,16},{49,17},{56,24},{57,25},{160,1... | collective-permute-start | bytes 147464 | tf_op jit(solution)/shard_map/root/ppermute | solution.py:36
  97.1 5.0 %collective-permute-start.23 = (bf16[2,16,768]{2,1,0:T(8,128)(2,1)S(1)}, bf16[2,16,768]{2,1,0:T(8,128)(2,1)S(1)}, u32[]{:S(2)}, u32[]{:S(2)}) collective-permute-start(bf16[2,16,768]{2,1,0:T(8,128)(2,1)S(1)} %root.17), channel_id=1, source_target_pairs={{0,1},{1,0},{8,9},{9,8},{16,17},{17,16},{24,25},{25,24},{128,129},... | collective-permute-start | bytes 147464 | tf_op jit(solution)/shard_map/root/ppermute | solution.py:36
  99.2 2.9 %collective-permute-start.22 = (bf16[2,16,768]{2,1,0:T(8,128)(2,1)S(1)}, bf16[2,16,768]{2,1,0:T(8,128)(2,1)S(1)}, u32[]{:S(2)}, u32[]{:S(2)}) collective-permute-start(bf16[2,16,768]{2,1,0:T(8,128)(2,1)S(1)} %root.17), channel_id=1, source_target_pairs={{0,7},{1,6},{8,15},{9,14},{16,23},{17,22},{24,31},{25,30},{34,35},... | collective-permute-start | bytes 147464 | tf_op jit(solution)/shard_map/root/ppermute | solution.py:36
  100.5 4.1 %collective-permute-start.21 = (bf16[2,16,768]{2,1,0:T(8,128)(2,1)S(1)}, bf16[2,16,768]{2,1,0:T(8,128)(2,1)S(1)}, u32[]{:S(2)}, u32[]{:S(2)}) collective-permute-start(bf16[2,16,768]{2,1,0:T(8,128)(2,1)S(1)} %root.17), channel_id=1, source_target_pairs={{0,6},{1,7},{8,14},{9,15},{16,22},{17,23},{24,30},{25,31},{32,38},... | collective-permute-start | bytes 147464 | tf_op jit(solution)/shard_map/root/ppermute | solution.py:36
  104.6 3.0 %collective-permute-start.24 = (bf16[2,16,768]{2,1,0:T(8,128)(2,1)S(1)}, bf16[2,16,768]{2,1,0:T(8,128)(2,1)S(1)}, u32[]{:S(2)}, u32[]{:S(2)}) collective-permute-start(bf16[2,16,768]{2,1,0:T(8,128)(2,1)S(1)} %add_convert_fusion.8), channel_id=1, source_target_pairs={{0,2},{1,3},{8,10},{9,11},{16,18},{17,19},{24,26},{25,27},{6,4},{7... | collective-permute-start | bytes 147464 | tf_op jit(solution)/shard_map/root/ppermute | solution.py:36
  105.9 28.9 %collective-permute-start.29 = (bf16[512,1024]{1,0:T(8,128)(2,1)}, bf16[512,1024]{1,0:T(8,128)(2,1)}, u32[]{:S(2)}, u32[]{:S(2)}) collective-permute-start(bf16[512,1024]{1,0:T(8,128)(2,1)} %bitcast.2), channel_id=1, source_target_pairs={{64,72},{72,64},{80,88},{88,80},{96,104},{104,96},{112,120},{120,1... | collective-permute-start | bytes 3145736 | tf_op jit(solution)/shard_map/root/ppermute | solution.py:223
  118.5 9.5 %all-to-all-start.2 = ((bf16[4,32,1024]{2,1,0:T(8,128)(2,1)}), bf16[4,32,1024]{2,1,0:T(8,128)(2,1)S(1)}, u32[]{:S(2)}, u32[]{:S(2)}) async-start(bf16[4,32,1024]{2,1,0:T(8,128)(2,1)} %bitcast.10), calls=%async_computation.2 | async-start | bytes 524288 | tf_op jit(solution)/shard_map/coupling/all_to_all | solution.py:247
  122.8 20.5 %collective-permute-start.30 = (bf16[512,1024]{1,0:T(8,128)(2,1)}, bf16[512,1024]{1,0:T(8,128)(2,1)}, u32[]{:S(2)}, u32[]{:S(2)}) collective-permute-start(bf16[512,1024]{1,0:T(8,128)(2,1)} %collective-permute-done.25), channel_id=1, source_target_pairs={{64,72},{72,64},{80,88},{88,80},{96,104},{104,96},{112,120},{120,1... | collective-permute-start | bytes 3145736 | tf_op jit(solution)/shard_map/coupling/ppermute | solution.py:238
  128.0 8.4 %collective-permute-start.28 = (bf16[32,1024]{1,0:T(8,128)(2,1)S(1)}, bf16[32,1024]{1,0:T(8,128)(2,1)S(1)}, u32[]{:S(2)}, u32[]{:S(2)}) collective-permute-start(bf16[32,1024]{1,0:T(8,128)(2,1)S(1)} %reduce_sum.22), channel_id=1, source_target_pairs={{96,0},{97,1},{104,8},{105,9},{112,16},{113,17},{120,24},{121,25},... | collective-permute-start | bytes 196616 | tf_op jit(solution)/shard_map/coupling/ppermute | solution.py:36
  129.3 8.9 %collective-permute-start.27 = (bf16[32,1024]{1,0:T(8,128)(2,1)S(1)}, bf16[32,1024]{1,0:T(8,128)(2,1)S(1)}, u32[]{:S(2)}, u32[]{:S(2)}) collective-permute-start(bf16[32,1024]{1,0:T(8,128)(2,1)S(1)} %reduce_sum.22), channel_id=1, source_target_pairs={{64,0},{65,1},{72,8},{73,9},{80,16},{81,17},{88,24},{89,25},{98,34... | collective-permute-start | bytes 196616 | tf_op jit(solution)/shard_map/coupling/ppermute | solution.py:36
  130.6 9.2 %collective-permute-start.26 = (bf16[32,1024]{1,0:T(8,128)(2,1)S(1)}, bf16[32,1024]{1,0:T(8,128)(2,1)S(1)}, u32[]{:S(2)}, u32[]{:S(2)}) collective-permute-start(bf16[32,1024]{1,0:T(8,128)(2,1)S(1)} %reduce_sum.22), channel_id=1, source_target_pairs={{32,0},{33,1},{40,8},{41,9},{48,16},{49,17},{56,24},{57,25},{66,34... | collective-permute-start | bytes 196616 | tf_op jit(solution)/shard_map/coupling/ppermute | solution.py:36
  145.4 1.4 collective-permute-start.32
  149.3 2.0 collective-permute-start.33
  150.6 3.6 %collective-permute-start.34 = (bf16[32,2048]{1,0:T(8,128)(2,1)S(1)}, bf16[32,2048]{1,0:T(8,128)(2,1)S(1)}, u32[]{:S(2)}, u32[]{:S(2)}) collective-permute-start(bf16[32,2048]{1,0:T(8,128)(2,1)S(1)} %add_convert_fusion.6), channel_id=1, source_target_pairs={{100,98},{101,99},{108,106},{109,107},{116,114},{117,115},{124,122... | collective-permute-start | bytes 393224 | tf_op jit(solution)/shard_map/child/ppermute | solution.py:36
  154.3 1.5 collective-permute-start.36
  155.0 0.9 collective-permute-start.35
  158.4 2.6 %collective-permute-start.38 = (bf16[32,1024]{1,0:T(8,128)(2,1)S(1)}, bf16[32,1024]{1,0:T(8,128)(2,1)S(1)}, u32[]{:S(2)}, u32[]{:S(2)}) collective-permute-start(bf16[32,1024]{1,0:T(8,128)(2,1)S(1)} %fusion.4), channel_id=1, source_target_pairs={{98,34},{99,35},{106,42},{107,43},{114,50},{115,51},{122,58},{123,... | collective-permute-start | bytes 196616 | tf_op jit(solution)/shard_map/child/ppermute | solution.py:36
  159.0 2.0 collective-permute-start.37
  160.3 3.7 %collective-permute-start.39 = (bf16[32,2048]{1,0:T(8,128)(2,1)S(1)}, bf16[32,2048]{1,0:T(8,128)(2,1)S(1)}, u32[]{:S(2)}, u32[]{:S(2)}) collective-permute-start(bf16[32,2048]{1,0:T(8,128)(2,1)S(1)} %add_convert_fusion.4), channel_id=1, source_target_pairs={{66,64},{67,65},{74,72},{75,73},{82,80},{83,81},{90,88},{91,89},{1... | collective-permute-start | bytes 393224 | tf_op jit(solution)/shard_map/child/ppermute | solution.py:36
  164.1 1.4 collective-permute-start.41
  167.9 38.2 %collective-permute-start.43 = (bf16[32,1024]{1,0:T(8,128)(2,1)S(1)}, bf16[32,1024]{1,0:T(8,128)(2,1)S(1)}, u32[]{:S(2)}, u32[]{:S(2)}) collective-permute-start(bf16[32,1024]{1,0:T(8,128)(2,1)S(1)} %fusion.14), channel_id=1, source_target_pairs={{64,0},{65,1},{72,8},{73,9},{80,16},{81,17},{88,24},{89,25},{192,1... | collective-permute-start | bytes 196616 | tf_op jit(solution)/shard_map/child/ppermute | solution.py:36
  169.2 44.4 %collective-permute-start.42 = (bf16[32,1024]{1,0:T(8,128)(2,1)S(1)}, bf16[32,1024]{1,0:T(8,128)(2,1)S(1)}, u32[]{:S(2)}, u32[]{:S(2)}) collective-permute-start(bf16[32,1024]{1,0:T(8,128)(2,1)S(1)} %fusion.14), channel_id=1, source_target_pairs={{32,0},{33,1},{40,8},{41,9},{48,16},{49,17},{56,24},{57,25},{160,1... | collective-permute-start | bytes 196616 | tf_op jit(solution)/shard_map/child/ppermute | solution.py:36
  216.6 5.7 %collective-permute-start.46 = (bf16[32,2048]{1,0:T(8,128)(2,1)S(1)}, bf16[32,2048]{1,0:T(8,128)(2,1)S(1)}, u32[]{:S(2)}, u32[]{:S(2)}) collective-permute-start(bf16[32,2048]{1,0:T(8,128)(2,1)S(1)} %maximum_select_fusion.3), channel_id=1, source_target_pairs={{0,1},{1,0},{8,9},{9,8},{16,17},{17,16},{24,25},{25,24},{128,129},... | collective-permute-start | bytes 393224 | tf_op jit(solution)/shard_map/child/ppermute | solution.py:36
  218.6 3.8 %collective-permute-start.45 = (bf16[32,2048]{1,0:T(8,128)(2,1)S(1)}, bf16[32,2048]{1,0:T(8,128)(2,1)S(1)}, u32[]{:S(2)}, u32[]{:S(2)}) collective-permute-start(bf16[32,2048]{1,0:T(8,128)(2,1)S(1)} %maximum_select_fusion.3), channel_id=1, source_target_pairs={{0,7},{1,6},{8,15},{9,14},{16,23},{17,22},{24,31},{25,30},{34,35},... | collective-permute-start | bytes 393224 | tf_op jit(solution)/shard_map/child/ppermute | solution.py:36
  219.9 10.5 %collective-permute-start.44 = (bf16[32,2048]{1,0:T(8,128)(2,1)S(1)}, bf16[32,2048]{1,0:T(8,128)(2,1)S(1)}, u32[]{:S(2)}, u32[]{:S(2)}) collective-permute-start(bf16[32,2048]{1,0:T(8,128)(2,1)S(1)} %maximum_select_fusion.3), channel_id=1, source_target_pairs={{0,6},{1,7},{8,14},{9,15},{16,22},{17,23},{24,30},{25,31},{32,38},... | collective-permute-start | bytes 393224 | tf_op jit(solution)/shard_map/child/ppermute | solution.py:36
  230.4 3.2 %collective-permute-start.47 = (bf16[32,2048]{1,0:T(8,128)(2,1)S(1)}, bf16[32,2048]{1,0:T(8,128)(2,1)S(1)}, u32[]{:S(2)}, u32[]{:S(2)}) collective-permute-start(bf16[32,2048]{1,0:T(8,128)(2,1)S(1)} %add_convert_fusion.1), channel_id=1, source_target_pairs={{0,2},{1,3},{8,10},{9,11},{16,18},{17,19},{24,26},{25,27},{6,4},{7... | collective-permute-start | bytes 393224 | tf_op jit(solution)/shard_map/child/ppermute | solution.py:36
  (12 other events, 246.1 us)

commit v11 on v10

--- a/solution.py
+++ b/solution.py
@@ -255,7 +255,8 @@
         child_rhs = (2 * bits - 1).astype(F32) - coupled
 
     with jax.named_scope("child"):
-        blocks = [child_here] + [moved[0, flip] + moved[1, flip] for flip in (1, 2, 3)]
+        blocks = [moved[0, flip] + moved[1, flip] for flip in (1, 2, 3)]
+        blocks = [jnp.where(row_index < 0, blocks[0], child_here)] + blocks
         rows = child_here.shape[0]
 
         def child_terms(current, carried):

time: 245 us -> 235 us (0.959)
  matrix products: 19.9 us -> 11.3 us
  waiting for transfers between devices: 100 us -> 94.5 us
  blocking collectives: 17.9 us -> 22.1 us
    ppermute x40, waiting for transfers between devices: 78 us -> 70.4 us  [send(): return lax.ppermute(value, GRID, pairs)]
    dot_general x16, matrix products: 11.7 us -> 6.76 us  [dot_t(): lax.dot_general(a, b, (((1,), (1,)), ((), ())), preferred_element_type=F32)]
    all_to_all x1, blocking collectives: 9.68 us -> 13.9 us  [per_device(): lax.all_to_all(shared, ('gz', 'row'), 0, 0, tiled=True, axis_index_groups...]
    dot_general x13, matrix products: 8.2 us -> 4.51 us  [dot(): return jnp.dot(a, b, preferred_element_type=F32)]
    add x3 -> x2, other arithmetic: 4.85 us -> 2.03 us  [per_device(): blocks = [moved[0, flip] + moved[1, flip] for flip in (1, 2, 3)]]
  transfers between devices with their start and end apart: 50 -> 50, of which waited for: 14 -> 13; matrix products, arithmetic and copies ran while one was open for 7% -> 5% of each run, Pallas kernels for 7% -> 7%
where the time goes in v11:
time: 235 us; the launch traced here: 234 us
  waiting for transfers between devices  94.5 us (40%)
  starting transfers between devices  72.5 us (31%)
  blocking collectives  22.1 us (9%)
  Pallas kernels  16.9 us (7%)
  matrix products  11.3 us (5%)
  local copies, waits for them, and re-layouts  6.53 us (3%)
  other arithmetic  5.86 us (2%)
  between operations  4.47 us (2%)
    ppermute x40, waiting for transfers between devices, send(): return lax.ppermute(value, GRID, pairs)  70.4 us
    ppermute x40, starting transfers between devices, send(): return lax.ppermute(value, GRID, pairs)  39.9 us
    all_to_all x1, blocking collectives, per_device(): lax.all_to_all(shared, ('gz', 'row'), 0, 0, tiled=True, axis_index_groups...  13.9 us
    ppermute x2, waiting for transfers between devices, move_children(): moved[half, 2] = lax.ppermute(here, 'row', rows_of(half, 2))  11.4 us
    all_to_all x1, waiting for transfers between devices, per_device(): lax.all_to_all(pieces.reshape(layers * ROWS, 12, lanes), ('gz', 'row'), 0...  9.56 us
    ppermute x1, starting transfers between devices, per_device(): partner_factor = lax.ppermute(root_factor, 'row', swap)  8.92 us
    pallas_call x4, Pallas kernels, pieces_of(): pl.pallas_call(functools.partial(pieces_kernel, r, count), grid=(steps,),...  8.66 us
    pallas_call x5, Pallas kernels, terms_of(): pl.pallas_call(functools.partial(terms_kernel, count, len(keep) > 0), gri...  8.29 us
  transfers between devices with their start and end apart: 50, of which 13 were waited for; matrix products, arithmetic and copies ran while one was open for 5% of the time, Pallas kernels for 7%

profile of v11, /device:TPU:1, one launch (start us, length us, event | category | flops | bytes accessed | tf_op | source)
XLA Modules:
  0.0 234.2 jit_solution(12223203856172493472)
XLA Ops:
  0.6 8.9 %collective-permute-start.1 = (bf16[768,1536]{1,0:T(8,128)(2,1)}, bf16[768,1536]{1,0:T(8,128)(2,1)S(1)}, u32[]{:S(2)}, u32[]{:S(2)}) collective-permute-start(bf16[768,1536]{1,0:T(8,128)(2,1)} %refs_4_.5), channel_id=1, source_target_pairs={{0,8},{8,0},{16,24},{24,16},{32,40},{40,32},{48,56},{56,48},{64,72... | collective-permute-start | bytes 7077896 | tf_op jit(solution)/shard_map/mask/ppermute | solution.py:186
  11.1 4.9 %all-to-all-start = ((bf16[64,12,128]{2,1,0:T(8,128)(2,1)}), bf16[64,12,128]{2,1,0:T(8,128)(2,1)S(1)}, u32[]{:S(2)}, u32[]{:S(2)}) async-start(bf16[64,12,128]{2,1,0:T(8,128)(2,1)} %bitcast.76), calls=%async_computation | async-start | bytes 524288 | tf_op jit(solution)/shard_map/rhs/all_to_all | solution.py:199
  16.0 2.4 %collective-permute-start = (s32[3,6]{1,0:T(4,128)}, s32[3,6]{1,0:T(4,128)S(1)}, u32[]{:S(2)}, u32[]{:S(2)}) collective-permute-start(s32[3,6]{1,0:T(4,128)} %param.8), channel_id=1, source_target_pairs={{0,8},{8,0},{16,24},{24,16},{32,40},{40,32},{48,56},{56,48},{64,72... | collective-permute-start | bytes 224 | tf_op jit(solution)/shard_map/mask/ppermute | solution.py:187
  18.4 9.6 %all-to-all-done = bf16[64,12,128]{2,1,0:T(8,128)(2,1)S(1)} async-done(((bf16[64,12,128]{2,1,0:T(8,128)(2,1)}), bf16[64,12,128]{2,1,0:T(8,128)(2,1)S(1)}, u32[]{:S(2)}, u32[]{:S(2)}) %all-to-all-start) | async-done | bytes 196640 | tf_op jit(solution)/shard_map/rhs/all_to_all | solution.py:199
  28.1 1.7 copy-done.1
  29.7 2.1 root.9
  33.2 2.4 %collective-permute-start.10 = (bf16[512,1024]{1,0:T(8,128)(2,1)}, bf16[512,1024]{1,0:T(8,128)(2,1)S(1)}, u32[]{:S(2)}, u32[]{:S(2)}) collective-permute-start(bf16[512,1024]{1,0:T(8,128)(2,1)} %bitcast.2), channel_id=1, source_target_pairs={{0,8},{8,0},{16,24},{24,16},{32,40},{40,32},{48,56},{56,48},{1,9},... | collective-permute-start | bytes 3145736 | tf_op jit(solution)/shard_map/root/ppermute | solution.py:223
  35.6 3.0 %collective-permute-start.11 = (bf16[512,1024]{1,0:T(8,128)(2,1)}, bf16[512,1024]{1,0:T(8,128)(2,1)S(1)}, u32[]{:S(2)}, u32[]{:S(2)}) collective-permute-start(bf16[512,1024]{1,0:T(8,128)(2,1)} %bitcast.2), channel_id=1, source_target_pairs={{0,16},{8,24},{16,0},{24,8},{32,48},{40,56},{48,32},{56,40},{1,17}... | collective-permute-start | bytes 3145736 | tf_op jit(solution)/shard_map/root/ppermute | solution.py:222
  38.7 1.7 root.10
  42.4 2.2 root.11
  46.0 1.7 root.12
  48.4 1.7 root.13
  51.0 11.4 %collective-permute-done.11 = bf16[512,1024]{1,0:T(8,128)(2,1)S(1)} collective-permute-done((bf16[512,1024]{1,0:T(8,128)(2,1)}, bf16[512,1024]{1,0:T(8,128)(2,1)S(1)}, u32[]{:S(2)}, u32[]{:S(2)}) %collective-permute-start.11) | collective-permute-done | bytes 1048608 | tf_op jit(solution)/shard_map/root/ppermute | solution.py:222
  64.5 2.8 %collective-permute-start.18 = (bf16[512,1024]{1,0:T(8,128)(2,1)S(1)}, bf16[512,1024]{1,0:T(8,128)(2,1)S(1)}, u32[]{:S(2)}, u32[]{:S(2)}) collective-permute-start(bf16[512,1024]{1,0:T(8,128)(2,1)S(1)} %collective-permute-done.11), channel_id=1, source_target_pairs={{0,8},{8,0},{16,24},{24,16},{32,40},{40,32},{48,56},{56,48},{1,9},... | collective-permute-start | bytes 3145736 | tf_op jit(solution)/shard_map/root/ppermute | solution.py:216
  67.2 2.2 root.14
  70.8 1.7 root.15
  73.3 1.7 root.16
  75.0 1.6 collective-permute-start.25
  77.9 1.3 collective-permute-start.20
  79.2 11.1 %collective-permute-done.19.refs_2_ = bf16[16,1536]{1,0:T(8,128)(2,1)S(1)} collective-permute-done((bf16[16,1536]{1,0:T(8,128)(2,1)S(1)}, bf16[16,1536]{1,0:T(8,128)(2,1)S(1)}, u32[]{:S(2)}, u32[]{:S(2)}) %collective-permute-start.19) | collective-permute-done | bytes 49184 | tf_op jit(solution)/shard_map/root/ppermute | solution.py:36
  90.3 2.2 collective-permute-done.20.refs_3_
  92.4 2.2 root.17
  94.6 4.2 %collective-permute-start.23 = (bf16[2,16,768]{2,1,0:T(8,128)(2,1)S(1)}, bf16[2,16,768]{2,1,0:T(8,128)(2,1)S(1)}, u32[]{:S(2)}, u32[]{:S(2)}) collective-permute-start(bf16[2,16,768]{2,1,0:T(8,128)(2,1)S(1)} %root.17), channel_id=1, source_target_pairs={{0,1},{1,0},{8,9},{9,8},{16,17},{17,16},{24,25},{25,24},{128,129},... | collective-permute-start | bytes 147464 | tf_op jit(solution)/shard_map/root/ppermute | solution.py:36
  98.8 1.3 collective-permute-start.22
  100.2 1.3 collective-permute-start.21
  102.8 1.3 collective-permute-start.24
  104.1 1.7 collective-permute-start.29
  105.8 13.9 %all_to_all.32 = bf16[8,16,768]{2,1,0:T(8,128)(2,1)S(1)} all-to-all(bf16[8,16,768]{2,1,0:T(8,128)(2,1)S(1)} %bitcast.77), channel_id=1, replica_groups={{0,8,128,136,256,264,384,392},{16,24,144,152,272,280,400,408},{32,40,16..., dimensions={0} | all-to-all | bytes 393216 | tf_op jit(solution)/shard_map/coupling/all_to_all | solution.py:243
  120.9 4.3 %all-to-all-start.2 = ((bf16[4,32,1024]{2,1,0:T(8,128)(2,1)}), bf16[4,32,1024]{2,1,0:T(8,128)(2,1)S(1)}, u32[]{:S(2)}, u32[]{:S(2)}) async-start(bf16[4,32,1024]{2,1,0:T(8,128)(2,1)} %bitcast.10), calls=%async_computation.2 | async-start | bytes 524288 | tf_op jit(solution)/shard_map/coupling/all_to_all | solution.py:247
  127.2 3.1 %all-to-all-done.2 = bf16[4,32,1024]{2,1,0:T(8,128)(2,1)S(1)} async-done(((bf16[4,32,1024]{2,1,0:T(8,128)(2,1)}), bf16[4,32,1024]{2,1,0:T(8,128)(2,1)S(1)}, u32[]{:S(2)}, u32[]{:S(2)}) %all-to-all-start.2) | async-done | bytes 262176 | tf_op jit(solution)/shard_map/coupling/all_to_all | solution.py:247
  130.4 1.4 collective-permute-start.28
  131.9 1.3 collective-permute-start.27
  133.2 1.3 collective-permute-start.26
  134.5 1.7 broadcast_select_fusion
  136.2 1.6 add.173
  137.9 2.9 %collective-permute-done.27 = bf16[32,1024]{1,0:T(8,128)(2,1)S(1)} collective-permute-done((bf16[32,1024]{1,0:T(8,128)(2,1)S(1)}, bf16[32,1024]{1,0:T(8,128)(2,1)S(1)}, u32[]{:S(2)}, u32[]{:S(2)}) %collective-permute-start.27) | collective-permute-done | bytes 65568 | tf_op jit(solution)/shard_map/coupling/ppermute | solution.py:36
  140.8 1.6 collective-permute-done.26
  161.9 1.3 collective-permute-start.43
  163.2 1.3 collective-permute-start.42
  165.1 34.7 %collective-permute-done.43 = bf16[32,1024]{1,0:T(8,128)(2,1)S(1)} collective-permute-done((bf16[32,1024]{1,0:T(8,128)(2,1)S(1)}, bf16[32,1024]{1,0:T(8,128)(2,1)S(1)}, u32[]{:S(2)}, u32[]{:S(2)}) %collective-permute-start.43) | collective-permute-done | bytes 65568 | tf_op jit(solution)/shard_map/child/ppermute | solution.py:36
  199.8 5.5 %collective-permute-done.42 = bf16[32,1024]{1,0:T(8,128)(2,1)S(1)} collective-permute-done((bf16[32,1024]{1,0:T(8,128)(2,1)S(1)}, bf16[32,1024]{1,0:T(8,128)(2,1)S(1)}, u32[]{:S(2)}, u32[]{:S(2)}) %collective-permute-start.42) | collective-permute-done | bytes 65568 | tf_op jit(solution)/shard_map/child/ppermute | solution.py:36
  207.1 1.9 collective-permute-start.46
  209.1 1.3 collective-permute-start.45
  210.4 1.3 collective-permute-start.44
  212.8 8.0 %collective-permute-done.44 = bf16[32,2048]{1,0:T(8,128)(2,1)S(1)} collective-permute-done((bf16[32,2048]{1,0:T(8,128)(2,1)S(1)}, bf16[32,2048]{1,0:T(8,128)(2,1)S(1)}, u32[]{:S(2)}, u32[]{:S(2)}) %collective-permute-start.44) | collective-permute-done | bytes 131104 | tf_op jit(solution)/shard_map/child/ppermute | solution.py:36
  220.9 1.3 collective-permute-start.47
  222.3 1.9 collective-permute-done.47
  225.4 8.2 %all_to_all.33 = bf16[4,32,512]{2,1,0:T(8,128)(2,1)S(1)} all-to-all(bf16[4,32,512]{2,1,0:T(8,128)(2,1)S(1)} %bitcast.79), channel_id=1, replica_groups={{0,8,16,24},{32,40,48,56},{64,72,80,88},{96,104,112,120},{1,9,17,25},{3..., dimensions={0} | all-to-all | bytes 262144 | tf_op jit(solution)/shard_map/child/all_to_all | solution.py:281
  (161 shorter events, 40.0 us)
Async XLA Ops:
  0.6 27.4 %collective-permute-start.1 = (bf16[768,1536]{1,0:T(8,128)(2,1)}, bf16[768,1536]{1,0:T(8,128)(2,1)S(1)}, u32[]{:S(2)}, u32[]{:S(2)}) collective-permute-start(bf16[768,1536]{1,0:T(8,128)(2,1)} %refs_4_.5), channel_id=1, source_target_pairs={{0,8},{8,0},{16,24},{24,16},{32,40},{40,32},{48,56},{56,48},{64,72... | collective-permute-start | bytes 7077896 | tf_op jit(solution)/shard_map/mask/ppermute | solution.py:186
  11.1 16.9 %all-to-all-start = ((bf16[64,12,128]{2,1,0:T(8,128)(2,1)}), bf16[64,12,128]{2,1,0:T(8,128)(2,1)S(1)}, u32[]{:S(2)}, u32[]{:S(2)}) async-start(bf16[64,12,128]{2,1,0:T(8,128)(2,1)} %bitcast.76), calls=%async_computation | async-start | bytes 524288 | tf_op jit(solution)/shard_map/rhs/all_to_all | solution.py:199
  16.0 17.3 %collective-permute-start = (s32[3,6]{1,0:T(4,128)}, s32[3,6]{1,0:T(4,128)S(1)}, u32[]{:S(2)}, u32[]{:S(2)}) collective-permute-start(s32[3,6]{1,0:T(4,128)} %param.8), channel_id=1, source_target_pairs={{0,8},{8,0},{16,24},{24,16},{32,40},{40,32},{48,56},{56,48},{64,72... | collective-permute-start | bytes 224 | tf_op jit(solution)/shard_map/mask/ppermute | solution.py:187
  31.9 6.7 %collective-permute-start.3 = (bf16[2,16,768]{2,1,0:T(8,128)(2,1)S(1)}, bf16[2,16,768]{2,1,0:T(8,128)(2,1)S(1)}, u32[]{:S(2)}, u32[]{:S(2)}) collective-permute-start(bf16[2,16,768]{2,1,0:T(8,128)(2,1)S(1)} %root.9), channel_id=1, source_target_pairs={{102,101},{103,100},{110,109},{111,108},{118,117},{119,116},{126,1... | collective-permute-start | bytes 147464 | tf_op jit(solution)/shard_map/root/ppermute | solution.py:36
  32.5 6.0 %collective-permute-start.2 = (bf16[2,16,768]{2,1,0:T(8,128)(2,1)S(1)}, bf16[2,16,768]{2,1,0:T(8,128)(2,1)S(1)}, u32[]{:S(2)}, u32[]{:S(2)}) collective-permute-start(bf16[2,16,768]{2,1,0:T(8,128)(2,1)S(1)} %root.9), channel_id=1, source_target_pairs={{102,100},{103,101},{110,108},{111,109},{118,116},{119,117},{126,1... | collective-permute-start | bytes 147464 | tf_op jit(solution)/shard_map/root/ppermute | solution.py:36
  33.2 16.8 %collective-permute-start.10 = (bf16[512,1024]{1,0:T(8,128)(2,1)}, bf16[512,1024]{1,0:T(8,128)(2,1)S(1)}, u32[]{:S(2)}, u32[]{:S(2)}) collective-permute-start(bf16[512,1024]{1,0:T(8,128)(2,1)} %bitcast.2), channel_id=1, source_target_pairs={{0,8},{8,0},{16,24},{24,16},{32,40},{40,32},{48,56},{56,48},{1,9},... | collective-permute-start | bytes 3145736 | tf_op jit(solution)/shard_map/root/ppermute | solution.py:223
  35.6 26.8 %collective-permute-start.11 = (bf16[512,1024]{1,0:T(8,128)(2,1)}, bf16[512,1024]{1,0:T(8,128)(2,1)S(1)}, u32[]{:S(2)}, u32[]{:S(2)}) collective-permute-start(bf16[512,1024]{1,0:T(8,128)(2,1)} %bitcast.2), channel_id=1, source_target_pairs={{0,16},{8,24},{16,0},{24,8},{32,48},{40,56},{48,32},{56,40},{1,17}... | collective-permute-start | bytes 3145736 | tf_op jit(solution)/shard_map/root/ppermute | solution.py:222
  40.3 2.0 collective-permute-start.4
  41.0 1.4 collective-permute-start.5
  41.7 2.9 %collective-permute-start.6 = (bf16[2,16,768]{2,1,0:T(8,128)(2,1)S(1)}, bf16[2,16,768]{2,1,0:T(8,128)(2,1)S(1)}, u32[]{:S(2)}, u32[]{:S(2)}) collective-permute-start(bf16[2,16,768]{2,1,0:T(8,128)(2,1)S(1)} %add_convert_fusion.13.refs_2_.refs_6_), channel_id=1, source_target_pairs={{100,98},{101,99},{108,106},{109,107},{116,114},{117,115},{124,122... | collective-permute-start | bytes 147464 | tf_op jit(solution)/shard_map/root/ppermute | solution.py:36
  44.6 3.7 %collective-permute-start.8 = (bf16[2,16,768]{2,1,0:T(8,128)(2,1)S(1)}, bf16[2,16,768]{2,1,0:T(8,128)(2,1)S(1)}, u32[]{:S(2)}, u32[]{:S(2)}) collective-permute-start(bf16[2,16,768]{2,1,0:T(8,128)(2,1)S(1)} %add_convert_fusion.12.refs_2_), channel_id=1, source_target_pairs={{68,67},{69,66},{76,75},{77,74},{84,83},{85,82},{92,91},{93,90},{1... | collective-permute-start | bytes 147464 | tf_op jit(solution)/shard_map/root/ppermute | solution.py:36
  45.3 3.0 %collective-permute-start.7 = (bf16[2,16,768]{2,1,0:T(8,128)(2,1)S(1)}, bf16[2,16,768]{2,1,0:T(8,128)(2,1)S(1)}, u32[]{:S(2)}, u32[]{:S(2)}) collective-permute-start(bf16[2,16,768]{2,1,0:T(8,128)(2,1)S(1)} %add_convert_fusion.12.refs_2_), channel_id=1, source_target_pairs={{68,66},{69,67},{76,74},{77,75},{84,82},{85,83},{92,90},{93,91},{9... | collective-permute-start | bytes 147464 | tf_op jit(solution)/shard_map/root/ppermute | solution.py:36
  47.6 0.7 collective-permute-start.9
  62.5 4.8 %collective-permute-start.12 = (bf16[16,1536]{1,0:T(8,128)(2,1)S(1)}, bf16[16,1536]{1,0:T(8,128)(2,1)S(1)}, u32[]{:S(2)}, u32[]{:S(2)}) collective-permute-start(bf16[16,1536]{1,0:T(8,128)(2,1)S(1)} %root.13), channel_id=1, source_target_pairs={{66,34},{67,35},{74,42},{75,43},{82,50},{83,51},{90,58},{91,59},{9... | collective-permute-start | bytes 147464 | tf_op jit(solution)/shard_map/root/ppermute | solution.py:36
  63.1 4.1 %collective-permute-start.13 = (bf16[16,1536]{1,0:T(8,128)(2,1)S(1)}, bf16[16,1536]{1,0:T(8,128)(2,1)S(1)}, u32[]{:S(2)}, u32[]{:S(2)}) collective-permute-start(bf16[16,1536]{1,0:T(8,128)(2,1)S(1)} %root.13), channel_id=1, source_target_pairs={{66,50},{67,51},{74,58},{75,59},{82,34},{83,35},{90,42},{91,43},{1... | collective-permute-start | bytes 147464 | tf_op jit(solution)/shard_map/root/ppermute | solution.py:36
  63.8 5.7 %collective-permute-start.14 = (bf16[2,16,768]{2,1,0:T(8,128)(2,1)S(1)}, bf16[2,16,768]{2,1,0:T(8,128)(2,1)S(1)}, u32[]{:S(2)}, u32[]{:S(2)}) collective-permute-start(bf16[2,16,768]{2,1,0:T(8,128)(2,1)S(1)} %add_convert_fusion.11.refs_2_.refs_6_), channel_id=1, source_target_pairs={{66,64},{67,65},{74,72},{75,73},{82,80},{83,81},{90,88},{91,89},{1... | collective-permute-start | bytes 147464 | tf_op jit(solution)/shard_map/root/ppermute | solution.py:36
  64.5 10.5 %collective-permute-start.18 = (bf16[512,1024]{1,0:T(8,128)(2,1)S(1)}, bf16[512,1024]{1,0:T(8,128)(2,1)S(1)}, u32[]{:S(2)}, u32[]{:S(2)}) collective-permute-start(bf16[512,1024]{1,0:T(8,128)(2,1)S(1)} %collective-permute-done.11), channel_id=1, source_target_pairs={{0,8},{8,0},{16,24},{24,16},{32,40},{40,32},{48,56},{56,48},{1,9},... | collective-permute-start | bytes 3145736 | tf_op jit(solution)/shard_map/root/ppermute | solution.py:216
  69.5 3.7 %collective-permute-start.16 = (bf16[2,16,768]{2,1,0:T(8,128)(2,1)S(1)}, bf16[2,16,768]{2,1,0:T(8,128)(2,1)S(1)}, u32[]{:S(2)}, u32[]{:S(2)}) collective-permute-start(bf16[2,16,768]{2,1,0:T(8,128)(2,1)S(1)} %add_convert_fusion.10.refs_2_), channel_id=1, source_target_pairs={{34,33},{35,32},{42,41},{43,40},{50,49},{51,48},{58,57},{59,56},{6... | collective-permute-start | bytes 147464 | tf_op jit(solution)/shard_map/root/ppermute | solution.py:36
  70.2 3.0 %collective-permute-start.15 = (bf16[2,16,768]{2,1,0:T(8,128)(2,1)S(1)}, bf16[2,16,768]{2,1,0:T(8,128)(2,1)S(1)}, u32[]{:S(2)}, u32[]{:S(2)}) collective-permute-start(bf16[2,16,768]{2,1,0:T(8,128)(2,1)S(1)} %add_convert_fusion.10.refs_2_), channel_id=1, source_target_pairs={{34,32},{35,33},{42,40},{43,41},{50,48},{51,49},{58,56},{59,57},{6... | collective-permute-start | bytes 147464 | tf_op jit(solution)/shard_map/root/ppermute | solution.py:36
  72.5 0.7 collective-permute-start.17
  75.0 30.8 %collective-permute-start.25 = (bf16[512,1024]{1,0:T(8,128)(2,1)}, bf16[512,1024]{1,0:T(8,128)(2,1)}, u32[]{:S(2)}, u32[]{:S(2)}) collective-permute-start(bf16[512,1024]{1,0:T(8,128)(2,1)} %bitcast.2), channel_id=1, source_target_pairs={{64,80},{72,88},{80,64},{88,72},{96,112},{104,120},{112,96},{120,1... | collective-permute-start | bytes 3145736 | tf_op jit(solution)/shard_map/root/ppermute | solution.py:222
  76.6 13.7 %collective-permute-start.19 = (bf16[16,1536]{1,0:T(8,128)(2,1)S(1)}, bf16[16,1536]{1,0:T(8,128)(2,1)S(1)}, u32[]{:S(2)}, u32[]{:S(2)}) collective-permute-start(bf16[16,1536]{1,0:T(8,128)(2,1)S(1)} %root.16), channel_id=1, source_target_pairs={{32,0},{33,1},{40,8},{41,9},{48,16},{49,17},{56,24},{57,25},{160,1... | collective-permute-start | bytes 147464 | tf_op jit(solution)/shard_map/root/ppermute | solution.py:36
  77.9 14.5 %collective-permute-start.20 = (bf16[16,1536]{1,0:T(8,128)(2,1)S(1)}, bf16[16,1536]{1,0:T(8,128)(2,1)S(1)}, u32[]{:S(2)}, u32[]{:S(2)}) collective-permute-start(bf16[16,1536]{1,0:T(8,128)(2,1)S(1)} %root.16), channel_id=1, source_target_pairs={{32,16},{33,17},{40,24},{41,25},{48,0},{49,1},{56,8},{57,9},{160,1... | collective-permute-start | bytes 147464 | tf_op jit(solution)/shard_map/root/ppermute | solution.py:36
  94.6 6.8 %collective-permute-start.23 = (bf16[2,16,768]{2,1,0:T(8,128)(2,1)S(1)}, bf16[2,16,768]{2,1,0:T(8,128)(2,1)S(1)}, u32[]{:S(2)}, u32[]{:S(2)}) collective-permute-start(bf16[2,16,768]{2,1,0:T(8,128)(2,1)S(1)} %root.17), channel_id=1, source_target_pairs={{0,1},{1,0},{8,9},{9,8},{16,17},{17,16},{24,25},{25,24},{128,129},... | collective-permute-start | bytes 147464 | tf_op jit(solution)/shard_map/root/ppermute | solution.py:36
  98.8 2.6 %collective-permute-start.22 = (bf16[2,16,768]{2,1,0:T(8,128)(2,1)S(1)}, bf16[2,16,768]{2,1,0:T(8,128)(2,1)S(1)}, u32[]{:S(2)}, u32[]{:S(2)}) collective-permute-start(bf16[2,16,768]{2,1,0:T(8,128)(2,1)S(1)} %root.17), channel_id=1, source_target_pairs={{0,7},{1,6},{8,15},{9,14},{16,23},{17,22},{24,31},{25,30},{34,35},... | collective-permute-start | bytes 147464 | tf_op jit(solution)/shard_map/root/ppermute | solution.py:36
  100.2 2.6 %collective-permute-start.21 = (bf16[2,16,768]{2,1,0:T(8,128)(2,1)S(1)}, bf16[2,16,768]{2,1,0:T(8,128)(2,1)S(1)}, u32[]{:S(2)}, u32[]{:S(2)}) collective-permute-start(bf16[2,16,768]{2,1,0:T(8,128)(2,1)S(1)} %root.17), channel_id=1, source_target_pairs={{0,6},{1,7},{8,14},{9,15},{16,22},{17,23},{24,30},{25,31},{32,38},... | collective-permute-start | bytes 147464 | tf_op jit(solution)/shard_map/root/ppermute | solution.py:36
  102.8 3.0 %collective-permute-start.24 = (bf16[2,16,768]{2,1,0:T(8,128)(2,1)S(1)}, bf16[2,16,768]{2,1,0:T(8,128)(2,1)S(1)}, u32[]{:S(2)}, u32[]{:S(2)}) collective-permute-start(bf16[2,16,768]{2,1,0:T(8,128)(2,1)S(1)} %add_convert_fusion.8), channel_id=1, source_target_pairs={{0,2},{1,3},{8,10},{9,11},{16,18},{17,19},{24,26},{25,27},{6,4},{7... | collective-permute-start | bytes 147464 | tf_op jit(solution)/shard_map/root/ppermute | solution.py:36
  104.1 30.4 %collective-permute-start.29 = (bf16[512,1024]{1,0:T(8,128)(2,1)}, bf16[512,1024]{1,0:T(8,128)(2,1)}, u32[]{:S(2)}, u32[]{:S(2)}) collective-permute-start(bf16[512,1024]{1,0:T(8,128)(2,1)} %bitcast.2), channel_id=1, source_target_pairs={{64,72},{72,64},{80,88},{88,80},{96,104},{104,96},{112,120},{120,1... | collective-permute-start | bytes 3145736 | tf_op jit(solution)/shard_map/root/ppermute | solution.py:223
  120.9 9.5 %all-to-all-start.2 = ((bf16[4,32,1024]{2,1,0:T(8,128)(2,1)}), bf16[4,32,1024]{2,1,0:T(8,128)(2,1)S(1)}, u32[]{:S(2)}, u32[]{:S(2)}) async-start(bf16[4,32,1024]{2,1,0:T(8,128)(2,1)} %bitcast.10), calls=%async_computation.2 | async-start | bytes 524288 | tf_op jit(solution)/shard_map/coupling/all_to_all | solution.py:247
  126.5 18.1 %collective-permute-start.30 = (bf16[512,1024]{1,0:T(8,128)(2,1)}, bf16[512,1024]{1,0:T(8,128)(2,1)S(1)}, u32[]{:S(2)}, u32[]{:S(2)}) collective-permute-start(bf16[512,1024]{1,0:T(8,128)(2,1)} %collective-permute-done.25), channel_id=1, source_target_pairs={{64,72},{72,64},{80,88},{88,80},{96,104},{104,96},{112,120},{120,1... | collective-permute-start | bytes 3145736 | tf_op jit(solution)/shard_map/coupling/ppermute | solution.py:238
  130.4 7.4 %collective-permute-start.28 = (bf16[32,1024]{1,0:T(8,128)(2,1)S(1)}, bf16[32,1024]{1,0:T(8,128)(2,1)S(1)}, u32[]{:S(2)}, u32[]{:S(2)}) collective-permute-start(bf16[32,1024]{1,0:T(8,128)(2,1)S(1)} %reduce_sum.22), channel_id=1, source_target_pairs={{96,0},{97,1},{104,8},{105,9},{112,16},{113,17},{120,24},{121,25},... | collective-permute-start | bytes 196616 | tf_op jit(solution)/shard_map/coupling/ppermute | solution.py:36
  131.9 8.9 %collective-permute-start.27 = (bf16[32,1024]{1,0:T(8,128)(2,1)S(1)}, bf16[32,1024]{1,0:T(8,128)(2,1)S(1)}, u32[]{:S(2)}, u32[]{:S(2)}) collective-permute-start(bf16[32,1024]{1,0:T(8,128)(2,1)S(1)} %reduce_sum.22), channel_id=1, source_target_pairs={{64,0},{65,1},{72,8},{73,9},{80,16},{81,17},{88,24},{89,25},{98,34... | collective-permute-start | bytes 196616 | tf_op jit(solution)/shard_map/coupling/ppermute | solution.py:36
  133.2 9.2 %collective-permute-start.26 = (bf16[32,1024]{1,0:T(8,128)(2,1)S(1)}, bf16[32,1024]{1,0:T(8,128)(2,1)S(1)}, u32[]{:S(2)}, u32[]{:S(2)}) collective-permute-start(bf16[32,1024]{1,0:T(8,128)(2,1)S(1)} %reduce_sum.22), channel_id=1, source_target_pairs={{32,0},{33,1},{40,8},{41,9},{48,16},{49,17},{56,24},{57,25},{66,34... | collective-permute-start | bytes 196616 | tf_op jit(solution)/shard_map/coupling/ppermute | solution.py:36
  145.5 1.4 collective-permute-start.32
  148.1 2.0 collective-permute-start.33
  149.5 2.4 %collective-permute-start.34 = (bf16[32,2048]{1,0:T(8,128)(2,1)S(1)}, bf16[32,2048]{1,0:T(8,128)(2,1)S(1)}, u32[]{:S(2)}, u32[]{:S(2)}) collective-permute-start(bf16[32,2048]{1,0:T(8,128)(2,1)S(1)} %add_convert_fusion.6), channel_id=1, source_target_pairs={{100,98},{101,99},{108,106},{109,107},{116,114},{117,115},{124,122... | collective-permute-start | bytes 393224 | tf_op jit(solution)/shard_map/child/ppermute | solution.py:36
  152.0 1.5 collective-permute-start.36
  152.7 0.9 collective-permute-start.35
  154.8 2.7 %collective-permute-start.37 = (bf16[32,1024]{1,0:T(8,128)(2,1)S(1)}, bf16[32,1024]{1,0:T(8,128)(2,1)S(1)}, u32[]{:S(2)}, u32[]{:S(2)}) collective-permute-start(bf16[32,1024]{1,0:T(8,128)(2,1)S(1)} %fusion.5), channel_id=1, source_target_pairs={{66,34},{67,35},{74,42},{75,43},{82,50},{83,51},{90,58},{91,59},{9... | collective-permute-start | bytes 196616 | tf_op jit(solution)/shard_map/child/ppermute | solution.py:36
  155.5 2.0 collective-permute-start.38
  156.8 2.4 %collective-permute-start.39 = (bf16[32,2048]{1,0:T(8,128)(2,1)S(1)}, bf16[32,2048]{1,0:T(8,128)(2,1)S(1)}, u32[]{:S(2)}, u32[]{:S(2)}) collective-permute-start(bf16[32,2048]{1,0:T(8,128)(2,1)S(1)} %add_convert_fusion.4), channel_id=1, source_target_pairs={{66,64},{67,65},{74,72},{75,73},{82,80},{83,81},{90,88},{91,89},{1... | collective-permute-start | bytes 393224 | tf_op jit(solution)/shard_map/child/ppermute | solution.py:36
  159.3 1.4 collective-permute-start.41
  161.9 37.9 %collective-permute-start.43 = (bf16[32,1024]{1,0:T(8,128)(2,1)S(1)}, bf16[32,1024]{1,0:T(8,128)(2,1)S(1)}, u32[]{:S(2)}, u32[]{:S(2)}) collective-permute-start(bf16[32,1024]{1,0:T(8,128)(2,1)S(1)} %fusion.15), channel_id=1, source_target_pairs={{64,0},{65,1},{72,8},{73,9},{80,16},{81,17},{88,24},{89,25},{192,1... | collective-permute-start | bytes 196616 | tf_op jit(solution)/shard_map/child/ppermute | solution.py:36
  163.2 42.2 %collective-permute-start.42 = (bf16[32,1024]{1,0:T(8,128)(2,1)S(1)}, bf16[32,1024]{1,0:T(8,128)(2,1)S(1)}, u32[]{:S(2)}, u32[]{:S(2)}) collective-permute-start(bf16[32,1024]{1,0:T(8,128)(2,1)S(1)} %fusion.15), channel_id=1, source_target_pairs={{32,0},{33,1},{40,8},{41,9},{48,16},{49,17},{56,24},{57,25},{160,1... | collective-permute-start | bytes 196616 | tf_op jit(solution)/shard_map/child/ppermute | solution.py:36
  207.1 5.7 %collective-permute-start.46 = (bf16[32,2048]{1,0:T(8,128)(2,1)S(1)}, bf16[32,2048]{1,0:T(8,128)(2,1)S(1)}, u32[]{:S(2)}, u32[]{:S(2)}) collective-permute-start(bf16[32,2048]{1,0:T(8,128)(2,1)S(1)} %maximum_select_fusion.3), channel_id=1, source_target_pairs={{0,1},{1,0},{8,9},{9,8},{16,17},{17,16},{24,25},{25,24},{128,129},... | collective-permute-start | bytes 393224 | tf_op jit(solution)/shard_map/child/ppermute | solution.py:36
  209.1 3.8 %collective-permute-start.45 = (bf16[32,2048]{1,0:T(8,128)(2,1)S(1)}, bf16[32,2048]{1,0:T(8,128)(2,1)S(1)}, u32[]{:S(2)}, u32[]{:S(2)}) collective-permute-start(bf16[32,2048]{1,0:T(8,128)(2,1)S(1)} %maximum_select_fusion.3), channel_id=1, source_target_pairs={{0,7},{1,6},{8,15},{9,14},{16,23},{17,22},{24,31},{25,30},{34,35},... | collective-permute-start | bytes 393224 | tf_op jit(solution)/shard_map/child/ppermute | solution.py:36
  210.4 10.5 %collective-permute-start.44 = (bf16[32,2048]{1,0:T(8,128)(2,1)S(1)}, bf16[32,2048]{1,0:T(8,128)(2,1)S(1)}, u32[]{:S(2)}, u32[]{:S(2)}) collective-permute-start(bf16[32,2048]{1,0:T(8,128)(2,1)S(1)} %maximum_select_fusion.3), channel_id=1, source_target_pairs={{0,6},{1,7},{8,14},{9,15},{16,22},{17,23},{24,30},{25,31},{32,38},... | collective-permute-start | bytes 393224 | tf_op jit(solution)/shard_map/child/ppermute | solution.py:36
  220.9 3.2 %collective-permute-start.47 = (bf16[32,2048]{1,0:T(8,128)(2,1)S(1)}, bf16[32,2048]{1,0:T(8,128)(2,1)S(1)}, u32[]{:S(2)}, u32[]{:S(2)}) collective-permute-start(bf16[32,2048]{1,0:T(8,128)(2,1)S(1)} %add_convert_fusion.1), channel_id=1, source_target_pairs={{0,2},{1,3},{8,10},{9,11},{16,18},{17,19},{24,26},{25,27},{6,4},{7... | collective-permute-start | bytes 393224 | tf_op jit(solution)/shard_map/child/ppermute | solution.py:36
  (12 other events, 227.6 us)

commit v12 on v10

--- a/solution.py
+++ b/solution.py
@@ -211,7 +211,7 @@
 
     def move_children(r, value):
         if r == 1:
-            value, moved[0, 1], there = lax.optimization_barrier((value, moved[0, 1], moved[0, 2]))
+            value, moved[1], there = lax.optimization_barrier((value, moved[1], moved[0, 2]))
             moved[0, 2] = there
             moved[0, 3] = lax.ppermute(there, "row", rows_of(0, 1))
         if r == 0:
@@ -220,7 +220,8 @@
             half = 0 if r == 3 else 1
             value, here = lax.optimization_barrier((value, child_here))
             moved[half, 2] = lax.ppermute(here, "row", rows_of(half, 2))
-            moved[half, 1] = lax.ppermute(here, "row", rows_of(half, 1))
+            if r == 3:
+                moved[1] = lax.ppermute(here, "row", swap)
         return value
 
     with jax.named_scope("root"):
@@ -255,7 +256,8 @@
         child_rhs = (2 * bits - 1).astype(F32) - coupled
 
     with jax.named_scope("child"):
-        blocks = [child_here] + [moved[0, flip] + moved[1, flip] for flip in (1, 2, 3)]
+        blocks = [moved[0, flip] + moved[1, flip] for flip in (2, 3)]
+        blocks = [jnp.where(row_index < 0, blocks[0], near) for near in (child_here, moved[1])] + blocks
         rows = child_here.shape[0]
 
         def child_terms(current, carried):

time: 245 us -> 235 us (0.959)
  waiting for transfers between devices: 100 us -> 87.1 us
  blocking collectives: 17.9 us -> 28.6 us
  matrix products: 19.9 us -> 11.3 us
    ppermute x40, waiting for transfers between devices: 78 us -> 65.9 us  [send(): return lax.ppermute(value, GRID, pairs)]
    all_to_all x1, blocking collectives: 8.17 us -> 14.1 us  [per_device(): lax.all_to_all(child_rows, 'row', 0, 0, tiled=True, axis_index_groups=qua...]
    dot_general x16, matrix products: 11.7 us -> 6.75 us  [dot_t(): lax.dot_general(a, b, (((1,), (1,)), ((), ())), preferred_element_type=F32)]
    all_to_all x1, blocking collectives: 9.68 us -> 14.5 us  [per_device(): lax.all_to_all(shared, ('gz', 'row'), 0, 0, tiled=True, axis_index_groups...]
    dot_general x13, matrix products: 8.2 us -> 4.51 us  [dot(): return jnp.dot(a, b, preferred_element_type=F32)]
    all_to_all x1, waiting for transfers between devices: 3.51 us -> 0.14 us  [per_device(): lax.all_to_all(terms, 'row', 0, 0, tiled=True, axis_index_groups=quarters)]
    select_n x0 -> x2, other arithmetic: none -> 3.37 us  [per_device(): jnp.where(row_index < 0, blocks[0], near)]
    add x3 -> x1, other arithmetic: 4.85 us -> 1.62 us  [per_device(): blocks = [moved[0, flip] + moved[1, flip] for flip in (2, 3)]]
  transfers between devices with their start and end apart: 50 -> 49, of which waited for: 14 -> 13; matrix products, arithmetic and copies ran while one was open for 7% -> 5% of each run, Pallas kernels for 7% -> 7%
where the time goes in v12:
time: 235 us; the launch traced here: 233 us
  waiting for transfers between devices  87.1 us (37%)
  starting transfers between devices  71.5 us (30%)
  blocking collectives  28.6 us (12%)
  Pallas kernels  16.9 us (7%)
  matrix products  11.3 us (5%)
  other arithmetic  7.11 us (3%)
  local copies, waits for them, and re-layouts  6.48 us (3%)
  between operations  4.37 us (2%)
    ppermute x40, waiting for transfers between devices, send(): return lax.ppermute(value, GRID, pairs)  65.9 us
    ppermute x40, starting transfers between devices, send(): return lax.ppermute(value, GRID, pairs)  39.6 us
    all_to_all x1, blocking collectives, per_device(): lax.all_to_all(shared, ('gz', 'row'), 0, 0, tiled=True, axis_index_groups...  14.5 us
    all_to_all x1, blocking collectives, per_device(): lax.all_to_all(child_rows, 'row', 0, 0, tiled=True, axis_index_groups=qua...  14.1 us
    ppermute x2, waiting for transfers between devices, move_children(): moved[half, 2] = lax.ppermute(here, 'row', rows_of(half, 2))  11.4 us
    all_to_all x1, waiting for transfers between devices, per_device(): lax.all_to_all(pieces.reshape(layers * ROWS, 12, lanes), ('gz', 'row'), 0...  9.56 us
    ppermute x1, starting transfers between devices, per_device(): partner_factor = lax.ppermute(root_factor, 'row', swap)  8.92 us
    pallas_call x4, Pallas kernels, pieces_of(): pl.pallas_call(functools.partial(pieces_kernel, r, count), grid=(steps,),...  8.66 us
  transfers between devices with their start and end apart: 49, of which 13 were waited for; matrix products, arithmetic and copies ran while one was open for 5% of the time, Pallas kernels for 7%

profile of v12, /device:TPU:1, one launch (start us, length us, event | category | flops | bytes accessed | tf_op | source)
XLA Modules:
  0.0 233.4 jit_solution(4146452544838230567)
XLA Ops:
  0.6 8.9 %collective-permute-start.1 = (bf16[768,1536]{1,0:T(8,128)(2,1)}, bf16[768,1536]{1,0:T(8,128)(2,1)S(1)}, u32[]{:S(2)}, u32[]{:S(2)}) collective-permute-start(bf16[768,1536]{1,0:T(8,128)(2,1)} %refs_4_.5), channel_id=1, source_target_pairs={{0,8},{8,0},{16,24},{24,16},{32,40},{40,32},{48,56},{56,48},{64,72... | collective-permute-start | bytes 7077896 | tf_op jit(solution)/shard_map/mask/ppermute | solution.py:186
  11.1 4.9 %all-to-all-start = ((bf16[64,12,128]{2,1,0:T(8,128)(2,1)}), bf16[64,12,128]{2,1,0:T(8,128)(2,1)S(1)}, u32[]{:S(2)}, u32[]{:S(2)}) async-start(bf16[64,12,128]{2,1,0:T(8,128)(2,1)} %bitcast.76), calls=%async_computation | async-start | bytes 524288 | tf_op jit(solution)/shard_map/rhs/all_to_all | solution.py:199
  15.9 2.4 %collective-permute-start = (s32[3,6]{1,0:T(4,128)}, s32[3,6]{1,0:T(4,128)S(1)}, u32[]{:S(2)}, u32[]{:S(2)}) collective-permute-start(s32[3,6]{1,0:T(4,128)} %param.8), channel_id=1, source_target_pairs={{0,8},{8,0},{16,24},{24,16},{32,40},{40,32},{48,56},{56,48},{64,72... | collective-permute-start | bytes 224 | tf_op jit(solution)/shard_map/mask/ppermute | solution.py:187
  18.4 9.6 %all-to-all-done = bf16[64,12,128]{2,1,0:T(8,128)(2,1)S(1)} async-done(((bf16[64,12,128]{2,1,0:T(8,128)(2,1)}), bf16[64,12,128]{2,1,0:T(8,128)(2,1)S(1)}, u32[]{:S(2)}, u32[]{:S(2)}) %all-to-all-start) | async-done | bytes 196640 | tf_op jit(solution)/shard_map/rhs/all_to_all | solution.py:199
  28.1 1.7 copy-done.1
  29.7 2.1 root.9
  33.2 2.4 %collective-permute-start.10 = (bf16[512,1024]{1,0:T(8,128)(2,1)}, bf16[512,1024]{1,0:T(8,128)(2,1)S(1)}, u32[]{:S(2)}, u32[]{:S(2)}) collective-permute-start(bf16[512,1024]{1,0:T(8,128)(2,1)} %bitcast.2), channel_id=1, source_target_pairs={{0,8},{8,0},{16,24},{24,16},{32,40},{40,32},{48,56},{56,48},{64,72... | collective-permute-start | bytes 3145736 | tf_op jit(solution)/shard_map/root/ppermute | solution.py:224
  35.6 3.0 %collective-permute-start.11 = (bf16[512,1024]{1,0:T(8,128)(2,1)}, bf16[512,1024]{1,0:T(8,128)(2,1)S(1)}, u32[]{:S(2)}, u32[]{:S(2)}) collective-permute-start(bf16[512,1024]{1,0:T(8,128)(2,1)} %bitcast.2), channel_id=1, source_target_pairs={{0,16},{8,24},{16,0},{24,8},{32,48},{40,56},{48,32},{56,40},{1,17}... | collective-permute-start | bytes 3145736 | tf_op jit(solution)/shard_map/root/ppermute | solution.py:222
  38.6 1.7 root.10
  42.3 2.2 root.11
  45.9 1.7 root.12
  48.4 1.7 root.13
  51.0 11.4 %collective-permute-done.11 = bf16[512,1024]{1,0:T(8,128)(2,1)S(1)} collective-permute-done((bf16[512,1024]{1,0:T(8,128)(2,1)}, bf16[512,1024]{1,0:T(8,128)(2,1)S(1)}, u32[]{:S(2)}, u32[]{:S(2)}) %collective-permute-start.11) | collective-permute-done | bytes 1048608 | tf_op jit(solution)/shard_map/root/ppermute | solution.py:222
  64.4 2.8 %collective-permute-start.18 = (bf16[512,1024]{1,0:T(8,128)(2,1)S(1)}, bf16[512,1024]{1,0:T(8,128)(2,1)S(1)}, u32[]{:S(2)}, u32[]{:S(2)}) collective-permute-start(bf16[512,1024]{1,0:T(8,128)(2,1)S(1)} %collective-permute-done.11), channel_id=1, source_target_pairs={{0,8},{8,0},{16,24},{24,16},{32,40},{40,32},{48,56},{56,48},{1,9},... | collective-permute-start | bytes 3145736 | tf_op jit(solution)/shard_map/root/ppermute | solution.py:216
  67.2 2.2 root.14
  70.8 1.7 root.15
  73.2 1.7 root.16
  74.9 1.7 collective-permute-start.25
  76.6 1.3 collective-permute-start.19
  77.9 1.3 collective-permute-start.20
  79.2 11.1 %collective-permute-done.19.refs_2_ = bf16[16,1536]{1,0:T(8,128)(2,1)S(1)} collective-permute-done((bf16[16,1536]{1,0:T(8,128)(2,1)S(1)}, bf16[16,1536]{1,0:T(8,128)(2,1)S(1)}, u32[]{:S(2)}, u32[]{:S(2)}) %collective-permute-start.19) | collective-permute-done | bytes 49184 | tf_op jit(solution)/shard_map/root/ppermute | solution.py:36
  90.3 2.2 collective-permute-done.20.refs_3_
  92.4 2.2 root.17
  94.6 4.1 %collective-permute-start.23 = (bf16[2,16,768]{2,1,0:T(8,128)(2,1)S(1)}, bf16[2,16,768]{2,1,0:T(8,128)(2,1)S(1)}, u32[]{:S(2)}, u32[]{:S(2)}) collective-permute-start(bf16[2,16,768]{2,1,0:T(8,128)(2,1)S(1)} %root.17), channel_id=1, source_target_pairs={{0,1},{1,0},{8,9},{9,8},{16,17},{17,16},{24,25},{25,24},{128,129},... | collective-permute-start | bytes 147464 | tf_op jit(solution)/shard_map/root/ppermute | solution.py:36
  98.7 1.3 collective-permute-start.22
  100.0 1.3 collective-permute-start.21
  102.6 1.3 collective-permute-start.24
  105.1 14.5 %all_to_all.32 = bf16[8,16,768]{2,1,0:T(8,128)(2,1)S(1)} all-to-all(bf16[8,16,768]{2,1,0:T(8,128)(2,1)S(1)} %bitcast.77), channel_id=1, replica_groups={{0,8,128,136,256,264,384,392},{16,24,144,152,272,280,400,408},{32,40,16..., dimensions={0} | all-to-all | bytes 393216 | tf_op jit(solution)/shard_map/coupling/all_to_all | solution.py:244
  120.7 4.3 %all-to-all-start.2 = ((bf16[4,32,1024]{2,1,0:T(8,128)(2,1)}), bf16[4,32,1024]{2,1,0:T(8,128)(2,1)S(1)}, u32[]{:S(2)}, u32[]{:S(2)}) async-start(bf16[4,32,1024]{2,1,0:T(8,128)(2,1)} %bitcast.10), calls=%async_computation.2 | async-start | bytes 524288 | tf_op jit(solution)/shard_map/coupling/all_to_all | solution.py:248
  126.4 1.7 collective-permute-start.29
  128.0 2.0 broadcast_select_fusion.1
  130.3 1.3 collective-permute-start.28
  131.6 1.3 collective-permute-start.27
  132.9 1.3 collective-permute-start.26
  134.2 1.3 broadcast_select_fusion
  135.5 1.9 collective-permute-done.28
  137.4 3.0 %collective-permute-done.27 = bf16[32,1024]{1,0:T(8,128)(2,1)S(1)} collective-permute-done((bf16[32,1024]{1,0:T(8,128)(2,1)S(1)}, bf16[32,1024]{1,0:T(8,128)(2,1)S(1)}, u32[]{:S(2)}, u32[]{:S(2)}) %collective-permute-start.27) | collective-permute-done | bytes 65568 | tf_op jit(solution)/shard_map/coupling/ppermute | solution.py:36
  142.7 1.6 add.170
  161.1 1.3 collective-permute-start.42
  162.4 1.3 collective-permute-start.41
  164.4 34.5 %collective-permute-done.42 = bf16[32,1024]{1,0:T(8,128)(2,1)S(1)} collective-permute-done((bf16[32,1024]{1,0:T(8,128)(2,1)S(1)}, bf16[32,1024]{1,0:T(8,128)(2,1)S(1)}, u32[]{:S(2)}, u32[]{:S(2)}) %collective-permute-start.42) | collective-permute-done | bytes 65568 | tf_op jit(solution)/shard_map/child/ppermute | solution.py:36
  200.6 1.9 collective-permute-start.45
  202.6 1.3 collective-permute-start.44
  203.9 1.3 collective-permute-start.43
  206.3 7.7 %collective-permute-done.43 = bf16[32,2048]{1,0:T(8,128)(2,1)S(1)} collective-permute-done((bf16[32,2048]{1,0:T(8,128)(2,1)S(1)}, bf16[32,2048]{1,0:T(8,128)(2,1)S(1)}, u32[]{:S(2)}, u32[]{:S(2)}) %collective-permute-start.43) | collective-permute-done | bytes 131104 | tf_op jit(solution)/shard_map/child/ppermute | solution.py:36
  214.1 1.3 collective-permute-start.46
  215.4 1.9 collective-permute-done.46
  218.6 14.1 %all_to_all.33 = bf16[4,32,512]{2,1,0:T(8,128)(2,1)S(1)} all-to-all(bf16[4,32,512]{2,1,0:T(8,128)(2,1)S(1)} %bitcast.79), channel_id=1, replica_groups={{0,8,16,24},{32,40,48,56},{64,72,80,88},{96,104,112,120},{1,9,17,25},{3..., dimensions={0} | all-to-all | bytes 262144 | tf_op jit(solution)/shard_map/child/all_to_all | solution.py:282
  (155 shorter events, 38.9 us)
Async XLA Ops:
  0.6 27.4 %collective-permute-start.1 = (bf16[768,1536]{1,0:T(8,128)(2,1)}, bf16[768,1536]{1,0:T(8,128)(2,1)S(1)}, u32[]{:S(2)}, u32[]{:S(2)}) collective-permute-start(bf16[768,1536]{1,0:T(8,128)(2,1)} %refs_4_.5), channel_id=1, source_target_pairs={{0,8},{8,0},{16,24},{24,16},{32,40},{40,32},{48,56},{56,48},{64,72... | collective-permute-start | bytes 7077896 | tf_op jit(solution)/shard_map/mask/ppermute | solution.py:186
  11.1 16.9 %all-to-all-start = ((bf16[64,12,128]{2,1,0:T(8,128)(2,1)}), bf16[64,12,128]{2,1,0:T(8,128)(2,1)S(1)}, u32[]{:S(2)}, u32[]{:S(2)}) async-start(bf16[64,12,128]{2,1,0:T(8,128)(2,1)} %bitcast.76), calls=%async_computation | async-start | bytes 524288 | tf_op jit(solution)/shard_map/rhs/all_to_all | solution.py:199
  15.9 17.3 %collective-permute-start = (s32[3,6]{1,0:T(4,128)}, s32[3,6]{1,0:T(4,128)S(1)}, u32[]{:S(2)}, u32[]{:S(2)}) collective-permute-start(s32[3,6]{1,0:T(4,128)} %param.8), channel_id=1, source_target_pairs={{0,8},{8,0},{16,24},{24,16},{32,40},{40,32},{48,56},{56,48},{64,72... | collective-permute-start | bytes 224 | tf_op jit(solution)/shard_map/mask/ppermute | solution.py:187
  31.8 6.7 %collective-permute-start.3 = (bf16[2,16,768]{2,1,0:T(8,128)(2,1)S(1)}, bf16[2,16,768]{2,1,0:T(8,128)(2,1)S(1)}, u32[]{:S(2)}, u32[]{:S(2)}) collective-permute-start(bf16[2,16,768]{2,1,0:T(8,128)(2,1)S(1)} %root.9), channel_id=1, source_target_pairs={{102,101},{103,100},{110,109},{111,108},{118,117},{119,116},{126,1... | collective-permute-start | bytes 147464 | tf_op jit(solution)/shard_map/root/ppermute | solution.py:36
  32.5 6.0 %collective-permute-start.2 = (bf16[2,16,768]{2,1,0:T(8,128)(2,1)S(1)}, bf16[2,16,768]{2,1,0:T(8,128)(2,1)S(1)}, u32[]{:S(2)}, u32[]{:S(2)}) collective-permute-start(bf16[2,16,768]{2,1,0:T(8,128)(2,1)S(1)} %root.9), channel_id=1, source_target_pairs={{102,100},{103,101},{110,108},{111,109},{118,116},{119,117},{126,1... | collective-permute-start | bytes 147464 | tf_op jit(solution)/shard_map/root/ppermute | solution.py:36
  33.2 16.8 %collective-permute-start.10 = (bf16[512,1024]{1,0:T(8,128)(2,1)}, bf16[512,1024]{1,0:T(8,128)(2,1)S(1)}, u32[]{:S(2)}, u32[]{:S(2)}) collective-permute-start(bf16[512,1024]{1,0:T(8,128)(2,1)} %bitcast.2), channel_id=1, source_target_pairs={{0,8},{8,0},{16,24},{24,16},{32,40},{40,32},{48,56},{56,48},{64,72... | collective-permute-start | bytes 3145736 | tf_op jit(solution)/shard_map/root/ppermute | solution.py:224
  35.6 26.8 %collective-permute-start.11 = (bf16[512,1024]{1,0:T(8,128)(2,1)}, bf16[512,1024]{1,0:T(8,128)(2,1)S(1)}, u32[]{:S(2)}, u32[]{:S(2)}) collective-permute-start(bf16[512,1024]{1,0:T(8,128)(2,1)} %bitcast.2), channel_id=1, source_target_pairs={{0,16},{8,24},{16,0},{24,8},{32,48},{40,56},{48,32},{56,40},{1,17}... | collective-permute-start | bytes 3145736 | tf_op jit(solution)/shard_map/root/ppermute | solution.py:222
  40.3 2.0 collective-permute-start.4
  41.0 1.4 collective-permute-start.5
  41.6 2.9 %collective-permute-start.6 = (bf16[2,16,768]{2,1,0:T(8,128)(2,1)S(1)}, bf16[2,16,768]{2,1,0:T(8,128)(2,1)S(1)}, u32[]{:S(2)}, u32[]{:S(2)}) collective-permute-start(bf16[2,16,768]{2,1,0:T(8,128)(2,1)S(1)} %add_convert_fusion.13.refs_2_.refs_6_), channel_id=1, source_target_pairs={{100,98},{101,99},{108,106},{109,107},{116,114},{117,115},{124,122... | collective-permute-start | bytes 147464 | tf_op jit(solution)/shard_map/root/ppermute | solution.py:36
  44.6 3.7 %collective-permute-start.8 = (bf16[2,16,768]{2,1,0:T(8,128)(2,1)S(1)}, bf16[2,16,768]{2,1,0:T(8,128)(2,1)S(1)}, u32[]{:S(2)}, u32[]{:S(2)}) collective-permute-start(bf16[2,16,768]{2,1,0:T(8,128)(2,1)S(1)} %add_convert_fusion.12.refs_2_), channel_id=1, source_target_pairs={{68,67},{69,66},{76,75},{77,74},{84,83},{85,82},{92,91},{93,90},{1... | collective-permute-start | bytes 147464 | tf_op jit(solution)/shard_map/root/ppermute | solution.py:36
  45.2 3.0 %collective-permute-start.7 = (bf16[2,16,768]{2,1,0:T(8,128)(2,1)S(1)}, bf16[2,16,768]{2,1,0:T(8,128)(2,1)S(1)}, u32[]{:S(2)}, u32[]{:S(2)}) collective-permute-start(bf16[2,16,768]{2,1,0:T(8,128)(2,1)S(1)} %add_convert_fusion.12.refs_2_), channel_id=1, source_target_pairs={{68,66},{69,67},{76,74},{77,75},{84,82},{85,83},{92,90},{93,91},{9... | collective-permute-start | bytes 147464 | tf_op jit(solution)/shard_map/root/ppermute | solution.py:36
  47.6 0.7 collective-permute-start.9
  62.4 4.8 %collective-permute-start.12 = (bf16[16,1536]{1,0:T(8,128)(2,1)S(1)}, bf16[16,1536]{1,0:T(8,128)(2,1)S(1)}, u32[]{:S(2)}, u32[]{:S(2)}) collective-permute-start(bf16[16,1536]{1,0:T(8,128)(2,1)S(1)} %root.13), channel_id=1, source_target_pairs={{66,34},{67,35},{74,42},{75,43},{82,50},{83,51},{90,58},{91,59},{9... | collective-permute-start | bytes 147464 | tf_op jit(solution)/shard_map/root/ppermute | solution.py:36
  63.1 4.1 %collective-permute-start.13 = (bf16[16,1536]{1,0:T(8,128)(2,1)S(1)}, bf16[16,1536]{1,0:T(8,128)(2,1)S(1)}, u32[]{:S(2)}, u32[]{:S(2)}) collective-permute-start(bf16[16,1536]{1,0:T(8,128)(2,1)S(1)} %root.13), channel_id=1, source_target_pairs={{66,50},{67,51},{74,58},{75,59},{82,34},{83,35},{90,42},{91,43},{1... | collective-permute-start | bytes 147464 | tf_op jit(solution)/shard_map/root/ppermute | solution.py:36
  63.8 5.7 %collective-permute-start.14 = (bf16[2,16,768]{2,1,0:T(8,128)(2,1)S(1)}, bf16[2,16,768]{2,1,0:T(8,128)(2,1)S(1)}, u32[]{:S(2)}, u32[]{:S(2)}) collective-permute-start(bf16[2,16,768]{2,1,0:T(8,128)(2,1)S(1)} %add_convert_fusion.11.refs_2_.refs_6_), channel_id=1, source_target_pairs={{66,64},{67,65},{74,72},{75,73},{82,80},{83,81},{90,88},{91,89},{1... | collective-permute-start | bytes 147464 | tf_op jit(solution)/shard_map/root/ppermute | solution.py:36
  64.4 10.5 %collective-permute-start.18 = (bf16[512,1024]{1,0:T(8,128)(2,1)S(1)}, bf16[512,1024]{1,0:T(8,128)(2,1)S(1)}, u32[]{:S(2)}, u32[]{:S(2)}) collective-permute-start(bf16[512,1024]{1,0:T(8,128)(2,1)S(1)} %collective-permute-done.11), channel_id=1, source_target_pairs={{0,8},{8,0},{16,24},{24,16},{32,40},{40,32},{48,56},{56,48},{1,9},... | collective-permute-start | bytes 3145736 | tf_op jit(solution)/shard_map/root/ppermute | solution.py:216
  69.5 3.7 %collective-permute-start.16 = (bf16[2,16,768]{2,1,0:T(8,128)(2,1)S(1)}, bf16[2,16,768]{2,1,0:T(8,128)(2,1)S(1)}, u32[]{:S(2)}, u32[]{:S(2)}) collective-permute-start(bf16[2,16,768]{2,1,0:T(8,128)(2,1)S(1)} %add_convert_fusion.10.refs_2_), channel_id=1, source_target_pairs={{34,33},{35,32},{42,41},{43,40},{50,49},{51,48},{58,57},{59,56},{6... | collective-permute-start | bytes 147464 | tf_op jit(solution)/shard_map/root/ppermute | solution.py:36
  70.1 3.0 %collective-permute-start.15 = (bf16[2,16,768]{2,1,0:T(8,128)(2,1)S(1)}, bf16[2,16,768]{2,1,0:T(8,128)(2,1)S(1)}, u32[]{:S(2)}, u32[]{:S(2)}) collective-permute-start(bf16[2,16,768]{2,1,0:T(8,128)(2,1)S(1)} %add_convert_fusion.10.refs_2_), channel_id=1, source_target_pairs={{34,32},{35,33},{42,40},{43,41},{50,48},{51,49},{58,56},{59,57},{6... | collective-permute-start | bytes 147464 | tf_op jit(solution)/shard_map/root/ppermute | solution.py:36
  72.5 0.7 collective-permute-start.17
  74.9 30.1 %collective-permute-start.25 = (bf16[512,1024]{1,0:T(8,128)(2,1)}, bf16[512,1024]{1,0:T(8,128)(2,1)}, u32[]{:S(2)}, u32[]{:S(2)}) collective-permute-start(bf16[512,1024]{1,0:T(8,128)(2,1)} %bitcast.2), channel_id=1, source_target_pairs={{64,80},{72,88},{80,64},{88,72},{96,112},{104,120},{112,96},{120,1... | collective-permute-start | bytes 3145736 | tf_op jit(solution)/shard_map/root/ppermute | solution.py:222
  76.6 13.7 %collective-permute-start.19 = (bf16[16,1536]{1,0:T(8,128)(2,1)S(1)}, bf16[16,1536]{1,0:T(8,128)(2,1)S(1)}, u32[]{:S(2)}, u32[]{:S(2)}) collective-permute-start(bf16[16,1536]{1,0:T(8,128)(2,1)S(1)} %root.16), channel_id=1, source_target_pairs={{32,0},{33,1},{40,8},{41,9},{48,16},{49,17},{56,24},{57,25},{160,1... | collective-permute-start | bytes 147464 | tf_op jit(solution)/shard_map/root/ppermute | solution.py:36
  77.9 14.5 %collective-permute-start.20 = (bf16[16,1536]{1,0:T(8,128)(2,1)S(1)}, bf16[16,1536]{1,0:T(8,128)(2,1)S(1)}, u32[]{:S(2)}, u32[]{:S(2)}) collective-permute-start(bf16[16,1536]{1,0:T(8,128)(2,1)S(1)} %root.16), channel_id=1, source_target_pairs={{32,16},{33,17},{40,24},{41,25},{48,0},{49,1},{56,8},{57,9},{160,1... | collective-permute-start | bytes 147464 | tf_op jit(solution)/shard_map/root/ppermute | solution.py:36
  94.6 6.7 %collective-permute-start.23 = (bf16[2,16,768]{2,1,0:T(8,128)(2,1)S(1)}, bf16[2,16,768]{2,1,0:T(8,128)(2,1)S(1)}, u32[]{:S(2)}, u32[]{:S(2)}) collective-permute-start(bf16[2,16,768]{2,1,0:T(8,128)(2,1)S(1)} %root.17), channel_id=1, source_target_pairs={{0,1},{1,0},{8,9},{9,8},{16,17},{17,16},{24,25},{25,24},{128,129},... | collective-permute-start | bytes 147464 | tf_op jit(solution)/shard_map/root/ppermute | solution.py:36
  98.7 2.6 %collective-permute-start.22 = (bf16[2,16,768]{2,1,0:T(8,128)(2,1)S(1)}, bf16[2,16,768]{2,1,0:T(8,128)(2,1)S(1)}, u32[]{:S(2)}, u32[]{:S(2)}) collective-permute-start(bf16[2,16,768]{2,1,0:T(8,128)(2,1)S(1)} %root.17), channel_id=1, source_target_pairs={{0,7},{1,6},{8,15},{9,14},{16,23},{17,22},{24,31},{25,30},{34,35},... | collective-permute-start | bytes 147464 | tf_op jit(solution)/shard_map/root/ppermute | solution.py:36
  100.0 2.6 %collective-permute-start.21 = (bf16[2,16,768]{2,1,0:T(8,128)(2,1)S(1)}, bf16[2,16,768]{2,1,0:T(8,128)(2,1)S(1)}, u32[]{:S(2)}, u32[]{:S(2)}) collective-permute-start(bf16[2,16,768]{2,1,0:T(8,128)(2,1)S(1)} %root.17), channel_id=1, source_target_pairs={{0,6},{1,7},{8,14},{9,15},{16,22},{17,23},{24,30},{25,31},{32,38},... | collective-permute-start | bytes 147464 | tf_op jit(solution)/shard_map/root/ppermute | solution.py:36
  102.6 2.5 %collective-permute-start.24 = (bf16[2,16,768]{2,1,0:T(8,128)(2,1)S(1)}, bf16[2,16,768]{2,1,0:T(8,128)(2,1)S(1)}, u32[]{:S(2)}, u32[]{:S(2)}) collective-permute-start(bf16[2,16,768]{2,1,0:T(8,128)(2,1)S(1)} %add_convert_fusion.8), channel_id=1, source_target_pairs={{0,2},{1,3},{8,10},{9,11},{16,18},{17,19},{24,26},{25,27},{6,4},{7... | collective-permute-start | bytes 147464 | tf_op jit(solution)/shard_map/root/ppermute | solution.py:36
  120.7 9.5 %all-to-all-start.2 = ((bf16[4,32,1024]{2,1,0:T(8,128)(2,1)}), bf16[4,32,1024]{2,1,0:T(8,128)(2,1)S(1)}, u32[]{:S(2)}, u32[]{:S(2)}) async-start(bf16[4,32,1024]{2,1,0:T(8,128)(2,1)} %bitcast.10), calls=%async_computation.2 | async-start | bytes 524288 | tf_op jit(solution)/shard_map/coupling/all_to_all | solution.py:248
  126.4 16.3 %collective-permute-start.29 = (bf16[512,1024]{1,0:T(8,128)(2,1)}, bf16[512,1024]{1,0:T(8,128)(2,1)}, u32[]{:S(2)}, u32[]{:S(2)}) collective-permute-start(bf16[512,1024]{1,0:T(8,128)(2,1)} %collective-permute-done.25), channel_id=1, source_target_pairs={{64,72},{72,64},{80,88},{88,80},{96,104},{104,96},{112,120},{120,1... | collective-permute-start | bytes 3145736 | tf_op jit(solution)/shard_map/coupling/ppermute | solution.py:239
  130.3 7.2 %collective-permute-start.28 = (bf16[32,1024]{1,0:T(8,128)(2,1)S(1)}, bf16[32,1024]{1,0:T(8,128)(2,1)S(1)}, u32[]{:S(2)}, u32[]{:S(2)}) collective-permute-start(bf16[32,1024]{1,0:T(8,128)(2,1)S(1)} %reduce_sum.22), channel_id=1, source_target_pairs={{96,0},{97,1},{104,8},{105,9},{112,16},{113,17},{120,24},{121,25},... | collective-permute-start | bytes 196616 | tf_op jit(solution)/shard_map/coupling/ppermute | solution.py:36
  131.6 8.9 %collective-permute-start.27 = (bf16[32,1024]{1,0:T(8,128)(2,1)S(1)}, bf16[32,1024]{1,0:T(8,128)(2,1)S(1)}, u32[]{:S(2)}, u32[]{:S(2)}) collective-permute-start(bf16[32,1024]{1,0:T(8,128)(2,1)S(1)} %reduce_sum.22), channel_id=1, source_target_pairs={{64,0},{65,1},{72,8},{73,9},{80,16},{81,17},{88,24},{89,25},{98,34... | collective-permute-start | bytes 196616 | tf_op jit(solution)/shard_map/coupling/ppermute | solution.py:36
  132.9 7.6 %collective-permute-start.26 = (bf16[32,1024]{1,0:T(8,128)(2,1)S(1)}, bf16[32,1024]{1,0:T(8,128)(2,1)S(1)}, u32[]{:S(2)}, u32[]{:S(2)}) collective-permute-start(bf16[32,1024]{1,0:T(8,128)(2,1)S(1)} %reduce_sum.22), channel_id=1, source_target_pairs={{32,0},{33,1},{40,8},{41,9},{48,16},{49,17},{56,24},{57,25},{66,34... | collective-permute-start | bytes 196616 | tf_op jit(solution)/shard_map/coupling/ppermute | solution.py:36
  144.8 1.4 collective-permute-start.31
  145.5 0.7 collective-permute-start.30
  147.4 2.0 collective-permute-start.32
  148.7 2.4 %collective-permute-start.33 = (bf16[32,2048]{1,0:T(8,128)(2,1)S(1)}, bf16[32,2048]{1,0:T(8,128)(2,1)S(1)}, u32[]{:S(2)}, u32[]{:S(2)}) collective-permute-start(bf16[32,2048]{1,0:T(8,128)(2,1)S(1)} %add_convert_fusion.6), channel_id=1, source_target_pairs={{100,98},{101,99},{108,106},{109,107},{116,114},{117,115},{124,122... | collective-permute-start | bytes 393224 | tf_op jit(solution)/shard_map/child/ppermute | solution.py:36
  151.2 1.5 collective-permute-start.35
  151.9 0.9 collective-permute-start.34
  154.0 2.7 %collective-permute-start.36 = (bf16[32,1024]{1,0:T(8,128)(2,1)S(1)}, bf16[32,1024]{1,0:T(8,128)(2,1)S(1)}, u32[]{:S(2)}, u32[]{:S(2)}) collective-permute-start(bf16[32,1024]{1,0:T(8,128)(2,1)S(1)} %fusion.5), channel_id=1, source_target_pairs={{66,34},{67,35},{74,42},{75,43},{82,50},{83,51},{90,58},{91,59},{9... | collective-permute-start | bytes 196616 | tf_op jit(solution)/shard_map/child/ppermute | solution.py:36
  154.7 2.0 collective-permute-start.37
  156.0 2.4 %collective-permute-start.38 = (bf16[32,2048]{1,0:T(8,128)(2,1)S(1)}, bf16[32,2048]{1,0:T(8,128)(2,1)S(1)}, u32[]{:S(2)}, u32[]{:S(2)}) collective-permute-start(bf16[32,2048]{1,0:T(8,128)(2,1)S(1)} %add_convert_fusion.4), channel_id=1, source_target_pairs={{66,64},{67,65},{74,72},{75,73},{82,80},{83,81},{90,88},{91,89},{1... | collective-permute-start | bytes 393224 | tf_op jit(solution)/shard_map/child/ppermute | solution.py:36
  158.5 1.4 collective-permute-start.40
  161.1 37.7 %collective-permute-start.42 = (bf16[32,1024]{1,0:T(8,128)(2,1)S(1)}, bf16[32,1024]{1,0:T(8,128)(2,1)S(1)}, u32[]{:S(2)}, u32[]{:S(2)}) collective-permute-start(bf16[32,1024]{1,0:T(8,128)(2,1)S(1)} %fusion.15), channel_id=1, source_target_pairs={{64,0},{65,1},{72,8},{73,9},{80,16},{81,17},{88,24},{89,25},{192,1... | collective-permute-start | bytes 196616 | tf_op jit(solution)/shard_map/child/ppermute | solution.py:36
  162.4 36.4 %collective-permute-start.41 = (bf16[32,1024]{1,0:T(8,128)(2,1)S(1)}, bf16[32,1024]{1,0:T(8,128)(2,1)S(1)}, u32[]{:S(2)}, u32[]{:S(2)}) collective-permute-start(bf16[32,1024]{1,0:T(8,128)(2,1)S(1)} %fusion.15), channel_id=1, source_target_pairs={{32,0},{33,1},{40,8},{41,9},{48,16},{49,17},{56,24},{57,25},{160,1... | collective-permute-start | bytes 196616 | tf_op jit(solution)/shard_map/child/ppermute | solution.py:36
  200.6 5.7 %collective-permute-start.45 = (bf16[32,2048]{1,0:T(8,128)(2,1)S(1)}, bf16[32,2048]{1,0:T(8,128)(2,1)S(1)}, u32[]{:S(2)}, u32[]{:S(2)}) collective-permute-start(bf16[32,2048]{1,0:T(8,128)(2,1)S(1)} %maximum_select_fusion.3), channel_id=1, source_target_pairs={{0,1},{1,0},{8,9},{9,8},{16,17},{17,16},{24,25},{25,24},{128,129},... | collective-permute-start | bytes 393224 | tf_op jit(solution)/shard_map/child/ppermute | solution.py:36
  202.6 3.8 %collective-permute-start.44 = (bf16[32,2048]{1,0:T(8,128)(2,1)S(1)}, bf16[32,2048]{1,0:T(8,128)(2,1)S(1)}, u32[]{:S(2)}, u32[]{:S(2)}) collective-permute-start(bf16[32,2048]{1,0:T(8,128)(2,1)S(1)} %maximum_select_fusion.3), channel_id=1, source_target_pairs={{0,7},{1,6},{8,15},{9,14},{16,23},{17,22},{24,31},{25,30},{34,35},... | collective-permute-start | bytes 393224 | tf_op jit(solution)/shard_map/child/ppermute | solution.py:36
  203.9 10.1 %collective-permute-start.43 = (bf16[32,2048]{1,0:T(8,128)(2,1)S(1)}, bf16[32,2048]{1,0:T(8,128)(2,1)S(1)}, u32[]{:S(2)}, u32[]{:S(2)}) collective-permute-start(bf16[32,2048]{1,0:T(8,128)(2,1)S(1)} %maximum_select_fusion.3), channel_id=1, source_target_pairs={{0,6},{1,7},{8,14},{9,15},{16,22},{17,23},{24,30},{25,31},{32,38},... | collective-permute-start | bytes 393224 | tf_op jit(solution)/shard_map/child/ppermute | solution.py:36
  214.1 3.2 %collective-permute-start.46 = (bf16[32,2048]{1,0:T(8,128)(2,1)S(1)}, bf16[32,2048]{1,0:T(8,128)(2,1)S(1)}, u32[]{:S(2)}, u32[]{:S(2)}) collective-permute-start(bf16[32,2048]{1,0:T(8,128)(2,1)S(1)} %add_convert_fusion.1), channel_id=1, source_target_pairs={{0,2},{1,3},{8,10},{9,11},{16,18},{17,19},{24,26},{25,27},{6,4},{7... | collective-permute-start | bytes 393224 | tf_op jit(solution)/shard_map/child/ppermute | solution.py:36
  (9 other events, 175.6 us)
